TPU v7x, 32 devices: a whole 2x2x4 slice. The times are simulated.
32 devices in a mesh: dp: 4 (over x, core), row: 2 (over y), col: 4 (over z).
Axes of the slice: x: 2, y: 2, z: 4, core: 2. Of those that a mesh axis runs over, the one named last changes fastest.
Arguments:
- inputs: bfloat16 [768, 4096], P('dp', 'row'), may hold values from -6 to 6
- weight: bfloat16 [4096, 14336], P('row', 'col'), may hold values from -0.09375 to 0.09375
- cotangent: bfloat16 [768, 14336], P(('dp', 'row'), 'col'), may hold values from -6 to 6
- anchor: bfloat16 [4096, 14336], P(('row', 'dp'), 'col'), may hold values from -0.09375 to 0.09375
- first_moment: float32 [4096, 14336], P(('row', 'dp'), 'col'), may hold values from -0.15625 to 0.15625
- second_moment: float32 [4096, 14336], P(('row', 'dp'), 'col'), may hold values from 1e-06 to 0.0001
Outputs:
- outputs: bfloat16 [768, 14336], P(('dp', 'row'), 'col')
- input_grad: bfloat16 [768, 4096], P(('dp', 'col'), 'row')
- new_weight: bfloat16 [4096, 14336], P(('row', 'dp'), 'col')
- new_first: float32 [4096, 14336], P(('row', 'dp'), 'col')
- new_second: float32 [4096, 14336], P(('row', 'dp'), 'col')
All inputs are finite; a program needn't handle non-finite values.
Results may differ from a plain program's by a relative error of at most 0.013.
Values may be sent and summed in bfloat16 or wider, within the bound.
No kernel may reach another device: no remote copies, remote signals or barrier semaphores. Data moves between devices by JAX's collectives and lax.ppermute only.
A program may use at most 128 MiB of HBM per device.

v0:
```python
import jax
import jax.numpy as jnp
from jax import lax
from jax.sharding import PartitionSpec as P

beta_one = 0.9
beta_two = 0.999
learn_rate = 0.002
anchor_pull = 0.5
epsilon = 1e-08
step_count = 100.0


def forward_pass(inputs, weight):
    return lax.psum_scatter(
        jnp.dot(inputs, weight, preferred_element_type=jnp.float32).astype(jnp.bfloat16),
        "row",
        scatter_dimension=0,
        tiled=True,
    )


def gather_cotangent(cotangent):
    return lax.all_gather(cotangent, "row", axis=0, tiled=True)


def per_device(inputs, weight, cotangent, anchor, first_moment, second_moment):
    outputs = forward_pass(inputs, weight)
    gathered = gather_cotangent(cotangent)
    input_grad = lax.psum_scatter(
        lax.dot_general(
            gathered, weight, (((1,), (1,)), ((), ())), preferred_element_type=jnp.float32
        ).astype(jnp.bfloat16),
        "col",
        scatter_dimension=0,
        tiled=True,
    )
    slice_rows = weight.shape[0] // lax.axis_size("dp")
    full_grad = lax.dot_general(
        inputs, gathered, (((0,), (0,)), ((), ())), preferred_element_type=jnp.float32
    )
    summed = lax.psum_scatter(
        full_grad.astype(jnp.bfloat16), "dp", scatter_dimension=0, tiled=True
    ).astype(jnp.float32)
    tokens_all = inputs.shape[0] * lax.axis_size("dp")
    own_start = lax.axis_index("dp") * slice_rows
    current = lax.dynamic_slice_in_dim(weight, own_start, slice_rows, 0).astype(jnp.float32)
    grad = summed / tokens_all + anchor_pull * (current - anchor.astype(jnp.float32))
    new_first = beta_one * first_moment + (1.0 - beta_one) * grad
    new_second = beta_two * second_moment + (1.0 - beta_two) * grad * grad
    mhat = new_first / (1.0 - beta_one**step_count)
    vhat = new_second / (1.0 - beta_two**step_count)
    new_weight = (current - learn_rate * mhat / (jnp.sqrt(vhat) + epsilon)).astype(jnp.bfloat16)
    return (outputs, input_grad, new_weight, new_first, new_second)


def solution(mesh):
    in_specs = (
        P("dp", "row"),
        P("row", "col"),
        P(("dp", "row"), "col"),
        P(("row", "dp"), "col"),
        P(("row", "dp"), "col"),
        P(("row", "dp"), "col"),
    )
    out_specs = (
        P(("dp", "row"), "col"),
        P(("dp", "col"), "row"),
        P(("row", "dp"), "col"),
        P(("row", "dp"), "col"),
        P(("row", "dp"), "col"),
    )
    return jax.shard_map(
        per_device, mesh=mesh, in_specs=in_specs, out_specs=out_specs, check_vma=False
    )
```

profile of v0, /device:TPU:0, one launch (start us, length us, event | category | flops | bytes accessed | tf_op | source)
XLA Modules:
  0.0 218.6 jit_solution(9244404194577523754)
XLA Ops:
  7.2 0.0 copy-start
  7.2 0.0 all-gather.2.cloned.1.call-start
  7.2 0.7 all-gather.2.cloned.1.call-update
  7.9 0.0 reduce-scatter.8.cloned.1.call-start
  8.0 29.3 %all-gather.2.cloned.1.call-done = bf16[192,3584]{1,0:T(8,128)(2,1)} async-done(((bf16[96,3584]{1,0:T(8,128)(2,1)}), bf16[192,3584]{1,0:T(8,128)(2,1)}) %all-gather.2.cloned.1.call-update) | async-done | bytes 1376272 | tf_op jit(solution)/shard_map/all_gather | solution.py:24
  37.3 0.0 copy-done
  37.3 8.7 %convolution_convert_fusion = bf16[2048,3584]{1,0:T(8,128)(2,1)} fusion(bf16[192,2048]{1,0:T(8,128)(2,1)S(1)} %copy-done, bf16[192,3584]{1,0:T(8,128)(2,1)} %all-gather.2.cloned.1.call-done), kind=kOutput, calls=%fused_computation | convolution fusion | flops 2825912320 | bytes 16842752 | tf_op jit(solution)/shard_map/dot_general | solution.py:39
  45.9 0.0 reduce-scatter.8.cloned.1.call-update
  46.0 0.0 copy-start.2
  46.0 0.0 reduce-scatter.4.cloned.1.call-start
  46.0 9.4 %convolution_convert_fusion.1 = bf16[192,3584]{1,0:T(8,128)(2,1)} fusion(bf16[192,2048]{1,0:T(8,128)(2,1)S(1)} %copy-done, bf16[2048,3584]{1,0:T(8,128)(2,1)} %param.7), kind=kOutput, calls=%fused_computation.9 | convolution fusion | flops 2819260416 | bytes 16842752 | tf_op jit(solution)/shard_map/dot_general | solution.py:16
  55.4 0.0 reduce-scatter.4.cloned.1.call-update
  55.4 0.0 reduce-scatter.6.cloned.1.call-start
  55.5 0.0 copy-done.2
  55.5 14.4 %convolution_convert_fusion.2 = bf16[192,2048]{1,0:T(8,128)(2,1)} fusion(bf16[192,3584]{1,0:T(8,128)(2,1)S(1)} %copy-done.2, bf16[2048,3584]{1,0:T(8,128)(2,1)} %param.7), kind=kOutput, calls=%fused_computation.10 | convolution fusion | flops 2818965504 | bytes 16842752 | tf_op jit(solution)/shard_map/dot_general | solution.py:31
  69.9 0.0 reduce-scatter.6.cloned.1.call-update
  69.9 89.1 %reduce-scatter.8.cloned.1.call-done = bf16[512,3584]{1,0:T(8,128)(2,1)} async-done(((bf16[2048,3584]{1,0:T(8,128)(2,1)}), bf16[512,3584]{1,0:T(8,128)(2,1)}) %reduce-scatter.8.cloned.1.call-update) | async-done | bytes 3670032 | tf_op jit(solution)/shard_map/reduce_scatter | solution.py:42
  159.1 0.0 copy-start.1
  159.1 17.1 %fusion.2 = (bf16[512,3584]{1,0:T(8,128)(2,1)}, f32[512,3584]{1,0:T(8,128)}, f32[512,3584]{1,0:T(8,128)}) fusion(bf16[2048,3584]{1,0:T(8,128)(2,1)} %param.7, s32[]{:T(128)S(6)} %select_n.3, bf16[512,3584]{1,0:T(8,128)(2,1)} %param.9, bf16[512,3584]{1,0:T(8,128)(2,1)} %reduce-scatter.8.cloned.1.call-done, f32[512,3584]{1,0:T(8,128)} %param.10, ...), kind=kLoop, calls=%fused_computation.6 | loop fusion | flops 36700160 | bytes 44040196 | tf_op jit(solution)/shard_map/convert_element_type | solution.py:53
  176.2 9.7 %reduce-scatter.4.cloned.1.call-done = bf16[96,3584]{1,0:T(8,128)(2,1)} async-done(((bf16[192,3584]{1,0:T(8,128)(2,1)}), bf16[96,3584]{1,0:T(8,128)(2,1)}) %reduce-scatter.4.cloned.1.call-update) | async-done | bytes 688144 | tf_op jit(solution)/shard_map/reduce_scatter | solution.py:15
  185.9 26.2 %reduce-scatter.6.cloned.1.call-done = bf16[48,2048]{1,0:T(8,128)(2,1)} async-done(((bf16[192,2048]{1,0:T(8,128)(2,1)}), bf16[48,2048]{1,0:T(8,128)(2,1)}) %reduce-scatter.6.cloned.1.call-update) | async-done | bytes 196624 | tf_op jit(solution)/shard_map/reduce_scatter | solution.py:30
  212.0 0.0 copy-done.1
Async XLA Ops:
  7.2 30.1 %copy-start = (bf16[192,2048]{1,0:T(8,128)(2,1)S(1)}, bf16[192,2048]{1,0:T(8,128)(2,1)}, u32[]{:S(2)}) copy-start(bf16[192,2048]{1,0:T(8,128)(2,1)} %param.6) | copy-start | bytes 2359300
  7.2 30.1 %all-gather.2.cloned.1.call-start = ((), (), s32[]{:S(2)}) async-start(), calls=%async_computation.4 | async-start | bytes 2064384 | tf_op jit(solution)/shard_map/all_gather | solution.py:24
  7.9 151.2 %reduce-scatter.8.cloned.1.call-start = ((), (), s32[]{:S(2)}) async-start(), calls=%async_computation.6 | async-start | bytes 18350080 | tf_op jit(solution)/shard_map/reduce_scatter | solution.py:42
  46.0 9.5 %copy-start.2 = (bf16[192,3584]{1,0:T(8,128)(2,1)S(1)}, bf16[192,3584]{1,0:T(8,128)(2,1)}, u32[]{:S(2)}) copy-start(bf16[192,3584]{1,0:T(8,128)(2,1)} %all-gather.2.cloned.1.call-done) | copy-start | bytes 4128772
  46.0 139.9 %reduce-scatter.4.cloned.1.call-start = ((), (), s32[]{:S(2)}) async-start(), calls=%async_computation.3 | async-start | bytes 2064384 | tf_op jit(solution)/shard_map/reduce_scatter | solution.py:15
  55.4 156.6 %reduce-scatter.6.cloned.1.call-start = ((), (), s32[]{:S(2)}) async-start(), calls=%async_computation.5 | async-start | bytes 983040 | tf_op jit(solution)/shard_map/reduce_scatter | solution.py:30
  159.1 53.0 %copy-start.1 = (bf16[192,2048]{1,0:T(8,128)(2,1)S(1)}, bf16[192,2048]{1,0:T(8,128)(2,1)}, u32[]{:S(2)}) copy-start(bf16[192,2048]{1,0:T(8,128)(2,1)} %param.6) | copy-start | bytes 2359300
Sparse Core Ops, SparseCore 0:
  9.6 27.6 all-gather.1
  46.1 112.9 reduce-scatter.7
  161.9 23.9 reduce-scatter.3
  188.7 23.2 reduce-scatter.5
where the time goes:
time: 219 us
  waiting for transfers between devices  155 us (71%)
  matrix products  32.4 us (15%)
  other arithmetic  17.1 us (8%)
  between operations  13.8 us (6%)
    reduce_scatter x1, waiting for transfers between devices, per_device(): lax.psum_scatter(full_grad.astype(jnp.bfloat16), 'dp', scatter_dimension=...  89.1 us
    all_gather x1, waiting for transfers between devices, gather_cotangent(): return lax.all_gather(cotangent, 'row', axis=0, tiled=True)  29.3 us
    reduce_scatter x1, waiting for transfers between devices, per_device(): lax.psum_scatter(lax.dot_general(gathered, weight, (((1,), (1,)), ((), ()...  26.2 us
    convert_element_type x1, other arithmetic, per_device(): (current - learn_rate * mhat / (jnp.sqrt(vhat) + epsilon)).astype(jnp.bfl...  17.1 us
    dot_general x1, matrix products, per_device(): lax.dot_general(gathered, weight, (((1,), (1,)), ((), ())), preferred_ele...  14.4 us
    reduce_scatter x1, waiting for transfers between devices, forward_pass(): lax.psum_scatter(jnp.dot(inputs, weight, preferred_element_type=jnp.float...  9.66 us
    dot_general x1, matrix products, forward_pass(): jnp.dot(inputs, weight, preferred_element_type=jnp.float32)  9.37 us
    dot_general x1, matrix products, per_device(): lax.dot_general(inputs, gathered, (((0,), (0,)), ((), ())), preferred_ele...  8.65 us
  transfers between devices with their start and end apart: 4, of which 4 were waited for; matrix products, arithmetic and copies ran while one was open for 19% of the time, Pallas kernels for 0%

commit v1 on v0

v1 whole, which is shorter than its diff:
```python
import jax
import jax.numpy as jnp
from jax import lax
from jax.sharding import PartitionSpec as P

beta_one = 0.9
beta_two = 0.999
learn_rate = 0.002
anchor_pull = 0.5
epsilon = 1e-08
step_count = 100.0


def per_device(inputs, weight, cotangent, anchor, first_moment, second_moment):
    n_dp, n_row, n_col = (lax.axis_size(a) for a in ("dp", "row", "col"))
    dp, row, col = (lax.axis_index(a) for a in ("dp", "row", "col"))
    cores = 2 if n_dp % 2 == 0 else 1
    chips = n_dp // cores
    tokens = inputs.shape[0]
    own_tokens = cotangent.shape[0]
    slice_rows = weight.shape[0] // n_dp

    def along(axis, n, shift):
        return lambda a: lax.ppermute(a, axis, [(i, (i + shift) % n) for i in range(n)])

    def chip_shift(shift):
        return lambda a: lax.ppermute(
            a, "dp", [(i, (i + shift * cores) % n_dp) for i in range(n_dp)]
        )

    def swap_cores(a):
        return lax.ppermute(a, "dp", [(i, i ^ 1) for i in range(n_dp)])

    def in_row_order(pieces):
        whole = jnp.zeros((n_row * own_tokens, cotangent.shape[1]), cotangent.dtype)
        for shift, piece in enumerate(pieces):
            start = lax.rem(row - shift + n_row, n_row) * own_tokens
            whole = lax.dynamic_update_slice_in_dim(whole, piece, start, 0)
        return whole

    by_row = [cotangent] + [along("row", n_row, s)(cotangent) for s in range(1, n_row)]
    mine = {(0, s): p for s, p in enumerate(by_row)}
    for c in range(1, chips):
        for s, p in enumerate(by_row):
            mine[c, s] = chip_shift(c)(p)

    def columns_for(peer):
        return lax.dynamic_slice_in_dim(inputs, peer * slice_rows, slice_rows, 1)

    held = {0: columns_for(dp)}
    for s in range(1, n_dp):
        held[s] = along("dp", n_dp, s)(columns_for(lax.rem(dp + s, n_dp)))

    part = jnp.dot(inputs, weight, preferred_element_type=jnp.float32)
    outputs = lax.dynamic_slice_in_dim(part, row * own_tokens, own_tokens, 0)
    for s in range(1, n_row):
        start = lax.rem(row + s, n_row) * own_tokens
        sent = lax.dynamic_slice_in_dim(part.astype(jnp.bfloat16), start, own_tokens, 0)
        outputs = outputs + along("row", n_row, s)(sent).astype(jnp.float32)
    outputs = outputs.astype(jnp.bfloat16)

    gathered = in_row_order(by_row)
    gpart = lax.dot_general(
        gathered, weight, (((1,), (1,)), ((), ())), preferred_element_type=jnp.float32
    )
    share = tokens // n_col
    input_grad = lax.dynamic_slice_in_dim(gpart, col * share, share, 0)
    for s in range(1, n_col):
        start = lax.rem(col + s, n_col) * share
        sent = lax.dynamic_slice_in_dim(gpart.astype(jnp.bfloat16), start, share, 0)
        input_grad = input_grad + along("col", n_col, s)(sent).astype(jnp.float32)
    input_grad = input_grad.astype(jnp.bfloat16)

    lefts, rights = [], []
    for c in range(chips):
        for other in range(cores):
            pieces = [mine[c, s] for s in range(n_row)]
            if other:
                pieces = [swap_cores(p) for p in pieces]
            rights.append(gathered if (c, other) == (0, 0) else in_row_order(pieces))
            came = lax.rem((dp ^ 1 if other else dp) - c * cores + n_dp, n_dp)
            shift = lax.rem(dp - came + n_dp, n_dp)
            lefts.append(lax.dynamic_index_in_dim(jnp.stack([held[k] for k in range(n_dp)]), shift, 0, keepdims=False))
    summed = lax.dot_general(
        jnp.concatenate(lefts, 0),
        jnp.concatenate(rights, 0),
        (((0,), (0,)), ((), ())),
        preferred_element_type=jnp.float32,
    )

    tokens_all = tokens * n_dp
    current = lax.dynamic_slice_in_dim(weight, dp * slice_rows, slice_rows, 0).astype(jnp.float32)
    grad = summed / tokens_all + anchor_pull * (current - anchor.astype(jnp.float32))
    new_first = beta_one * first_moment + (1.0 - beta_one) * grad
    new_second = beta_two * second_moment + (1.0 - beta_two) * grad * grad
    mhat = new_first / (1.0 - beta_one**step_count)
    vhat = new_second / (1.0 - beta_two**step_count)
    new_weight = (current - learn_rate * mhat / (jnp.sqrt(vhat) + epsilon)).astype(jnp.bfloat16)
    return (outputs, input_grad, new_weight, new_first, new_second)


def solution(mesh):
    in_specs = (
        P("dp", "row"),
        P("row", "col"),
        P(("dp", "row"), "col"),
        P(("row", "dp"), "col"),
        P(("row", "dp"), "col"),
        P(("row", "dp"), "col"),
    )
    out_specs = (
        P(("dp", "row"), "col"),
        P(("dp", "col"), "row"),
        P(("row", "dp"), "col"),
        P(("row", "dp"), "col"),
        P(("row", "dp"), "col"),
    )
    return jax.shard_map(
        per_device, mesh=mesh, in_specs=in_specs, out_specs=out_specs, check_vma=False
    )
```

time: 219 us -> 85.5 us (0.39)
  waiting for transfers between devices: 155 us -> 20.9 us
  starting transfers between devices: 0.16 us -> 15.8 us
  other arithmetic: 17.1 us -> 2.78 us
  between operations: 13.8 us -> 0.76 us
  local copies, waits for them, and re-layouts: 0.02 us -> 11.7 us
    reduce_scatter x3 -> x0, waiting for transfers between devices: 125 us -> none  [the longest x1 89.1 us: per_device(): lax.psum_scatter(full_grad.astype(jnp.bfloat16), 'dp', scatter_dimension=...]
    all_gather x1 -> x0, waiting for transfers between devices: 29.3 us -> none  [gather_cotangent(): return lax.all_gather(cotangent, 'row', axis=0, tiled=True)]
    ppermute x0 -> x14, waiting for transfers between devices: none -> 20.9 us  [the longest x8 13.1 us: along(): lax.ppermute(a, axis, [(i, (i + shift) % n) for i in range(n)])]
    ppermute x0 -> x14, starting transfers between devices: none -> 15.8 us  [the longest x8 11.2 us: along(): lax.ppermute(a, axis, [(i, (i + shift) % n) for i in range(n)])]
    convert_element_type x1 -> x2, other arithmetic: 17.1 us -> 1.75 us  [the longest x1 0.99 us: per_device(): outputs = outputs.astype(jnp.bfloat16)]
    dot_general x2, matrix products: 18 us -> 24.7 us  [the longest x1 17.7 us: per_device(): lax.dot_general(jnp.concatenate(lefts, 0), jnp.concatenate(rights, 0), ((...]
    dot_general x1, matrix products: 14.4 us -> 8.52 us  [per_device(): lax.dot_general(gathered, weight, (((1,), (1,)), ((), ())), preferred_ele...]
    dynamic_update_slice x0 -> x8, local copies, waits for them, and re-layouts: none -> 5.42 us  [in_row_order(): whole = lax.dynamic_update_slice_in_dim(whole, piece, start, 0)]
  transfers between devices with their start and end apart: 4 -> 14, of which waited for: 4 -> 7; matrix products, arithmetic and copies ran while one was open for 19% -> 34% of each run, Pallas kernels for 0% -> 0%
where the time goes in v1:
time: 85.5 us; the launch traced here: 85.2 us
  matrix products  33.2 us (39%)
  waiting for transfers between devices  20.9 us (24%)
  starting transfers between devices  15.8 us (18%)
  local copies, waits for them, and re-layouts  11.7 us (14%)
  other arithmetic  2.78 us (3%)
    dot_general x1, matrix products, per_device(): lax.dot_general(jnp.concatenate(lefts, 0), jnp.concatenate(rights, 0), ((...  17.7 us
    ppermute x8, waiting for transfers between devices, along(): lax.ppermute(a, axis, [(i, (i + shift) % n) for i in range(n)])  13.1 us
    ppermute x8, starting transfers between devices, along(): lax.ppermute(a, axis, [(i, (i + shift) % n) for i in range(n)])  11.2 us
    dot_general x1, matrix products, per_device(): lax.dot_general(gathered, weight, (((1,), (1,)), ((), ())), preferred_ele...  8.52 us
    ppermute x2, waiting for transfers between devices, chip_shift(): lax.ppermute(a, 'dp', [(i, (i + shift * cores) % n_dp) for i in range(n_d...  7.06 us
    dot_general x1, matrix products, per_device(): part = jnp.dot(inputs, weight, preferred_element_type=jnp.float32)  7.01 us
    dynamic_update_slice x8, local copies, waits for them, and re-layouts, in_row_order(): whole = lax.dynamic_update_slice_in_dim(whole, piece, start, 0)  5.42 us
    ppermute x2, starting transfers between devices, chip_shift(): lax.ppermute(a, 'dp', [(i, (i + shift * cores) % n_dp) for i in range(n_d...  4.56 us
  transfers between devices with their start and end apart: 14, of which 7 were waited for; matrix products, arithmetic and copies ran while one was open for 34% of the time, Pallas kernels for 0%

profile of v1, /device:TPU:0, one launch (start us, length us, event | category | flops | bytes accessed | tf_op | source)
XLA Modules:
  0.0 85.2 jit_solution(11828429647482240928)
XLA Ops:
  0.6 3.0 %collective-permute-start.10 = (bf16[96,3584]{1,0:T(8,128)(2,1)}, bf16[96,3584]{1,0:T(8,128)(2,1)}, u32[]{:S(2)}, u32[]{:S(2)}) collective-permute-start(bf16[96,3584]{1,0:T(8,128)(2,1)} %param.8), channel_id=1, source_target_pairs={{0,16},{8,24},{16,0},{24,8},{1,17},{9,25},{17,1},{25,9},{2,18},{10... | collective-permute-start | bytes 2064392 | tf_op jit(solution)/shard_map/ppermute | solution.py:27
  3.6 1.5 %collective-permute-start.1 = (bf16[96,3584]{1,0:T(8,128)(2,1)}, bf16[96,3584]{1,0:T(8,128)(2,1)}, u32[]{:S(2)}, u32[]{:S(2)}) collective-permute-start(bf16[96,3584]{1,0:T(8,128)(2,1)} %param.8), channel_id=1, source_target_pairs={{0,4},{4,0},{1,5},{5,1},{2,6},{6,2},{3,7},{7,3},{8,12},{12,8},{9,1... | collective-permute-start | bytes 2064392 | tf_op jit(solution)/shard_map/ppermute | solution.py:24
  5.2 2.0 %dynamic-slice_bitcast_fusion.4 = (bf16[1,192,512]{2,1,0:T(8,128)(2,1)S(1)}, bf16[192,512]{1,0:T(8,128)(2,1)}, bf16[192,512]{1,0:T(8,128)(2,1)S(1)}, bf16[192,512]{1,0:T(8,128)(2,1)}) fusion(bf16[192,2048]{1,0:T(8,128)(2,1)} %param.6, s32[]{:T(128)S(6)} %select_n.61, s32[]{:T(128)S(6)} %select_n.62, s32[]{:T(128)S(6)} %select_n.64, s32[]{:T(128)S(6)} %select_n.63), kind=kLoop, calls=%fused_computation.30 | loop fusion | bytes 1572880 | tf_op jit(solution)/shard_map/stack | solution.py:83
  7.2 0.0 collective-permute-start.5
  7.2 0.6 collective-permute-start.6
  7.8 1.4 %collective-permute-start.7 = (bf16[192,512]{1,0:T(8,128)(2,1)S(1)}, bf16[192,512]{1,0:T(8,128)(2,1)}, u32[]{:S(2)}, u32[]{:S(2)}) collective-permute-start(bf16[192,512]{1,0:T(8,128)(2,1)S(1)} %get-tuple-element.14), channel_id=1, source_target_pairs={{0,24},{8,0},{16,8},{24,16},{1,25},{9,1},{17,9},{25,17},{2,26},{10... | collective-permute-start | bytes 589832 | tf_op jit(solution)/shard_map/ppermute | solution.py:24
  9.2 7.0 %fusion.21 = f32[192,3584]{1,0:T(8,128)S(1)} fusion(bf16[192,2048]{1,0:T(8,128)(2,1)} %param.6, bf16[2048,3584]{1,0:T(8,128)(2,1)} %param.7), kind=kOutput, calls=%fused_computation.47 | convolution fusion | flops 2818572288 | bytes 18219008 | tf_op jit(solution)/shard_map/dot_general | solution.py:54
  16.2 1.2 %broadcast.24.clone = bf16[192,3584]{1,0:T(8,128)(2,1)} broadcast(bf16[]{:T(256)} %constant.90.clone.1), dimensions={} | broadcast | bytes 1376258 | tf_op jit(solution)/shard_map/broadcast.1
  17.4 2.0 %constant_dynamic-update-slice_fusion.7 = bf16[192,3584]{1,0:T(8,128)(2,1)} fusion(bf16[192,3584]{1,0:T(8,128)(2,1)} %broadcast.24.clone, bf16[96,3584]{1,0:T(8,128)(2,1)} %param.8, s32[]{:T(128)S(6)} %select_n.56), kind=kLoop, calls=%fused_computation.44 | loop fusion | bytes 1376260 | tf_op jit(solution)/shard_map/dynamic_update_slice | solution.py:38
  19.4 0.9 %dynamic-slice_convert_fusion = bf16[96,3584]{1,0:T(8,128)(2,1)} fusion(f32[192,3584]{1,0:T(8,128)S(1)} %fusion.21, s32[]{:T(128)S(6)} %select_n.55), kind=kLoop, calls=%fused_computation.15 | loop fusion | bytes 1376260 | tf_op jit(solution)/shard_map/convert_element_type | solution.py:58
  20.3 2.3 %collective-permute-done.5 = bf16[192,512]{1,0:T(8,128)(2,1)S(1)} collective-permute-done((bf16[192,512]{1,0:T(8,128)(2,1)}, bf16[192,512]{1,0:T(8,128)(2,1)S(1)}, u32[]{:S(2)}, u32[]{:S(2)}) %collective-permute-start.5) | collective-permute-done | bytes 196640 | tf_op jit(solution)/shard_map/ppermute | solution.py:24
  22.7 0.0 collective-permute-start.8
  22.7 1.7 %collective-permute-done.6 = bf16[192,512]{1,0:T(8,128)(2,1)S(1)} collective-permute-done((bf16[192,512]{1,0:T(8,128)(2,1)}, bf16[192,512]{1,0:T(8,128)(2,1)S(1)}, u32[]{:S(2)}, u32[]{:S(2)}) %collective-permute-start.6) | collective-permute-done | bytes 196640 | tf_op jit(solution)/shard_map/ppermute | solution.py:24
  24.3 2.1 %collective-permute-start = (bf16[96,3584]{1,0:T(8,128)(2,1)}, bf16[96,3584]{1,0:T(8,128)(2,1)S(1)}, u32[]{:S(2)}, u32[]{:S(2)}) collective-permute-start(bf16[96,3584]{1,0:T(8,128)(2,1)} %dynamic-slice_convert_fusion), channel_id=1, source_target_pairs={{0,4},{4,0},{1,5},{5,1},{2,6},{6,2},{3,7},{7,3},{8,12},{12,8},{9,1... | collective-permute-start | bytes 2064392 | tf_op jit(solution)/shard_map/ppermute | solution.py:24
  26.4 0.6 collective-permute-done.7
  27.0 1.0 %pad_maximum_fusion = bf16[4,192,512]{2,1,0:T(8,128)(2,1)S(1)} fusion(bf16[1,192,512]{2,1,0:T(8,128)(2,1)} %bitcast.3, bf16[1,192,512]{2,1,0:T(8,128)(2,1)S(1)} %bitcast.18, bf16[1,192,512]{2,1,0:T(8,128)(2,1)S(1)} %bitcast.17, bf16[1,192,512]{2,1,0:T(8,128)(2,1)S(1)} %get-tuple-element.12), kind=kLoop, calls=%fused_computation.17 | loop fusion | flops 1179648 | bytes 1572864 | tf_op jit(solution)/shard_map/stack | solution.py:83
  28.0 0.7 dynamic-slice_bitcast_fusion.3
  28.7 0.0 collective-permute-done.1
  28.7 2.0 %constant_dynamic-update-slice_fusion.6 = bf16[192,3584]{1,0:T(8,128)(2,1)} fusion(bf16[192,3584]{1,0:T(8,128)(2,1)} %constant_dynamic-update-slice_fusion.7, bf16[96,3584]{1,0:T(8,128)(2,1)} %collective-permute-done.1, s32[]{:T(128)S(6)} %select_n.55), kind=kLoop, calls=%fused_computation.43 | loop fusion | bytes 1376260 | tf_op jit(solution)/shard_map/dynamic_update_slice | solution.py:38
  30.7 8.5 %fusion.20 = (bf16[192,2048]{1,0:T(8,128)(2,1)S(1)}, f32[192,2048]{1,0:T(8,128)S(1)}) fusion(bf16[192,3584]{1,0:T(8,128)(2,1)} %constant_dynamic-update-slice_fusion.6, bf16[2048,3584]{1,0:T(8,128)(2,1)} %param.7), kind=kOutput, calls=%fused_computation.46 | convolution fusion | flops 2818965504 | bytes 18415616 | tf_op jit(solution)/shard_map/dot_general | solution.py:63
  39.3 0.1 constant_dynamic-slice_fusion.5
  39.3 1.6 %collective-permute-start.2 = (bf16[48,2048]{1,0:T(8,128)(2,1)S(1)}, bf16[48,2048]{1,0:T(8,128)(2,1)S(1)}, u32[]{:S(2)}, u32[]{:S(2)}) collective-permute-start(bf16[48,2048]{1,0:T(8,128)(2,1)S(1)} %get-tuple-element.16), channel_id=1, source_target_pairs={{0,1},{1,2},{2,3},{3,0},{4,5},{5,6},{6,7},{7,4},{8,9},{9,10},{10,1... | collective-permute-start | bytes 589832 | tf_op jit(solution)/shard_map/ppermute | solution.py:24
  41.0 2.6 %collective-permute-start.3 = (bf16[48,2048]{1,0:T(8,128)(2,1)S(1)}, bf16[48,2048]{1,0:T(8,128)(2,1)S(1)}, u32[]{:S(2)}, u32[]{:S(2)}) collective-permute-start(bf16[48,2048]{1,0:T(8,128)(2,1)S(1)} %get-tuple-element.18), channel_id=1, source_target_pairs={{0,2},{1,3},{2,0},{3,1},{4,6},{5,7},{6,4},{7,5},{8,10},{9,11},{10,... | collective-permute-start | bytes 589832 | tf_op jit(solution)/shard_map/ppermute | solution.py:24
  43.6 0.0 collective-permute-done.10
  43.6 1.3 %collective-permute-start.4 = (bf16[48,2048]{1,0:T(8,128)(2,1)S(1)}, bf16[48,2048]{1,0:T(8,128)(2,1)S(1)}, u32[]{:S(2)}, u32[]{:S(2)}) collective-permute-start(bf16[48,2048]{1,0:T(8,128)(2,1)S(1)} %get-tuple-element.17), channel_id=1, source_target_pairs={{0,3},{1,0},{2,1},{3,2},{4,7},{5,4},{6,5},{7,6},{8,11},{9,8},{10,9... | collective-permute-start | bytes 589832 | tf_op jit(solution)/shard_map/ppermute | solution.py:24
  44.9 0.0 collective-permute-done
  44.9 0.1 collective-permute-start.12
  45.0 1.0 %add_convert_fusion = bf16[96,3584]{1,0:T(8,128)(2,1)} fusion(bf16[96,3584]{1,0:T(8,128)(2,1)S(1)} %collective-permute-done, f32[192,3584]{1,0:T(8,128)S(1)} %fusion.21, s32[]{:T(128)S(6)} %select_n.54), kind=kLoop, calls=%fused_computation.16 | loop fusion | flops 1032192 | bytes 2752516 | tf_op jit(solution)/shard_map/convert_element_type | solution.py:60
  46.0 0.1 broadcast.24.clone.2
  46.1 1.2 %constant_dynamic-update-slice_fusion.3 = bf16[192,3584]{1,0:T(8,128)(2,1)S(1)} fusion(bf16[192,3584]{1,0:T(8,128)(2,1)S(1)} %broadcast.24.clone.2, bf16[96,3584]{1,0:T(8,128)(2,1)} %collective-permute-done.10, s32[]{:T(128)S(6)} %select_n.56), kind=kLoop, calls=%fused_computation.34 | loop fusion | bytes 1376260 | tf_op jit(solution)/shard_map/dynamic_update_slice | solution.py:38
  47.2 0.0 collective-permute-done.8
  47.2 1.6 %collective-permute-start.11 = (bf16[96,3584]{1,0:T(8,128)(2,1)}, bf16[96,3584]{1,0:T(8,128)(2,1)S(1)}, u32[]{:S(2)}, u32[]{:S(2)}) collective-permute-start(bf16[96,3584]{1,0:T(8,128)(2,1)} %collective-permute-done.1), channel_id=1, source_target_pairs={{0,16},{8,24},{16,0},{24,8},{1,17},{9,25},{17,1},{25,9},{2,18},{10... | collective-permute-start | bytes 2064392 | tf_op jit(solution)/shard_map/ppermute | solution.py:27
  48.8 0.1 broadcast.24.clone.3
  48.9 0.1 constant_dynamic-update-slice_fusion.5
  48.9 0.2 collective-permute-done.2
  49.1 0.0 collective-permute-start.9
  49.1 8.3 %collective-permute-done.3 = bf16[48,2048]{1,0:T(8,128)(2,1)S(1)} collective-permute-done((bf16[48,2048]{1,0:T(8,128)(2,1)S(1)}, bf16[48,2048]{1,0:T(8,128)(2,1)S(1)}, u32[]{:S(2)}, u32[]{:S(2)}) %collective-permute-start.3) | collective-permute-done | bytes 196640 | tf_op jit(solution)/shard_map/ppermute | solution.py:24
  57.5 0.0 collective-permute-done.4
  57.5 0.8 add_convert_fusion.1
  58.2 0.0 copy-start.1
  58.2 7.1 %collective-permute-done.11 = bf16[96,3584]{1,0:T(8,128)(2,1)S(1)} collective-permute-done((bf16[96,3584]{1,0:T(8,128)(2,1)}, bf16[96,3584]{1,0:T(8,128)(2,1)S(1)}, u32[]{:S(2)}, u32[]{:S(2)}) %collective-permute-start.11) | collective-permute-done | bytes 688160 | tf_op jit(solution)/shard_map/ppermute | solution.py:27
  65.3 0.0 collective-permute-start.13
  65.3 0.1 constant_dynamic-update-slice_fusion.2
  65.3 0.0 copy-start
  65.4 1.1 %copy-done = bf16[192,3584]{1,0:T(8,128)(2,1)} copy-done((bf16[192,3584]{1,0:T(8,128)(2,1)}, bf16[192,3584]{1,0:T(8,128)(2,1)S(1)}, u32[]{:S(2)}) %copy-start) | copy-done | bytes 1376280
  66.4 0.0 collective-permute-done.12
  66.4 0.1 broadcast.24.clone.1
  66.5 0.1 constant_dynamic-update-slice_fusion.1
  66.6 0.0 collective-permute-done.9
  66.6 0.1 constant_dynamic-update-slice_fusion.4
  66.7 0.8 collective-permute-done.13
  67.4 0.1 constant_dynamic-update-slice_fusion
  67.5 0.0 copy-done.1
  67.5 17.7 %fusion.2 = (bf16[512,3584]{1,0:T(8,128)(2,1)}, f32[512,3584]{1,0:T(8,128)}, f32[512,3584]{1,0:T(8,128)}) fusion(bf16[2048,3584]{1,0:T(8,128)(2,1)} %param.7, s32[]{:T(128)S(6)} %select_n.61, f32[512,3584]{1,0:T(8,128)} %param.10, f32[512,3584]{1,0:T(8,128)} %param.11, bf16[512,3584]{1,0:T(8,128)(2,1)} %param.9, ...), kind=kOutput, calls=%fused_computation.5 | convolution fusion | flops 2878603264 | bytes 46661636 | tf_op jit(solution)/shard_map/dot_general | solution.py:84
Async XLA Ops:
  0.6 42.9 %collective-permute-start.10 = (bf16[96,3584]{1,0:T(8,128)(2,1)}, bf16[96,3584]{1,0:T(8,128)(2,1)}, u32[]{:S(2)}, u32[]{:S(2)}) collective-permute-start(bf16[96,3584]{1,0:T(8,128)(2,1)} %param.8), channel_id=1, source_target_pairs={{0,16},{8,24},{16,0},{24,8},{1,17},{9,25},{17,1},{25,9},{2,18},{10... | collective-permute-start | bytes 2064392 | tf_op jit(solution)/shard_map/ppermute | solution.py:27
  3.6 25.1 %collective-permute-start.1 = (bf16[96,3584]{1,0:T(8,128)(2,1)}, bf16[96,3584]{1,0:T(8,128)(2,1)}, u32[]{:S(2)}, u32[]{:S(2)}) collective-permute-start(bf16[96,3584]{1,0:T(8,128)(2,1)} %param.8), channel_id=1, source_target_pairs={{0,4},{4,0},{1,5},{5,1},{2,6},{6,2},{3,7},{7,3},{8,12},{12,8},{9,1... | collective-permute-start | bytes 2064392 | tf_op jit(solution)/shard_map/ppermute | solution.py:24
  7.2 15.5 %collective-permute-start.5 = (bf16[192,512]{1,0:T(8,128)(2,1)}, bf16[192,512]{1,0:T(8,128)(2,1)S(1)}, u32[]{:S(2)}, u32[]{:S(2)}) collective-permute-start(bf16[192,512]{1,0:T(8,128)(2,1)} %get-tuple-element.13), channel_id=1, source_target_pairs={{0,8},{8,16},{16,24},{24,0},{1,9},{9,17},{17,25},{25,1},{2,10},{10... | collective-permute-start | bytes 589832 | tf_op jit(solution)/shard_map/ppermute | solution.py:24
  7.2 17.1 %collective-permute-start.6 = (bf16[192,512]{1,0:T(8,128)(2,1)}, bf16[192,512]{1,0:T(8,128)(2,1)S(1)}, u32[]{:S(2)}, u32[]{:S(2)}) collective-permute-start(bf16[192,512]{1,0:T(8,128)(2,1)} %get-tuple-element.15), channel_id=1, source_target_pairs={{0,16},{8,24},{16,0},{24,8},{1,17},{9,25},{17,1},{25,9},{2,18},{10... | collective-permute-start | bytes 589832 | tf_op jit(solution)/shard_map/ppermute | solution.py:24
  7.8 19.2 %collective-permute-start.7 = (bf16[192,512]{1,0:T(8,128)(2,1)S(1)}, bf16[192,512]{1,0:T(8,128)(2,1)}, u32[]{:S(2)}, u32[]{:S(2)}) collective-permute-start(bf16[192,512]{1,0:T(8,128)(2,1)S(1)} %get-tuple-element.14), channel_id=1, source_target_pairs={{0,24},{8,0},{16,8},{24,16},{1,25},{9,1},{17,9},{25,17},{2,26},{10... | collective-permute-start | bytes 589832 | tf_op jit(solution)/shard_map/ppermute | solution.py:24
  22.7 24.6 %collective-permute-start.8 = (bf16[96,3584]{1,0:T(8,128)(2,1)}, bf16[96,3584]{1,0:T(8,128)(2,1)S(1)}, u32[]{:S(2)}, u32[]{:S(2)}) collective-permute-start(bf16[96,3584]{1,0:T(8,128)(2,1)} %param.8), channel_id=1, source_target_pairs={{0,8},{8,0},{16,24},{24,16},{1,9},{9,1},{17,25},{25,17},{2,10},{10... | collective-permute-start | bytes 2064392 | tf_op jit(solution)/shard_map/ppermute | solution.py:32
  24.3 20.6 %collective-permute-start = (bf16[96,3584]{1,0:T(8,128)(2,1)}, bf16[96,3584]{1,0:T(8,128)(2,1)S(1)}, u32[]{:S(2)}, u32[]{:S(2)}) collective-permute-start(bf16[96,3584]{1,0:T(8,128)(2,1)} %dynamic-slice_convert_fusion), channel_id=1, source_target_pairs={{0,4},{4,0},{1,5},{5,1},{2,6},{6,2},{3,7},{7,3},{8,12},{12,8},{9,1... | collective-permute-start | bytes 2064392 | tf_op jit(solution)/shard_map/ppermute | solution.py:24
  39.3 9.8 %collective-permute-start.2 = (bf16[48,2048]{1,0:T(8,128)(2,1)S(1)}, bf16[48,2048]{1,0:T(8,128)(2,1)S(1)}, u32[]{:S(2)}, u32[]{:S(2)}) collective-permute-start(bf16[48,2048]{1,0:T(8,128)(2,1)S(1)} %get-tuple-element.16), channel_id=1, source_target_pairs={{0,1},{1,2},{2,3},{3,0},{4,5},{5,6},{6,7},{7,4},{8,9},{9,10},{10,1... | collective-permute-start | bytes 589832 | tf_op jit(solution)/shard_map/ppermute | solution.py:24
  41.0 16.5 %collective-permute-start.3 = (bf16[48,2048]{1,0:T(8,128)(2,1)S(1)}, bf16[48,2048]{1,0:T(8,128)(2,1)S(1)}, u32[]{:S(2)}, u32[]{:S(2)}) collective-permute-start(bf16[48,2048]{1,0:T(8,128)(2,1)S(1)} %get-tuple-element.18), channel_id=1, source_target_pairs={{0,2},{1,3},{2,0},{3,1},{4,6},{5,7},{6,4},{7,5},{8,10},{9,11},{10,... | collective-permute-start | bytes 589832 | tf_op jit(solution)/shard_map/ppermute | solution.py:24
  43.6 13.9 %collective-permute-start.4 = (bf16[48,2048]{1,0:T(8,128)(2,1)S(1)}, bf16[48,2048]{1,0:T(8,128)(2,1)S(1)}, u32[]{:S(2)}, u32[]{:S(2)}) collective-permute-start(bf16[48,2048]{1,0:T(8,128)(2,1)S(1)} %get-tuple-element.17), channel_id=1, source_target_pairs={{0,3},{1,0},{2,1},{3,2},{4,7},{5,4},{6,5},{7,6},{8,11},{9,8},{10,9... | collective-permute-start | bytes 589832 | tf_op jit(solution)/shard_map/ppermute | solution.py:24
  44.9 21.5 %collective-permute-start.12 = (bf16[96,3584]{1,0:T(8,128)(2,1)}, bf16[96,3584]{1,0:T(8,128)(2,1)S(1)}, u32[]{:S(2)}, u32[]{:S(2)}) collective-permute-start(bf16[96,3584]{1,0:T(8,128)(2,1)} %collective-permute-done.10), channel_id=1, source_target_pairs={{0,8},{8,0},{16,24},{24,16},{1,9},{9,1},{17,25},{25,17},{2,10},{10... | collective-permute-start | bytes 2064392 | tf_op jit(solution)/shard_map/ppermute | solution.py:32
  47.2 18.1 %collective-permute-start.11 = (bf16[96,3584]{1,0:T(8,128)(2,1)}, bf16[96,3584]{1,0:T(8,128)(2,1)S(1)}, u32[]{:S(2)}, u32[]{:S(2)}) collective-permute-start(bf16[96,3584]{1,0:T(8,128)(2,1)} %collective-permute-done.1), channel_id=1, source_target_pairs={{0,16},{8,24},{16,0},{24,8},{1,17},{9,25},{17,1},{25,9},{2,18},{10... | collective-permute-start | bytes 2064392 | tf_op jit(solution)/shard_map/ppermute | solution.py:27
  49.1 17.4 %collective-permute-start.9 = (bf16[96,3584]{1,0:T(8,128)(2,1)}, bf16[96,3584]{1,0:T(8,128)(2,1)S(1)}, u32[]{:S(2)}, u32[]{:S(2)}) collective-permute-start(bf16[96,3584]{1,0:T(8,128)(2,1)} %collective-permute-done.1), channel_id=1, source_target_pairs={{0,8},{8,0},{16,24},{24,16},{1,9},{9,1},{17,25},{25,17},{2,10},{10... | collective-permute-start | bytes 2064392 | tf_op jit(solution)/shard_map/ppermute | solution.py:32
  58.2 9.3 %copy-start.1 = (bf16[192,512]{1,0:T(8,128)(2,1)S(1)}, bf16[192,512]{1,0:T(8,128)(2,1)}, u32[]{:S(2)}) copy-start(bf16[192,512]{1,0:T(8,128)(2,1)} %get-tuple-element.11) | copy-start | bytes 589828
  65.3 2.1 %collective-permute-start.13 = (bf16[96,3584]{1,0:T(8,128)(2,1)S(1)}, bf16[96,3584]{1,0:T(8,128)(2,1)S(1)}, u32[]{:S(2)}, u32[]{:S(2)}) collective-permute-start(bf16[96,3584]{1,0:T(8,128)(2,1)S(1)} %collective-permute-done.11), channel_id=1, source_target_pairs={{0,8},{8,0},{16,24},{24,16},{1,9},{9,1},{17,25},{25,17},{2,10},{10... | collective-permute-start | bytes 2064392 | tf_op jit(solution)/shard_map/ppermute | solution.py:32
  65.3 1.1 %copy-start = (bf16[192,3584]{1,0:T(8,128)(2,1)}, bf16[192,3584]{1,0:T(8,128)(2,1)S(1)}, u32[]{:S(2)}) copy-start(bf16[192,3584]{1,0:T(8,128)(2,1)S(1)} %constant_dynamic-update-slice_fusion.2) | copy-start | bytes 4128772

commit v2 on v0

v2 whole, which is shorter than its diff:
```python
import functools
import math

import jax
import jax.numpy as jnp
from jax import lax
from jax.experimental import pallas as pl
from jax.experimental.pallas import tpu as pltpu
from jax.sharding import PartitionSpec as P

beta_one = 0.9
beta_two = 0.999
learn_rate = 0.002
anchor_pull = 0.5
epsilon = 1e-08
step_count = 100.0

BF16, F32 = jnp.bfloat16, jnp.float32
MIB = 1 << 20


def block_of(size, most):
    return max(b for b in range(128, most + 1, 128) if size % b == 0)


def struct(shape, dtype):
    return jax.ShapeDtypeStruct(shape, dtype)


def run(kernel, name, grid, in_specs, out_specs, out_shape, scratch, limit, args):
    return pl.pallas_call(
        kernel,
        name=name,
        grid_spec=pltpu.PrefetchScalarGridSpec(
            num_scalar_prefetch=1,
            grid=grid,
            in_specs=in_specs,
            out_specs=out_specs,
            scratch_shapes=scratch,
        ),
        out_shape=out_shape,
        compiler_params=pltpu.CompilerParams(vmem_limit_bytes=limit * MIB),
        cost_estimate=pl.CostEstimate(flops=1, bytes_accessed=1, transcendentals=0),
    )(*args)


def fixed(shape):
    return pl.BlockSpec(shape, lambda j, place: (0,) * len(shape))


def columns(rows, width):
    return pl.BlockSpec((rows, width), lambda j, place: (0, j))


def forward_kernel(n_dp, n_row, own, slice_rows, place, x_ref, w_ref, *rest):
    parts, sent, xs = rest[:n_row], rest[n_row : n_row + n_dp - 1], rest[-1]
    dp, row = place[0], place[1]

    @pl.when(pl.program_id(0) == 0)
    def _():
        for s in range(n_row):
            start = pl.multiple_of(lax.rem(row + s, n_row) * own, own)
            xs[s * own : (s + 1) * own, :] = x_ref[pl.ds(start, own), :]
        for s in range(1, n_dp):
            start = pl.multiple_of(lax.rem(dp + s, n_dp) * slice_rows, slice_rows)
            sent[s - 1][...] = x_ref[:, pl.ds(start, slice_rows)]

    acc = jnp.dot(xs[...], w_ref[...], preferred_element_type=F32)
    for s in range(n_row):
        parts[s][...] = acc[s * own : (s + 1) * own].astype(parts[s].dtype)


def forward_call(place, inputs, weight, own, n_dp, n_row, slice_rows):
    tokens, depth = inputs.shape
    width = weight.shape[1]
    block = block_of(width, 512)
    return run(
        functools.partial(forward_kernel, n_dp, n_row, own, slice_rows),
        "forward",
        (width // block,),
        [fixed((tokens, depth)), columns(depth, block)],
        [columns(own, block)] * n_row + [fixed((tokens, slice_rows))] * (n_dp - 1),
        [struct((own, width), F32)]
        + [struct((own, width), BF16)] * (n_row - 1)
        + [struct((tokens, slice_rows), BF16)] * (n_dp - 1),
        [pltpu.VMEM((tokens, depth), BF16)],
        24,
        (place, inputs, weight),
    )


def input_grad_kernel(n_row, n_col, own, share, place, *rest):
    pieces, w_ref = rest[:n_row], rest[n_row]
    parts, (cs, acc) = rest[n_row + 1 : n_row + 1 + n_col], rest[-2:]
    row, col = place[1], place[2]

    @pl.when(pl.program_id(0) == 0)
    def _():
        for s in range(n_row):
            start = pl.multiple_of(lax.rem(row - s + n_row, n_row) * own, own)
            cs[pl.ds(start, own), :] = pieces[s][...]

    acc[...] = lax.dot_general(
        cs[...], w_ref[...], (((1,), (1,)), ((), ())), preferred_element_type=F32
    )
    for s in range(n_col):
        start = pl.multiple_of(lax.rem(col + s, n_col) * share, share)
        parts[s][...] = acc[pl.ds(start, share), :].astype(parts[s].dtype)


def input_grad_call(place, by_row, weight, share, n_row, n_col):
    own, width = by_row[0].shape
    depth = weight.shape[0]
    block = block_of(depth, 256)
    return run(
        functools.partial(input_grad_kernel, n_row, n_col, own, share),
        "input_grad",
        (depth // block,),
        [fixed((own, width))] * n_row + [pl.BlockSpec((block, width), lambda j, place: (j, 0))],
        [columns(share, block)] * n_col,
        [struct((share, depth), F32)] + [struct((share, depth), BF16)] * (n_col - 1),
        [pltpu.VMEM((n_row * own, width), BF16), pltpu.VMEM((n_row * own, block), F32)],
        24,
        (place, *by_row, weight),
    )


def transpose_kernel(n_dp, tokens, place, *rest):
    pieces, out, xs = rest[:n_dp], rest[n_dp], rest[n_dp + 1]
    for s in range(n_dp):
        start = pl.multiple_of(lax.rem(place[0] - s + n_dp, n_dp) * tokens, tokens)
        xs[pl.ds(start, tokens), :] = pieces[s][...]
    out[...] = xs[...].T


def transpose_call(place, inputs, pieces, slice_rows):
    tokens, n_dp = inputs.shape[0], len(pieces) + 1
    return run(
        functools.partial(transpose_kernel, n_dp, tokens),
        "features",
        (1,),
        [pl.BlockSpec((tokens, slice_rows), lambda j, place: (0, place[0]))]
        + [fixed((tokens, slice_rows))] * (n_dp - 1),
        fixed((slice_rows, n_dp * tokens)),
        struct((slice_rows, n_dp * tokens), BF16),
        [pltpu.VMEM((n_dp * tokens, slice_rows), BF16)],
        16,
        (place, inputs, *pieces),
    )


def updated(grad_sum, tokens_all, current, anchor, first, second):
    grad = grad_sum * (1.0 / tokens_all) + anchor_pull * (current - anchor)
    first = beta_one * first + (1.0 - beta_one) * grad
    second = beta_two * second + (1.0 - beta_two) * grad * grad
    scale = learn_rate / (1.0 - beta_one**step_count)
    spread = jnp.sqrt(second * (1.0 / (1.0 - beta_two**step_count))) + epsilon
    return current - scale * first / spread, first, second


def update_kernel(origins, tokens_all, chunk, place, x_ref, *rest):
    n = len(origins)
    pieces = rest[:n]
    w_ref, a_ref, m_ref, v_ref, new_w, new_m, new_v, cs, acc = rest[n:]
    own = pieces[0].shape[0]
    for piece, origin in zip(pieces, origins):
        cs[pl.ds(pl.multiple_of(origin(place[0], place[1]) * own, own), own), :] = piece[...]
    acc[...] = jnp.dot(x_ref[...], cs[...], preferred_element_type=F32)

    @pl.loop(0, acc.shape[0] // chunk)
    def _(i):
        at = pl.ds(pl.multiple_of(i * chunk, chunk), chunk)
        weight, first, second = updated(
            acc[at, :],
            tokens_all,
            w_ref[at, :].astype(F32),
            a_ref[at, :].astype(F32),
            m_ref[at, :],
            v_ref[at, :],
        )
        new_w[at, :] = weight.astype(BF16)
        new_m[at, :] = first
        new_v[at, :] = second


def update_call(place, features, pieces, origins, weight, anchor, first, second):
    rows, width = first.shape
    tokens_all = features.shape[1]
    block = block_of(width, 512)
    own = pieces[0].shape[0]
    tile = columns(rows, block)
    return run(
        functools.partial(update_kernel, origins, tokens_all, math.gcd(rows, 16)),
        "update",
        (width // block,),
        [fixed((rows, tokens_all))]
        + [columns(own, block)] * len(pieces)
        + [pl.BlockSpec((rows, block), lambda j, place: (place[0], j)), tile, tile, tile],
        [tile] * 3,
        [struct((rows, width), BF16), struct((rows, width), F32), struct((rows, width), F32)],
        [pltpu.VMEM((tokens_all, block), BF16), pltpu.VMEM((rows, block), F32)],
        32,
        (place, features, *pieces, weight, anchor, first, second),
    )


def per_device(inputs, weight, cotangent, anchor, first_moment, second_moment):
    n_dp, n_row, n_col = (lax.axis_size(a) for a in ("dp", "row", "col"))
    dp, row, col = (lax.axis_index(a) for a in ("dp", "row", "col"))
    place = jnp.stack([dp, row, col]).astype(jnp.int32)
    cores = 2 if n_dp % 2 == 0 else 1
    chips = n_dp // cores
    tokens = inputs.shape[0]
    own = cotangent.shape[0]
    share = tokens // n_col
    slice_rows = weight.shape[0] // n_dp
    tiled = own % 16 == 0 and share % 16 == 0 and slice_rows % 128 == 0

    def along(axis, n, shift):
        return lambda a: lax.ppermute(a, axis, [(i, (i + shift) % n) for i in range(n)])

    def chip_shift(shift):
        return along("dp", n_dp, shift * cores)

    def swap_cores(a):
        return lax.ppermute(a, "dp", [(i, i ^ 1) for i in range(n_dp)])

    def in_order(pieces, places, rows):
        whole = jnp.zeros((len(pieces) * rows, pieces[0].shape[1]), pieces[0].dtype)
        for piece, at in zip(pieces, places):
            whole = lax.dynamic_update_slice_in_dim(whole, piece, at * rows, 0)
        return whole

    by_row = [cotangent] + [along("row", n_row, s)(cotangent) for s in range(1, n_row)]
    pieces, origins = [], []
    for c in range(chips):
        for s in range(n_row):
            piece = chip_shift(c)(by_row[s]) if c else by_row[s]

            def origin(dp, row, c=c, s=s, flip=0):
                core = lax.rem(dp, cores)
                from_core = 1 - core if flip else core
                from_dp = lax.rem(dp - core - c * cores + n_dp, n_dp) + from_core
                return from_dp * n_row + lax.rem(row - s + n_row, n_row)

            pieces.append(piece)
            origins.append(origin)
            if cores == 2:
                pieces.append(swap_cores(piece))
                origins.append(functools.partial(origin, flip=1))

    if tiled:
        made = forward_call(place, inputs, weight, own, n_dp, n_row, slice_rows)
        parts, to_send = made[:n_row], made[n_row:]
    else:
        part = jnp.dot(inputs, weight, preferred_element_type=F32)
        parts = [
            lax.dynamic_slice_in_dim(part, lax.rem(row + s, n_row) * own, own, 0).astype(
                BF16 if s else F32
            )
            for s in range(n_row)
        ]
        to_send = [
            lax.dynamic_slice_in_dim(
                inputs, lax.rem(dp + s, n_dp) * slice_rows, slice_rows, 1
            )
            for s in range(1, n_dp)
        ]
    held = [along("dp", n_dp, s)(to_send[s - 1]) for s in range(1, n_dp)]
    outputs = parts[0]
    for s in range(1, n_row):
        outputs = outputs + along("row", n_row, s)(parts[s]).astype(F32)
    outputs = outputs.astype(BF16)

    if tiled:
        gparts = input_grad_call(place, by_row, weight, share, n_row, n_col)
    else:
        gathered = in_order(by_row, [lax.rem(row - s + n_row, n_row) for s in range(n_row)], own)
        gpart = lax.dot_general(
            gathered, weight, (((1,), (1,)), ((), ())), preferred_element_type=F32
        )
        gparts = [
            lax.dynamic_slice_in_dim(gpart, lax.rem(col + s, n_col) * share, share, 0).astype(
                BF16 if s else F32
            )
            for s in range(n_col)
        ]
    input_grad = gparts[0]
    for s in range(1, n_col):
        input_grad = input_grad + along("col", n_col, s)(gparts[s]).astype(F32)
    input_grad = input_grad.astype(BF16)

    if tiled:
        features = transpose_call(place, inputs, held, slice_rows)
        new_weight, new_first, new_second = update_call(
            place, features, pieces, origins, weight, anchor, first_moment, second_moment
        )
    else:
        mine = lax.dynamic_slice_in_dim(inputs, dp * slice_rows, slice_rows, 1)
        features = in_order(
            [mine] + held, [lax.rem(dp - s + n_dp, n_dp) for s in range(n_dp)], tokens
        )
        gathered = in_order(pieces, [origin(dp, row) for origin in origins], own)
        summed = lax.dot_general(
            features, gathered, (((0,), (0,)), ((), ())), preferred_element_type=F32
        )
        current = lax.dynamic_slice_in_dim(weight, dp * slice_rows, slice_rows, 0).astype(F32)
        new_weight, new_first, new_second = updated(
            summed,
            tokens * n_dp,
            current,
            anchor.astype(F32),
            first_moment,
            second_moment,
        )
        new_weight = new_weight.astype(BF16)
    return (outputs, input_grad, new_weight, new_first, new_second)


def solution(mesh):
    in_specs = (
        P("dp", "row"),
        P("row", "col"),
        P(("dp", "row"), "col"),
        P(("row", "dp"), "col"),
        P(("row", "dp"), "col"),
        P(("row", "dp"), "col"),
    )
    out_specs = (
        P(("dp", "row"), "col"),
        P(("dp", "col"), "row"),
        P(("row", "dp"), "col"),
        P(("row", "dp"), "col"),
        P(("row", "dp"), "col"),
    )
    return jax.shard_map(
        per_device, mesh=mesh, in_specs=in_specs, out_specs=out_specs, check_vma=False
    )
```

time: 219 us -> 86.9 us (0.40)
  waiting for transfers between devices: 155 us -> 28.6 us
  Pallas kernels: 0 us -> 33.7 us
  matrix products: 32.4 us -> 0 us
  other arithmetic: 17.1 us -> 1.8 us
  starting transfers between devices: 0.16 us -> 13.3 us
  between operations: 13.8 us -> 0.75 us
  local copies, waits for them, and re-layouts: 0.02 us -> 7.41 us
    reduce_scatter x3 -> x0, waiting for transfers between devices: 125 us -> none  [the longest x1 89.1 us: per_device(): lax.psum_scatter(full_grad.astype(jnp.bfloat16), 'dp', scatter_dimension=...]
    pallas_call x0 -> x4, Pallas kernels: none -> 33.7 us  [run(): pl.pallas_call(kernel, name=name, grid_spec=pltpu.PrefetchScalarGridSpec(...]
    dot_general x3 -> x0, matrix products: 32.4 us -> none  [the longest x1 14.4 us: per_device(): lax.dot_general(gathered, weight, (((1,), (1,)), ((), ())), preferred_ele...]
    all_gather x1 -> x0, waiting for transfers between devices: 29.3 us -> none  [gather_cotangent(): return lax.all_gather(cotangent, 'row', axis=0, tiled=True)]
    ppermute x0 -> x14, waiting for transfers between devices: none -> 28.6 us  [the longest x10 27.6 us: along(): lax.ppermute(a, axis, [(i, (i + shift) % n) for i in range(n)])]
    convert_element_type x1 -> x2, other arithmetic: 17.1 us -> 1.73 us  [the longest x1 0.96 us: per_device(): outputs = outputs.astype(BF16)]
    ppermute x0 -> x14, starting transfers between devices: none -> 13.3 us  [the longest x10 12.7 us: along(): lax.ppermute(a, axis, [(i, (i + shift) % n) for i in range(n)])]
    unnamed x6 -> x18, local copies, waits for them, and re-layouts: 0.02 us -> 7.41 us
  transfers between devices with their start and end apart: 4 -> 14, of which waited for: 4 -> 4; matrix products, arithmetic and copies ran while one was open for 19% -> 2% of each run, Pallas kernels for 0% -> 17%
where the time goes in v2:
time: 86.9 us; the launch traced here: 85.6 us
  Pallas kernels  33.7 us (39%)
  waiting for transfers between devices  28.6 us (33%)
  starting transfers between devices  13.3 us (15%)
  local copies, waits for them, and re-layouts  7.41 us (9%)
  other arithmetic  1.8 us (2%)
    pallas_call x4, Pallas kernels, run(): pl.pallas_call(kernel, name=name, grid_spec=pltpu.PrefetchScalarGridSpec(...  33.7 us
    ppermute x10, waiting for transfers between devices, along(): lax.ppermute(a, axis, [(i, (i + shift) % n) for i in range(n)])  27.6 us
    ppermute x10, starting transfers between devices, along(): lax.ppermute(a, axis, [(i, (i + shift) % n) for i in range(n)])  12.7 us
    unnamed x18, local copies, waits for them, and re-layouts  7.41 us
  transfers between devices with their start and end apart: 14, of which 4 were waited for; matrix products, arithmetic and copies ran while one was open for 2% of the time, Pallas kernels for 17%

profile of v2, /device:TPU:0, one launch (start us, length us, event | category | flops | bytes accessed | tf_op | source)
XLA Modules:
  0.0 85.6 jit_solution(3654119597582991032)
XLA Ops:
  0.6 3.0 %collective-permute-start.1 = (bf16[96,3584]{1,0:T(8,128)(2,1)}, bf16[96,3584]{1,0:T(8,128)(2,1)S(1)}, u32[]{:S(2)}, u32[]{:S(2)}) collective-permute-start(bf16[96,3584]{1,0:T(8,128)(2,1)} %rest_0_.5), channel_id=1, source_target_pairs={{0,4},{4,0},{1,5},{5,1},{2,6},{6,2},{3,7},{7,3},{8,12},{12,8},{9,1... | collective-permute-start | bytes 2064392 | tf_op jit(solution)/shard_map/ppermute | solution.py:220
  3.7 1.5 %collective-permute-start.10 = (bf16[96,3584]{1,0:T(8,128)(2,1)}, bf16[96,3584]{1,0:T(8,128)(2,1)}, u32[]{:S(2)}, u32[]{:S(2)}) collective-permute-start(bf16[96,3584]{1,0:T(8,128)(2,1)} %rest_0_.5), channel_id=1, source_target_pairs={{0,16},{8,24},{16,0},{24,8},{1,17},{9,25},{17,1},{25,9},{2,18},{10... | collective-permute-start | bytes 2064392 | tf_op jit(solution)/shard_map/ppermute | solution.py:220
  5.2 0.1 pad_add_fusion.place
  5.2 0.0 copy-start
  5.2 5.2 %copy-done = bf16[2048,3584]{1,0:T(8,128)(2,1)S(1)} copy-done((bf16[2048,3584]{1,0:T(8,128)(2,1)S(1)}, bf16[2048,3584]{1,0:T(8,128)(2,1)}, u32[]{:S(2)}) %copy-start) | copy-done | bytes 14680088
  10.4 0.0 copy-start.3
  10.4 1.1 %copy-done.3 = bf16[192,2048]{1,0:T(8,128)(2,1)S(1)} copy-done((bf16[192,2048]{1,0:T(8,128)(2,1)S(1)}, bf16[192,2048]{1,0:T(8,128)(2,1)}, u32[]{:S(2)}) %copy-start.3) | copy-done | bytes 786456
  11.5 0.0 copy-start.1
  11.5 0.0 copy-start.4
  11.5 6.6 %forward.1 = (f32[96,3584]{1,0:T(8,128)S(1)}, bf16[96,3584]{1,0:T(8,128)(2,1)}, bf16[192,512]{1,0:T(8,128)(2,1)S(1)}, bf16[192,512]{1,0:T(8,128)(2,1)}, bf16[192,512]{1,0:T(8,128)(2,1)}) custom-call(s32[3]{0:T(128)S(1)} %pad_add_fusion.place, bf16[192,2048]{1,0:T(8,128)(2,1)S(1)} %copy-done.3, bf16[2048,3584]{1,0:T(8,128)(2,1)S(1)} %copy-done), custom_call_target="tpu_custom_call" | custom-call | flops 1 | bytes 1 | tf_op jit(solution)/shard_map/forward/pallas_call | solution.py:31
  18.2 0.0 copy-start.5
  18.2 1.1 %copy-done.5 = f32[96,3584]{1,0:T(8,128)} copy-done((f32[96,3584]{1,0:T(8,128)}, f32[96,3584]{1,0:T(8,128)S(1)}, u32[]{:S(2)}) %copy-start.5) | copy-done | bytes 1376280
  19.3 0.5 collective-permute-start
  19.8 0.0 collective-permute-done.1.rest_1_.rest_2_
  19.8 1.2 %collective-permute-start.12 = (bf16[96,3584]{1,0:T(8,128)(2,1)S(1)}, bf16[96,3584]{1,0:T(8,128)(2,1)S(1)}, u32[]{:S(2)}, u32[]{:S(2)}) collective-permute-start(bf16[96,3584]{1,0:T(8,128)(2,1)S(1)} %collective-permute-done.1.rest_1_.rest_2_), channel_id=1, source_target_pairs={{0,16},{8,24},{16,0},{24,8},{1,17},{9,25},{17,1},{25,9},{2,18},{10... | collective-permute-start | bytes 2064392 | tf_op jit(solution)/shard_map/ppermute | solution.py:220
  21.0 0.0 collective-permute-start.5
  21.0 0.8 collective-permute-start.6
  21.8 16.5 %collective-permute-done.5.rest_1_ = bf16[192,512]{1,0:T(8,128)(2,1)S(1)} collective-permute-done((bf16[192,512]{1,0:T(8,128)(2,1)S(1)}, bf16[192,512]{1,0:T(8,128)(2,1)S(1)}, u32[]{:S(2)}, u32[]{:S(2)}) %collective-permute-start.5) | collective-permute-done | bytes 196640 | tf_op jit(solution)/shard_map/ppermute | solution.py:220
  38.3 0.0 slice-start
  38.3 0.0 copy-start.6
  38.3 0.0 slice-start.1
  38.3 0.0 collective-permute-start.7
  38.3 0.0 copy-done.1
  38.3 0.0 copy-done.4
  38.3 7.1 %input_grad.1 = (f32[48,2048]{1,0:T(8,128)S(1)}, bf16[48,2048]{1,0:T(8,128)(2,1)S(1)}, bf16[48,2048]{1,0:T(8,128)(2,1)S(1)}, bf16[48,2048]{1,0:T(8,128)(2,1)S(1)}) custom-call(s32[3]{0:T(128)S(1)} %pad_add_fusion.place, bf16[96,3584]{1,0:T(8,128)(2,1)S(1)} %copy-done.4, bf16[96,3584]{1,0:T(8,128)(2,1)S(1)} %collective-permute-done.1.rest_1_.rest_2_, ...), custom_call_target="tpu_custom_call" | custom-call | flops 1 | bytes 1 | tf_op jit(solution)/shard_map/input_grad/pallas_call | solution.py:31
  45.4 0.0 copy-start.2
  45.5 0.0 collective-permute-done.6.rest_2_
  45.5 1.6 %collective-permute-start.2 = (bf16[48,2048]{1,0:T(8,128)(2,1)S(1)}, bf16[48,2048]{1,0:T(8,128)(2,1)S(1)}, u32[]{:S(2)}, u32[]{:S(2)}) collective-permute-start(bf16[48,2048]{1,0:T(8,128)(2,1)S(1)} %get-tuple-element.20), channel_id=1, source_target_pairs={{0,1},{1,2},{2,3},{3,0},{4,5},{5,6},{6,7},{7,4},{8,9},{9,10},{10,1... | collective-permute-start | bytes 589832 | tf_op jit(solution)/shard_map/ppermute | solution.py:220
  47.1 0.0 collective-permute-done.7.rest_3_
  47.1 2.6 %collective-permute-start.3 = (bf16[48,2048]{1,0:T(8,128)(2,1)S(1)}, bf16[48,2048]{1,0:T(8,128)(2,1)S(1)}, u32[]{:S(2)}, u32[]{:S(2)}) collective-permute-start(bf16[48,2048]{1,0:T(8,128)(2,1)S(1)} %get-tuple-element.21), channel_id=1, source_target_pairs={{0,2},{1,3},{2,0},{3,1},{4,6},{5,7},{6,4},{7,5},{8,10},{9,11},{10,... | collective-permute-start | bytes 589832 | tf_op jit(solution)/shard_map/ppermute | solution.py:220
  49.7 0.9 %features.1.x_ref = bf16[512,768]{1,0:T(8,128)(2,1)S(1)} custom-call(s32[3]{0:T(128)S(1)} %pad_add_fusion.place, bf16[192,2048]{1,0:T(8,128)(2,1)S(1)} %copy-done.3, bf16[192,512]{1,0:T(8,128)(2,1)S(1)} %collective-permute-done.5.rest_1_, bf16[192,512]{1,0:T(8,128)(2,1)S(1)} %collective-permute-done.6.rest_2_, ...), custom_call_target="tpu_custom_call" | custom-call | flops 1 | bytes 1 | tf_op jit(solution)/shard_map/features/pallas_call | solution.py:31
  50.6 0.0 collective-permute-done.10.rest_4_
  50.6 0.1 collective-permute-start.8
  50.7 0.0 collective-permute-done
  50.7 1.4 %collective-permute-start.4 = (bf16[48,2048]{1,0:T(8,128)(2,1)S(1)}, bf16[48,2048]{1,0:T(8,128)(2,1)S(1)}, u32[]{:S(2)}, u32[]{:S(2)}) collective-permute-start(bf16[48,2048]{1,0:T(8,128)(2,1)S(1)} %get-tuple-element.22), channel_id=1, source_target_pairs={{0,3},{1,0},{2,1},{3,2},{4,7},{5,4},{6,5},{7,6},{8,11},{9,8},{10,9... | collective-permute-start | bytes 589832 | tf_op jit(solution)/shard_map/ppermute | solution.py:220
  52.1 3.0 %collective-permute-done.2 = bf16[48,2048]{1,0:T(8,128)(2,1)S(1)} collective-permute-done((bf16[48,2048]{1,0:T(8,128)(2,1)S(1)}, bf16[48,2048]{1,0:T(8,128)(2,1)S(1)}, u32[]{:S(2)}, u32[]{:S(2)}) %collective-permute-start.2) | collective-permute-done | bytes 196640 | tf_op jit(solution)/shard_map/ppermute | solution.py:220
  55.1 0.0 collective-permute-start.9
  55.1 8.1 %collective-permute-done.3 = bf16[48,2048]{1,0:T(8,128)(2,1)S(1)} collective-permute-done((bf16[48,2048]{1,0:T(8,128)(2,1)S(1)}, bf16[48,2048]{1,0:T(8,128)(2,1)S(1)}, u32[]{:S(2)}, u32[]{:S(2)}) %collective-permute-start.3) | collective-permute-done | bytes 196640 | tf_op jit(solution)/shard_map/ppermute | solution.py:220
  63.2 0.0 collective-permute-start.11
  63.2 0.0 collective-permute-done.12.rest_6_
  63.2 0.5 collective-permute-start.13
  63.7 0.0 copy-done.6
  63.7 1.0 %add_convert_fusion = bf16[96,3584]{1,0:T(8,128)(2,1)} fusion(f32[96,3584]{1,0:T(8,128)S(1)} %copy-done.6, bf16[96,3584]{1,0:T(8,128)(2,1)S(1)} %collective-permute-done), kind=kLoop, calls=%fused_computation | loop fusion | flops 1032192 | bytes 2752512 | tf_op jit(solution)/shard_map/convert_element_type | solution.py:273
  64.6 0.0 collective-permute-done.4
  64.7 0.8 add_convert_fusion.1
  65.4 0.0 collective-permute-done.8.rest_1_
  65.4 0.0 collective-permute-done.9.rest_3_
  65.4 1.0 %collective-permute-done.11.rest_5_ = bf16[96,3584]{1,0:T(8,128)(2,1)S(1)} collective-permute-done((bf16[96,3584]{1,0:T(8,128)(2,1)}, bf16[96,3584]{1,0:T(8,128)(2,1)S(1)}, u32[]{:S(2)}, u32[]{:S(2)}) %collective-permute-start.11) | collective-permute-done | bytes 688160 | tf_op jit(solution)/shard_map/ppermute | solution.py:226
  66.4 0.0 collective-permute-done.13.rest_7_
  66.4 0.0 slice-done
  66.4 0.0 slice-done.1
  66.4 0.0 copy-done.2
  66.5 19.1 %update.1 = (bf16[512,3584]{1,0:T(8,128)(2,1)}, f32[512,3584]{1,0:T(8,128)}, f32[512,3584]{1,0:T(8,128)}) custom-call(s32[3]{0:T(128)S(1)} %pad_add_fusion.place, bf16[512,768]{1,0:T(8,128)(2,1)S(1)} %features.1.x_ref, bf16[96,3584]{1,0:T(8,128)(2,1)S(1)} %copy-done.4, bf16[96,3584]{1,0:T(8,128)(2,1)S(1)} %collective-permute-done.8.rest_1_, ...), custom_call_target="tpu_custom_call" | custom-call | flops 1 | bytes 1 | tf_op jit(solution)/shard_map/update/pallas_call | solution.py:31
  (1 shorter events, 0.0 us)
Async XLA Ops:
  0.6 19.1 %collective-permute-start.1 = (bf16[96,3584]{1,0:T(8,128)(2,1)}, bf16[96,3584]{1,0:T(8,128)(2,1)S(1)}, u32[]{:S(2)}, u32[]{:S(2)}) collective-permute-start(bf16[96,3584]{1,0:T(8,128)(2,1)} %rest_0_.5), channel_id=1, source_target_pairs={{0,4},{4,0},{1,5},{5,1},{2,6},{6,2},{3,7},{7,3},{8,12},{12,8},{9,1... | collective-permute-start | bytes 2064392 | tf_op jit(solution)/shard_map/ppermute | solution.py:220
  3.7 46.9 %collective-permute-start.10 = (bf16[96,3584]{1,0:T(8,128)(2,1)}, bf16[96,3584]{1,0:T(8,128)(2,1)}, u32[]{:S(2)}, u32[]{:S(2)}) collective-permute-start(bf16[96,3584]{1,0:T(8,128)(2,1)} %rest_0_.5), channel_id=1, source_target_pairs={{0,16},{8,24},{16,0},{24,8},{1,17},{9,25},{17,1},{25,9},{2,18},{10... | collective-permute-start | bytes 2064392 | tf_op jit(solution)/shard_map/ppermute | solution.py:220
  5.2 5.2 %copy-start = (bf16[2048,3584]{1,0:T(8,128)(2,1)S(1)}, bf16[2048,3584]{1,0:T(8,128)(2,1)}, u32[]{:S(2)}) copy-start(bf16[2048,3584]{1,0:T(8,128)(2,1)} %rest_8_.1) | copy-start | bytes 44040196
  10.4 1.1 %copy-start.3 = (bf16[192,2048]{1,0:T(8,128)(2,1)S(1)}, bf16[192,2048]{1,0:T(8,128)(2,1)}, u32[]{:S(2)}) copy-start(bf16[192,2048]{1,0:T(8,128)(2,1)} %rest_0_.4) | copy-start | bytes 2359300
  11.5 26.8 %copy-start.1 = (bf16[2048,3584]{1,0:T(8,128)(2,1)S(1)}, bf16[2048,3584]{1,0:T(8,128)(2,1)}, u32[]{:S(2)}) copy-start(bf16[2048,3584]{1,0:T(8,128)(2,1)} %rest_8_.1) | copy-start | bytes 44040196
  11.5 26.8 %copy-start.4 = (bf16[96,3584]{1,0:T(8,128)(2,1)S(1)}, bf16[96,3584]{1,0:T(8,128)(2,1)}, u32[]{:S(2)}) copy-start(bf16[96,3584]{1,0:T(8,128)(2,1)} %rest_0_.5) | copy-start | bytes 2064388
  18.2 1.1 %copy-start.5 = (f32[96,3584]{1,0:T(8,128)}, f32[96,3584]{1,0:T(8,128)S(1)}, u32[]{:S(2)}) copy-start(f32[96,3584]{1,0:T(8,128)S(1)} %get-tuple-element.17) | copy-start | bytes 4128772
  19.3 31.4 %collective-permute-start = (bf16[96,3584]{1,0:T(8,128)(2,1)}, bf16[96,3584]{1,0:T(8,128)(2,1)S(1)}, u32[]{:S(2)}, u32[]{:S(2)}) collective-permute-start(bf16[96,3584]{1,0:T(8,128)(2,1)} %get-tuple-element.18), channel_id=1, source_target_pairs={{0,4},{4,0},{1,5},{5,1},{2,6},{6,2},{3,7},{7,3},{8,12},{12,8},{9,1... | collective-permute-start | bytes 2064392 | tf_op jit(solution)/shard_map/ppermute | solution.py:220
  19.8 43.4 %collective-permute-start.12 = (bf16[96,3584]{1,0:T(8,128)(2,1)S(1)}, bf16[96,3584]{1,0:T(8,128)(2,1)S(1)}, u32[]{:S(2)}, u32[]{:S(2)}) collective-permute-start(bf16[96,3584]{1,0:T(8,128)(2,1)S(1)} %collective-permute-done.1.rest_1_.rest_2_), channel_id=1, source_target_pairs={{0,16},{8,24},{16,0},{24,8},{1,17},{9,25},{17,1},{25,9},{2,18},{10... | collective-permute-start | bytes 2064392 | tf_op jit(solution)/shard_map/ppermute | solution.py:220
  21.0 17.3 %collective-permute-start.5 = (bf16[192,512]{1,0:T(8,128)(2,1)S(1)}, bf16[192,512]{1,0:T(8,128)(2,1)S(1)}, u32[]{:S(2)}, u32[]{:S(2)}) collective-permute-start(bf16[192,512]{1,0:T(8,128)(2,1)S(1)} %get-tuple-element.23), channel_id=1, source_target_pairs={{0,8},{8,16},{16,24},{24,0},{1,9},{9,17},{17,25},{25,1},{2,10},{10... | collective-permute-start | bytes 589832 | tf_op jit(solution)/shard_map/ppermute | solution.py:220
  21.0 24.4 %collective-permute-start.6 = (bf16[192,512]{1,0:T(8,128)(2,1)}, bf16[192,512]{1,0:T(8,128)(2,1)S(1)}, u32[]{:S(2)}, u32[]{:S(2)}) collective-permute-start(bf16[192,512]{1,0:T(8,128)(2,1)} %get-tuple-element.24), channel_id=1, source_target_pairs={{0,16},{8,24},{16,0},{24,8},{1,17},{9,25},{17,1},{25,9},{2,18},{10... | collective-permute-start | bytes 589832 | tf_op jit(solution)/shard_map/ppermute | solution.py:220
  38.3 28.1 %slice-start = ((s8[7340032]{0:T(1024)(128)(4,1)}), s8[4194304]{0:T(1024)(128)(4,1)S(1)}, s32[]{:S(2)}) async-start(s8[7340032]{0:T(1024)(128)(4,1)} %bitcast.3), calls=%async_computation | async-start | bytes 8388608
  38.3 25.4 %copy-start.6 = (f32[96,3584]{1,0:T(8,128)S(1)}, f32[96,3584]{1,0:T(8,128)}, u32[]{:S(2)}) copy-start(f32[96,3584]{1,0:T(8,128)} %copy-done.5) | copy-start | bytes 4128772
  38.3 28.1 %slice-start.1 = ((s8[7340032]{0:T(1024)(128)(4,1)}), s8[3145728]{0:T(1024)(128)(4,1)S(1)}, s32[]{:S(2)}) async-start(s8[7340032]{0:T(1024)(128)(4,1)} %bitcast.3), calls=%async_computation.1 | async-start | bytes 6291456
  38.3 8.8 %collective-permute-start.7 = (bf16[192,512]{1,0:T(8,128)(2,1)}, bf16[192,512]{1,0:T(8,128)(2,1)S(1)}, u32[]{:S(2)}, u32[]{:S(2)}) collective-permute-start(bf16[192,512]{1,0:T(8,128)(2,1)} %get-tuple-element.25), channel_id=1, source_target_pairs={{0,24},{8,0},{16,8},{24,16},{1,25},{9,1},{17,9},{25,17},{2,26},{10... | collective-permute-start | bytes 589832 | tf_op jit(solution)/shard_map/ppermute | solution.py:220
  45.4 21.0 %copy-start.2 = (bf16[512,3584]{1,0:T(8,128)(2,1)S(1)}, bf16[512,3584]{1,0:T(8,128)(2,1)}, u32[]{:S(2)}) copy-start(bf16[512,3584]{1,0:T(8,128)(2,1)} %rest_9_.1) | copy-start | bytes 11010052
  45.5 9.6 %collective-permute-start.2 = (bf16[48,2048]{1,0:T(8,128)(2,1)S(1)}, bf16[48,2048]{1,0:T(8,128)(2,1)S(1)}, u32[]{:S(2)}, u32[]{:S(2)}) collective-permute-start(bf16[48,2048]{1,0:T(8,128)(2,1)S(1)} %get-tuple-element.20), channel_id=1, source_target_pairs={{0,1},{1,2},{2,3},{3,0},{4,5},{5,6},{6,7},{7,4},{8,9},{9,10},{10,1... | collective-permute-start | bytes 589832 | tf_op jit(solution)/shard_map/ppermute | solution.py:220
  47.1 16.1 %collective-permute-start.3 = (bf16[48,2048]{1,0:T(8,128)(2,1)S(1)}, bf16[48,2048]{1,0:T(8,128)(2,1)S(1)}, u32[]{:S(2)}, u32[]{:S(2)}) collective-permute-start(bf16[48,2048]{1,0:T(8,128)(2,1)S(1)} %get-tuple-element.21), channel_id=1, source_target_pairs={{0,2},{1,3},{2,0},{3,1},{4,6},{5,7},{6,4},{7,5},{8,10},{9,11},{10,... | collective-permute-start | bytes 589832 | tf_op jit(solution)/shard_map/ppermute | solution.py:220
  50.6 14.8 %collective-permute-start.8 = (bf16[96,3584]{1,0:T(8,128)(2,1)S(1)}, bf16[96,3584]{1,0:T(8,128)(2,1)S(1)}, u32[]{:S(2)}, u32[]{:S(2)}) collective-permute-start(bf16[96,3584]{1,0:T(8,128)(2,1)S(1)} %copy-done.4), channel_id=1, source_target_pairs={{0,8},{8,0},{16,24},{24,16},{1,9},{9,1},{17,25},{25,17},{2,10},{10... | collective-permute-start | bytes 2064392 | tf_op jit(solution)/shard_map/ppermute | solution.py:226
  50.7 14.0 %collective-permute-start.4 = (bf16[48,2048]{1,0:T(8,128)(2,1)S(1)}, bf16[48,2048]{1,0:T(8,128)(2,1)S(1)}, u32[]{:S(2)}, u32[]{:S(2)}) collective-permute-start(bf16[48,2048]{1,0:T(8,128)(2,1)S(1)} %get-tuple-element.22), channel_id=1, source_target_pairs={{0,3},{1,0},{2,1},{3,2},{4,7},{5,4},{6,5},{7,6},{8,11},{9,8},{10,9... | collective-permute-start | bytes 589832 | tf_op jit(solution)/shard_map/ppermute | solution.py:220
  55.1 10.3 %collective-permute-start.9 = (bf16[96,3584]{1,0:T(8,128)(2,1)S(1)}, bf16[96,3584]{1,0:T(8,128)(2,1)S(1)}, u32[]{:S(2)}, u32[]{:S(2)}) collective-permute-start(bf16[96,3584]{1,0:T(8,128)(2,1)S(1)} %collective-permute-done.1.rest_1_.rest_2_), channel_id=1, source_target_pairs={{0,8},{8,0},{16,24},{24,16},{1,9},{9,1},{17,25},{25,17},{2,10},{10... | collective-permute-start | bytes 2064392 | tf_op jit(solution)/shard_map/ppermute | solution.py:226
  63.2 3.3 %collective-permute-start.11 = (bf16[96,3584]{1,0:T(8,128)(2,1)}, bf16[96,3584]{1,0:T(8,128)(2,1)S(1)}, u32[]{:S(2)}, u32[]{:S(2)}) collective-permute-start(bf16[96,3584]{1,0:T(8,128)(2,1)} %collective-permute-done.10.rest_4_), channel_id=1, source_target_pairs={{0,8},{8,0},{16,24},{24,16},{1,9},{9,1},{17,25},{25,17},{2,10},{10... | collective-permute-start | bytes 2064392 | tf_op jit(solution)/shard_map/ppermute | solution.py:226
  63.2 3.3 %collective-permute-start.13 = (bf16[96,3584]{1,0:T(8,128)(2,1)S(1)}, bf16[96,3584]{1,0:T(8,128)(2,1)S(1)}, u32[]{:S(2)}, u32[]{:S(2)}) collective-permute-start(bf16[96,3584]{1,0:T(8,128)(2,1)S(1)} %collective-permute-done.12.rest_6_), channel_id=1, source_target_pairs={{0,8},{8,0},{16,24},{24,16},{1,9},{9,1},{17,25},{25,17},{2,10},{10... | collective-permute-start | bytes 2064392 | tf_op jit(solution)/shard_map/ppermute | solution.py:226

commit v3 on v2

--- a/solution.py
+++ b/solution.py
@@ -27,7 +27,7 @@
     return jax.ShapeDtypeStruct(shape, dtype)
 
 
-def run(kernel, name, grid, in_specs, out_specs, out_shape, scratch, limit, args):
+def run(kernel, name, grid, in_specs, out_specs, out_shape, scratch, limit, args, bytes_moved=1):
     return pl.pallas_call(
         kernel,
         name=name,
@@ -40,7 +40,9 @@
         ),
         out_shape=out_shape,
         compiler_params=pltpu.CompilerParams(vmem_limit_bytes=limit * MIB),
-        cost_estimate=pl.CostEstimate(flops=1, bytes_accessed=1, transcendentals=0),
+        cost_estimate=pl.CostEstimate(
+            flops=1, bytes_accessed=bytes_moved, transcendentals=0
+        ),
     )(*args)
 
 
@@ -52,39 +54,42 @@
     return pl.BlockSpec((rows, width), lambda j, place: (0, j))
 
 
-def forward_kernel(n_dp, n_row, own, slice_rows, place, x_ref, w_ref, *rest):
-    parts, sent, xs = rest[:n_row], rest[n_row : n_row + n_dp - 1], rest[-1]
+def forward_kernel(n_row, own, slice_rows, targets, place, x_ref, w_ref, *rest):
+    parts, sent, xs = rest[:n_row], rest[n_row:-1], rest[-1]
     dp, row = place[0], place[1]
+    tokens = x_ref.shape[0]
 
     @pl.when(pl.program_id(0) == 0)
     def _():
         for s in range(n_row):
             start = pl.multiple_of(lax.rem(row + s, n_row) * own, own)
             xs[s * own : (s + 1) * own, :] = x_ref[pl.ds(start, own), :]
-        for s in range(1, n_dp):
-            start = pl.multiple_of(lax.rem(dp + s, n_dp) * slice_rows, slice_rows)
-            sent[s - 1][...] = x_ref[:, pl.ds(start, slice_rows)]
+        for out, owners in zip(sent, targets):
+            for k, owner in enumerate(owners):
+                start = pl.multiple_of(owner(dp) * slice_rows, slice_rows)
+                out[k * tokens : (k + 1) * tokens, :] = x_ref[:, pl.ds(start, slice_rows)]
 
     acc = jnp.dot(xs[...], w_ref[...], preferred_element_type=F32)
     for s in range(n_row):
         parts[s][...] = acc[s * own : (s + 1) * own].astype(parts[s].dtype)
 
 
-def forward_call(place, inputs, weight, own, n_dp, n_row, slice_rows):
+def forward_call(place, inputs, weight, own, n_row, slice_rows, targets):
     tokens, depth = inputs.shape
     width = weight.shape[1]
     block = block_of(width, 512)
+    sent = [(len(owners) * tokens, slice_rows) for owners in targets]
     return run(
-        functools.partial(forward_kernel, n_dp, n_row, own, slice_rows),
+        functools.partial(forward_kernel, n_row, own, slice_rows, targets),
         "forward",
         (width // block,),
         [fixed((tokens, depth)), columns(depth, block)],
-        [columns(own, block)] * n_row + [fixed((tokens, slice_rows))] * (n_dp - 1),
+        [columns(own, block)] * n_row + [fixed(shape) for shape in sent],
         [struct((own, width), F32)]
         + [struct((own, width), BF16)] * (n_row - 1)
-        + [struct((tokens, slice_rows), BF16)] * (n_dp - 1),
+        + [struct(shape, BF16) for shape in sent],
         [pltpu.VMEM((tokens, depth), BF16)],
-        24,
+        52,
         (place, inputs, weight),
     )
 
@@ -120,32 +125,33 @@
         [columns(share, block)] * n_col,
         [struct((share, depth), F32)] + [struct((share, depth), BF16)] * (n_col - 1),
         [pltpu.VMEM((n_row * own, width), BF16), pltpu.VMEM((n_row * own, block), F32)],
-        24,
+        52,
         (place, *by_row, weight),
     )
 
 
-def transpose_kernel(n_dp, tokens, place, *rest):
-    pieces, out, xs = rest[:n_dp], rest[n_dp], rest[n_dp + 1]
-    for s in range(n_dp):
-        start = pl.multiple_of(lax.rem(place[0] - s + n_dp, n_dp) * tokens, tokens)
-        xs[pl.ds(start, tokens), :] = pieces[s][...]
+def features_kernel(sources, tokens, place, *rest):
+    n = len(sources)
+    pieces, out, xs = rest[:n], rest[n], rest[n + 1]
+    for piece, (origin, skip) in zip(pieces, sources):
+        start = pl.multiple_of(origin(place[0]) * tokens, tokens)
+        xs[pl.ds(start, tokens), :] = piece[skip : skip + tokens, :]
     out[...] = xs[...].T
 
 
-def transpose_call(place, inputs, pieces, slice_rows):
-    tokens, n_dp = inputs.shape[0], len(pieces) + 1
+def features_call(place, inputs, held, sources, slice_rows):
+    tokens, n_dp = inputs.shape[0], len(sources)
     return run(
-        functools.partial(transpose_kernel, n_dp, tokens),
+        functools.partial(features_kernel, sources, tokens),
         "features",
         (1,),
         [pl.BlockSpec((tokens, slice_rows), lambda j, place: (0, place[0]))]
-        + [fixed((tokens, slice_rows))] * (n_dp - 1),
+        + [fixed(piece.shape) for piece in held],
         fixed((slice_rows, n_dp * tokens)),
         struct((slice_rows, n_dp * tokens), BF16),
         [pltpu.VMEM((n_dp * tokens, slice_rows), BF16)],
         16,
-        (place, inputs, *pieces),
+        (place, inputs, *held),
     )
 
 
@@ -167,7 +173,7 @@
         cs[pl.ds(pl.multiple_of(origin(place[0], place[1]) * own, own), own), :] = piece[...]
     acc[...] = jnp.dot(x_ref[...], cs[...], preferred_element_type=F32)
 
-    @pl.loop(0, acc.shape[0] // chunk)
+    @pl.loop(0, acc.shape[0] // chunk, unroll=4)
     def _(i):
         at = pl.ds(pl.multiple_of(i * chunk, chunk), chunk)
         weight, first, second = updated(
@@ -190,7 +196,7 @@
     own = pieces[0].shape[0]
     tile = columns(rows, block)
     return run(
-        functools.partial(update_kernel, origins, tokens_all, math.gcd(rows, 16)),
+        functools.partial(update_kernel, origins, tokens_all, math.gcd(rows, 32)),
         "update",
         (width // block,),
         [fixed((rows, tokens_all))]
@@ -199,9 +205,13 @@
         [tile] * 3,
         [struct((rows, width), BF16), struct((rows, width), F32), struct((rows, width), F32)],
         [pltpu.VMEM((tokens_all, block), BF16), pltpu.VMEM((rows, block), F32)],
-        32,
+        40,
         (place, features, *pieces, weight, anchor, first, second),
     )
+
+
+def after(value, *others):
+    return lax.optimization_barrier((value, *others))[0]
 
 
 def per_device(inputs, weight, cotangent, anchor, first_moment, second_moment):
@@ -231,26 +241,19 @@
             whole = lax.dynamic_update_slice_in_dim(whole, piece, at * rows, 0)
         return whole
 
+    def dp_of(dp, c, flip):
+        core = lax.rem(dp, cores)
+        return lax.rem(dp - core - c * cores + n_dp, n_dp) + (1 - core if flip else core)
+
     by_row = [cotangent] + [along("row", n_row, s)(cotangent) for s in range(1, n_row)]
-    pieces, origins = [], []
-    for c in range(chips):
-        for s in range(n_row):
-            piece = chip_shift(c)(by_row[s]) if c else by_row[s]
-
-            def origin(dp, row, c=c, s=s, flip=0):
-                core = lax.rem(dp, cores)
-                from_core = 1 - core if flip else core
-                from_dp = lax.rem(dp - core - c * cores + n_dp, n_dp) + from_core
-                return from_dp * n_row + lax.rem(row - s + n_row, n_row)
-
-            pieces.append(piece)
-            origins.append(origin)
-            if cores == 2:
-                pieces.append(swap_cores(piece))
-                origins.append(functools.partial(origin, flip=1))
-
+    by_chip = {(c, 0): chip_shift(c)(cotangent) for c in range(1, chips)}
+    swapped = {(0, 0): swap_cores(cotangent)} if cores == 2 else {}
+
+    flips = range(cores)
+    targets = [[functools.partial(dp_of, c=0, flip=1)]] if cores == 2 else []
+    targets += [[functools.partial(dp_of, c=chips - c, flip=f) for f in flips] for c in range(1, chips)]
     if tiled:
-        made = forward_call(place, inputs, weight, own, n_dp, n_row, slice_rows)
+        made = forward_call(place, inputs, weight, own, n_row, slice_rows, targets)
         parts, to_send = made[:n_row], made[n_row:]
     else:
         part = jnp.dot(inputs, weight, preferred_element_type=F32)
@@ -261,16 +264,29 @@
             for s in range(n_row)
         ]
         to_send = [
-            lax.dynamic_slice_in_dim(
-                inputs, lax.rem(dp + s, n_dp) * slice_rows, slice_rows, 1
+            jnp.concatenate(
+                [
+                    lax.dynamic_slice_in_dim(inputs, owner(dp) * slice_rows, slice_rows, 1)
+                    for owner in owners
+                ],
+                0,
             )
-            for s in range(1, n_dp)
+            for owners in targets
         ]
-    held = [along("dp", n_dp, s)(to_send[s - 1]) for s in range(1, n_dp)]
-    outputs = parts[0]
+    to_send = list(to_send)
+    sums = [
+        along("row", n_row, s)(after(parts[s], *swapped.values())) for s in range(1, n_row)
+    ]
+    near = [swap_cores(to_send.pop(0))] if cores == 2 else []
+    first = [by_chip[c, 0] for c in range(1, chips)]
+    far = [chip_shift(c)(after(to_send[c - 1], *first)) for c in range(1, chips)]
     for s in range(1, n_row):
-        outputs = outputs + along("row", n_row, s)(parts[s]).astype(F32)
-    outputs = outputs.astype(BF16)
+        by_row[s] = after(by_row[s], parts[0], *near, *first, *swapped.values())
+        if cores == 2:
+            swapped[0, s] = swap_cores(by_row[s])
+    if cores == 2:
+        for c in range(1, chips):
+            swapped[c, 0] = swap_cores(by_chip[c, 0])
 
     if tiled:
         gparts = input_grad_call(place, by_row, weight, share, n_row, n_col)
@@ -285,20 +301,74 @@
             )
             for s in range(n_col)
         ]
-    input_grad = gparts[0]
-    for s in range(1, n_col):
-        input_grad = input_grad + along("col", n_col, s)(gparts[s]).astype(F32)
-    input_grad = input_grad.astype(BF16)
+    held, sources = [], [(functools.partial(dp_of, c=0, flip=0), 0)]
+    if cores == 2:
+        held.append(swap_cores(after(near, gparts[0])))
+        sources.append((functools.partial(dp_of, c=0, flip=1), 0))
+    for c in range(1, chips):
+        for f in flips:
+            piece = far[c - 1]
+            held.append(swap_cores(after(piece, gparts[0])) if f else piece)
+            sources.append((functools.partial(dp_of, c=c, flip=f), f * tokens))
+    pieces, origins = [], []
+    for (c, s), piece in by_chip.items():
+
+        def origin(dp, row, c=c, s=s, flip=0):
+            return dp_of(dp, c, flip) * n_row + lax.rem(row - s + n_row, n_row)
+
+        pieces.append(piece)
+        origins.append(origin)
+        if cores == 2:
+            pieces.append(swap_cores(after(piece, gparts[0])))
+            origins.append(functools.partial(origin, flip=1))
+
+    early = [swapped[k] for k in swapped]
+    for s in range(1, n_row):
+        relayed = after(by_row[s], gparts[0])
+        for c in range(1, chips):
+            by_chip[c, s] = chip_shift(c)(relayed)
+    shares = [None] * n_col
+    for s in sorted(range(1, n_col), key=lambda s: (abs(2 * s - n_col), s)):
+        shares[s] = along("col", n_col, s)(after(gparts[s], *early))
+    outputs = parts[0]
+    for part in sums:
+        outputs = outputs + part.astype(F32)
+    outputs = outputs.astype(BF16)
+
+    held, sources = list(near), [(functools.partial(dp_of, c=0, flip=0), 0)]
+    if cores == 2:
+        sources.append((functools.partial(dp_of, c=0, flip=1), 0))
+    for c in range(1, chips):
+        for f in flips:
+            piece = far[c - 1]
+            held.append(swap_cores(after(piece, *shares[1:])) if f else piece)
+            sources.append((functools.partial(dp_of, c=c, flip=f), f * tokens))
+    pieces, origins = [], []
+    for c in range(chips):
+        for s in range(n_row):
+
+            def origin(dp, row, c=c, s=s, flip=0):
+                return dp_of(dp, c, flip) * n_row + lax.rem(row - s + n_row, n_row)
+
+            piece = by_chip[c, s] if c else by_row[s]
+            pieces.append(piece)
+            origins.append(origin)
+            if cores == 2:
+                other = swapped[c, s] if (c, s) in swapped else swap_cores(after(piece, *shares[1:]))
+                pieces.append(other)
+                origins.append(functools.partial(origin, flip=1))
 
     if tiled:
-        features = transpose_call(place, inputs, held, slice_rows)
+        features = features_call(place, inputs, held, sources, slice_rows)
         new_weight, new_first, new_second = update_call(
             place, features, pieces, origins, weight, anchor, first_moment, second_moment
         )
     else:
         mine = lax.dynamic_slice_in_dim(inputs, dp * slice_rows, slice_rows, 1)
         features = in_order(
-            [mine] + held, [lax.rem(dp - s + n_dp, n_dp) for s in range(n_dp)], tokens
+            [mine] + [h[skip : skip + tokens] for h, (_, skip) in zip(held, sources[1:])],
+            [origin(dp) for origin, _ in sources],
+            tokens,
         )
         gathered = in_order(pieces, [origin(dp, row) for origin in origins], own)
         summed = lax.dot_general(
@@ -314,6 +384,10 @@
             second_moment,
         )
         new_weight = new_weight.astype(BF16)
+    input_grad = after(gparts[0], new_first)
+    for s in range(1, n_col):
+        input_grad = input_grad + shares[s].astype(F32)
+    input_grad = input_grad.astype(BF16)
     return (outputs, input_grad, new_weight, new_first, new_second)
 
 

time: 86.9 us -> 89.6 us (1.031)
  Pallas kernels: 33.7 us -> 41.9 us
  local copies, waits for them, and re-layouts: 7.41 us -> 0.28 us
  starting transfers between devices: 13.3 us -> 14.9 us
  waiting for transfers between devices: 28.6 us -> 29.5 us
    pallas_call x4, Pallas kernels: 33.7 us -> 41.9 us  [run(): pl.pallas_call(kernel, name=name, grid_spec=pltpu.PrefetchScalarGridSpec(...]
    unnamed x18 -> x12, local copies, waits for them, and re-layouts: 7.41 us -> 0.28 us
    ppermute x4 -> x6, starting transfers between devices: 0.58 us -> 1.59 us  [swap_cores(): return lax.ppermute(a, 'dp', [(i, i ^ 1) for i in range(n_dp)])]
    ppermute x10 -> x8, starting transfers between devices: 12.7 us -> 13.3 us  [along(): lax.ppermute(a, axis, [(i, (i + shift) % n) for i in range(n)])]
    ppermute x10 -> x8, waiting for transfers between devices: 27.6 us -> 28.1 us  [along(): lax.ppermute(a, axis, [(i, (i + shift) % n) for i in range(n)])]
  transfers between devices with their start and end apart: 14 -> 14, of which waited for: 4 -> 7; matrix products, arithmetic and copies ran while one was open for 2% -> 1% of each run, Pallas kernels for 17% -> 25%
where the time goes in v3:
time: 89.6 us; the launch traced here: 89.1 us
  Pallas kernels  41.9 us (47%)
  waiting for transfers between devices  29.5 us (33%)
  starting transfers between devices  14.9 us (17%)
  other arithmetic  1.81 us (2%)
    pallas_call x4, Pallas kernels, run(): pl.pallas_call(kernel, name=name, grid_spec=pltpu.PrefetchScalarGridSpec(...  41.9 us
    ppermute x8, waiting for transfers between devices, along(): lax.ppermute(a, axis, [(i, (i + shift) % n) for i in range(n)])  28.1 us
    ppermute x8, starting transfers between devices, along(): lax.ppermute(a, axis, [(i, (i + shift) % n) for i in range(n)])  13.3 us
  transfers between devices with their start and end apart: 14, of which 7 were waited for; matrix products, arithmetic and copies ran while one was open for 1% of the time, Pallas kernels for 25%

profile of v3, /device:TPU:0, one launch (start us, length us, event | category | flops | bytes accessed | tf_op | source)
XLA Modules:
  0.0 89.1 jit_solution(15593250267712715615)
XLA Ops:
  0.6 3.0 %collective-permute-start.4 = (bf16[96,3584]{1,0:T(8,128)(2,1)}, bf16[96,3584]{1,0:T(8,128)(2,1)S(1)}, u32[]{:S(2)}, u32[]{:S(2)}) collective-permute-start(bf16[96,3584]{1,0:T(8,128)(2,1)} %rest_0_.5), channel_id=1, source_target_pairs={{0,16},{8,24},{16,0},{24,8},{1,17},{9,25},{17,1},{25,9},{2,18},{10... | collective-permute-start | bytes 2064392 | tf_op jit(solution)/shard_map/ppermute | solution.py:230
  3.6 1.5 %collective-permute-start.2 = (bf16[96,3584]{1,0:T(8,128)(2,1)}, bf16[96,3584]{1,0:T(8,128)(2,1)S(1)}, u32[]{:S(2)}, u32[]{:S(2)}) collective-permute-start(bf16[96,3584]{1,0:T(8,128)(2,1)} %rest_0_.5), channel_id=1, source_target_pairs={{0,4},{4,0},{1,5},{5,1},{2,6},{6,2},{3,7},{7,3},{8,12},{12,8},{9,1... | collective-permute-start | bytes 2064392 | tf_op jit(solution)/shard_map/ppermute | solution.py:230
  5.2 0.0 collective-permute-start
  5.2 0.1 pad_add_fusion.place
  5.2 0.0 copy-start.2
  5.2 10.5 %forward.1 = (f32[96,3584]{1,0:T(8,128)}, bf16[96,3584]{1,0:T(8,128)(2,1)S(1)}, bf16[192,512]{1,0:T(8,128)(2,1)S(1)}, bf16[384,512]{1,0:T(8,128)(2,1)S(1)}) custom-call(s32[3]{0:T(128)S(1)} %pad_add_fusion.place, bf16[192,2048]{1,0:T(8,128)(2,1)} %rest_0_.4, bf16[2048,3584]{1,0:T(8,128)(2,1)} %rest_8_.1), custom_call_target="tpu_custom_call" | custom-call | flops 1 | bytes 1 | tf_op jit(solution)/shard_map/forward/pallas_call | solution.py:31
  15.8 0.5 collective-permute-start.3
  16.3 1.1 %collective-permute-done.3.rest_1_ = bf16[192,512]{1,0:T(8,128)(2,1)S(1)} collective-permute-done((bf16[192,512]{1,0:T(8,128)(2,1)S(1)}, bf16[192,512]{1,0:T(8,128)(2,1)S(1)}, u32[]{:S(2)}, u32[]{:S(2)}) %collective-permute-start.3) | collective-permute-done | bytes 196640 | tf_op jit(solution)/shard_map/ppermute | solution.py:236
  17.4 1.9 %collective-permute-done.4.rest_4_ = bf16[96,3584]{1,0:T(8,128)(2,1)S(1)} collective-permute-done((bf16[96,3584]{1,0:T(8,128)(2,1)}, bf16[96,3584]{1,0:T(8,128)(2,1)S(1)}, u32[]{:S(2)}, u32[]{:S(2)}) %collective-permute-start.4) | collective-permute-done | bytes 688160 | tf_op jit(solution)/shard_map/ppermute | solution.py:230
  19.3 1.5 %collective-permute-done.2.rest_1_.rest_2_ = bf16[96,3584]{1,0:T(8,128)(2,1)S(1)} collective-permute-done((bf16[96,3584]{1,0:T(8,128)(2,1)}, bf16[96,3584]{1,0:T(8,128)(2,1)S(1)}, u32[]{:S(2)}, u32[]{:S(2)}) %collective-permute-start.2) | collective-permute-done | bytes 688160 | tf_op jit(solution)/shard_map/ppermute | solution.py:230
  20.7 0.0 copy-start.3
  20.7 0.0 collective-permute-done.rest_1_
  20.7 0.0 copy-start.5
  20.7 0.0 copy-start.1
  20.8 0.1 collective-permute-start.7
  20.8 0.5 collective-permute-start.6
  21.3 0.3 copy-done.3
  21.6 0.0 copy-done.2
  21.6 11.2 %input_grad.1 = (f32[48,2048]{1,0:T(8,128)S(1)}, bf16[48,2048]{1,0:T(8,128)(2,1)S(1)}, bf16[48,2048]{1,0:T(8,128)(2,1)S(1)}, bf16[48,2048]{1,0:T(8,128)(2,1)S(1)}) custom-call(s32[3]{0:T(128)S(1)} %pad_add_fusion.place, bf16[96,3584]{1,0:T(8,128)(2,1)S(1)} %copy-done.2, bf16[96,3584]{1,0:T(8,128)(2,1)} %copy-done.3, bf16[2048,3584]{1,0:T(8,128)(2,1)} %rest_8_.1), custom_call_target="tpu_custom_call" | custom-call | flops 1 | bytes 1 | tf_op jit(solution)/shard_map/input_grad/pallas_call | solution.py:31
  32.8 0.0 copy-start
  32.8 0.0 copy-start.4
  32.8 0.4 collective-permute-start.12
  33.3 1.7 %collective-permute-start.1 = (bf16[96,3584]{1,0:T(8,128)(2,1)S(1)}, bf16[96,3584]{1,0:T(8,128)(2,1)S(1)}, u32[]{:S(2)}, u32[]{:S(2)}) collective-permute-start(bf16[96,3584]{1,0:T(8,128)(2,1)S(1)} %get-tuple-element.28), channel_id=1, source_target_pairs={{0,4},{4,0},{1,5},{5,1},{2,6},{6,2},{3,7},{7,3},{8,12},{12,8},{9,1... | collective-permute-start | bytes 2064392 | tf_op jit(solution)/shard_map/ppermute | solution.py:230
  35.0 1.5 %collective-permute-start.5 = (bf16[384,512]{1,0:T(8,128)(2,1)S(1)}, bf16[384,512]{1,0:T(8,128)(2,1)S(1)}, u32[]{:S(2)}, u32[]{:S(2)}) collective-permute-start(bf16[384,512]{1,0:T(8,128)(2,1)S(1)} %get-tuple-element.33), channel_id=1, source_target_pairs={{0,16},{8,24},{16,0},{24,8},{1,17},{9,25},{17,1},{25,9},{2,18},{10... | collective-permute-start | bytes 1179656 | tf_op jit(solution)/shard_map/ppermute | solution.py:230
  36.5 0.0 collective-permute-done.7.rest_5_
  36.5 0.0 collective-permute-done.6.rest_3_
  36.5 3.6 %collective-permute-start.10 = (bf16[48,2048]{1,0:T(8,128)(2,1)S(1)}, bf16[48,2048]{1,0:T(8,128)(2,1)S(1)}, u32[]{:S(2)}, u32[]{:S(2)}) collective-permute-start(bf16[48,2048]{1,0:T(8,128)(2,1)S(1)} %get-tuple-element.39), channel_id=1, source_target_pairs={{0,3},{1,0},{2,1},{3,2},{4,7},{5,4},{6,5},{7,6},{8,11},{9,8},{10,9... | collective-permute-start | bytes 589832 | tf_op jit(solution)/shard_map/ppermute | solution.py:230
  40.1 0.0 collective-permute-start.9
  40.1 18.6 %collective-permute-done.5.rest_2_ = bf16[384,512]{1,0:T(8,128)(2,1)S(1)} collective-permute-done((bf16[384,512]{1,0:T(8,128)(2,1)S(1)}, bf16[384,512]{1,0:T(8,128)(2,1)S(1)}, u32[]{:S(2)}, u32[]{:S(2)}) %collective-permute-start.5) | collective-permute-done | bytes 393248 | tf_op jit(solution)/shard_map/ppermute | solution.py:230
  58.7 1.6 %collective-permute-start.8 = (bf16[48,2048]{1,0:T(8,128)(2,1)S(1)}, bf16[48,2048]{1,0:T(8,128)(2,1)S(1)}, u32[]{:S(2)}, u32[]{:S(2)}) collective-permute-start(bf16[48,2048]{1,0:T(8,128)(2,1)S(1)} %get-tuple-element.35), channel_id=1, source_target_pairs={{0,1},{1,2},{2,3},{3,0},{4,5},{5,6},{6,7},{7,4},{8,9},{9,10},{10,1... | collective-permute-start | bytes 589832 | tf_op jit(solution)/shard_map/ppermute | solution.py:230
  60.3 0.0 collective-permute-done.10
  60.3 0.0 collective-permute-done.9
  60.3 6.0 %collective-permute-done.8 = bf16[48,2048]{1,0:T(8,128)(2,1)S(1)} collective-permute-done((bf16[48,2048]{1,0:T(8,128)(2,1)S(1)}, bf16[48,2048]{1,0:T(8,128)(2,1)S(1)}, u32[]{:S(2)}, u32[]{:S(2)}) %collective-permute-start.8) | collective-permute-done | bytes 196640 | tf_op jit(solution)/shard_map/ppermute | solution.py:230
  66.3 0.0 collective-permute-start.11
  66.4 0.0 collective-permute-done.12.rest_6_
  66.4 0.5 collective-permute-start.13
  66.9 0.0 collective-permute-done.1
  66.9 0.0 copy-done.5
  66.9 1.0 %add_convert_fusion = bf16[96,3584]{1,0:T(8,128)(2,1)} fusion(f32[96,3584]{1,0:T(8,128)S(1)} %copy-done.5, bf16[96,3584]{1,0:T(8,128)(2,1)S(1)} %collective-permute-done.1), kind=kLoop, calls=%fused_computation | loop fusion | flops 1032192 | bytes 2752512 | tf_op jit(solution)/shard_map/convert_element_type | solution.py:336
  67.8 0.2 collective-permute-done.11.rest_3_
  68.1 0.0 copy-done.1
  68.1 0.9 features.1.x_ref
  68.9 0.1 collective-permute-done.13.rest_7_
  69.1 0.0 copy-done
  69.1 0.0 copy-done.4
  69.1 19.3 %update.1 = (bf16[512,3584]{1,0:T(8,128)(2,1)}, f32[512,3584]{1,0:T(8,128)}, f32[512,3584]{1,0:T(8,128)}) custom-call(s32[3]{0:T(128)S(1)} %pad_add_fusion.place, bf16[512,768]{1,0:T(8,128)(2,1)S(1)} %features.1.x_ref, bf16[96,3584]{1,0:T(8,128)(2,1)S(1)} %copy-done.2, bf16[96,3584]{1,0:T(8,128)(2,1)S(1)} %collective-permute-done.rest_1_, ...), custom_call_target="tpu_custom_call" | custom-call | flops 1 | bytes 1 | tf_op jit(solution)/shard_map/update/pallas_call | solution.py:31
  88.3 0.8 add_convert_fusion.1
Async XLA Ops:
  0.6 18.7 %collective-permute-start.4 = (bf16[96,3584]{1,0:T(8,128)(2,1)}, bf16[96,3584]{1,0:T(8,128)(2,1)S(1)}, u32[]{:S(2)}, u32[]{:S(2)}) collective-permute-start(bf16[96,3584]{1,0:T(8,128)(2,1)} %rest_0_.5), channel_id=1, source_target_pairs={{0,16},{8,24},{16,0},{24,8},{1,17},{9,25},{17,1},{25,9},{2,18},{10... | collective-permute-start | bytes 2064392 | tf_op jit(solution)/shard_map/ppermute | solution.py:230
  3.6 17.1 %collective-permute-start.2 = (bf16[96,3584]{1,0:T(8,128)(2,1)}, bf16[96,3584]{1,0:T(8,128)(2,1)S(1)}, u32[]{:S(2)}, u32[]{:S(2)}) collective-permute-start(bf16[96,3584]{1,0:T(8,128)(2,1)} %rest_0_.5), channel_id=1, source_target_pairs={{0,4},{4,0},{1,5},{5,1},{2,6},{6,2},{3,7},{7,3},{8,12},{12,8},{9,1... | collective-permute-start | bytes 2064392 | tf_op jit(solution)/shard_map/ppermute | solution.py:230
  5.2 15.6 %collective-permute-start = (bf16[96,3584]{1,0:T(8,128)(2,1)}, bf16[96,3584]{1,0:T(8,128)(2,1)S(1)}, u32[]{:S(2)}, u32[]{:S(2)}) collective-permute-start(bf16[96,3584]{1,0:T(8,128)(2,1)} %rest_0_.5), channel_id=1, source_target_pairs={{0,8},{8,0},{16,24},{24,16},{1,9},{9,1},{17,25},{25,17},{2,10},{10... | collective-permute-start | bytes 2064392 | tf_op jit(solution)/shard_map/ppermute | solution.py:236
  5.2 16.4 %copy-start.2 = (bf16[96,3584]{1,0:T(8,128)(2,1)S(1)}, bf16[96,3584]{1,0:T(8,128)(2,1)}, u32[]{:S(2)}) copy-start(bf16[96,3584]{1,0:T(8,128)(2,1)} %rest_0_.5) | copy-start | bytes 2064388
  15.8 1.6 %collective-permute-start.3 = (bf16[192,512]{1,0:T(8,128)(2,1)S(1)}, bf16[192,512]{1,0:T(8,128)(2,1)S(1)}, u32[]{:S(2)}, u32[]{:S(2)}) collective-permute-start(bf16[192,512]{1,0:T(8,128)(2,1)S(1)} %get-tuple-element.29), channel_id=1, source_target_pairs={{0,8},{8,0},{16,24},{24,16},{1,9},{9,1},{17,25},{25,17},{2,10},{10... | collective-permute-start | bytes 589832 | tf_op jit(solution)/shard_map/ppermute | solution.py:236
  20.7 0.8 copy-start.3
  20.7 46.1 %copy-start.5 = (f32[96,3584]{1,0:T(8,128)S(1)}, f32[96,3584]{1,0:T(8,128)}, u32[]{:S(2)}) copy-start(f32[96,3584]{1,0:T(8,128)} %get-tuple-element.26) | copy-start | bytes 4128772
  20.7 47.3 %copy-start.1 = (bf16[192,2048]{1,0:T(8,128)(2,1)S(1)}, bf16[192,2048]{1,0:T(8,128)(2,1)}, u32[]{:S(2)}) copy-start(bf16[192,2048]{1,0:T(8,128)(2,1)} %rest_0_.4) | copy-start | bytes 2359300
  20.8 15.7 %collective-permute-start.7 = (bf16[96,3584]{1,0:T(8,128)(2,1)S(1)}, bf16[96,3584]{1,0:T(8,128)(2,1)S(1)}, u32[]{:S(2)}, u32[]{:S(2)}) collective-permute-start(bf16[96,3584]{1,0:T(8,128)(2,1)S(1)} %collective-permute-done.4.rest_4_), channel_id=1, source_target_pairs={{0,8},{8,0},{16,24},{24,16},{1,9},{9,1},{17,25},{25,17},{2,10},{10... | collective-permute-start | bytes 2064392 | tf_op jit(solution)/shard_map/ppermute | solution.py:236
  20.8 15.6 %collective-permute-start.6 = (bf16[96,3584]{1,0:T(8,128)(2,1)S(1)}, bf16[96,3584]{1,0:T(8,128)(2,1)S(1)}, u32[]{:S(2)}, u32[]{:S(2)}) collective-permute-start(bf16[96,3584]{1,0:T(8,128)(2,1)S(1)} %collective-permute-done.2.rest_1_.rest_2_), channel_id=1, source_target_pairs={{0,8},{8,0},{16,24},{24,16},{1,9},{9,1},{17,25},{25,17},{2,10},{10... | collective-permute-start | bytes 2064392 | tf_op jit(solution)/shard_map/ppermute | solution.py:236
  32.8 36.2 %copy-start = (bf16[512,3584]{1,0:T(8,128)(2,1)S(1)}, bf16[512,3584]{1,0:T(8,128)(2,1)}, u32[]{:S(2)}) copy-start(bf16[512,3584]{1,0:T(8,128)(2,1)} %rest_9_.1) | copy-start | bytes 11010052
  32.8 36.2 %copy-start.4 = (bf16[96,3584]{1,0:T(8,128)(2,1)S(1)}, bf16[96,3584]{1,0:T(8,128)(2,1)}, u32[]{:S(2)}) copy-start(bf16[96,3584]{1,0:T(8,128)(2,1)} %copy-done.3) | copy-start | bytes 2064388
  32.8 33.5 %collective-permute-start.12 = (bf16[96,3584]{1,0:T(8,128)(2,1)}, bf16[96,3584]{1,0:T(8,128)(2,1)S(1)}, u32[]{:S(2)}, u32[]{:S(2)}) collective-permute-start(bf16[96,3584]{1,0:T(8,128)(2,1)} %copy-done.3), channel_id=1, source_target_pairs={{0,16},{8,24},{16,0},{24,8},{1,17},{9,25},{17,1},{25,9},{2,18},{10... | collective-permute-start | bytes 2064392 | tf_op jit(solution)/shard_map/ppermute | solution.py:230
  33.3 33.6 %collective-permute-start.1 = (bf16[96,3584]{1,0:T(8,128)(2,1)S(1)}, bf16[96,3584]{1,0:T(8,128)(2,1)S(1)}, u32[]{:S(2)}, u32[]{:S(2)}) collective-permute-start(bf16[96,3584]{1,0:T(8,128)(2,1)S(1)} %get-tuple-element.28), channel_id=1, source_target_pairs={{0,4},{4,0},{1,5},{5,1},{2,6},{6,2},{3,7},{7,3},{8,12},{12,8},{9,1... | collective-permute-start | bytes 2064392 | tf_op jit(solution)/shard_map/ppermute | solution.py:230
  35.0 23.7 %collective-permute-start.5 = (bf16[384,512]{1,0:T(8,128)(2,1)S(1)}, bf16[384,512]{1,0:T(8,128)(2,1)S(1)}, u32[]{:S(2)}, u32[]{:S(2)}) collective-permute-start(bf16[384,512]{1,0:T(8,128)(2,1)S(1)} %get-tuple-element.33), channel_id=1, source_target_pairs={{0,16},{8,24},{16,0},{24,8},{1,17},{9,25},{17,1},{25,9},{2,18},{10... | collective-permute-start | bytes 1179656 | tf_op jit(solution)/shard_map/ppermute | solution.py:230
  36.5 23.8 %collective-permute-start.10 = (bf16[48,2048]{1,0:T(8,128)(2,1)S(1)}, bf16[48,2048]{1,0:T(8,128)(2,1)S(1)}, u32[]{:S(2)}, u32[]{:S(2)}) collective-permute-start(bf16[48,2048]{1,0:T(8,128)(2,1)S(1)} %get-tuple-element.39), channel_id=1, source_target_pairs={{0,3},{1,0},{2,1},{3,2},{4,7},{5,4},{6,5},{7,6},{8,11},{9,8},{10,9... | collective-permute-start | bytes 589832 | tf_op jit(solution)/shard_map/ppermute | solution.py:230
  40.1 20.2 %collective-permute-start.9 = (bf16[48,2048]{1,0:T(8,128)(2,1)S(1)}, bf16[48,2048]{1,0:T(8,128)(2,1)S(1)}, u32[]{:S(2)}, u32[]{:S(2)}) collective-permute-start(bf16[48,2048]{1,0:T(8,128)(2,1)S(1)} %get-tuple-element.37), channel_id=1, source_target_pairs={{0,2},{1,3},{2,0},{3,1},{4,6},{5,7},{6,4},{7,5},{8,10},{9,11},{10,... | collective-permute-start | bytes 589832 | tf_op jit(solution)/shard_map/ppermute | solution.py:230
  58.7 7.6 %collective-permute-start.8 = (bf16[48,2048]{1,0:T(8,128)(2,1)S(1)}, bf16[48,2048]{1,0:T(8,128)(2,1)S(1)}, u32[]{:S(2)}, u32[]{:S(2)}) collective-permute-start(bf16[48,2048]{1,0:T(8,128)(2,1)S(1)} %get-tuple-element.35), channel_id=1, source_target_pairs={{0,1},{1,2},{2,3},{3,0},{4,5},{5,6},{6,7},{7,4},{8,9},{9,10},{10,1... | collective-permute-start | bytes 589832 | tf_op jit(solution)/shard_map/ppermute | solution.py:230
  66.3 1.7 %collective-permute-start.11 = (bf16[384,512]{1,0:T(8,128)(2,1)S(1)}, bf16[384,512]{1,0:T(8,128)(2,1)S(1)}, u32[]{:S(2)}, u32[]{:S(2)}) collective-permute-start(bf16[384,512]{1,0:T(8,128)(2,1)S(1)} %collective-permute-done.5.rest_2_), channel_id=1, source_target_pairs={{0,8},{8,0},{16,24},{24,16},{1,9},{9,1},{17,25},{25,17},{2,10},{10... | collective-permute-start | bytes 1179656 | tf_op jit(solution)/shard_map/ppermute | solution.py:236
  66.4 2.7 %collective-permute-start.13 = (bf16[96,3584]{1,0:T(8,128)(2,1)S(1)}, bf16[96,3584]{1,0:T(8,128)(2,1)S(1)}, u32[]{:S(2)}, u32[]{:S(2)}) collective-permute-start(bf16[96,3584]{1,0:T(8,128)(2,1)S(1)} %collective-permute-done.12.rest_6_), channel_id=1, source_target_pairs={{0,8},{8,0},{16,24},{24,16},{1,9},{9,1},{17,25},{25,17},{2,10},{10... | collective-permute-start | bytes 2064392 | tf_op jit(solution)/shard_map/ppermute | solution.py:236

commit v4 on v3

--- a/solution.py
+++ b/solution.py
@@ -54,7 +54,8 @@
     return pl.BlockSpec((rows, width), lambda j, place: (0, j))
 
 
-def forward_kernel(n_row, own, slice_rows, targets, place, x_ref, w_ref, *rest):
+def forward_kernel(n_row, own, slice_rows, targets, cuts, place, x_ref, *rest):
+    w_refs, rest = rest[:cuts], rest[cuts:]
     parts, sent, xs = rest[:n_row], rest[n_row:-1], rest[-1]
     dp, row = place[0], place[1]
     tokens = x_ref.shape[0]
@@ -69,7 +70,11 @@
                 start = pl.multiple_of(owner(dp) * slice_rows, slice_rows)
                 out[k * tokens : (k + 1) * tokens, :] = x_ref[:, pl.ds(start, slice_rows)]
 
-    acc = jnp.dot(xs[...], w_ref[...], preferred_element_type=F32)
+    acc, at = None, 0
+    for w_ref in w_refs:
+        deep = w_ref.shape[0]
+        part = jnp.dot(xs[:, at : at + deep], w_ref[...], preferred_element_type=F32)
+        acc, at = part if acc is None else acc + part, at + deep
     for s in range(n_row):
         parts[s][...] = acc[s * own : (s + 1) * own].astype(parts[s].dtype)
 
@@ -78,26 +83,33 @@
     tokens, depth = inputs.shape
     width = weight.shape[1]
     block = block_of(width, 512)
+    cuts = 4 if depth % 1024 == 0 else 1
     sent = [(len(owners) * tokens, slice_rows) for owners in targets]
     return run(
-        functools.partial(forward_kernel, n_row, own, slice_rows, targets),
+        functools.partial(forward_kernel, n_row, own, slice_rows, targets, cuts),
         "forward",
         (width // block,),
-        [fixed((tokens, depth)), columns(depth, block)],
+        [fixed((tokens, depth))]
+        + [
+            pl.BlockSpec(
+                (depth // cuts, block), lambda j, place, k=k: (k, j)
+            )
+            for k in range(cuts)
+        ],
         [columns(own, block)] * n_row + [fixed(shape) for shape in sent],
         [struct((own, width), F32)]
         + [struct((own, width), BF16)] * (n_row - 1)
         + [struct(shape, BF16) for shape in sent],
         [pltpu.VMEM((tokens, depth), BF16)],
         52,
-        (place, inputs, weight),
-    )
-
-
-def input_grad_kernel(n_row, n_col, own, share, place, *rest):
-    pieces, w_ref = rest[:n_row], rest[n_row]
-    parts, (cs, acc) = rest[n_row + 1 : n_row + 1 + n_col], rest[-2:]
-    row, col = place[1], place[2]
+        (place, inputs, *[weight] * cuts),
+    )
+
+
+def input_grad_kernel(n_row, own, cuts, place, *rest):
+    pieces, w_refs = rest[:n_row], rest[n_row : n_row + cuts]
+    out, cs = rest[n_row + cuts :]
+    row = place[1]
 
     @pl.when(pl.program_id(0) == 0)
     def _():
@@ -105,28 +117,40 @@
             start = pl.multiple_of(lax.rem(row - s + n_row, n_row) * own, own)
             cs[pl.ds(start, own), :] = pieces[s][...]
 
-    acc[...] = lax.dot_general(
-        cs[...], w_ref[...], (((1,), (1,)), ((), ())), preferred_element_type=F32
-    )
-    for s in range(n_col):
-        start = pl.multiple_of(lax.rem(col + s, n_col) * share, share)
-        parts[s][...] = acc[pl.ds(start, share), :].astype(parts[s].dtype)
-
-
-def input_grad_call(place, by_row, weight, share, n_row, n_col):
+    acc, at = None, 0
+    for w_ref in w_refs:
+        deep = w_ref.shape[1]
+        part = lax.dot_general(
+            cs[:, at : at + deep],
+            w_ref[...],
+            (((1,), (1,)), ((), ())),
+            preferred_element_type=F32,
+        )
+        acc, at = part if acc is None else acc + part, at + deep
+    out[...] = acc.astype(BF16)
+
+
+def input_grad_call(place, by_row, weight, n_row):
     own, width = by_row[0].shape
     depth = weight.shape[0]
     block = block_of(depth, 256)
+    cuts = 2 if width % 512 == 0 else 1
     return run(
-        functools.partial(input_grad_kernel, n_row, n_col, own, share),
+        functools.partial(input_grad_kernel, n_row, own, cuts),
         "input_grad",
         (depth // block,),
-        [fixed((own, width))] * n_row + [pl.BlockSpec((block, width), lambda j, place: (j, 0))],
-        [columns(share, block)] * n_col,
-        [struct((share, depth), F32)] + [struct((share, depth), BF16)] * (n_col - 1),
-        [pltpu.VMEM((n_row * own, width), BF16), pltpu.VMEM((n_row * own, block), F32)],
+        [fixed((own, width))] * n_row
+        + [
+            pl.BlockSpec(
+                (block, width // cuts), lambda j, place, k=k: (j, k)
+            )
+            for k in range(cuts)
+        ],
+        columns(n_row * own, block),
+        struct((n_row * own, depth), BF16),
+        [pltpu.VMEM((n_row * own, width), BF16)],
         52,
-        (place, *by_row, weight),
+        (place, *by_row, *[weight] * cuts),
     )
 
 
@@ -155,13 +179,19 @@
     )
 
 
-def updated(grad_sum, tokens_all, current, anchor, first, second):
+def inverse(value):
+    guess = pl.reciprocal(value, approx=True)
+    return guess * (2.0 - value * guess)
+
+
+def updated(grad_sum, tokens_all, current, anchor, first, second, invert):
     grad = grad_sum * (1.0 / tokens_all) + anchor_pull * (current - anchor)
     first = beta_one * first + (1.0 - beta_one) * grad
     second = beta_two * second + (1.0 - beta_two) * grad * grad
-    scale = learn_rate / (1.0 - beta_one**step_count)
-    spread = jnp.sqrt(second * (1.0 / (1.0 - beta_two**step_count))) + epsilon
-    return current - scale * first / spread, first, second
+    root = math.sqrt(1.0 / (1.0 - beta_two**step_count))
+    scale = learn_rate / (1.0 - beta_one**step_count) / root
+    spread = second * lax.rsqrt(second) + epsilon / root
+    return current - (scale * first) * invert(spread), first, second
 
 
 def update_kernel(origins, tokens_all, chunk, place, x_ref, *rest):
@@ -183,6 +213,7 @@
             a_ref[at, :].astype(F32),
             m_ref[at, :],
             v_ref[at, :],
+            inverse,
         )
         new_w[at, :] = weight.astype(BF16)
         new_m[at, :] = first
@@ -289,47 +320,16 @@
             swapped[c, 0] = swap_cores(by_chip[c, 0])
 
     if tiled:
-        gparts = input_grad_call(place, by_row, weight, share, n_row, n_col)
+        gpart = input_grad_call(place, by_row, weight, n_row)
     else:
         gathered = in_order(by_row, [lax.rem(row - s + n_row, n_row) for s in range(n_row)], own)
         gpart = lax.dot_general(
             gathered, weight, (((1,), (1,)), ((), ())), preferred_element_type=F32
-        )
-        gparts = [
-            lax.dynamic_slice_in_dim(gpart, lax.rem(col + s, n_col) * share, share, 0).astype(
-                BF16 if s else F32
-            )
-            for s in range(n_col)
-        ]
-    held, sources = [], [(functools.partial(dp_of, c=0, flip=0), 0)]
-    if cores == 2:
-        held.append(swap_cores(after(near, gparts[0])))
-        sources.append((functools.partial(dp_of, c=0, flip=1), 0))
-    for c in range(1, chips):
-        for f in flips:
-            piece = far[c - 1]
-            held.append(swap_cores(after(piece, gparts[0])) if f else piece)
-            sources.append((functools.partial(dp_of, c=c, flip=f), f * tokens))
-    pieces, origins = [], []
-    for (c, s), piece in by_chip.items():
-
-        def origin(dp, row, c=c, s=s, flip=0):
-            return dp_of(dp, c, flip) * n_row + lax.rem(row - s + n_row, n_row)
-
-        pieces.append(piece)
-        origins.append(origin)
-        if cores == 2:
-            pieces.append(swap_cores(after(piece, gparts[0])))
-            origins.append(functools.partial(origin, flip=1))
-
-    early = [swapped[k] for k in swapped]
+        ).astype(BF16)
+    gparts = lax.all_to_all(gpart, "col", 0, 0, tiled=True)
     for s in range(1, n_row):
-        relayed = after(by_row[s], gparts[0])
         for c in range(1, chips):
-            by_chip[c, s] = chip_shift(c)(relayed)
-    shares = [None] * n_col
-    for s in sorted(range(1, n_col), key=lambda s: (abs(2 * s - n_col), s)):
-        shares[s] = along("col", n_col, s)(after(gparts[s], *early))
+            by_chip[c, s] = chip_shift(c)(by_row[s])
     outputs = parts[0]
     for part in sums:
         outputs = outputs + part.astype(F32)
@@ -341,7 +341,7 @@
     for c in range(1, chips):
         for f in flips:
             piece = far[c - 1]
-            held.append(swap_cores(after(piece, *shares[1:])) if f else piece)
+            held.append(swap_cores(piece) if f else piece)
             sources.append((functools.partial(dp_of, c=c, flip=f), f * tokens))
     pieces, origins = [], []
     for c in range(chips):
@@ -354,7 +354,7 @@
             pieces.append(piece)
             origins.append(origin)
             if cores == 2:
-                other = swapped[c, s] if (c, s) in swapped else swap_cores(after(piece, *shares[1:]))
+                other = swapped[c, s] if (c, s) in swapped else swap_cores(piece)
                 pieces.append(other)
                 origins.append(functools.partial(origin, flip=1))
 
@@ -382,12 +382,12 @@
             anchor.astype(F32),
             first_moment,
             second_moment,
+            lambda value: 1.0 / value,
         )
         new_weight = new_weight.astype(BF16)
-    input_grad = after(gparts[0], new_first)
-    for s in range(1, n_col):
-        input_grad = input_grad + shares[s].astype(F32)
-    input_grad = input_grad.astype(BF16)
+    input_grad = sum(
+        lax.slice_in_dim(gparts, k * share, (k + 1) * share).astype(F32) for k in range(n_col)
+    ).astype(BF16)
     return (outputs, input_grad, new_weight, new_first, new_second)
 
 

time: 89.6 us -> 87 us (0.971)
  waiting for transfers between devices: 29.5 us -> 19.1 us
  local copies, waits for them, and re-layouts: 0.28 us -> 3.98 us
  other arithmetic: 1.81 us -> 4.55 us
  Pallas kernels: 41.9 us -> 43.8 us
    ppermute x8 -> x5, waiting for transfers between devices: 28.1 us -> 8.64 us  [along(): lax.ppermute(a, axis, [(i, (i + shift) % n) for i in range(n)])]
    all_to_all x0 -> x1, waiting for transfers between devices: none -> 9.88 us  [per_device(): gparts = lax.all_to_all(gpart, 'col', 0, 0, tiled=True)]
    ppermute x8 -> x5, starting transfers between devices: 13.3 us -> 7.63 us  [along(): lax.ppermute(a, axis, [(i, (i + shift) % n) for i in range(n)])]
    all_to_all x0 -> x1, starting transfers between devices: none -> 4.99 us  [per_device(): gparts = lax.all_to_all(gpart, 'col', 0, 0, tiled=True)]
    unnamed x12 -> x10, local copies, waits for them, and re-layouts: 0.28 us -> 3.98 us
    add x0 -> x1, other arithmetic: none -> 2 us  [per_device(): sum((lax.slice_in_dim(gparts, k * share, (k + 1) * share).astype(F32) for...]
    pallas_call x4, Pallas kernels: 41.9 us -> 43.8 us  [run(): pl.pallas_call(kernel, name=name, grid_spec=pltpu.PrefetchScalarGridSpec(...]
    convert_element_type x1, other arithmetic: 0.96 us -> 2.47 us  [per_device(): outputs = outputs.astype(BF16)]
  transfers between devices with their start and end apart: 14 -> 12, of which waited for: 7 -> 5; matrix products, arithmetic and copies ran while one was open for 1% -> 5% of each run, Pallas kernels for 25% -> 27%
where the time goes in v4:
time: 87 us; the launch traced here: 86.3 us
  Pallas kernels  43.8 us (50%)
  waiting for transfers between devices  19.1 us (22%)
  starting transfers between devices  14.2 us (16%)
  other arithmetic  4.55 us (5%)
  local copies, waits for them, and re-layouts  3.98 us (5%)
    pallas_call x4, Pallas kernels, run(): pl.pallas_call(kernel, name=name, grid_spec=pltpu.PrefetchScalarGridSpec(...  43.8 us
    all_to_all x1, waiting for transfers between devices, per_device(): gparts = lax.all_to_all(gpart, 'col', 0, 0, tiled=True)  9.88 us
    ppermute x5, waiting for transfers between devices, along(): lax.ppermute(a, axis, [(i, (i + shift) % n) for i in range(n)])  8.64 us
    ppermute x5, starting transfers between devices, along(): lax.ppermute(a, axis, [(i, (i + shift) % n) for i in range(n)])  7.63 us
    all_to_all x1, starting transfers between devices, per_device(): gparts = lax.all_to_all(gpart, 'col', 0, 0, tiled=True)  4.99 us
    unnamed x10, local copies, waits for them, and re-layouts  3.98 us
    convert_element_type x1, other arithmetic, per_device(): outputs = outputs.astype(BF16)  2.47 us
    add x1, other arithmetic, per_device(): sum((lax.slice_in_dim(gparts, k * share, (k + 1) * share).astype(F32) for...  2 us
  transfers between devices with their start and end apart: 12, of which 5 were waited for; matrix products, arithmetic and copies ran while one was open for 5% of the time, Pallas kernels for 27%

profile of v4, /device:TPU:0, one launch (start us, length us, event | category | flops | bytes accessed | tf_op | source)
XLA Modules:
  0.0 86.3 jit_solution(6316032837176473581)
XLA Ops:
  0.6 0.5 collective-permute-start
  1.1 2.6 %collective-permute-start.4 = (bf16[96,3584]{1,0:T(8,128)(2,1)}, bf16[96,3584]{1,0:T(8,128)(2,1)}, u32[]{:S(2)}, u32[]{:S(2)}) collective-permute-start(bf16[96,3584]{1,0:T(8,128)(2,1)} %rest_0_.7), channel_id=1, source_target_pairs={{0,16},{8,24},{16,0},{24,8},{1,17},{9,25},{17,1},{25,9},{2,18},{10... | collective-permute-start | bytes 2064392 | tf_op jit(solution)/shard_map/ppermute | solution.py:261
  3.7 1.5 %collective-permute-start.2 = (bf16[96,3584]{1,0:T(8,128)(2,1)}, bf16[96,3584]{1,0:T(8,128)(2,1)S(1)}, u32[]{:S(2)}, u32[]{:S(2)}) collective-permute-start(bf16[96,3584]{1,0:T(8,128)(2,1)} %rest_0_.7), channel_id=1, source_target_pairs={{0,4},{4,0},{1,5},{5,1},{2,6},{6,2},{3,7},{7,3},{8,12},{12,8},{9,1... | collective-permute-start | bytes 2064392 | tf_op jit(solution)/shard_map/ppermute | solution.py:261
  5.2 0.1 pad_add_fusion.place
  5.3 0.0 copy-start.2
  5.3 10.7 %forward.1 = (f32[96,3584]{1,0:T(8,128)}, bf16[96,3584]{1,0:T(8,128)(2,1)S(1)}, bf16[192,512]{1,0:T(8,128)(2,1)S(1)}, bf16[384,512]{1,0:T(8,128)(2,1)}) custom-call(s32[3]{0:T(128)S(1)} %pad_add_fusion.place, bf16[192,2048]{1,0:T(8,128)(2,1)} %rest_0_.6, bf16[2048,3584]{1,0:T(8,128)(2,1)} %rest_8_.1, bf16[2048,3584]{1,0:T(8,128)(2,1)} %rest_8_.1, ...), custom_call_target="tpu_custom_call" | custom-call | flops 1 | bytes 1 | tf_op jit(solution)/shard_map/forward/pallas_call | solution.py:31
  16.0 0.0 collective-permute-start.3
  16.0 0.0 collective-permute-done.rest_1_
  16.0 0.0 copy-start.3
  16.0 0.8 copy-done.3
  16.8 0.6 collective-permute-done.3.rest_1_
  17.4 2.6 %collective-permute-done.4.rest_4_ = bf16[96,3584]{1,0:T(8,128)(2,1)} collective-permute-done((bf16[96,3584]{1,0:T(8,128)(2,1)}, bf16[96,3584]{1,0:T(8,128)(2,1)}, u32[]{:S(2)}, u32[]{:S(2)}) %collective-permute-start.4) | collective-permute-done | bytes 688160 | tf_op jit(solution)/shard_map/ppermute | solution.py:261
  20.1 1.4 %collective-permute-done.2.rest_1_.rest_2_ = bf16[96,3584]{1,0:T(8,128)(2,1)S(1)} collective-permute-done((bf16[96,3584]{1,0:T(8,128)(2,1)}, bf16[96,3584]{1,0:T(8,128)(2,1)S(1)}, u32[]{:S(2)}, u32[]{:S(2)}) %collective-permute-start.2) | collective-permute-done | bytes 688160 | tf_op jit(solution)/shard_map/ppermute | solution.py:261
  21.4 0.4 collective-permute-start.9
  21.8 1.7 %collective-permute-start.1 = (bf16[96,3584]{1,0:T(8,128)(2,1)S(1)}, bf16[96,3584]{1,0:T(8,128)(2,1)}, u32[]{:S(2)}, u32[]{:S(2)}) collective-permute-start(bf16[96,3584]{1,0:T(8,128)(2,1)S(1)} %get-tuple-element.17), channel_id=1, source_target_pairs={{0,4},{4,0},{1,5},{5,1},{2,6},{6,2},{3,7},{7,3},{8,12},{12,8},{9,1... | collective-permute-start | bytes 2064392 | tf_op jit(solution)/shard_map/ppermute | solution.py:261
  23.5 1.5 %collective-permute-start.5 = (bf16[384,512]{1,0:T(8,128)(2,1)}, bf16[384,512]{1,0:T(8,128)(2,1)S(1)}, u32[]{:S(2)}, u32[]{:S(2)}) collective-permute-start(bf16[384,512]{1,0:T(8,128)(2,1)} %get-tuple-element.21), channel_id=1, source_target_pairs={{0,16},{8,24},{16,0},{24,8},{1,17},{9,25},{17,1},{25,9},{2,18},{10... | collective-permute-start | bytes 1179656 | tf_op jit(solution)/shard_map/ppermute | solution.py:261
  25.0 0.0 copy-done.2
  25.0 11.4 %input_grad.1 = bf16[192,2048]{1,0:T(8,128)(2,1)} custom-call(s32[3]{0:T(128)S(1)} %pad_add_fusion.place, bf16[96,3584]{1,0:T(8,128)(2,1)S(1)} %copy-done.2, bf16[96,3584]{1,0:T(8,128)(2,1)S(1)} %collective-permute-done.2.rest_1_.rest_2_, bf16[2048,3584]{1,0:T(8,128)(2,1)} %rest_8_.1, bf16[2048,3584]{1,0:T(8,128)(2,1)} %rest_8_.1), custom_call_target="tpu_custom_call" | custom-call | flops 1 | bytes 1 | tf_op jit(solution)/shard_map/input_grad/pallas_call | solution.py:31
  36.4 0.0 copy-start.1
  36.4 5.0 %all-to-all-start = ((bf16[4,48,2048]{2,1,0:T(8,128)(2,1)}), bf16[4,48,2048]{2,1,0:T(8,128)(2,1)}, u32[]{:S(2)}, u32[]{:S(2)}) async-start(bf16[4,48,2048]{2,1,0:T(8,128)(2,1)} %bitcast.6), calls=%async_computation | async-start | bytes 1572864 | tf_op jit(solution)/shard_map/all_to_all | solution.py:329
  41.4 0.0 collective-permute-start.7
  41.4 0.5 collective-permute-start.8
  41.9 4.6 %collective-permute-done.5.rest_2_ = bf16[384,512]{1,0:T(8,128)(2,1)S(1)} collective-permute-done((bf16[384,512]{1,0:T(8,128)(2,1)}, bf16[384,512]{1,0:T(8,128)(2,1)S(1)}, u32[]{:S(2)}, u32[]{:S(2)}) %collective-permute-start.5) | collective-permute-done | bytes 393248 | tf_op jit(solution)/shard_map/ppermute | solution.py:261
  46.5 0.0 collective-permute-start.6
  46.5 0.0 collective-permute-done.9.rest_6_
  46.5 0.5 collective-permute-start.10
  47.0 0.0 collective-permute-done.1
  47.1 2.5 %add_convert_fusion = bf16[96,3584]{1,0:T(8,128)(2,1)} fusion(f32[96,3584]{1,0:T(8,128)} %get-tuple-element.15, bf16[96,3584]{1,0:T(8,128)(2,1)} %collective-permute-done.1), kind=kLoop, calls=%fused_computation | loop fusion | flops 1032192 | bytes 2752512 | tf_op jit(solution)/shard_map/convert_element_type | solution.py:336
  49.5 0.0 collective-permute-done.6.rest_3_
  49.5 0.0 copy-done.1
  49.5 0.9 features.1.x_ref
  50.4 9.9 %all-to-all-done = bf16[4,48,2048]{2,1,0:T(8,128)(2,1)} async-done(((bf16[4,48,2048]{2,1,0:T(8,128)(2,1)}), bf16[4,48,2048]{2,1,0:T(8,128)(2,1)}, u32[]{:S(2)}, u32[]{:S(2)}) %all-to-all-start) | async-done | bytes 786464 | tf_op jit(solution)/shard_map/all_to_all | solution.py:329
  60.3 2.0 %fusion = bf16[48,2048]{1,0:T(8,128)(2,1)} fusion(bf16[4,48,2048]{2,1,0:T(8,128)(2,1)} %all-to-all-done), kind=kLoop, calls=%fused_computation.2 | loop fusion | flops 786432 | bytes 983040 | tf_op jit(solution)/shard_map/add | solution.py:388
  62.3 0.0 collective-permute-done.8.rest_5_
  62.3 0.0 collective-permute-done.7.rest_3_
  62.3 0.0 collective-permute-done.10.rest_7_
  62.3 0.0 copy-start
  62.3 2.0 %copy-done = bf16[512,3584]{1,0:T(8,128)(2,1)S(1)} copy-done((bf16[512,3584]{1,0:T(8,128)(2,1)S(1)}, bf16[512,3584]{1,0:T(8,128)(2,1)}, u32[]{:S(2)}) %copy-start) | copy-done | bytes 3670040
  64.3 0.0 copy-start.4
  64.3 1.1 %copy-done.4 = bf16[96,3584]{1,0:T(8,128)(2,1)S(1)} copy-done((bf16[96,3584]{1,0:T(8,128)(2,1)S(1)}, bf16[96,3584]{1,0:T(8,128)(2,1)}, u32[]{:S(2)}) %copy-start.4) | copy-done | bytes 688152
  65.4 20.8 %update.1 = (bf16[512,3584]{1,0:T(8,128)(2,1)}, f32[512,3584]{1,0:T(8,128)}, f32[512,3584]{1,0:T(8,128)}) custom-call(s32[3]{0:T(128)S(1)} %pad_add_fusion.place, bf16[512,768]{1,0:T(8,128)(2,1)S(1)} %features.1.x_ref, bf16[96,3584]{1,0:T(8,128)(2,1)S(1)} %copy-done.2, bf16[96,3584]{1,0:T(8,128)(2,1)S(1)} %copy-done.4, ...), custom_call_target="tpu_custom_call" | custom-call | flops 1 | bytes 1 | tf_op jit(solution)/shard_map/update/pallas_call | solution.py:31
Async XLA Ops:
  0.6 15.3 %collective-permute-start = (bf16[96,3584]{1,0:T(8,128)(2,1)}, bf16[96,3584]{1,0:T(8,128)(2,1)S(1)}, u32[]{:S(2)}, u32[]{:S(2)}) collective-permute-start(bf16[96,3584]{1,0:T(8,128)(2,1)} %rest_0_.7), channel_id=1, source_target_pairs={{0,8},{8,0},{16,24},{24,16},{1,9},{9,1},{17,25},{25,17},{2,10},{10... | collective-permute-start | bytes 2064392 | tf_op jit(solution)/shard_map/ppermute | solution.py:267
  1.1 18.9 %collective-permute-start.4 = (bf16[96,3584]{1,0:T(8,128)(2,1)}, bf16[96,3584]{1,0:T(8,128)(2,1)}, u32[]{:S(2)}, u32[]{:S(2)}) collective-permute-start(bf16[96,3584]{1,0:T(8,128)(2,1)} %rest_0_.7), channel_id=1, source_target_pairs={{0,16},{8,24},{16,0},{24,8},{1,17},{9,25},{17,1},{25,9},{2,18},{10... | collective-permute-start | bytes 2064392 | tf_op jit(solution)/shard_map/ppermute | solution.py:261
  3.7 17.7 %collective-permute-start.2 = (bf16[96,3584]{1,0:T(8,128)(2,1)}, bf16[96,3584]{1,0:T(8,128)(2,1)S(1)}, u32[]{:S(2)}, u32[]{:S(2)}) collective-permute-start(bf16[96,3584]{1,0:T(8,128)(2,1)} %rest_0_.7), channel_id=1, source_target_pairs={{0,4},{4,0},{1,5},{5,1},{2,6},{6,2},{3,7},{7,3},{8,12},{12,8},{9,1... | collective-permute-start | bytes 2064392 | tf_op jit(solution)/shard_map/ppermute | solution.py:261
  5.3 19.7 %copy-start.2 = (bf16[96,3584]{1,0:T(8,128)(2,1)S(1)}, bf16[96,3584]{1,0:T(8,128)(2,1)}, u32[]{:S(2)}) copy-start(bf16[96,3584]{1,0:T(8,128)(2,1)} %rest_0_.7) | copy-start | bytes 2064388
  16.0 1.4 %collective-permute-start.3 = (bf16[192,512]{1,0:T(8,128)(2,1)S(1)}, bf16[192,512]{1,0:T(8,128)(2,1)S(1)}, u32[]{:S(2)}, u32[]{:S(2)}) collective-permute-start(bf16[192,512]{1,0:T(8,128)(2,1)S(1)} %get-tuple-element.18), channel_id=1, source_target_pairs={{0,8},{8,0},{16,24},{24,16},{1,9},{9,1},{17,25},{25,17},{2,10},{10... | collective-permute-start | bytes 589832 | tf_op jit(solution)/shard_map/ppermute | solution.py:267
  16.0 0.8 copy-start.3
  21.4 25.1 %collective-permute-start.9 = (bf16[96,3584]{1,0:T(8,128)(2,1)S(1)}, bf16[96,3584]{1,0:T(8,128)(2,1)}, u32[]{:S(2)}, u32[]{:S(2)}) collective-permute-start(bf16[96,3584]{1,0:T(8,128)(2,1)S(1)} %collective-permute-done.2.rest_1_.rest_2_), channel_id=1, source_target_pairs={{0,16},{8,24},{16,0},{24,8},{1,17},{9,25},{17,1},{25,9},{2,18},{10... | collective-permute-start | bytes 2064392 | tf_op jit(solution)/shard_map/ppermute | solution.py:261
  21.8 25.2 %collective-permute-start.1 = (bf16[96,3584]{1,0:T(8,128)(2,1)S(1)}, bf16[96,3584]{1,0:T(8,128)(2,1)}, u32[]{:S(2)}, u32[]{:S(2)}) collective-permute-start(bf16[96,3584]{1,0:T(8,128)(2,1)S(1)} %get-tuple-element.17), channel_id=1, source_target_pairs={{0,4},{4,0},{1,5},{5,1},{2,6},{6,2},{3,7},{7,3},{8,12},{12,8},{9,1... | collective-permute-start | bytes 2064392 | tf_op jit(solution)/shard_map/ppermute | solution.py:261
  23.5 23.0 %collective-permute-start.5 = (bf16[384,512]{1,0:T(8,128)(2,1)}, bf16[384,512]{1,0:T(8,128)(2,1)S(1)}, u32[]{:S(2)}, u32[]{:S(2)}) collective-permute-start(bf16[384,512]{1,0:T(8,128)(2,1)} %get-tuple-element.21), channel_id=1, source_target_pairs={{0,16},{8,24},{16,0},{24,8},{1,17},{9,25},{17,1},{25,9},{2,18},{10... | collective-permute-start | bytes 1179656 | tf_op jit(solution)/shard_map/ppermute | solution.py:261
  36.4 13.1 %copy-start.1 = (bf16[192,2048]{1,0:T(8,128)(2,1)S(1)}, bf16[192,2048]{1,0:T(8,128)(2,1)}, u32[]{:S(2)}) copy-start(bf16[192,2048]{1,0:T(8,128)(2,1)} %rest_0_.6) | copy-start | bytes 2359300
  36.4 23.9 %all-to-all-start = ((bf16[4,48,2048]{2,1,0:T(8,128)(2,1)}), bf16[4,48,2048]{2,1,0:T(8,128)(2,1)}, u32[]{:S(2)}, u32[]{:S(2)}) async-start(bf16[4,48,2048]{2,1,0:T(8,128)(2,1)} %bitcast.6), calls=%async_computation | async-start | bytes 1572864 | tf_op jit(solution)/shard_map/all_to_all | solution.py:329
  41.4 20.9 %collective-permute-start.7 = (bf16[96,3584]{1,0:T(8,128)(2,1)S(1)}, bf16[96,3584]{1,0:T(8,128)(2,1)}, u32[]{:S(2)}, u32[]{:S(2)}) collective-permute-start(bf16[96,3584]{1,0:T(8,128)(2,1)S(1)} %collective-permute-done.2.rest_1_.rest_2_), channel_id=1, source_target_pairs={{0,8},{8,0},{16,24},{24,16},{1,9},{9,1},{17,25},{25,17},{2,10},{10... | collective-permute-start | bytes 2064392 | tf_op jit(solution)/shard_map/ppermute | solution.py:267
  41.4 20.9 %collective-permute-start.8 = (bf16[96,3584]{1,0:T(8,128)(2,1)}, bf16[96,3584]{1,0:T(8,128)(2,1)}, u32[]{:S(2)}, u32[]{:S(2)}) collective-permute-start(bf16[96,3584]{1,0:T(8,128)(2,1)} %collective-permute-done.4.rest_4_), channel_id=1, source_target_pairs={{0,8},{8,0},{16,24},{24,16},{1,9},{9,1},{17,25},{25,17},{2,10},{10... | collective-permute-start | bytes 2064392 | tf_op jit(solution)/shard_map/ppermute | solution.py:267
  46.5 3.0 %collective-permute-start.6 = (bf16[384,512]{1,0:T(8,128)(2,1)S(1)}, bf16[384,512]{1,0:T(8,128)(2,1)S(1)}, u32[]{:S(2)}, u32[]{:S(2)}) collective-permute-start(bf16[384,512]{1,0:T(8,128)(2,1)S(1)} %collective-permute-done.5.rest_2_), channel_id=1, source_target_pairs={{0,8},{8,0},{16,24},{24,16},{1,9},{9,1},{17,25},{25,17},{2,10},{10... | collective-permute-start | bytes 1179656 | tf_op jit(solution)/shard_map/ppermute | solution.py:267
  46.5 15.7 %collective-permute-start.10 = (bf16[96,3584]{1,0:T(8,128)(2,1)}, bf16[96,3584]{1,0:T(8,128)(2,1)}, u32[]{:S(2)}, u32[]{:S(2)}) collective-permute-start(bf16[96,3584]{1,0:T(8,128)(2,1)} %collective-permute-done.9.rest_6_), channel_id=1, source_target_pairs={{0,8},{8,0},{16,24},{24,16},{1,9},{9,1},{17,25},{25,17},{2,10},{10... | collective-permute-start | bytes 2064392 | tf_op jit(solution)/shard_map/ppermute | solution.py:267
  62.3 2.0 %copy-start = (bf16[512,3584]{1,0:T(8,128)(2,1)S(1)}, bf16[512,3584]{1,0:T(8,128)(2,1)}, u32[]{:S(2)}) copy-start(bf16[512,3584]{1,0:T(8,128)(2,1)} %rest_9_.1) | copy-start | bytes 11010052
  64.3 1.1 %copy-start.4 = (bf16[96,3584]{1,0:T(8,128)(2,1)S(1)}, bf16[96,3584]{1,0:T(8,128)(2,1)}, u32[]{:S(2)}) copy-start(bf16[96,3584]{1,0:T(8,128)(2,1)} %copy-done.3) | copy-start | bytes 2064388

commit v5 on v4

--- a/solution.py
+++ b/solution.py
@@ -46,6 +46,20 @@
     )(*args)
 
 
+def in_hbm(array):
+    return pltpu.with_memory_space_constraint(array, pltpu.HBM)
+
+
+def load_parts(source, target, sems, axis, part):
+    loads = []
+    for k in range(source.shape[axis] // part):
+        at = (slice(None),) * axis + (pl.ds(k * part, part),)
+        loads.append((at, pltpu.make_async_copy(source.at[at], target.at[at], sems.at[k])))
+    for _, load in loads:
+        load.start()
+    return loads
+
+
 def fixed(shape):
     return pl.BlockSpec(shape, lambda j, place: (0,) * len(shape))
 
@@ -54,103 +68,81 @@
     return pl.BlockSpec((rows, width), lambda j, place: (0, j))
 
 
-def forward_kernel(n_row, own, slice_rows, targets, cuts, place, x_ref, *rest):
-    w_refs, rest = rest[:cuts], rest[cuts:]
-    parts, sent, xs = rest[:n_row], rest[n_row:-1], rest[-1]
+def forward_kernel(n_row, own, slice_rows, targets, part, place, x_ref, w_hbm, *rest):
+    outs, sent, (xs, ws, sems) = rest[:n_row], rest[n_row:-3], rest[-3:]
     dp, row = place[0], place[1]
     tokens = x_ref.shape[0]
-
-    @pl.when(pl.program_id(0) == 0)
-    def _():
+    loads = load_parts(w_hbm, ws, sems, 1, part)
+    for s in range(n_row):
+        start = pl.multiple_of(lax.rem(row + s, n_row) * own, own)
+        xs[s * own : (s + 1) * own, :] = x_ref[pl.ds(start, own), :]
+    for out, owners in zip(sent, targets):
+        for k, owner in enumerate(owners):
+            start = pl.multiple_of(owner(dp) * slice_rows, slice_rows)
+            out[k * tokens : (k + 1) * tokens, :] = x_ref[:, pl.ds(start, slice_rows)]
+    for at, load in loads:
+        load.wait()
+        acc = jnp.dot(xs[...], ws[at], preferred_element_type=F32)
         for s in range(n_row):
-            start = pl.multiple_of(lax.rem(row + s, n_row) * own, own)
-            xs[s * own : (s + 1) * own, :] = x_ref[pl.ds(start, own), :]
-        for out, owners in zip(sent, targets):
-            for k, owner in enumerate(owners):
-                start = pl.multiple_of(owner(dp) * slice_rows, slice_rows)
-                out[k * tokens : (k + 1) * tokens, :] = x_ref[:, pl.ds(start, slice_rows)]
-
-    acc, at = None, 0
-    for w_ref in w_refs:
-        deep = w_ref.shape[0]
-        part = jnp.dot(xs[:, at : at + deep], w_ref[...], preferred_element_type=F32)
-        acc, at = part if acc is None else acc + part, at + deep
-    for s in range(n_row):
-        parts[s][...] = acc[s * own : (s + 1) * own].astype(parts[s].dtype)
+            outs[s][at] = acc[s * own : (s + 1) * own].astype(outs[s].dtype)
 
 
 def forward_call(place, inputs, weight, own, n_row, slice_rows, targets):
     tokens, depth = inputs.shape
     width = weight.shape[1]
-    block = block_of(width, 512)
-    cuts = 4 if depth % 1024 == 0 else 1
+    part = block_of(width, 512)
     sent = [(len(owners) * tokens, slice_rows) for owners in targets]
     return run(
-        functools.partial(forward_kernel, n_row, own, slice_rows, targets, cuts),
+        functools.partial(forward_kernel, n_row, own, slice_rows, targets, part),
         "forward",
-        (width // block,),
-        [fixed((tokens, depth))]
-        + [
-            pl.BlockSpec(
-                (depth // cuts, block), lambda j, place, k=k: (k, j)
-            )
-            for k in range(cuts)
-        ],
-        [columns(own, block)] * n_row + [fixed(shape) for shape in sent],
+        (1,),
+        [fixed((tokens, depth)), pl.BlockSpec(memory_space=pltpu.HBM)],
+        [fixed((own, width))] * n_row + [fixed(shape) for shape in sent],
         [struct((own, width), F32)]
         + [struct((own, width), BF16)] * (n_row - 1)
         + [struct(shape, BF16) for shape in sent],
-        [pltpu.VMEM((tokens, depth), BF16)],
-        52,
-        (place, inputs, *[weight] * cuts),
-    )
-
-
-def input_grad_kernel(n_row, own, cuts, place, *rest):
-    pieces, w_refs = rest[:n_row], rest[n_row : n_row + cuts]
-    out, cs = rest[n_row + cuts :]
-    row = place[1]
-
-    @pl.when(pl.program_id(0) == 0)
-    def _():
-        for s in range(n_row):
-            start = pl.multiple_of(lax.rem(row - s + n_row, n_row) * own, own)
-            cs[pl.ds(start, own), :] = pieces[s][...]
-
-    acc, at = None, 0
-    for w_ref in w_refs:
-        deep = w_ref.shape[1]
-        part = lax.dot_general(
-            cs[:, at : at + deep],
-            w_ref[...],
-            (((1,), (1,)), ((), ())),
-            preferred_element_type=F32,
+        [
+            pltpu.VMEM((tokens, depth), BF16),
+            pltpu.VMEM((depth, width), BF16),
+            pltpu.SemaphoreType.DMA((width // part,)),
+        ],
+        28,
+        (place, inputs, in_hbm(weight)),
+    )
+
+
+def input_grad_kernel(n_row, own, part, place, *rest):
+    pieces, w_hbm, out, (cs, ws, sems) = rest[:n_row], rest[n_row], rest[n_row + 1], rest[-3:]
+    loads = load_parts(w_hbm, ws, sems, 0, part)
+    for s in range(n_row):
+        start = pl.multiple_of(lax.rem(place[1] - s + n_row, n_row) * own, own)
+        cs[pl.ds(start, own), :] = pieces[s][...]
+    for k, (at, load) in enumerate(loads):
+        load.wait()
+        acc = lax.dot_general(
+            cs[...], ws[at], (((1,), (1,)), ((), ())), preferred_element_type=F32
         )
-        acc, at = part if acc is None else acc + part, at + deep
-    out[...] = acc.astype(BF16)
+        out[:, k * part : (k + 1) * part] = acc.astype(BF16)
 
 
 def input_grad_call(place, by_row, weight, n_row):
     own, width = by_row[0].shape
     depth = weight.shape[0]
-    block = block_of(depth, 256)
-    cuts = 2 if width % 512 == 0 else 1
+    part = block_of(depth, 256)
     return run(
-        functools.partial(input_grad_kernel, n_row, own, cuts),
+        functools.partial(input_grad_kernel, n_row, own, part),
         "input_grad",
-        (depth // block,),
-        [fixed((own, width))] * n_row
-        + [
-            pl.BlockSpec(
-                (block, width // cuts), lambda j, place, k=k: (j, k)
-            )
-            for k in range(cuts)
+        (1,),
+        [fixed((own, width))] * n_row + [pl.BlockSpec(memory_space=pltpu.HBM)],
+        fixed((n_row * own, depth)),
+        struct((n_row * own, depth), BF16),
+        [
+            pltpu.VMEM((n_row * own, width), BF16),
+            pltpu.VMEM((depth, width), BF16),
+            pltpu.SemaphoreType.DMA((depth // part,)),
         ],
-        columns(n_row * own, block),
-        struct((n_row * own, depth), BF16),
-        [pltpu.VMEM((n_row * own, width), BF16)],
-        52,
-        (place, *by_row, *[weight] * cuts),
+        28,
+        (place, *by_row, in_hbm(weight)),
     )
 
 
@@ -197,7 +189,8 @@
 def update_kernel(origins, tokens_all, chunk, place, x_ref, *rest):
     n = len(origins)
     pieces = rest[:n]
-    w_ref, a_ref, m_ref, v_ref, new_w, new_m, new_v, cs, acc = rest[n:]
+    w_ref, a_ref, m_ref, v_ref = rest[n : n + 4]
+    new_w, new_m, new_v, cs, acc = rest[-5:]
     own = pieces[0].shape[0]
     for piece, origin in zip(pieces, origins):
         cs[pl.ds(pl.multiple_of(origin(place[0], place[1]) * own, own), own), :] = piece[...]
@@ -220,25 +213,41 @@
         new_v[at, :] = second
 
 
-def update_call(place, features, pieces, origins, weight, anchor, first, second):
+def update_call(place, features, pieces, origins, start, stop, held, made):
+    weight, anchor, first, second = held
     rows, width = first.shape
     tokens_all = features.shape[1]
-    block = block_of(width, 512)
+    block = block_of(math.gcd(start, stop), 512)
     own = pieces[0].shape[0]
-    tile = columns(rows, block)
-    return run(
+    base = start // block
+
+    def from_base(rows):
+        return pl.BlockSpec((rows, block), lambda j, place: (0, j + base))
+
+    tile = from_base(rows)
+    return pl.pallas_call(
         functools.partial(update_kernel, origins, tokens_all, math.gcd(rows, 32)),
-        "update",
-        (width // block,),
-        [fixed((rows, tokens_all))]
-        + [columns(own, block)] * len(pieces)
-        + [pl.BlockSpec((rows, block), lambda j, place: (place[0], j)), tile, tile, tile],
-        [tile] * 3,
-        [struct((rows, width), BF16), struct((rows, width), F32), struct((rows, width), F32)],
-        [pltpu.VMEM((tokens_all, block), BF16), pltpu.VMEM((rows, block), F32)],
-        40,
-        (place, features, *pieces, weight, anchor, first, second),
-    )
+        name="update",
+        grid_spec=pltpu.PrefetchScalarGridSpec(
+            num_scalar_prefetch=1,
+            grid=((stop - start) // block,),
+            in_specs=[fixed((rows, tokens_all))]
+            + [from_base(own) if p.shape[1] == width else columns(own, block) for p in pieces]
+            + [pl.BlockSpec((rows, block), lambda j, place: (place[0], j + base))]
+            + [tile] * 3
+            + [pl.BlockSpec(memory_space=pltpu.HBM)] * len(made),
+            out_specs=[tile] * 3,
+            scratch_shapes=[pltpu.VMEM((tokens_all, block), BF16), pltpu.VMEM((rows, block), F32)],
+        ),
+        out_shape=[
+            struct((rows, width), BF16),
+            struct((rows, width), F32),
+            struct((rows, width), F32),
+        ],
+        input_output_aliases={6 + len(pieces) + k: k for k in range(len(made))},
+        compiler_params=pltpu.CompilerParams(vmem_limit_bytes=28 * MIB),
+        cost_estimate=pl.CostEstimate(flops=1, bytes_accessed=1, transcendentals=0),
+    )(place, features, *pieces, *map(in_hbm, held), *made)
 
 
 def after(value, *others):
@@ -327,9 +336,18 @@
             gathered, weight, (((1,), (1,)), ((), ())), preferred_element_type=F32
         ).astype(BF16)
     gparts = lax.all_to_all(gpart, "col", 0, 0, tiled=True)
-    for s in range(1, n_row):
-        for c in range(1, chips):
-            by_chip[c, s] = chip_shift(c)(by_row[s])
+    width = cotangent.shape[1]
+    block = block_of(width, 512)
+    middle = (width // block + 1) // 2 * block
+    cuts = [(0, middle), (middle, width)] if tiled and middle < width else [(0, width)]
+    relayed = [{} for _ in cuts]
+    for k, (start, stop) in enumerate(cuts):
+        for s in range(1, n_row):
+            for c in range(1, chips):
+                piece = lax.slice_in_dim(by_row[s], start, stop, axis=1)
+                if k:
+                    piece = after(piece, *sums)
+                relayed[k][c, s] = chip_shift(c)(piece)
     outputs = parts[0]
     for part in sums:
         outputs = outputs + part.astype(F32)
@@ -343,26 +361,38 @@
             piece = far[c - 1]
             held.append(swap_cores(piece) if f else piece)
             sources.append((functools.partial(dp_of, c=c, flip=f), f * tokens))
-    pieces, origins = [], []
+    by_chip.update({(0, s): by_row[s] for s in range(n_row)})
+    origins = []
     for c in range(chips):
         for s in range(n_row):
-
-            def origin(dp, row, c=c, s=s, flip=0):
-                return dp_of(dp, c, flip) * n_row + lax.rem(row - s + n_row, n_row)
-
-            piece = by_chip[c, s] if c else by_row[s]
-            pieces.append(piece)
-            origins.append(origin)
-            if cores == 2:
-                other = swapped[c, s] if (c, s) in swapped else swap_cores(piece)
-                pieces.append(other)
-                origins.append(functools.partial(origin, flip=1))
+            for flip in range(cores):
+
+                def origin(dp, row, c=c, s=s, flip=flip):
+                    return dp_of(dp, c, flip) * n_row + lax.rem(row - s + n_row, n_row)
+
+                origins.append(origin)
+
+    def pieces_of(k, *before):
+        pieces = []
+        for c in range(chips):
+            for s in range(n_row):
+                piece = by_chip[c, s] if (c, s) in by_chip else relayed[k][c, s]
+                pieces.append(piece)
+                if cores == 2:
+                    if (c, s) in by_chip and (c, s) not in swapped:
+                        swapped[c, s] = swap_cores(piece)
+                    pieces.append(
+                        swapped[c, s] if (c, s) in swapped else swap_cores(after(piece, *before))
+                    )
+        return pieces
 
     if tiled:
         features = features_call(place, inputs, held, sources, slice_rows)
-        new_weight, new_first, new_second = update_call(
-            place, features, pieces, origins, weight, anchor, first_moment, second_moment
-        )
+        held = (weight, anchor, first_moment, second_moment)
+        made = []
+        for k, (start, stop) in enumerate(cuts):
+            made = update_call(place, features, pieces_of(k, *made[:1]), origins, start, stop, held, made)
+        new_weight, new_first, new_second = made
     else:
         mine = lax.dynamic_slice_in_dim(inputs, dp * slice_rows, slice_rows, 1)
         features = in_order(
@@ -370,7 +400,7 @@
             [origin(dp) for origin, _ in sources],
             tokens,
         )
-        gathered = in_order(pieces, [origin(dp, row) for origin in origins], own)
+        gathered = in_order(pieces_of(0), [origin(dp, row) for origin in origins], own)
         summed = lax.dot_general(
             features, gathered, (((0,), (0,)), ((), ())), preferred_element_type=F32
         )
@@ -385,6 +415,7 @@
             lambda value: 1.0 / value,
         )
         new_weight = new_weight.astype(BF16)
+    gparts = after(gparts, new_first)
     input_grad = sum(
         lax.slice_in_dim(gparts, k * share, (k + 1) * share).astype(F32) for k in range(n_col)
     ).astype(BF16)

time: 87 us -> 90.7 us (1.043)
  waiting for transfers between devices: 19.1 us -> 23.8 us
  other arithmetic: 4.55 us -> 3.07 us
    pallas_call x0 -> x2, Pallas kernels: none -> 24 us  [update_call(): pl.pallas_call(functools.partial(update_kernel, origins, tokens_all, math...]
    pallas_call x4 -> x3, Pallas kernels: 43.8 us -> 20.6 us  [run(): pl.pallas_call(kernel, name=name, grid_spec=pltpu.PrefetchScalarGridSpec(...]
    ppermute x5 -> x6, waiting for transfers between devices: 8.64 us -> 23.1 us  [along(): lax.ppermute(a, axis, [(i, (i + shift) % n) for i in range(n)])]
    all_to_all x1, waiting for transfers between devices: 9.88 us -> 0.01 us  [per_device(): gparts = lax.all_to_all(gpart, 'col', 0, 0, tiled=True)]
    convert_element_type x0 -> x1, other arithmetic: none -> 2 us  [per_device(): input_grad = sum((lax.slice_in_dim(gparts, k * share, (k + 1) * share).as...]
    add x1 -> x0, other arithmetic: 2 us -> none  [per_device(): sum((lax.slice_in_dim(gparts, k * share, (k + 1) * share).astype(F32) for...]
    convert_element_type x1, other arithmetic: 2.47 us -> 0.99 us  [per_device(): outputs = outputs.astype(BF16)]
    ppermute x5 -> x6, starting transfers between devices: 7.63 us -> 7.36 us  [along(): lax.ppermute(a, axis, [(i, (i + shift) % n) for i in range(n)])]
  transfers between devices with their start and end apart: 12 -> 14, of which waited for: 5 -> 5; matrix products, arithmetic and copies ran while one was open for 5% -> 2% of each run, Pallas kernels for 27% -> 49%
where the time goes in v5:
time: 90.7 us; the launch traced here: 90.4 us
  Pallas kernels  44.6 us (49%)
  waiting for transfers between devices  23.8 us (26%)
  starting transfers between devices  13.3 us (15%)
  local copies, waits for them, and re-layouts  4.81 us (5%)
  other arithmetic  3.07 us (3%)
    pallas_call x2, Pallas kernels, update_call(): pl.pallas_call(functools.partial(update_kernel, origins, tokens_all, math...  24 us
    ppermute x6, waiting for transfers between devices, along(): lax.ppermute(a, axis, [(i, (i + shift) % n) for i in range(n)])  23.1 us
    pallas_call x3, Pallas kernels, run(): pl.pallas_call(kernel, name=name, grid_spec=pltpu.PrefetchScalarGridSpec(...  20.6 us
    ppermute x6, starting transfers between devices, along(): lax.ppermute(a, axis, [(i, (i + shift) % n) for i in range(n)])  7.36 us
    all_to_all x1, starting transfers between devices, per_device(): gparts = lax.all_to_all(gpart, 'col', 0, 0, tiled=True)  4.88 us
    unnamed x18, local copies, waits for them, and re-layouts  4.03 us
    convert_element_type x1, other arithmetic, per_device(): input_grad = sum((lax.slice_in_dim(gparts, k * share, (k + 1) * share).as...  2 us
  transfers between devices with their start and end apart: 14, of which 5 were waited for; matrix products, arithmetic and copies ran while one was open for 2% of the time, Pallas kernels for 49%

profile of v5, /device:TPU:0, one launch (start us, length us, event | category | flops | bytes accessed | tf_op | source)
XLA Modules:
  0.0 90.4 jit_solution(6258532947570686817)
XLA Ops:
  0.6 0.5 collective-permute-start
  1.1 2.6 %collective-permute-start.4 = (bf16[96,3584]{1,0:T(8,128)(2,1)}, bf16[96,3584]{1,0:T(8,128)(2,1)S(1)}, u32[]{:S(2)}, u32[]{:S(2)}) collective-permute-start(bf16[96,3584]{1,0:T(8,128)(2,1)} %rest_0_.7), channel_id=1, source_target_pairs={{0,16},{8,24},{16,0},{24,8},{1,17},{9,25},{17,1},{25,9},{2,18},{10... | collective-permute-start | bytes 2064392 | tf_op jit(solution)/shard_map/ppermute | solution.py:270
  3.7 1.5 %collective-permute-start.2 = (bf16[96,3584]{1,0:T(8,128)(2,1)}, bf16[96,3584]{1,0:T(8,128)(2,1)S(1)}, u32[]{:S(2)}, u32[]{:S(2)}) collective-permute-start(bf16[96,3584]{1,0:T(8,128)(2,1)} %rest_0_.7), channel_id=1, source_target_pairs={{0,4},{4,0},{1,5},{5,1},{2,6},{6,2},{3,7},{7,3},{8,12},{12,8},{9,1... | collective-permute-start | bytes 2064392 | tf_op jit(solution)/shard_map/ppermute | solution.py:270
  5.2 0.1 pad_add_fusion.place
  5.3 0.0 copy-start.1
  5.3 1.1 %copy-done.1 = bf16[192,2048]{1,0:T(8,128)(2,1)S(1)} copy-done((bf16[192,2048]{1,0:T(8,128)(2,1)S(1)}, bf16[192,2048]{1,0:T(8,128)(2,1)}, u32[]{:S(2)}) %copy-start.1) | copy-done | bytes 786456
  6.4 0.0 copy-start
  6.4 6.5 %forward.1 = (f32[96,3584]{1,0:T(8,128)S(1)}, bf16[96,3584]{1,0:T(8,128)(2,1)S(1)}, bf16[192,512]{1,0:T(8,128)(2,1)S(1)}, bf16[384,512]{1,0:T(8,128)(2,1)S(1)}) custom-call(s32[3]{0:T(128)S(1)} %pad_add_fusion.place, bf16[192,2048]{1,0:T(8,128)(2,1)S(1)} %copy-done.1, bf16[2048,3584]{1,0:T(8,128)(2,1)} %rest_8_.3), custom_call_target="tpu_custom_call" | custom-call | flops 1 | bytes 1 | tf_op jit(solution)/shard_map/forward/pallas_call | solution.py:31
  13.0 0.0 copy-start.3
  13.0 1.1 %copy-done.3 = f32[96,3584]{1,0:T(8,128)} copy-done((f32[96,3584]{1,0:T(8,128)}, f32[96,3584]{1,0:T(8,128)S(1)}, u32[]{:S(2)}) %copy-start.3) | copy-done | bytes 1376280
  14.1 0.0 collective-permute-start.3
  14.1 0.0 collective-permute-done.rest_1_
  14.1 0.5 collective-permute-start.1
  14.6 5.3 %collective-permute-done.4.rest_4_ = bf16[96,3584]{1,0:T(8,128)(2,1)S(1)} collective-permute-done((bf16[96,3584]{1,0:T(8,128)(2,1)}, bf16[96,3584]{1,0:T(8,128)(2,1)S(1)}, u32[]{:S(2)}, u32[]{:S(2)}) %collective-permute-start.4) | collective-permute-done | bytes 688160 | tf_op jit(solution)/shard_map/ppermute | solution.py:270
  20.0 0.0 collective-permute-done.3.rest_1_
  20.0 0.0 copy-start.5
  20.0 2.2 %collective-permute-done.2.rest_1_.rest_2_ = bf16[96,3584]{1,0:T(8,128)(2,1)S(1)} collective-permute-done((bf16[96,3584]{1,0:T(8,128)(2,1)}, bf16[96,3584]{1,0:T(8,128)(2,1)S(1)}, u32[]{:S(2)}, u32[]{:S(2)}) %collective-permute-start.2) | collective-permute-done | bytes 688160 | tf_op jit(solution)/shard_map/ppermute | solution.py:270
  22.2 0.1 collective-permute-start.5
  22.3 2.0 %collective-permute-start.10 = (bf16[96,2048]{1,0:T(8,128)(2,1)S(1)}, bf16[96,2048]{1,0:T(8,128)(2,1)}, u32[]{:S(2)}, u32[]{:S(2)}) collective-permute-start(bf16[96,2048]{1,0:T(8,128)(2,1)S(1)} %slice.19), channel_id=1, source_target_pairs={{0,16},{8,24},{16,0},{24,8},{1,17},{9,25},{17,1},{25,9},{2,18},{10... | collective-permute-start | bytes 1179656 | tf_op jit(solution)/shard_map/ppermute | solution.py:270
  24.3 0.0 collective-permute-start.8
  24.3 0.5 collective-permute-start.7
  24.8 9.5 %collective-permute-done.5.rest_2_ = bf16[384,512]{1,0:T(8,128)(2,1)} collective-permute-done((bf16[384,512]{1,0:T(8,128)(2,1)S(1)}, bf16[384,512]{1,0:T(8,128)(2,1)}, u32[]{:S(2)}, u32[]{:S(2)}) %collective-permute-start.5) | collective-permute-done | bytes 393248 | tf_op jit(solution)/shard_map/ppermute | solution.py:270
  34.4 0.0 collective-permute-start.6
  34.4 6.0 %collective-permute-done.10.rest_6_ = bf16[96,2048]{1,0:T(8,128)(2,1)} collective-permute-done((bf16[96,2048]{1,0:T(8,128)(2,1)S(1)}, bf16[96,2048]{1,0:T(8,128)(2,1)}, u32[]{:S(2)}, u32[]{:S(2)}) %collective-permute-start.10) | collective-permute-done | bytes 393248 | tf_op jit(solution)/shard_map/ppermute | solution.py:270
  40.3 0.0 collective-permute-start.11
  40.3 0.0 copy-done.5
  40.3 0.8 slice.18
  41.1 0.0 copy-start.2
  41.1 0.0 collective-permute-done.1
  41.1 0.0 copy-start.7
  41.1 0.8 copy-done.7
  41.9 0.7 collective-permute-start.9
  42.6 0.0 copy-done
  42.6 12.1 %input_grad.1 = bf16[192,2048]{1,0:T(8,128)(2,1)} custom-call(s32[3]{0:T(128)S(1)} %pad_add_fusion.place, bf16[96,3584]{1,0:T(8,128)(2,1)S(1)} %copy-done, bf16[96,3584]{1,0:T(8,128)(2,1)S(1)} %collective-permute-done.2.rest_1_.rest_2_, bf16[2048,3584]{1,0:T(8,128)(2,1)} %rest_8_.3), custom_call_target="tpu_custom_call" | custom-call | flops 1 | bytes 1 | tf_op jit(solution)/shard_map/input_grad/pallas_call | solution.py:31
  54.8 4.9 %all-to-all-start = ((bf16[4,48,2048]{2,1,0:T(8,128)(2,1)}), bf16[4,48,2048]{2,1,0:T(8,128)(2,1)}, u32[]{:S(2)}, u32[]{:S(2)}) async-start(bf16[4,48,2048]{2,1,0:T(8,128)(2,1)} %bitcast.3), calls=%async_computation | async-start | bytes 1572864 | tf_op jit(solution)/shard_map/all_to_all | solution.py:338
  59.6 0.0 collective-permute-done.6.rest_3_
  59.6 0.0 copy-done.2
  59.6 0.0 copy-start.6
  59.7 0.9 %copy-done.6 = bf16[192,512]{1,0:T(8,128)(2,1)S(1)} copy-done((bf16[192,512]{1,0:T(8,128)(2,1)S(1)}, bf16[192,512]{1,0:T(8,128)(2,1)}, u32[]{:S(2)}) %copy-start.6) | copy-done | bytes 196632
  60.6 2.0 %features.1.x_ref = bf16[512,768]{1,0:T(8,128)(2,1)S(1)} custom-call(s32[3]{0:T(128)S(1)} %pad_add_fusion.place, bf16[192,2048]{1,0:T(8,128)(2,1)S(1)} %copy-done.2, bf16[192,512]{1,0:T(8,128)(2,1)S(1)} %copy-done.6, bf16[384,512]{1,0:T(8,128)(2,1)} %collective-permute-done.5.rest_2_, bf16[384,512]{1,0:T(8,128)(2,1)} %collective-permute-done.6.rest_3_), custom_call_target="tpu_custom_call" | custom-call | flops 1 | bytes 1 | tf_op jit(solution)/shard_map/features/pallas_call | solution.py:31
  62.6 0.0 copy-start.4
  62.6 0.0 copy-start.8
  62.6 0.0 collective-permute-done.8.rest_5_
  62.6 0.0 collective-permute-done.7.rest_3_
  62.6 0.0 collective-permute-done.11.rest_7_
  62.6 13.0 %update.2 = (bf16[512,3584]{1,0:T(8,128)(2,1)}, f32[512,3584]{1,0:T(8,128)}, f32[512,3584]{1,0:T(8,128)}) custom-call(s32[3]{0:T(128)S(1)} %pad_add_fusion.place, bf16[512,768]{1,0:T(8,128)(2,1)S(1)} %features.1.x_ref, bf16[96,3584]{1,0:T(8,128)(2,1)S(1)} %copy-done, bf16[96,3584]{1,0:T(8,128)(2,1)S(1)} %collective-permute-done.rest_1_, ...), custom_call_target="tpu_custom_call" | custom-call | flops 1 | bytes 1 | tf_op jit(solution)/shard_map/update/pallas_call | solution.py:228
  75.6 0.0 collective-permute-done.9.rest_6_
  75.6 0.1 collective-permute-start.12
  75.6 0.0 copy-done.4
  75.7 0.0 copy-done.8
  75.7 1.0 %add_convert_fusion = bf16[96,3584]{1,0:T(8,128)(2,1)} fusion(f32[96,3584]{1,0:T(8,128)S(1)} %copy-done.4, bf16[96,3584]{1,0:T(8,128)(2,1)S(1)} %copy-done.8), kind=kLoop, calls=%fused_computation | loop fusion | flops 1032192 | bytes 2752512 | tf_op jit(solution)/shard_map/convert_element_type | solution.py:354
  76.7 0.8 collective-permute-done.12.rest_7_
  77.4 11.0 %update.3 = (bf16[512,3584]{1,0:T(8,128)(2,1)}, f32[512,3584]{1,0:T(8,128)}, f32[512,3584]{1,0:T(8,128)}) custom-call(s32[3]{0:T(128)S(1)} %pad_add_fusion.place, bf16[512,768]{1,0:T(8,128)(2,1)S(1)} %features.1.x_ref, bf16[96,3584]{1,0:T(8,128)(2,1)S(1)} %copy-done, ...), custom_call_target="tpu_custom_call", output_to_operand_aliasing={{0}: (14, {}), {1}: (15, {}), {2}: (16, {})} | custom-call | flops 1 | bytes 1 | tf_op jit(solution)/shard_map/update/pallas_call | solution.py:228
  88.4 0.0 all-to-all-done
  88.4 2.0 %add_convert_fusion.1 = bf16[48,2048]{1,0:T(8,128)(2,1)} fusion(bf16[192,2048]{1,0:T(8,128)(2,1)} %bitcast.4), kind=kLoop, calls=%fused_computation.1 | loop fusion | flops 786432 | bytes 983040 | tf_op jit(solution)/shard_map/convert_element_type | solution.py:421
  (1 shorter events, 0.0 us)
Async XLA Ops:
  0.6 13.5 %collective-permute-start = (bf16[96,3584]{1,0:T(8,128)(2,1)}, bf16[96,3584]{1,0:T(8,128)(2,1)S(1)}, u32[]{:S(2)}, u32[]{:S(2)}) collective-permute-start(bf16[96,3584]{1,0:T(8,128)(2,1)} %rest_0_.7), channel_id=1, source_target_pairs={{0,8},{8,0},{16,24},{24,16},{1,9},{9,1},{17,25},{25,17},{2,10},{10... | collective-permute-start | bytes 2064392 | tf_op jit(solution)/shard_map/ppermute | solution.py:276
  1.1 18.8 %collective-permute-start.4 = (bf16[96,3584]{1,0:T(8,128)(2,1)}, bf16[96,3584]{1,0:T(8,128)(2,1)S(1)}, u32[]{:S(2)}, u32[]{:S(2)}) collective-permute-start(bf16[96,3584]{1,0:T(8,128)(2,1)} %rest_0_.7), channel_id=1, source_target_pairs={{0,16},{8,24},{16,0},{24,8},{1,17},{9,25},{17,1},{25,9},{2,18},{10... | collective-permute-start | bytes 2064392 | tf_op jit(solution)/shard_map/ppermute | solution.py:270
  3.7 18.5 %collective-permute-start.2 = (bf16[96,3584]{1,0:T(8,128)(2,1)}, bf16[96,3584]{1,0:T(8,128)(2,1)S(1)}, u32[]{:S(2)}, u32[]{:S(2)}) collective-permute-start(bf16[96,3584]{1,0:T(8,128)(2,1)} %rest_0_.7), channel_id=1, source_target_pairs={{0,4},{4,0},{1,5},{5,1},{2,6},{6,2},{3,7},{7,3},{8,12},{12,8},{9,1... | collective-permute-start | bytes 2064392 | tf_op jit(solution)/shard_map/ppermute | solution.py:270
  5.3 1.1 %copy-start.1 = (bf16[192,2048]{1,0:T(8,128)(2,1)S(1)}, bf16[192,2048]{1,0:T(8,128)(2,1)}, u32[]{:S(2)}) copy-start(bf16[192,2048]{1,0:T(8,128)(2,1)} %rest_0_.5) | copy-start | bytes 2359300
  6.4 36.2 %copy-start = (bf16[96,3584]{1,0:T(8,128)(2,1)S(1)}, bf16[96,3584]{1,0:T(8,128)(2,1)}, u32[]{:S(2)}) copy-start(bf16[96,3584]{1,0:T(8,128)(2,1)} %rest_0_.7) | copy-start | bytes 2064388
  13.0 1.1 %copy-start.3 = (f32[96,3584]{1,0:T(8,128)}, f32[96,3584]{1,0:T(8,128)S(1)}, u32[]{:S(2)}) copy-start(f32[96,3584]{1,0:T(8,128)S(1)} %get-tuple-element.21) | copy-start | bytes 4128772
  14.1 5.8 %collective-permute-start.3 = (bf16[192,512]{1,0:T(8,128)(2,1)S(1)}, bf16[192,512]{1,0:T(8,128)(2,1)S(1)}, u32[]{:S(2)}, u32[]{:S(2)}) collective-permute-start(bf16[192,512]{1,0:T(8,128)(2,1)S(1)} %get-tuple-element.24), channel_id=1, source_target_pairs={{0,8},{8,0},{16,24},{24,16},{1,9},{9,1},{17,25},{25,17},{2,10},{10... | collective-permute-start | bytes 589832 | tf_op jit(solution)/shard_map/ppermute | solution.py:276
  14.1 27.0 %collective-permute-start.1 = (bf16[96,3584]{1,0:T(8,128)(2,1)S(1)}, bf16[96,3584]{1,0:T(8,128)(2,1)S(1)}, u32[]{:S(2)}, u32[]{:S(2)}) collective-permute-start(bf16[96,3584]{1,0:T(8,128)(2,1)S(1)} %get-tuple-element.23), channel_id=1, source_target_pairs={{0,4},{4,0},{1,5},{5,1},{2,6},{6,2},{3,7},{7,3},{8,12},{12,8},{9,1... | collective-permute-start | bytes 2064392 | tf_op jit(solution)/shard_map/ppermute | solution.py:270
  20.0 20.4 %copy-start.5 = (bf16[192,512]{1,0:T(8,128)(2,1)}, bf16[192,512]{1,0:T(8,128)(2,1)S(1)}, u32[]{:S(2)}) copy-start(bf16[192,512]{1,0:T(8,128)(2,1)S(1)} %collective-permute-done.3.rest_1_) | copy-start | bytes 589828
  22.2 12.2 %collective-permute-start.5 = (bf16[384,512]{1,0:T(8,128)(2,1)S(1)}, bf16[384,512]{1,0:T(8,128)(2,1)}, u32[]{:S(2)}, u32[]{:S(2)}) collective-permute-start(bf16[384,512]{1,0:T(8,128)(2,1)S(1)} %get-tuple-element.27), channel_id=1, source_target_pairs={{0,16},{8,24},{16,0},{24,8},{1,17},{9,25},{17,1},{25,9},{2,18},{10... | collective-permute-start | bytes 1179656 | tf_op jit(solution)/shard_map/ppermute | solution.py:270
  22.3 18.0 %collective-permute-start.10 = (bf16[96,2048]{1,0:T(8,128)(2,1)S(1)}, bf16[96,2048]{1,0:T(8,128)(2,1)}, u32[]{:S(2)}, u32[]{:S(2)}) collective-permute-start(bf16[96,2048]{1,0:T(8,128)(2,1)S(1)} %slice.19), channel_id=1, source_target_pairs={{0,16},{8,24},{16,0},{24,8},{1,17},{9,25},{17,1},{25,9},{2,18},{10... | collective-permute-start | bytes 1179656 | tf_op jit(solution)/shard_map/ppermute | solution.py:270
  24.3 38.2 %collective-permute-start.8 = (bf16[96,3584]{1,0:T(8,128)(2,1)S(1)}, bf16[96,3584]{1,0:T(8,128)(2,1)}, u32[]{:S(2)}, u32[]{:S(2)}) collective-permute-start(bf16[96,3584]{1,0:T(8,128)(2,1)S(1)} %collective-permute-done.4.rest_4_), channel_id=1, source_target_pairs={{0,8},{8,0},{16,24},{24,16},{1,9},{9,1},{17,25},{25,17},{2,10},{10... | collective-permute-start | bytes 2064392 | tf_op jit(solution)/shard_map/ppermute | solution.py:276
  24.3 38.3 %collective-permute-start.7 = (bf16[96,3584]{1,0:T(8,128)(2,1)S(1)}, bf16[96,3584]{1,0:T(8,128)(2,1)}, u32[]{:S(2)}, u32[]{:S(2)}) collective-permute-start(bf16[96,3584]{1,0:T(8,128)(2,1)S(1)} %collective-permute-done.2.rest_1_.rest_2_), channel_id=1, source_target_pairs={{0,8},{8,0},{16,24},{24,16},{1,9},{9,1},{17,25},{25,17},{2,10},{10... | collective-permute-start | bytes 2064392 | tf_op jit(solution)/shard_map/ppermute | solution.py:276
  34.4 25.3 %collective-permute-start.6 = (bf16[384,512]{1,0:T(8,128)(2,1)}, bf16[384,512]{1,0:T(8,128)(2,1)}, u32[]{:S(2)}, u32[]{:S(2)}) collective-permute-start(bf16[384,512]{1,0:T(8,128)(2,1)} %collective-permute-done.5.rest_2_), channel_id=1, source_target_pairs={{0,8},{8,0},{16,24},{24,16},{1,9},{9,1},{17,25},{25,17},{2,10},{10... | collective-permute-start | bytes 1179656 | tf_op jit(solution)/shard_map/ppermute | solution.py:276
  40.3 22.3 %collective-permute-start.11 = (bf16[96,2048]{1,0:T(8,128)(2,1)}, bf16[96,2048]{1,0:T(8,128)(2,1)}, u32[]{:S(2)}, u32[]{:S(2)}) collective-permute-start(bf16[96,2048]{1,0:T(8,128)(2,1)} %collective-permute-done.10.rest_6_), channel_id=1, source_target_pairs={{0,8},{8,0},{16,24},{24,16},{1,9},{9,1},{17,25},{25,17},{2,10},{10... | collective-permute-start | bytes 1179656 | tf_op jit(solution)/shard_map/ppermute | solution.py:276
  41.1 18.6 %copy-start.2 = (bf16[192,2048]{1,0:T(8,128)(2,1)S(1)}, bf16[192,2048]{1,0:T(8,128)(2,1)}, u32[]{:S(2)}) copy-start(bf16[192,2048]{1,0:T(8,128)(2,1)} %rest_0_.5) | copy-start | bytes 2359300
  41.1 0.8 copy-start.7
  41.9 33.6 %collective-permute-start.9 = (bf16[96,1536]{1,0:T(8,128)(2,1)}, bf16[96,1536]{1,0:T(8,128)(2,1)}, u32[]{:S(2)}, u32[]{:S(2)}) collective-permute-start(bf16[96,1536]{1,0:T(8,128)(2,1)} %slice.18), channel_id=1, source_target_pairs={{0,16},{8,24},{16,0},{24,8},{1,17},{9,25},{17,1},{25,9},{2,18},{10... | collective-permute-start | bytes 884744 | tf_op jit(solution)/shard_map/ppermute | solution.py:270
  54.8 33.7 %all-to-all-start = ((bf16[4,48,2048]{2,1,0:T(8,128)(2,1)}), bf16[4,48,2048]{2,1,0:T(8,128)(2,1)}, u32[]{:S(2)}, u32[]{:S(2)}) async-start(bf16[4,48,2048]{2,1,0:T(8,128)(2,1)} %bitcast.3), calls=%async_computation | async-start | bytes 1572864 | tf_op jit(solution)/shard_map/all_to_all | solution.py:338
  59.6 0.9 %copy-start.6 = (bf16[192,512]{1,0:T(8,128)(2,1)S(1)}, bf16[192,512]{1,0:T(8,128)(2,1)}, u32[]{:S(2)}) copy-start(bf16[192,512]{1,0:T(8,128)(2,1)} %copy-done.5) | copy-start | bytes 589828
  62.6 13.1 %copy-start.4 = (f32[96,3584]{1,0:T(8,128)S(1)}, f32[96,3584]{1,0:T(8,128)}, u32[]{:S(2)}) copy-start(f32[96,3584]{1,0:T(8,128)} %copy-done.3) | copy-start | bytes 4128772
  62.6 13.1 %copy-start.8 = (bf16[96,3584]{1,0:T(8,128)(2,1)S(1)}, bf16[96,3584]{1,0:T(8,128)(2,1)}, u32[]{:S(2)}) copy-start(bf16[96,3584]{1,0:T(8,128)(2,1)} %copy-done.7) | copy-start | bytes 2064388
  75.6 1.9 %collective-permute-start.12 = (bf16[96,1536]{1,0:T(8,128)(2,1)}, bf16[96,1536]{1,0:T(8,128)(2,1)S(1)}, u32[]{:S(2)}, u32[]{:S(2)}) collective-permute-start(bf16[96,1536]{1,0:T(8,128)(2,1)} %collective-permute-done.9.rest_6_), channel_id=1, source_target_pairs={{0,8},{8,0},{16,24},{24,16},{1,9},{9,1},{17,25},{25,17},{2,10},{10... | collective-permute-start | bytes 884744 | tf_op jit(solution)/shard_map/ppermute | solution.py:276

commit v6 on v5

--- a/solution.py
+++ b/solution.py
@@ -112,17 +112,17 @@
 
 
 def input_grad_kernel(n_row, own, part, place, *rest):
-    pieces, w_hbm, out, (cs, ws, sems) = rest[:n_row], rest[n_row], rest[n_row + 1], rest[-3:]
+    pieces, w_hbm, out = rest[:n_row], rest[n_row], rest[n_row + 1]
+    cs, turned, ws, sems = rest[-4:]
     loads = load_parts(w_hbm, ws, sems, 0, part)
     for s in range(n_row):
         start = pl.multiple_of(lax.rem(place[1] - s + n_row, n_row) * own, own)
         cs[pl.ds(start, own), :] = pieces[s][...]
+    turned[...] = cs[...].T
     for k, (at, load) in enumerate(loads):
         load.wait()
-        acc = lax.dot_general(
-            cs[...], ws[at], (((1,), (1,)), ((), ())), preferred_element_type=F32
-        )
-        out[:, k * part : (k + 1) * part] = acc.astype(BF16)
+        acc = jnp.dot(ws[at], turned[...], preferred_element_type=F32)
+        out[:, k * part : (k + 1) * part] = acc.T.astype(BF16)
 
 
 def input_grad_call(place, by_row, weight, n_row):
@@ -138,6 +138,7 @@
         struct((n_row * own, depth), BF16),
         [
             pltpu.VMEM((n_row * own, width), BF16),
+            pltpu.VMEM((width, n_row * own), BF16),
             pltpu.VMEM((depth, width), BF16),
             pltpu.SemaphoreType.DMA((depth // part,)),
         ],
@@ -217,7 +218,7 @@
     weight, anchor, first, second = held
     rows, width = first.shape
     tokens_all = features.shape[1]
-    block = block_of(math.gcd(start, stop), 512)
+    block = block_of(math.gcd(start, stop), 256)
     own = pieces[0].shape[0]
     base = start // block
 
@@ -346,7 +347,7 @@
             for c in range(1, chips):
                 piece = lax.slice_in_dim(by_row[s], start, stop, axis=1)
                 if k:
-                    piece = after(piece, *sums)
+                    piece = after(piece, gpart)
                 relayed[k][c, s] = chip_shift(c)(piece)
     outputs = parts[0]
     for part in sums:

time: 90.7 us -> 92 us (1.014)
  waiting for transfers between devices: 23.8 us -> 18.8 us
  starting transfers between devices: 13.3 us -> 15.3 us
  local copies, waits for them, and re-layouts: 4.81 us -> 6.7 us
  other arithmetic: 3.07 us -> 4.16 us
  Pallas kernels: 44.6 us -> 45.6 us
    ppermute x6, waiting for transfers between devices: 23.1 us -> 17.3 us  [along(): lax.ppermute(a, axis, [(i, (i + shift) % n) for i in range(n)])]
    ppermute x6, starting transfers between devices: 7.36 us -> 9.87 us  [along(): lax.ppermute(a, axis, [(i, (i + shift) % n) for i in range(n)])]
    unnamed x18 -> x22, local copies, waits for them, and re-layouts: 4.03 us -> 5.93 us
    convert_element_type x1, other arithmetic: 0.99 us -> 2.09 us  [per_device(): outputs = outputs.astype(BF16)]
  transfers between devices with their start and end apart: 14 -> 14, of which waited for: 5 -> 4; matrix products, arithmetic and copies ran while one was open for 2% -> 3% of each run, Pallas kernels for 49% -> 50%
where the time goes in v6:
time: 92 us; the launch traced here: 91.3 us
  Pallas kernels  45.6 us (50%)
  waiting for transfers between devices  18.8 us (20%)
  starting transfers between devices  15.3 us (17%)
  local copies, waits for them, and re-layouts  6.7 us (7%)
  other arithmetic  4.16 us (5%)
    pallas_call x2, Pallas kernels, update_call(): pl.pallas_call(functools.partial(update_kernel, origins, tokens_all, math...  24.7 us
    pallas_call x3, Pallas kernels, run(): pl.pallas_call(kernel, name=name, grid_spec=pltpu.PrefetchScalarGridSpec(...  20.8 us
    ppermute x6, waiting for transfers between devices, along(): lax.ppermute(a, axis, [(i, (i + shift) % n) for i in range(n)])  17.3 us
    ppermute x6, starting transfers between devices, along(): lax.ppermute(a, axis, [(i, (i + shift) % n) for i in range(n)])  9.87 us
    unnamed x22, local copies, waits for them, and re-layouts  5.93 us
    all_to_all x1, starting transfers between devices, per_device(): gparts = lax.all_to_all(gpart, 'col', 0, 0, tiled=True)  4.87 us
    convert_element_type x1, other arithmetic, per_device(): outputs = outputs.astype(BF16)  2.09 us
    convert_element_type x1, other arithmetic, per_device(): input_grad = sum((lax.slice_in_dim(gparts, k * share, (k + 1) * share).as...  2 us
  transfers between devices with their start and end apart: 14, of which 4 were waited for; matrix products, arithmetic and copies ran while one was open for 3% of the time, Pallas kernels for 50%

profile of v6, /device:TPU:0, one launch (start us, length us, event | category | flops | bytes accessed | tf_op | source)
XLA Modules:
  0.0 91.3 jit_solution(15287659812996450186)
XLA Ops:
  0.6 3.0 %collective-permute-start.4 = (bf16[96,3584]{1,0:T(8,128)(2,1)}, bf16[96,3584]{1,0:T(8,128)(2,1)S(1)}, u32[]{:S(2)}, u32[]{:S(2)}) collective-permute-start(bf16[96,3584]{1,0:T(8,128)(2,1)} %rest_0_.7), channel_id=1, source_target_pairs={{0,16},{8,24},{16,0},{24,8},{1,17},{9,25},{17,1},{25,9},{2,18},{10... | collective-permute-start | bytes 2064392 | tf_op jit(solution)/shard_map/ppermute | solution.py:271
  3.6 1.5 %collective-permute-start.2 = (bf16[96,3584]{1,0:T(8,128)(2,1)}, bf16[96,3584]{1,0:T(8,128)(2,1)S(1)}, u32[]{:S(2)}, u32[]{:S(2)}) collective-permute-start(bf16[96,3584]{1,0:T(8,128)(2,1)} %rest_0_.7), channel_id=1, source_target_pairs={{0,4},{4,0},{1,5},{5,1},{2,6},{6,2},{3,7},{7,3},{8,12},{12,8},{9,1... | collective-permute-start | bytes 2064392 | tf_op jit(solution)/shard_map/ppermute | solution.py:271
  5.2 0.0 collective-permute-start
  5.2 0.1 pad_add_fusion.place
  5.2 0.0 copy-start.1
  5.2 1.1 %copy-done.1 = bf16[192,2048]{1,0:T(8,128)(2,1)S(1)} copy-done((bf16[192,2048]{1,0:T(8,128)(2,1)S(1)}, bf16[192,2048]{1,0:T(8,128)(2,1)}, u32[]{:S(2)}) %copy-start.1) | copy-done | bytes 786456
  6.4 0.0 copy-start
  6.4 7.4 %forward.1 = (f32[96,3584]{1,0:T(8,128)S(1)}, bf16[96,3584]{1,0:T(8,128)(2,1)}, bf16[192,512]{1,0:T(8,128)(2,1)S(1)}, bf16[384,512]{1,0:T(8,128)(2,1)S(1)}) custom-call(s32[3]{0:T(128)S(1)} %pad_add_fusion.place, bf16[192,2048]{1,0:T(8,128)(2,1)S(1)} %copy-done.1, bf16[2048,3584]{1,0:T(8,128)(2,1)} %rest_8_.3), custom_call_target="tpu_custom_call" | custom-call | flops 1 | bytes 1 | tf_op jit(solution)/shard_map/forward/pallas_call | solution.py:31
  13.8 0.0 copy-start.3
  13.8 1.1 %copy-done.3 = f32[96,3584]{1,0:T(8,128)} copy-done((f32[96,3584]{1,0:T(8,128)}, f32[96,3584]{1,0:T(8,128)S(1)}, u32[]{:S(2)}) %copy-start.3) | copy-done | bytes 1376280
  14.9 4.4 %collective-permute-done.4.rest_4_ = bf16[96,3584]{1,0:T(8,128)(2,1)S(1)} collective-permute-done((bf16[96,3584]{1,0:T(8,128)(2,1)}, bf16[96,3584]{1,0:T(8,128)(2,1)S(1)}, u32[]{:S(2)}, u32[]{:S(2)}) %collective-permute-start.4) | collective-permute-done | bytes 688160 | tf_op jit(solution)/shard_map/ppermute | solution.py:271
  19.3 1.7 %collective-permute-start.5 = (bf16[384,512]{1,0:T(8,128)(2,1)S(1)}, bf16[384,512]{1,0:T(8,128)(2,1)S(1)}, u32[]{:S(2)}, u32[]{:S(2)}) collective-permute-start(bf16[384,512]{1,0:T(8,128)(2,1)S(1)} %get-tuple-element.27), channel_id=1, source_target_pairs={{0,16},{8,24},{16,0},{24,8},{1,17},{9,25},{17,1},{25,9},{2,18},{10... | collective-permute-start | bytes 1179656 | tf_op jit(solution)/shard_map/ppermute | solution.py:271
  21.0 0.0 collective-permute-start.3
  21.0 1.4 %collective-permute-done.3.rest_1_ = bf16[192,512]{1,0:T(8,128)(2,1)S(1)} collective-permute-done((bf16[192,512]{1,0:T(8,128)(2,1)S(1)}, bf16[192,512]{1,0:T(8,128)(2,1)S(1)}, u32[]{:S(2)}, u32[]{:S(2)}) %collective-permute-start.3) | collective-permute-done | bytes 196640 | tf_op jit(solution)/shard_map/ppermute | solution.py:277
  22.5 0.0 copy-start.9
  22.5 0.0 collective-permute-done.2.rest_1_.rest_2_
  22.5 0.0 collective-permute-done.rest_1_
  22.5 0.4 collective-permute-start.10
  22.9 0.0 collective-permute-start.8
  22.9 0.5 collective-permute-start.7
  23.4 8.0 %collective-permute-done.5.rest_2_ = bf16[384,512]{1,0:T(8,128)(2,1)S(1)} collective-permute-done((bf16[384,512]{1,0:T(8,128)(2,1)S(1)}, bf16[384,512]{1,0:T(8,128)(2,1)S(1)}, u32[]{:S(2)}, u32[]{:S(2)}) %collective-permute-start.5) | collective-permute-done | bytes 393248 | tf_op jit(solution)/shard_map/ppermute | solution.py:271
  31.3 0.0 copy-start.5
  31.3 0.0 collective-permute-start.6
  31.3 0.0 copy-done.9
  31.3 0.0 copy-start.2
  31.4 1.8 %collective-permute-start.1 = (bf16[96,3584]{1,0:T(8,128)(2,1)}, bf16[96,3584]{1,0:T(8,128)(2,1)}, u32[]{:S(2)}, u32[]{:S(2)}) collective-permute-start(bf16[96,3584]{1,0:T(8,128)(2,1)} %get-tuple-element.23), channel_id=1, source_target_pairs={{0,4},{4,0},{1,5},{5,1},{2,6},{6,2},{3,7},{7,3},{8,12},{12,8},{9,1... | collective-permute-start | bytes 2064392 | tf_op jit(solution)/shard_map/ppermute | solution.py:271
  33.2 4.9 %collective-permute-done.10.rest_6_ = bf16[96,2048]{1,0:T(8,128)(2,1)} collective-permute-done((bf16[96,2048]{1,0:T(8,128)(2,1)S(1)}, bf16[96,2048]{1,0:T(8,128)(2,1)}, u32[]{:S(2)}, u32[]{:S(2)}) %collective-permute-start.10) | collective-permute-done | bytes 393248 | tf_op jit(solution)/shard_map/ppermute | solution.py:271
  38.1 0.0 collective-permute-start.11
  38.1 0.0 copy-done
  38.1 12.6 %input_grad.1 = bf16[192,2048]{1,0:T(8,128)(2,1)} custom-call(s32[3]{0:T(128)S(1)} %pad_add_fusion.place, bf16[96,3584]{1,0:T(8,128)(2,1)S(1)} %copy-done, bf16[96,3584]{1,0:T(8,128)(2,1)S(1)} %collective-permute-done.2.rest_1_.rest_2_, bf16[2048,3584]{1,0:T(8,128)(2,1)} %rest_8_.3), custom_call_target="tpu_custom_call" | custom-call | flops 1 | bytes 1 | tf_op jit(solution)/shard_map/input_grad/pallas_call | solution.py:31
  50.7 0.0 copy-done.5
  50.7 0.7 slice.18
  51.5 0.0 collective-permute-done.6.rest_3_
  51.5 0.0 copy-start.7
  51.5 0.7 copy-done.7
  52.2 1.4 %collective-permute-start.9 = (bf16[96,1536]{1,0:T(8,128)(2,1)}, bf16[96,1536]{1,0:T(8,128)(2,1)}, u32[]{:S(2)}, u32[]{:S(2)}) collective-permute-start(bf16[96,1536]{1,0:T(8,128)(2,1)} %slice.18), channel_id=1, source_target_pairs={{0,16},{8,24},{16,0},{24,8},{1,17},{9,25},{17,1},{25,9},{2,18},{10... | collective-permute-start | bytes 884744 | tf_op jit(solution)/shard_map/ppermute | solution.py:271
  53.6 4.9 %all-to-all-start = ((bf16[4,48,2048]{2,1,0:T(8,128)(2,1)}), bf16[4,48,2048]{2,1,0:T(8,128)(2,1)}, u32[]{:S(2)}, u32[]{:S(2)}) async-start(bf16[4,48,2048]{2,1,0:T(8,128)(2,1)} %bitcast.3), calls=%async_computation | async-start | bytes 1572864 | tf_op jit(solution)/shard_map/all_to_all | solution.py:339
  58.5 0.0 copy-done.2
  58.5 0.0 copy-start.6
  58.5 1.0 %copy-done.6 = bf16[384,512]{1,0:T(8,128)(2,1)S(1)} copy-done((bf16[384,512]{1,0:T(8,128)(2,1)S(1)}, bf16[384,512]{1,0:T(8,128)(2,1)}, u32[]{:S(2)}) %copy-start.6) | copy-done | bytes 393240
  59.5 0.0 copy-start.8
  59.5 1.0 %copy-done.8 = bf16[384,512]{1,0:T(8,128)(2,1)S(1)} copy-done((bf16[384,512]{1,0:T(8,128)(2,1)S(1)}, bf16[384,512]{1,0:T(8,128)(2,1)}, u32[]{:S(2)}) %copy-start.8) | copy-done | bytes 393240
  60.5 0.0 copy-start.10
  60.5 0.9 %copy-done.10 = bf16[192,512]{1,0:T(8,128)(2,1)S(1)} copy-done((bf16[192,512]{1,0:T(8,128)(2,1)S(1)}, bf16[192,512]{1,0:T(8,128)(2,1)}, u32[]{:S(2)}) %copy-start.10) | copy-done | bytes 196632
  61.4 0.9 features.1.x_ref
  62.3 0.0 copy-start.4
  62.3 0.0 collective-permute-done.8.rest_5_
  62.3 0.0 collective-permute-done.7.rest_3_
  62.3 0.0 collective-permute-done.11.rest_7_
  62.3 13.9 %update.2 = (bf16[512,3584]{1,0:T(8,128)(2,1)}, f32[512,3584]{1,0:T(8,128)}, f32[512,3584]{1,0:T(8,128)}) custom-call(s32[3]{0:T(128)S(1)} %pad_add_fusion.place, bf16[512,768]{1,0:T(8,128)(2,1)S(1)} %features.1.x_ref, bf16[96,3584]{1,0:T(8,128)(2,1)S(1)} %copy-done, bf16[96,3584]{1,0:T(8,128)(2,1)S(1)} %collective-permute-done.rest_1_, ...), custom_call_target="tpu_custom_call" | custom-call | flops 1 | bytes 1 | tf_op jit(solution)/shard_map/update/pallas_call | solution.py:229
  76.2 0.0 collective-permute-done.9.rest_6_
  76.3 0.1 collective-permute-start.12
  76.3 0.0 collective-permute-done.1
  76.3 0.0 copy-done.4
  76.3 2.1 %add_convert_fusion = bf16[96,3584]{1,0:T(8,128)(2,1)} fusion(f32[96,3584]{1,0:T(8,128)S(1)} %copy-done.4, bf16[96,3584]{1,0:T(8,128)(2,1)} %collective-permute-done.1), kind=kLoop, calls=%fused_computation | loop fusion | flops 1032192 | bytes 2752512 | tf_op jit(solution)/shard_map/convert_element_type | solution.py:355
  78.4 0.0 collective-permute-done.12.rest_7_
  78.4 10.8 %update.3 = (bf16[512,3584]{1,0:T(8,128)(2,1)}, f32[512,3584]{1,0:T(8,128)}, f32[512,3584]{1,0:T(8,128)}) custom-call(s32[3]{0:T(128)S(1)} %pad_add_fusion.place, bf16[512,768]{1,0:T(8,128)(2,1)S(1)} %features.1.x_ref, bf16[96,3584]{1,0:T(8,128)(2,1)S(1)} %copy-done, ...), custom_call_target="tpu_custom_call", output_to_operand_aliasing={{0}: (14, {}), {1}: (15, {}), {2}: (16, {})} | custom-call | flops 1 | bytes 1 | tf_op jit(solution)/shard_map/update/pallas_call | solution.py:229
  89.3 0.0 all-to-all-done
  89.3 2.0 %add_convert_fusion.1 = bf16[48,2048]{1,0:T(8,128)(2,1)} fusion(bf16[192,2048]{1,0:T(8,128)(2,1)} %bitcast.4), kind=kLoop, calls=%fused_computation.1 | loop fusion | flops 786432 | bytes 983040 | tf_op jit(solution)/shard_map/convert_element_type | solution.py:422
  (1 shorter events, 0.0 us)
Async XLA Ops:
  0.6 18.7 %collective-permute-start.4 = (bf16[96,3584]{1,0:T(8,128)(2,1)}, bf16[96,3584]{1,0:T(8,128)(2,1)S(1)}, u32[]{:S(2)}, u32[]{:S(2)}) collective-permute-start(bf16[96,3584]{1,0:T(8,128)(2,1)} %rest_0_.7), channel_id=1, source_target_pairs={{0,16},{8,24},{16,0},{24,8},{1,17},{9,25},{17,1},{25,9},{2,18},{10... | collective-permute-start | bytes 2064392 | tf_op jit(solution)/shard_map/ppermute | solution.py:271
  3.6 18.8 %collective-permute-start.2 = (bf16[96,3584]{1,0:T(8,128)(2,1)}, bf16[96,3584]{1,0:T(8,128)(2,1)S(1)}, u32[]{:S(2)}, u32[]{:S(2)}) collective-permute-start(bf16[96,3584]{1,0:T(8,128)(2,1)} %rest_0_.7), channel_id=1, source_target_pairs={{0,4},{4,0},{1,5},{5,1},{2,6},{6,2},{3,7},{7,3},{8,12},{12,8},{9,1... | collective-permute-start | bytes 2064392 | tf_op jit(solution)/shard_map/ppermute | solution.py:271
  5.2 17.3 %collective-permute-start = (bf16[96,3584]{1,0:T(8,128)(2,1)}, bf16[96,3584]{1,0:T(8,128)(2,1)S(1)}, u32[]{:S(2)}, u32[]{:S(2)}) collective-permute-start(bf16[96,3584]{1,0:T(8,128)(2,1)} %rest_0_.7), channel_id=1, source_target_pairs={{0,8},{8,0},{16,24},{24,16},{1,9},{9,1},{17,25},{25,17},{2,10},{10... | collective-permute-start | bytes 2064392 | tf_op jit(solution)/shard_map/ppermute | solution.py:277
  5.2 1.1 %copy-start.1 = (bf16[192,2048]{1,0:T(8,128)(2,1)S(1)}, bf16[192,2048]{1,0:T(8,128)(2,1)}, u32[]{:S(2)}) copy-start(bf16[192,2048]{1,0:T(8,128)(2,1)} %rest_0_.5) | copy-start | bytes 2359300
  6.4 31.8 %copy-start = (bf16[96,3584]{1,0:T(8,128)(2,1)S(1)}, bf16[96,3584]{1,0:T(8,128)(2,1)}, u32[]{:S(2)}) copy-start(bf16[96,3584]{1,0:T(8,128)(2,1)} %rest_0_.7) | copy-start | bytes 2064388
  13.8 1.1 %copy-start.3 = (f32[96,3584]{1,0:T(8,128)}, f32[96,3584]{1,0:T(8,128)S(1)}, u32[]{:S(2)}) copy-start(f32[96,3584]{1,0:T(8,128)S(1)} %get-tuple-element.21) | copy-start | bytes 4128772
  19.3 12.1 %collective-permute-start.5 = (bf16[384,512]{1,0:T(8,128)(2,1)S(1)}, bf16[384,512]{1,0:T(8,128)(2,1)S(1)}, u32[]{:S(2)}, u32[]{:S(2)}) collective-permute-start(bf16[384,512]{1,0:T(8,128)(2,1)S(1)} %get-tuple-element.27), channel_id=1, source_target_pairs={{0,16},{8,24},{16,0},{24,8},{1,17},{9,25},{17,1},{25,9},{2,18},{10... | collective-permute-start | bytes 1179656 | tf_op jit(solution)/shard_map/ppermute | solution.py:271
  21.0 1.4 %collective-permute-start.3 = (bf16[192,512]{1,0:T(8,128)(2,1)S(1)}, bf16[192,512]{1,0:T(8,128)(2,1)S(1)}, u32[]{:S(2)}, u32[]{:S(2)}) collective-permute-start(bf16[192,512]{1,0:T(8,128)(2,1)S(1)} %get-tuple-element.24), channel_id=1, source_target_pairs={{0,8},{8,0},{16,24},{24,16},{1,9},{9,1},{17,25},{25,17},{2,10},{10... | collective-permute-start | bytes 589832 | tf_op jit(solution)/shard_map/ppermute | solution.py:277
  22.5 8.9 %copy-start.9 = (bf16[192,512]{1,0:T(8,128)(2,1)}, bf16[192,512]{1,0:T(8,128)(2,1)S(1)}, u32[]{:S(2)}) copy-start(bf16[192,512]{1,0:T(8,128)(2,1)S(1)} %collective-permute-done.3.rest_1_) | copy-start | bytes 589828
  22.5 15.6 %collective-permute-start.10 = (bf16[96,2048]{1,0:T(8,128)(2,1)S(1)}, bf16[96,2048]{1,0:T(8,128)(2,1)}, u32[]{:S(2)}, u32[]{:S(2)}) collective-permute-start(bf16[96,2048]{1,0:T(8,128)(2,1)S(1)} %slice.19), channel_id=1, source_target_pairs={{0,16},{8,24},{16,0},{24,8},{1,17},{9,25},{17,1},{25,9},{2,18},{10... | collective-permute-start | bytes 1179656 | tf_op jit(solution)/shard_map/ppermute | solution.py:271
  22.9 39.4 %collective-permute-start.8 = (bf16[96,3584]{1,0:T(8,128)(2,1)S(1)}, bf16[96,3584]{1,0:T(8,128)(2,1)}, u32[]{:S(2)}, u32[]{:S(2)}) collective-permute-start(bf16[96,3584]{1,0:T(8,128)(2,1)S(1)} %collective-permute-done.4.rest_4_), channel_id=1, source_target_pairs={{0,8},{8,0},{16,24},{24,16},{1,9},{9,1},{17,25},{25,17},{2,10},{10... | collective-permute-start | bytes 2064392 | tf_op jit(solution)/shard_map/ppermute | solution.py:277
  22.9 39.5 %collective-permute-start.7 = (bf16[96,3584]{1,0:T(8,128)(2,1)S(1)}, bf16[96,3584]{1,0:T(8,128)(2,1)}, u32[]{:S(2)}, u32[]{:S(2)}) collective-permute-start(bf16[96,3584]{1,0:T(8,128)(2,1)S(1)} %collective-permute-done.2.rest_1_.rest_2_), channel_id=1, source_target_pairs={{0,8},{8,0},{16,24},{24,16},{1,9},{9,1},{17,25},{25,17},{2,10},{10... | collective-permute-start | bytes 2064392 | tf_op jit(solution)/shard_map/ppermute | solution.py:277
  31.3 19.4 %copy-start.5 = (bf16[384,512]{1,0:T(8,128)(2,1)}, bf16[384,512]{1,0:T(8,128)(2,1)S(1)}, u32[]{:S(2)}) copy-start(bf16[384,512]{1,0:T(8,128)(2,1)S(1)} %collective-permute-done.5.rest_2_) | copy-start | bytes 1179652
  31.3 20.1 %collective-permute-start.6 = (bf16[384,512]{1,0:T(8,128)(2,1)S(1)}, bf16[384,512]{1,0:T(8,128)(2,1)S(1)}, u32[]{:S(2)}, u32[]{:S(2)}) collective-permute-start(bf16[384,512]{1,0:T(8,128)(2,1)S(1)} %collective-permute-done.5.rest_2_), channel_id=1, source_target_pairs={{0,8},{8,0},{16,24},{24,16},{1,9},{9,1},{17,25},{25,17},{2,10},{10... | collective-permute-start | bytes 1179656 | tf_op jit(solution)/shard_map/ppermute | solution.py:277
  31.3 27.2 %copy-start.2 = (bf16[192,2048]{1,0:T(8,128)(2,1)S(1)}, bf16[192,2048]{1,0:T(8,128)(2,1)}, u32[]{:S(2)}) copy-start(bf16[192,2048]{1,0:T(8,128)(2,1)} %rest_0_.5) | copy-start | bytes 2359300
  31.4 45.0 %collective-permute-start.1 = (bf16[96,3584]{1,0:T(8,128)(2,1)}, bf16[96,3584]{1,0:T(8,128)(2,1)}, u32[]{:S(2)}, u32[]{:S(2)}) collective-permute-start(bf16[96,3584]{1,0:T(8,128)(2,1)} %get-tuple-element.23), channel_id=1, source_target_pairs={{0,4},{4,0},{1,5},{5,1},{2,6},{6,2},{3,7},{7,3},{8,12},{12,8},{9,1... | collective-permute-start | bytes 2064392 | tf_op jit(solution)/shard_map/ppermute | solution.py:271
  38.1 24.2 %collective-permute-start.11 = (bf16[96,2048]{1,0:T(8,128)(2,1)}, bf16[96,2048]{1,0:T(8,128)(2,1)}, u32[]{:S(2)}, u32[]{:S(2)}) collective-permute-start(bf16[96,2048]{1,0:T(8,128)(2,1)} %collective-permute-done.10.rest_6_), channel_id=1, source_target_pairs={{0,8},{8,0},{16,24},{24,16},{1,9},{9,1},{17,25},{25,17},{2,10},{10... | collective-permute-start | bytes 1179656 | tf_op jit(solution)/shard_map/ppermute | solution.py:277
  51.5 0.7 copy-start.7
  52.2 24.0 %collective-permute-start.9 = (bf16[96,1536]{1,0:T(8,128)(2,1)}, bf16[96,1536]{1,0:T(8,128)(2,1)}, u32[]{:S(2)}, u32[]{:S(2)}) collective-permute-start(bf16[96,1536]{1,0:T(8,128)(2,1)} %slice.18), channel_id=1, source_target_pairs={{0,16},{8,24},{16,0},{24,8},{1,17},{9,25},{17,1},{25,9},{2,18},{10... | collective-permute-start | bytes 884744 | tf_op jit(solution)/shard_map/ppermute | solution.py:271
  53.6 35.6 %all-to-all-start = ((bf16[4,48,2048]{2,1,0:T(8,128)(2,1)}), bf16[4,48,2048]{2,1,0:T(8,128)(2,1)}, u32[]{:S(2)}, u32[]{:S(2)}) async-start(bf16[4,48,2048]{2,1,0:T(8,128)(2,1)} %bitcast.3), calls=%async_computation | async-start | bytes 1572864 | tf_op jit(solution)/shard_map/all_to_all | solution.py:339
  58.5 1.0 %copy-start.6 = (bf16[384,512]{1,0:T(8,128)(2,1)S(1)}, bf16[384,512]{1,0:T(8,128)(2,1)}, u32[]{:S(2)}) copy-start(bf16[384,512]{1,0:T(8,128)(2,1)} %copy-done.5) | copy-start | bytes 1179652
  59.5 1.0 %copy-start.8 = (bf16[384,512]{1,0:T(8,128)(2,1)S(1)}, bf16[384,512]{1,0:T(8,128)(2,1)}, u32[]{:S(2)}) copy-start(bf16[384,512]{1,0:T(8,128)(2,1)} %copy-done.7) | copy-start | bytes 1179652
  60.5 0.9 %copy-start.10 = (bf16[192,512]{1,0:T(8,128)(2,1)S(1)}, bf16[192,512]{1,0:T(8,128)(2,1)}, u32[]{:S(2)}) copy-start(bf16[192,512]{1,0:T(8,128)(2,1)} %copy-done.9) | copy-start | bytes 589828
  62.3 14.0 %copy-start.4 = (f32[96,3584]{1,0:T(8,128)S(1)}, f32[96,3584]{1,0:T(8,128)}, u32[]{:S(2)}) copy-start(f32[96,3584]{1,0:T(8,128)} %copy-done.3) | copy-start | bytes 4128772
  76.3 2.2 %collective-permute-start.12 = (bf16[96,1536]{1,0:T(8,128)(2,1)}, bf16[96,1536]{1,0:T(8,128)(2,1)S(1)}, u32[]{:S(2)}, u32[]{:S(2)}) collective-permute-start(bf16[96,1536]{1,0:T(8,128)(2,1)} %collective-permute-done.9.rest_6_), channel_id=1, source_target_pairs={{0,8},{8,0},{16,24},{24,16},{1,9},{9,1},{17,25},{25,17},{2,10},{10... | collective-permute-start | bytes 884744 | tf_op jit(solution)/shard_map/ppermute | solution.py:277

commit v7 on v6

--- a/solution.py
+++ b/solution.py
@@ -68,23 +68,33 @@
     return pl.BlockSpec((rows, width), lambda j, place: (0, j))
 
 
-def forward_kernel(n_row, own, slice_rows, targets, part, place, x_ref, w_hbm, *rest):
-    outs, sent, (xs, ws, sems) = rest[:n_row], rest[n_row:-3], rest[-3:]
+def forward_kernel(n_row, own, slice_rows, targets, part, place, x_hbm, w_hbm, *rest):
+    outs, sent = rest[:n_row], rest[n_row:-4]
+    xs, ws, x_sems, w_sems = rest[-4:]
     dp, row = place[0], place[1]
-    tokens = x_ref.shape[0]
-    loads = load_parts(w_hbm, ws, sems, 1, part)
+    tokens = xs.shape[0]
+    x_loads = []
     for s in range(n_row):
         start = pl.multiple_of(lax.rem(row + s, n_row) * own, own)
-        xs[s * own : (s + 1) * own, :] = x_ref[pl.ds(start, own), :]
+        at = pl.ds(s * own, own)
+        x_loads.append(
+            pltpu.make_async_copy(x_hbm.at[pl.ds(start, own), :], xs.at[at, :], x_sems.at[s])
+        )
+        x_loads[-1].start()
+    loads = load_parts(w_hbm, ws, w_sems, 1, part)
+    for load in x_loads:
+        load.wait()
     for out, owners in zip(sent, targets):
         for k, owner in enumerate(owners):
-            start = pl.multiple_of(owner(dp) * slice_rows, slice_rows)
-            out[k * tokens : (k + 1) * tokens, :] = x_ref[:, pl.ds(start, slice_rows)]
+            columns = pl.ds(pl.multiple_of(owner(dp) * slice_rows, slice_rows), slice_rows)
+            for s in range(n_row):
+                start = pl.multiple_of(k * tokens + lax.rem(row + s, n_row) * own, own)
+                out[pl.ds(start, own), :] = xs[s * own : (s + 1) * own, columns]
     for at, load in loads:
         load.wait()
-        acc = jnp.dot(xs[...], ws[at], preferred_element_type=F32)
+        acc = jnp.dot(xs[...], ws[at], preferred_element_type=F32).astype(BF16)
         for s in range(n_row):
-            outs[s][at] = acc[s * own : (s + 1) * own].astype(outs[s].dtype)
+            outs[s][at] = acc[s * own : (s + 1) * own]
 
 
 def forward_call(place, inputs, weight, own, n_row, slice_rows, targets):
@@ -96,53 +106,61 @@
         functools.partial(forward_kernel, n_row, own, slice_rows, targets, part),
         "forward",
         (1,),
-        [fixed((tokens, depth)), pl.BlockSpec(memory_space=pltpu.HBM)],
+        [pl.BlockSpec(memory_space=pltpu.HBM)] * 2,
         [fixed((own, width))] * n_row + [fixed(shape) for shape in sent],
-        [struct((own, width), F32)]
-        + [struct((own, width), BF16)] * (n_row - 1)
-        + [struct(shape, BF16) for shape in sent],
+        [struct((own, width), BF16)] * n_row + [struct(shape, BF16) for shape in sent],
         [
             pltpu.VMEM((tokens, depth), BF16),
             pltpu.VMEM((depth, width), BF16),
+            pltpu.SemaphoreType.DMA((n_row,)),
             pltpu.SemaphoreType.DMA((width // part,)),
         ],
         28,
-        (place, inputs, in_hbm(weight)),
+        (place, in_hbm(inputs), in_hbm(weight)),
     )
 
 
 def input_grad_kernel(n_row, own, part, place, *rest):
     pieces, w_hbm, out = rest[:n_row], rest[n_row], rest[n_row + 1]
-    cs, turned, ws, sems = rest[-4:]
-    loads = load_parts(w_hbm, ws, sems, 0, part)
+    cs, turned, ws, acc, c_sems, w_sems = rest[-6:]
+    c_loads = []
     for s in range(n_row):
         start = pl.multiple_of(lax.rem(place[1] - s + n_row, n_row) * own, own)
-        cs[pl.ds(start, own), :] = pieces[s][...]
+        c_loads.append(pltpu.make_async_copy(pieces[s], cs.at[pl.ds(start, own), :], c_sems.at[s]))
+        c_loads[-1].start()
+    loads = load_parts(w_hbm, ws, w_sems, 1, part)
+    for load in c_loads:
+        load.wait()
     turned[...] = cs[...].T
     for k, (at, load) in enumerate(loads):
         load.wait()
-        acc = jnp.dot(ws[at], turned[...], preferred_element_type=F32)
-        out[:, k * part : (k + 1) * part] = acc.T.astype(BF16)
+        product = jnp.dot(
+            ws[at], turned[k * part : (k + 1) * part, :], preferred_element_type=F32
+        )
+        acc[...] = acc[...] + product if k else product
+    out[...] = acc[...].T.astype(BF16)
 
 
 def input_grad_call(place, by_row, weight, n_row):
     own, width = by_row[0].shape
     depth = weight.shape[0]
-    part = block_of(depth, 256)
+    part = block_of(width, 512)
     return run(
         functools.partial(input_grad_kernel, n_row, own, part),
         "input_grad",
         (1,),
-        [fixed((own, width))] * n_row + [pl.BlockSpec(memory_space=pltpu.HBM)],
+        [pl.BlockSpec(memory_space=pl.ANY)] * n_row + [pl.BlockSpec(memory_space=pltpu.HBM)],
         fixed((n_row * own, depth)),
         struct((n_row * own, depth), BF16),
         [
             pltpu.VMEM((n_row * own, width), BF16),
             pltpu.VMEM((width, n_row * own), BF16),
             pltpu.VMEM((depth, width), BF16),
-            pltpu.SemaphoreType.DMA((depth // part,)),
+            pltpu.VMEM((depth, n_row * own), F32),
+            pltpu.SemaphoreType.DMA((n_row,)),
+            pltpu.SemaphoreType.DMA((width // part,)),
         ],
-        28,
+        32,
         (place, *by_row, in_hbm(weight)),
     )
 
@@ -168,7 +186,7 @@
         struct((slice_rows, n_dp * tokens), BF16),
         [pltpu.VMEM((n_dp * tokens, slice_rows), BF16)],
         16,
-        (place, inputs, *held),
+        (place, in_hbm(inputs), *held),
     )
 
 
@@ -248,7 +266,7 @@
         input_output_aliases={6 + len(pieces) + k: k for k in range(len(made))},
         compiler_params=pltpu.CompilerParams(vmem_limit_bytes=28 * MIB),
         cost_estimate=pl.CostEstimate(flops=1, bytes_accessed=1, transcendentals=0),
-    )(place, features, *pieces, *map(in_hbm, held), *made)
+    )(place, features, *pieces, *map(in_hbm, [*held, *made]))
 
 
 def after(value, *others):
@@ -300,7 +318,7 @@
         part = jnp.dot(inputs, weight, preferred_element_type=F32)
         parts = [
             lax.dynamic_slice_in_dim(part, lax.rem(row + s, n_row) * own, own, 0).astype(
-                BF16 if s else F32
+                BF16
             )
             for s in range(n_row)
         ]
@@ -323,11 +341,6 @@
     far = [chip_shift(c)(after(to_send[c - 1], *first)) for c in range(1, chips)]
     for s in range(1, n_row):
         by_row[s] = after(by_row[s], parts[0], *near, *first, *swapped.values())
-        if cores == 2:
-            swapped[0, s] = swap_cores(by_row[s])
-    if cores == 2:
-        for c in range(1, chips):
-            swapped[c, 0] = swap_cores(by_chip[c, 0])
 
     if tiled:
         gpart = input_grad_call(place, by_row, weight, n_row)
@@ -349,7 +362,7 @@
                 if k:
                     piece = after(piece, gpart)
                 relayed[k][c, s] = chip_shift(c)(piece)
-    outputs = parts[0]
+    outputs = parts[0].astype(F32)
     for part in sums:
         outputs = outputs + part.astype(F32)
     outputs = outputs.astype(BF16)
@@ -360,7 +373,7 @@
     for c in range(1, chips):
         for f in flips:
             piece = far[c - 1]
-            held.append(swap_cores(piece) if f else piece)
+            held.append(swap_cores(after(piece, gpart)) if f else piece)
             sources.append((functools.partial(dp_of, c=c, flip=f), f * tokens))
     by_chip.update({(0, s): by_row[s] for s in range(n_row)})
     origins = []
@@ -381,7 +394,7 @@
                 pieces.append(piece)
                 if cores == 2:
                     if (c, s) in by_chip and (c, s) not in swapped:
-                        swapped[c, s] = swap_cores(piece)
+                        swapped[c, s] = swap_cores(after(piece, gpart))
                     pieces.append(
                         swapped[c, s] if (c, s) in swapped else swap_cores(after(piece, *before))
                     )
@@ -390,9 +403,11 @@
     if tiled:
         features = features_call(place, inputs, held, sources, slice_rows)
         held = (weight, anchor, first_moment, second_moment)
-        made = []
+        made, before = [], [gpart]
         for k, (start, stop) in enumerate(cuts):
-            made = update_call(place, features, pieces_of(k, *made[:1]), origins, start, stop, held, made)
+            pieces = pieces_of(k, *before)
+            made = update_call(place, features, pieces, origins, start, stop, held, made)
+            before = [made[0], gparts]
         new_weight, new_first, new_second = made
     else:
         mine = lax.dynamic_slice_in_dim(inputs, dp * slice_rows, slice_rows, 1)
@@ -401,7 +416,7 @@
             [origin(dp) for origin, _ in sources],
             tokens,
         )
-        gathered = in_order(pieces_of(0), [origin(dp, row) for origin in origins], own)
+        gathered = in_order(pieces_of(0, gpart), [origin(dp, row) for origin in origins], own)
         summed = lax.dot_general(
             features, gathered, (((0,), (0,)), ((), ())), preferred_element_type=F32
         )

time: 92 us -> 91 us (0.989)
  Pallas kernels: 45.6 us -> 49 us
  waiting for transfers between devices: 18.8 us -> 16.5 us
  local copies, waits for them, and re-layouts: 6.7 us -> 4.7 us
    pallas_call x3, Pallas kernels: 20.8 us -> 24.8 us  [run(): pl.pallas_call(kernel, name=name, grid_spec=pltpu.PrefetchScalarGridSpec(...]
    ppermute x6, waiting for transfers between devices: 17.3 us -> 15.4 us  [along(): lax.ppermute(a, axis, [(i, (i + shift) % n) for i in range(n)])]
    unnamed x22 -> x16, local copies, waits for them, and re-layouts: 5.93 us -> 4.65 us
    ppermute x6, starting transfers between devices: 9.87 us -> 8.74 us  [along(): lax.ppermute(a, axis, [(i, (i + shift) % n) for i in range(n)])]
  transfers between devices with their start and end apart: 14 -> 14, of which waited for: 4 -> 4; matrix products, arithmetic and copies ran while one was open for 3% -> 3% of each run, Pallas kernels for 50% -> 29%
where the time goes in v7:
time: 91 us; the launch traced here: 90.3 us
  Pallas kernels  49 us (54%)
  waiting for transfers between devices  16.5 us (18%)
  starting transfers between devices  14.9 us (16%)
  local copies, waits for them, and re-layouts  4.7 us (5%)
  other arithmetic  4.38 us (5%)
    pallas_call x3, Pallas kernels, run(): pl.pallas_call(kernel, name=name, grid_spec=pltpu.PrefetchScalarGridSpec(...  24.8 us
    pallas_call x2, Pallas kernels, update_call(): pl.pallas_call(functools.partial(update_kernel, origins, tokens_all, math...  24.2 us
    ppermute x6, waiting for transfers between devices, along(): lax.ppermute(a, axis, [(i, (i + shift) % n) for i in range(n)])  15.4 us
    ppermute x6, starting transfers between devices, along(): lax.ppermute(a, axis, [(i, (i + shift) % n) for i in range(n)])  8.74 us
    all_to_all x1, starting transfers between devices, per_device(): gparts = lax.all_to_all(gpart, 'col', 0, 0, tiled=True)  4.89 us
    unnamed x16, local copies, waits for them, and re-layouts  4.65 us
    convert_element_type x1, other arithmetic, per_device(): outputs = outputs.astype(BF16)  2.31 us
    convert_element_type x1, other arithmetic, per_device(): input_grad = sum((lax.slice_in_dim(gparts, k * share, (k + 1) * share).as...  1.99 us
  transfers between devices with their start and end apart: 14, of which 4 were waited for; matrix products, arithmetic and copies ran while one was open for 3% of the time, Pallas kernels for 29%

profile of v7, /device:TPU:0, one launch (start us, length us, event | category | flops | bytes accessed | tf_op | source)
XLA Modules:
  0.0 90.3 jit_solution(1194161940681467685)
XLA Ops:
  0.6 3.0 %collective-permute-start.4 = (bf16[96,3584]{1,0:T(8,128)(2,1)}, bf16[96,3584]{1,0:T(8,128)(2,1)S(1)}, u32[]{:S(2)}, u32[]{:S(2)}) collective-permute-start(bf16[96,3584]{1,0:T(8,128)(2,1)} %rest_0_.7), channel_id=1, source_target_pairs={{0,16},{8,24},{16,0},{24,8},{1,17},{9,25},{17,1},{25,9},{2,18},{10... | collective-permute-start | bytes 2064392 | tf_op jit(solution)/shard_map/ppermute | solution.py:289
  3.6 1.5 %collective-permute-start.2 = (bf16[96,3584]{1,0:T(8,128)(2,1)}, bf16[96,3584]{1,0:T(8,128)(2,1)S(1)}, u32[]{:S(2)}, u32[]{:S(2)}) collective-permute-start(bf16[96,3584]{1,0:T(8,128)(2,1)} %rest_0_.7), channel_id=1, source_target_pairs={{0,4},{4,0},{1,5},{5,1},{2,6},{6,2},{3,7},{7,3},{8,12},{12,8},{9,1... | collective-permute-start | bytes 2064392 | tf_op jit(solution)/shard_map/ppermute | solution.py:289
  5.2 0.0 collective-permute-start
  5.2 0.1 pad_add_fusion.place
  5.2 0.0 copy-start
  5.2 11.1 %forward.1 = (bf16[96,3584]{1,0:T(8,128)(2,1)S(1)}, bf16[96,3584]{1,0:T(8,128)(2,1)}, bf16[192,512]{1,0:T(8,128)(2,1)S(1)}, bf16[384,512]{1,0:T(8,128)(2,1)S(1)}) custom-call(s32[3]{0:T(128)S(1)} %pad_add_fusion.place, bf16[192,2048]{1,0:T(8,128)(2,1)} %rest_0_.5, bf16[2048,3584]{1,0:T(8,128)(2,1)} %rest_8_.3), custom_call_target="tpu_custom_call" | custom-call | flops 1 | bytes 1 | tf_op jit(solution)/shard_map/forward/pallas_call | solution.py:31
  16.3 0.0 copy-start.5
  16.3 0.8 copy-done.5
  17.1 0.5 collective-permute-start.3
  17.7 1.1 %collective-permute-done.3.rest_1_ = bf16[192,512]{1,0:T(8,128)(2,1)S(1)} collective-permute-done((bf16[192,512]{1,0:T(8,128)(2,1)S(1)}, bf16[192,512]{1,0:T(8,128)(2,1)S(1)}, u32[]{:S(2)}, u32[]{:S(2)}) %collective-permute-start.3) | collective-permute-done | bytes 196640 | tf_op jit(solution)/shard_map/ppermute | solution.py:295
  18.7 0.0 copy-start.6
  18.7 0.7 copy-done.6
  19.4 0.0 collective-permute-done.4.rest_4_
  19.4 1.3 %collective-permute-done.2.rest_1_.rest_2_ = bf16[96,3584]{1,0:T(8,128)(2,1)S(1)} collective-permute-done((bf16[96,3584]{1,0:T(8,128)(2,1)}, bf16[96,3584]{1,0:T(8,128)(2,1)S(1)}, u32[]{:S(2)}, u32[]{:S(2)}) %collective-permute-start.2) | collective-permute-done | bytes 688160 | tf_op jit(solution)/shard_map/ppermute | solution.py:289
  20.7 0.0 collective-permute-done.rest_1_
  20.7 0.0 copy-done
  20.7 12.0 %input_grad.1 = bf16[192,2048]{1,0:T(8,128)(2,1)} custom-call(s32[3]{0:T(128)S(1)} %pad_add_fusion.place, bf16[96,3584]{1,0:T(8,128)(2,1)S(1)} %copy-done, bf16[96,3584]{1,0:T(8,128)(2,1)S(1)} %collective-permute-done.2.rest_1_.rest_2_, bf16[2048,3584]{1,0:T(8,128)(2,1)} %rest_8_.3), custom_call_target="tpu_custom_call" | custom-call | flops 1 | bytes 1 | tf_op jit(solution)/shard_map/input_grad/pallas_call | solution.py:31
  32.7 4.9 %all-to-all-start = ((bf16[4,48,2048]{2,1,0:T(8,128)(2,1)}), bf16[4,48,2048]{2,1,0:T(8,128)(2,1)}, u32[]{:S(2)}, u32[]{:S(2)}) async-start(bf16[4,48,2048]{2,1,0:T(8,128)(2,1)} %bitcast.3), calls=%async_computation | async-start | bytes 1572864 | tf_op jit(solution)/shard_map/all_to_all | solution.py:352
  37.6 0.5 collective-permute-start.5
  38.2 1.6 %collective-permute-start.10 = (bf16[96,2048]{1,0:T(8,128)(2,1)S(1)}, bf16[96,2048]{1,0:T(8,128)(2,1)S(1)}, u32[]{:S(2)}, u32[]{:S(2)}) collective-permute-start(bf16[96,2048]{1,0:T(8,128)(2,1)S(1)} %slice.19), channel_id=1, source_target_pairs={{0,16},{8,24},{16,0},{24,8},{1,17},{9,25},{17,1},{25,9},{2,18},{10... | collective-permute-start | bytes 1179656 | tf_op jit(solution)/shard_map/ppermute | solution.py:289
  39.7 0.0 collective-permute-start.7
  39.7 0.5 collective-permute-start.8
  40.2 9.4 %collective-permute-done.5.rest_2_ = bf16[384,512]{1,0:T(8,128)(2,1)S(1)} collective-permute-done((bf16[384,512]{1,0:T(8,128)(2,1)S(1)}, bf16[384,512]{1,0:T(8,128)(2,1)S(1)}, u32[]{:S(2)}, u32[]{:S(2)}) %collective-permute-start.5) | collective-permute-done | bytes 393248 | tf_op jit(solution)/shard_map/ppermute | solution.py:289
  49.6 0.0 collective-permute-start.6
  49.6 1.5 %collective-permute-start.1 = (bf16[96,3584]{1,0:T(8,128)(2,1)}, bf16[96,3584]{1,0:T(8,128)(2,1)}, u32[]{:S(2)}, u32[]{:S(2)}) collective-permute-start(bf16[96,3584]{1,0:T(8,128)(2,1)} %get-tuple-element.27), channel_id=1, source_target_pairs={{0,4},{4,0},{1,5},{5,1},{2,6},{6,2},{3,7},{7,3},{8,12},{12,8},{9,1... | collective-permute-start | bytes 2064392 | tf_op jit(solution)/shard_map/ppermute | solution.py:289
  51.2 4.6 %collective-permute-done.10.rest_6_ = bf16[96,2048]{1,0:T(8,128)(2,1)S(1)} collective-permute-done((bf16[96,2048]{1,0:T(8,128)(2,1)S(1)}, bf16[96,2048]{1,0:T(8,128)(2,1)S(1)}, u32[]{:S(2)}, u32[]{:S(2)}) %collective-permute-start.10) | collective-permute-done | bytes 393248 | tf_op jit(solution)/shard_map/ppermute | solution.py:289
  55.8 0.0 collective-permute-start.11
  55.8 0.0 collective-permute-done.6.rest_3_
  55.8 0.6 collective-permute-start.9
  56.4 0.0 copy-start.7
  56.4 0.9 %copy-done.7 = bf16[192,512]{1,0:T(8,128)(2,1)S(1)} copy-done((bf16[192,512]{1,0:T(8,128)(2,1)S(1)}, bf16[192,512]{1,0:T(8,128)(2,1)}, u32[]{:S(2)}) %copy-start.7) | copy-done | bytes 196632
  57.4 1.8 %features.1.x_ref = bf16[512,768]{1,0:T(8,128)(2,1)S(1)} custom-call(s32[3]{0:T(128)S(1)} %pad_add_fusion.place, bf16[192,2048]{1,0:T(8,128)(2,1)} %rest_0_.5, bf16[192,512]{1,0:T(8,128)(2,1)S(1)} %copy-done.7, bf16[384,512]{1,0:T(8,128)(2,1)S(1)} %collective-permute-done.5.rest_2_, bf16[384,512]{1,0:T(8,128)(2,1)S(1)} %collective-permute-done.6.rest_3_), custom_call_target="tpu_custom_call" | custom-call | flops 1 | bytes 1 | tf_op jit(solution)/shard_map/features/pallas_call | solution.py:31
  59.2 0.0 collective-permute-done.7.rest_3_
  59.2 0.0 copy-start.1
  59.2 0.0 collective-permute-done.8.rest_5_
  59.2 0.0 copy-start.3
  59.2 0.0 collective-permute-done.11.rest_7_
  59.2 13.5 %update.2 = (bf16[512,3584]{1,0:T(8,128)(2,1)}, f32[512,3584]{1,0:T(8,128)}, f32[512,3584]{1,0:T(8,128)}) custom-call(s32[3]{0:T(128)S(1)} %pad_add_fusion.place, bf16[512,768]{1,0:T(8,128)(2,1)S(1)} %features.1.x_ref, bf16[96,3584]{1,0:T(8,128)(2,1)S(1)} %copy-done, bf16[96,3584]{1,0:T(8,128)(2,1)S(1)} %collective-permute-done.rest_1_, ...), custom_call_target="tpu_custom_call" | custom-call | flops 1 | bytes 1 | tf_op jit(solution)/shard_map/update/pallas_call | solution.py:247
  72.7 0.0 copy-done.1
  72.7 0.0 copy-done.3
  72.8 0.0 collective-permute-done.9.rest_6_
  72.8 0.0 all-to-all-done
  72.8 0.3 collective-permute-start.12
  73.1 0.0 collective-permute-done.1
  73.1 2.3 %add_convert_fusion = bf16[96,3584]{1,0:T(8,128)(2,1)} fusion(bf16[96,3584]{1,0:T(8,128)(2,1)} %collective-permute-done.1, bf16[96,3584]{1,0:T(8,128)(2,1)} %copy-done.5), kind=kLoop, calls=%fused_computation | loop fusion | flops 1376256 | bytes 2064384 | tf_op jit(solution)/shard_map/convert_element_type | solution.py:368
  75.4 0.0 collective-permute-done.12.rest_7_
  75.4 0.0 copy-start.2
  75.4 1.1 %copy-done.2 = bf16[96,3584]{1,0:T(8,128)(2,1)S(1)} copy-done((bf16[96,3584]{1,0:T(8,128)(2,1)S(1)}, bf16[96,3584]{1,0:T(8,128)(2,1)}, u32[]{:S(2)}) %copy-start.2) | copy-done | bytes 688152
  76.5 0.0 copy-start.4
  76.5 1.1 %copy-done.4 = bf16[96,3584]{1,0:T(8,128)(2,1)S(1)} copy-done((bf16[96,3584]{1,0:T(8,128)(2,1)S(1)}, bf16[96,3584]{1,0:T(8,128)(2,1)}, u32[]{:S(2)}) %copy-start.4) | copy-done | bytes 688152
  77.6 10.7 %update.3 = (bf16[512,3584]{1,0:T(8,128)(2,1)}, f32[512,3584]{1,0:T(8,128)}, f32[512,3584]{1,0:T(8,128)}) custom-call(s32[3]{0:T(128)S(1)} %pad_add_fusion.place, bf16[512,768]{1,0:T(8,128)(2,1)S(1)} %features.1.x_ref, bf16[96,3584]{1,0:T(8,128)(2,1)S(1)} %copy-done, ...), custom_call_target="tpu_custom_call", output_to_operand_aliasing={{0}: (14, {}), {1}: (15, {}), {2}: (16, {})} | custom-call | flops 1 | bytes 1 | tf_op jit(solution)/shard_map/update/pallas_call | solution.py:247
  88.3 2.0 %add_convert_fusion.1 = bf16[48,2048]{1,0:T(8,128)(2,1)} fusion(bf16[192,2048]{1,0:T(8,128)(2,1)} %bitcast.4), kind=kLoop, calls=%fused_computation.1 | loop fusion | flops 786432 | bytes 983040 | tf_op jit(solution)/shard_map/convert_element_type | solution.py:437
  (2 shorter events, 0.0 us)
Async XLA Ops:
  0.6 18.8 %collective-permute-start.4 = (bf16[96,3584]{1,0:T(8,128)(2,1)}, bf16[96,3584]{1,0:T(8,128)(2,1)S(1)}, u32[]{:S(2)}, u32[]{:S(2)}) collective-permute-start(bf16[96,3584]{1,0:T(8,128)(2,1)} %rest_0_.7), channel_id=1, source_target_pairs={{0,16},{8,24},{16,0},{24,8},{1,17},{9,25},{17,1},{25,9},{2,18},{10... | collective-permute-start | bytes 2064392 | tf_op jit(solution)/shard_map/ppermute | solution.py:289
  3.6 17.1 %collective-permute-start.2 = (bf16[96,3584]{1,0:T(8,128)(2,1)}, bf16[96,3584]{1,0:T(8,128)(2,1)S(1)}, u32[]{:S(2)}, u32[]{:S(2)}) collective-permute-start(bf16[96,3584]{1,0:T(8,128)(2,1)} %rest_0_.7), channel_id=1, source_target_pairs={{0,4},{4,0},{1,5},{5,1},{2,6},{6,2},{3,7},{7,3},{8,12},{12,8},{9,1... | collective-permute-start | bytes 2064392 | tf_op jit(solution)/shard_map/ppermute | solution.py:289
  5.2 15.6 %collective-permute-start = (bf16[96,3584]{1,0:T(8,128)(2,1)}, bf16[96,3584]{1,0:T(8,128)(2,1)S(1)}, u32[]{:S(2)}, u32[]{:S(2)}) collective-permute-start(bf16[96,3584]{1,0:T(8,128)(2,1)} %rest_0_.7), channel_id=1, source_target_pairs={{0,8},{8,0},{16,24},{24,16},{1,9},{9,1},{17,25},{25,17},{2,10},{10... | collective-permute-start | bytes 2064392 | tf_op jit(solution)/shard_map/ppermute | solution.py:295
  5.2 15.5 %copy-start = (bf16[96,3584]{1,0:T(8,128)(2,1)S(1)}, bf16[96,3584]{1,0:T(8,128)(2,1)}, u32[]{:S(2)}) copy-start(bf16[96,3584]{1,0:T(8,128)(2,1)} %rest_0_.7) | copy-start | bytes 2064388
  16.3 0.8 copy-start.5
  17.1 1.6 %collective-permute-start.3 = (bf16[192,512]{1,0:T(8,128)(2,1)S(1)}, bf16[192,512]{1,0:T(8,128)(2,1)S(1)}, u32[]{:S(2)}, u32[]{:S(2)}) collective-permute-start(bf16[192,512]{1,0:T(8,128)(2,1)S(1)} %get-tuple-element.28), channel_id=1, source_target_pairs={{0,8},{8,0},{16,24},{24,16},{1,9},{9,1},{17,25},{25,17},{2,10},{10... | collective-permute-start | bytes 589832 | tf_op jit(solution)/shard_map/ppermute | solution.py:295
  18.7 0.7 copy-start.6
  32.7 40.1 %all-to-all-start = ((bf16[4,48,2048]{2,1,0:T(8,128)(2,1)}), bf16[4,48,2048]{2,1,0:T(8,128)(2,1)}, u32[]{:S(2)}, u32[]{:S(2)}) async-start(bf16[4,48,2048]{2,1,0:T(8,128)(2,1)} %bitcast.3), calls=%async_computation | async-start | bytes 1572864 | tf_op jit(solution)/shard_map/all_to_all | solution.py:352
  37.6 12.1 %collective-permute-start.5 = (bf16[384,512]{1,0:T(8,128)(2,1)S(1)}, bf16[384,512]{1,0:T(8,128)(2,1)S(1)}, u32[]{:S(2)}, u32[]{:S(2)}) collective-permute-start(bf16[384,512]{1,0:T(8,128)(2,1)S(1)} %get-tuple-element.31), channel_id=1, source_target_pairs={{0,16},{8,24},{16,0},{24,8},{1,17},{9,25},{17,1},{25,9},{2,18},{10... | collective-permute-start | bytes 1179656 | tf_op jit(solution)/shard_map/ppermute | solution.py:289
  38.2 17.6 %collective-permute-start.10 = (bf16[96,2048]{1,0:T(8,128)(2,1)S(1)}, bf16[96,2048]{1,0:T(8,128)(2,1)S(1)}, u32[]{:S(2)}, u32[]{:S(2)}) collective-permute-start(bf16[96,2048]{1,0:T(8,128)(2,1)S(1)} %slice.19), channel_id=1, source_target_pairs={{0,16},{8,24},{16,0},{24,8},{1,17},{9,25},{17,1},{25,9},{2,18},{10... | collective-permute-start | bytes 1179656 | tf_op jit(solution)/shard_map/ppermute | solution.py:289
  39.7 19.4 %collective-permute-start.7 = (bf16[96,3584]{1,0:T(8,128)(2,1)S(1)}, bf16[96,3584]{1,0:T(8,128)(2,1)S(1)}, u32[]{:S(2)}, u32[]{:S(2)}) collective-permute-start(bf16[96,3584]{1,0:T(8,128)(2,1)S(1)} %collective-permute-done.2.rest_1_.rest_2_), channel_id=1, source_target_pairs={{0,8},{8,0},{16,24},{24,16},{1,9},{9,1},{17,25},{25,17},{2,10},{10... | collective-permute-start | bytes 2064392 | tf_op jit(solution)/shard_map/ppermute | solution.py:295
  39.7 19.5 %collective-permute-start.8 = (bf16[96,3584]{1,0:T(8,128)(2,1)S(1)}, bf16[96,3584]{1,0:T(8,128)(2,1)S(1)}, u32[]{:S(2)}, u32[]{:S(2)}) collective-permute-start(bf16[96,3584]{1,0:T(8,128)(2,1)S(1)} %collective-permute-done.4.rest_4_), channel_id=1, source_target_pairs={{0,8},{8,0},{16,24},{24,16},{1,9},{9,1},{17,25},{25,17},{2,10},{10... | collective-permute-start | bytes 2064392 | tf_op jit(solution)/shard_map/ppermute | solution.py:295
  49.6 6.2 %collective-permute-start.6 = (bf16[384,512]{1,0:T(8,128)(2,1)S(1)}, bf16[384,512]{1,0:T(8,128)(2,1)S(1)}, u32[]{:S(2)}, u32[]{:S(2)}) collective-permute-start(bf16[384,512]{1,0:T(8,128)(2,1)S(1)} %collective-permute-done.5.rest_2_), channel_id=1, source_target_pairs={{0,8},{8,0},{16,24},{24,16},{1,9},{9,1},{17,25},{25,17},{2,10},{10... | collective-permute-start | bytes 1179656 | tf_op jit(solution)/shard_map/ppermute | solution.py:295
  49.6 23.4 %collective-permute-start.1 = (bf16[96,3584]{1,0:T(8,128)(2,1)}, bf16[96,3584]{1,0:T(8,128)(2,1)}, u32[]{:S(2)}, u32[]{:S(2)}) collective-permute-start(bf16[96,3584]{1,0:T(8,128)(2,1)} %get-tuple-element.27), channel_id=1, source_target_pairs={{0,4},{4,0},{1,5},{5,1},{2,6},{6,2},{3,7},{7,3},{8,12},{12,8},{9,1... | collective-permute-start | bytes 2064392 | tf_op jit(solution)/shard_map/ppermute | solution.py:289
  55.8 3.4 %collective-permute-start.11 = (bf16[96,2048]{1,0:T(8,128)(2,1)S(1)}, bf16[96,2048]{1,0:T(8,128)(2,1)S(1)}, u32[]{:S(2)}, u32[]{:S(2)}) collective-permute-start(bf16[96,2048]{1,0:T(8,128)(2,1)S(1)} %collective-permute-done.10.rest_6_), channel_id=1, source_target_pairs={{0,8},{8,0},{16,24},{24,16},{1,9},{9,1},{17,25},{25,17},{2,10},{10... | collective-permute-start | bytes 1179656 | tf_op jit(solution)/shard_map/ppermute | solution.py:295
  55.8 16.9 %collective-permute-start.9 = (bf16[96,1536]{1,0:T(8,128)(2,1)S(1)}, bf16[96,1536]{1,0:T(8,128)(2,1)}, u32[]{:S(2)}, u32[]{:S(2)}) collective-permute-start(bf16[96,1536]{1,0:T(8,128)(2,1)S(1)} %slice.18), channel_id=1, source_target_pairs={{0,16},{8,24},{16,0},{24,8},{1,17},{9,25},{17,1},{25,9},{2,18},{10... | collective-permute-start | bytes 884744 | tf_op jit(solution)/shard_map/ppermute | solution.py:289
  56.4 0.9 %copy-start.7 = (bf16[192,512]{1,0:T(8,128)(2,1)S(1)}, bf16[192,512]{1,0:T(8,128)(2,1)}, u32[]{:S(2)}) copy-start(bf16[192,512]{1,0:T(8,128)(2,1)} %copy-done.6) | copy-start | bytes 589828
  59.2 13.6 %copy-start.1 = (bf16[96,3584]{1,0:T(8,128)(2,1)}, bf16[96,3584]{1,0:T(8,128)(2,1)S(1)}, u32[]{:S(2)}) copy-start(bf16[96,3584]{1,0:T(8,128)(2,1)S(1)} %collective-permute-done.7.rest_3_) | copy-start | bytes 2064388
  59.2 13.6 %copy-start.3 = (bf16[96,3584]{1,0:T(8,128)(2,1)}, bf16[96,3584]{1,0:T(8,128)(2,1)S(1)}, u32[]{:S(2)}) copy-start(bf16[96,3584]{1,0:T(8,128)(2,1)S(1)} %collective-permute-done.8.rest_5_) | copy-start | bytes 2064388
  72.8 2.6 %collective-permute-start.12 = (bf16[96,1536]{1,0:T(8,128)(2,1)}, bf16[96,1536]{1,0:T(8,128)(2,1)S(1)}, u32[]{:S(2)}, u32[]{:S(2)}) collective-permute-start(bf16[96,1536]{1,0:T(8,128)(2,1)} %collective-permute-done.9.rest_6_), channel_id=1, source_target_pairs={{0,8},{8,0},{16,24},{24,16},{1,9},{9,1},{17,25},{25,17},{2,10},{10... | collective-permute-start | bytes 884744 | tf_op jit(solution)/shard_map/ppermute | solution.py:295
  75.4 1.1 %copy-start.2 = (bf16[96,3584]{1,0:T(8,128)(2,1)S(1)}, bf16[96,3584]{1,0:T(8,128)(2,1)}, u32[]{:S(2)}) copy-start(bf16[96,3584]{1,0:T(8,128)(2,1)} %copy-done.1) | copy-start | bytes 2064388
  76.5 1.1 %copy-start.4 = (bf16[96,3584]{1,0:T(8,128)(2,1)S(1)}, bf16[96,3584]{1,0:T(8,128)(2,1)}, u32[]{:S(2)}) copy-start(bf16[96,3584]{1,0:T(8,128)(2,1)} %copy-done.3) | copy-start | bytes 2064388

commit v8 on v5

--- a/solution.py
+++ b/solution.py
@@ -50,6 +50,10 @@
     return pltpu.with_memory_space_constraint(array, pltpu.HBM)
 
 
+def in_vmem(array):
+    return pltpu.with_memory_space_constraint(array, pltpu.VMEM)
+
+
 def load_parts(source, target, sems, axis, part):
     loads = []
     for k in range(source.shape[axis] // part):
@@ -98,9 +102,7 @@
         (1,),
         [fixed((tokens, depth)), pl.BlockSpec(memory_space=pltpu.HBM)],
         [fixed((own, width))] * n_row + [fixed(shape) for shape in sent],
-        [struct((own, width), F32)]
-        + [struct((own, width), BF16)] * (n_row - 1)
-        + [struct(shape, BF16) for shape in sent],
+        [struct((own, width), BF16)] * n_row + [struct(shape, BF16) for shape in sent],
         [
             pltpu.VMEM((tokens, depth), BF16),
             pltpu.VMEM((depth, width), BF16),
@@ -111,38 +113,34 @@
     )
 
 
-def input_grad_kernel(n_row, own, part, place, *rest):
-    pieces, w_hbm, out, (cs, ws, sems) = rest[:n_row], rest[n_row], rest[n_row + 1], rest[-3:]
-    loads = load_parts(w_hbm, ws, sems, 0, part)
-    for s in range(n_row):
-        start = pl.multiple_of(lax.rem(place[1] - s + n_row, n_row) * own, own)
-        cs[pl.ds(start, own), :] = pieces[s][...]
-    for k, (at, load) in enumerate(loads):
-        load.wait()
-        acc = lax.dot_general(
-            cs[...], ws[at], (((1,), (1,)), ((), ())), preferred_element_type=F32
-        )
-        out[:, k * part : (k + 1) * part] = acc.astype(BF16)
+def input_grad_kernel(n_row, own, place, *rest):
+    pieces, w_ref, out, cs = rest[:n_row], rest[n_row], rest[n_row + 1], rest[n_row + 2]
+
+    @pl.when(pl.program_id(0) == 0)
+    def _():
+        for s in range(n_row):
+            start = pl.multiple_of(lax.rem(place[1] - s + n_row, n_row) * own, own)
+            cs[pl.ds(start, own), :] = pieces[s][...]
+
+    out[...] = lax.dot_general(
+        cs[...], w_ref[...], (((1,), (1,)), ((), ())), preferred_element_type=F32
+    ).astype(BF16)
 
 
 def input_grad_call(place, by_row, weight, n_row):
     own, width = by_row[0].shape
     depth = weight.shape[0]
-    part = block_of(depth, 256)
+    block = block_of(depth, 256)
     return run(
-        functools.partial(input_grad_kernel, n_row, own, part),
+        functools.partial(input_grad_kernel, n_row, own),
         "input_grad",
-        (1,),
-        [fixed((own, width))] * n_row + [pl.BlockSpec(memory_space=pltpu.HBM)],
-        fixed((n_row * own, depth)),
+        (depth // block,),
+        [fixed((own, width))] * n_row + [pl.BlockSpec((block, width), lambda j, place: (j, 0))],
+        columns(n_row * own, block),
         struct((n_row * own, depth), BF16),
-        [
-            pltpu.VMEM((n_row * own, width), BF16),
-            pltpu.VMEM((depth, width), BF16),
-            pltpu.SemaphoreType.DMA((depth // part,)),
-        ],
-        28,
-        (place, *by_row, in_hbm(weight)),
+        [pltpu.VMEM((n_row * own, width), BF16)],
+        14,
+        (place, *by_row, in_vmem(weight)),
     )
 
 
@@ -245,7 +243,7 @@
             struct((rows, width), F32),
         ],
         input_output_aliases={6 + len(pieces) + k: k for k in range(len(made))},
-        compiler_params=pltpu.CompilerParams(vmem_limit_bytes=28 * MIB),
+        compiler_params=pltpu.CompilerParams(vmem_limit_bytes=22 * MIB),
         cost_estimate=pl.CostEstimate(flops=1, bytes_accessed=1, transcendentals=0),
     )(place, features, *pieces, *map(in_hbm, held), *made)
 
@@ -299,7 +297,7 @@
         part = jnp.dot(inputs, weight, preferred_element_type=F32)
         parts = [
             lax.dynamic_slice_in_dim(part, lax.rem(row + s, n_row) * own, own, 0).astype(
-                BF16 if s else F32
+                BF16
             )
             for s in range(n_row)
         ]
@@ -337,9 +335,7 @@
         ).astype(BF16)
     gparts = lax.all_to_all(gpart, "col", 0, 0, tiled=True)
     width = cotangent.shape[1]
-    block = block_of(width, 512)
-    middle = (width // block + 1) // 2 * block
-    cuts = [(0, middle), (middle, width)] if tiled and middle < width else [(0, width)]
+    cuts = [(0, width)]
     relayed = [{} for _ in cuts]
     for k, (start, stop) in enumerate(cuts):
         for s in range(1, n_row):
@@ -348,7 +344,7 @@
                 if k:
                     piece = after(piece, *sums)
                 relayed[k][c, s] = chip_shift(c)(piece)
-    outputs = parts[0]
+    outputs = parts[0].astype(F32)
     for part in sums:
         outputs = outputs + part.astype(F32)
     outputs = outputs.astype(BF16)

time: 90.7 us -> 76.6 us (0.84)
  waiting for transfers between devices: 23.8 us -> 15.3 us
  Pallas kernels: 44.6 us -> 37.1 us
  other arithmetic: 3.07 us -> 4.17 us
  starting transfers between devices: 13.3 us -> 14.3 us
    ppermute x6 -> x5, waiting for transfers between devices: 23.1 us -> 14 us  [along(): lax.ppermute(a, axis, [(i, (i + shift) % n) for i in range(n)])]
    pallas_call x3, Pallas kernels: 20.6 us -> 16.8 us  [run(): pl.pallas_call(kernel, name=name, grid_spec=pltpu.PrefetchScalarGridSpec(...]
    pallas_call x2 -> x1, Pallas kernels: 24 us -> 20.4 us  [update_call(): pl.pallas_call(functools.partial(update_kernel, origins, tokens_all, math...]
    convert_element_type x1, other arithmetic: 0.99 us -> 2.1 us  [per_device(): outputs = outputs.astype(BF16)]
    ppermute x6 -> x5, starting transfers between devices: 7.36 us -> 8.07 us  [along(): lax.ppermute(a, axis, [(i, (i + shift) % n) for i in range(n)])]
    unnamed x18 -> x16, local copies, waits for them, and re-layouts: 4.03 us -> 4.69 us
  transfers between devices with their start and end apart: 14 -> 12, of which waited for: 5 -> 4; matrix products, arithmetic and copies ran while one was open for 2% -> 3% of each run, Pallas kernels for 49% -> 49%
where the time goes in v8:
time: 76.6 us; the launch traced here: 76.2 us
  Pallas kernels  37.1 us (48%)
  waiting for transfers between devices  15.3 us (20%)
  starting transfers between devices  14.3 us (19%)
  local copies, waits for them, and re-layouts  4.69 us (6%)
  other arithmetic  4.17 us (5%)
    pallas_call x1, Pallas kernels, update_call(): pl.pallas_call(functools.partial(update_kernel, origins, tokens_all, math...  20.4 us
    pallas_call x3, Pallas kernels, run(): pl.pallas_call(kernel, name=name, grid_spec=pltpu.PrefetchScalarGridSpec(...  16.8 us
    ppermute x5, waiting for transfers between devices, along(): lax.ppermute(a, axis, [(i, (i + shift) % n) for i in range(n)])  14 us
    ppermute x5, starting transfers between devices, along(): lax.ppermute(a, axis, [(i, (i + shift) % n) for i in range(n)])  8.07 us
    all_to_all x1, starting transfers between devices, per_device(): gparts = lax.all_to_all(gpart, 'col', 0, 0, tiled=True)  4.87 us
    unnamed x16, local copies, waits for them, and re-layouts  4.69 us
    convert_element_type x1, other arithmetic, per_device(): outputs = outputs.astype(BF16)  2.1 us
    convert_element_type x1, other arithmetic, per_device(): input_grad = sum((lax.slice_in_dim(gparts, k * share, (k + 1) * share).as...  2 us
  transfers between devices with their start and end apart: 12, of which 4 were waited for; matrix products, arithmetic and copies ran while one was open for 3% of the time, Pallas kernels for 49%

profile of v8, /device:TPU:0, one launch (start us, length us, event | category | flops | bytes accessed | tf_op | source)
XLA Modules:
  0.0 76.2 jit_solution(2815268361942799540)
XLA Ops:
  0.6 3.0 %collective-permute-start.4 = (bf16[96,3584]{1,0:T(8,128)(2,1)}, bf16[96,3584]{1,0:T(8,128)(2,1)S(1)}, u32[]{:S(2)}, u32[]{:S(2)}) collective-permute-start(bf16[96,3584]{1,0:T(8,128)(2,1)} %rest_0_.5), channel_id=1, source_target_pairs={{0,16},{8,24},{16,0},{24,8},{1,17},{9,25},{17,1},{25,9},{2,18},{10... | collective-permute-start | bytes 2064392 | tf_op jit(solution)/shard_map/ppermute | solution.py:268
  3.6 0.0 collective-permute-start
  3.6 1.5 %collective-permute-start.2 = (bf16[96,3584]{1,0:T(8,128)(2,1)}, bf16[96,3584]{1,0:T(8,128)(2,1)S(1)}, u32[]{:S(2)}, u32[]{:S(2)}) collective-permute-start(bf16[96,3584]{1,0:T(8,128)(2,1)} %rest_0_.5), channel_id=1, source_target_pairs={{0,4},{4,0},{1,5},{5,1},{2,6},{6,2},{3,7},{7,3},{8,12},{12,8},{9,1... | collective-permute-start | bytes 2064392 | tf_op jit(solution)/shard_map/ppermute | solution.py:268
  5.2 0.1 pad_add_fusion.place
  5.2 0.0 copy-start.1
  5.2 1.1 %copy-done.1 = bf16[192,2048]{1,0:T(8,128)(2,1)S(1)} copy-done((bf16[192,2048]{1,0:T(8,128)(2,1)S(1)}, bf16[192,2048]{1,0:T(8,128)(2,1)}, u32[]{:S(2)}) %copy-start.1) | copy-done | bytes 786456
  6.4 0.0 copy-start
  6.4 0.0 copy-start.3
  6.4 7.6 %forward.1 = (bf16[96,3584]{1,0:T(8,128)(2,1)S(1)}, bf16[96,3584]{1,0:T(8,128)(2,1)}, bf16[192,512]{1,0:T(8,128)(2,1)S(1)}, bf16[384,512]{1,0:T(8,128)(2,1)}) custom-call(s32[3]{0:T(128)S(1)} %pad_add_fusion.place, bf16[192,2048]{1,0:T(8,128)(2,1)S(1)} %copy-done.1, bf16[2048,3584]{1,0:T(8,128)(2,1)} %rest_8_.1), custom_call_target="tpu_custom_call" | custom-call | flops 1 | bytes 1 | tf_op jit(solution)/shard_map/forward/pallas_call | solution.py:31
  14.0 0.3 collective-permute-start.3
  14.3 1.2 %collective-permute-done.3.rest_1_ = bf16[192,512]{1,0:T(8,128)(2,1)S(1)} collective-permute-done((bf16[192,512]{1,0:T(8,128)(2,1)S(1)}, bf16[192,512]{1,0:T(8,128)(2,1)S(1)}, u32[]{:S(2)}, u32[]{:S(2)}) %collective-permute-start.3) | collective-permute-done | bytes 196640 | tf_op jit(solution)/shard_map/ppermute | solution.py:274
  15.5 0.0 copy-start.6
  15.5 0.7 copy-done.6
  16.2 3.1 %collective-permute-done.4.rest_4_ = bf16[96,3584]{1,0:T(8,128)(2,1)S(1)} collective-permute-done((bf16[96,3584]{1,0:T(8,128)(2,1)}, bf16[96,3584]{1,0:T(8,128)(2,1)S(1)}, u32[]{:S(2)}, u32[]{:S(2)}) %collective-permute-start.4) | collective-permute-done | bytes 688160 | tf_op jit(solution)/shard_map/ppermute | solution.py:268
  19.3 0.0 collective-permute-done.rest_1_
  19.3 0.0 copy-start.4
  19.3 0.8 %copy-done.4 = bf16[96,3584]{1,0:T(8,128)(2,1)} copy-done((bf16[96,3584]{1,0:T(8,128)(2,1)}, bf16[96,3584]{1,0:T(8,128)(2,1)S(1)}, u32[]{:S(2)}) %copy-start.4) | copy-done | bytes 688152
  20.1 1.6 %collective-permute-done.2.rest_1_.rest_2_ = bf16[96,3584]{1,0:T(8,128)(2,1)S(1)} collective-permute-done((bf16[96,3584]{1,0:T(8,128)(2,1)}, bf16[96,3584]{1,0:T(8,128)(2,1)S(1)}, u32[]{:S(2)}, u32[]{:S(2)}) %collective-permute-start.2) | collective-permute-done | bytes 688160 | tf_op jit(solution)/shard_map/ppermute | solution.py:268
  21.7 0.3 collective-permute-start.9
  22.0 1.7 %collective-permute-start.1 = (bf16[96,3584]{1,0:T(8,128)(2,1)}, bf16[96,3584]{1,0:T(8,128)(2,1)}, u32[]{:S(2)}, u32[]{:S(2)}) collective-permute-start(bf16[96,3584]{1,0:T(8,128)(2,1)} %get-tuple-element.18), channel_id=1, source_target_pairs={{0,4},{4,0},{1,5},{5,1},{2,6},{6,2},{3,7},{7,3},{8,12},{12,8},{9,1... | collective-permute-start | bytes 2064392 | tf_op jit(solution)/shard_map/ppermute | solution.py:268
  23.8 0.0 copy-start.2
  23.8 1.5 %collective-permute-start.5 = (bf16[384,512]{1,0:T(8,128)(2,1)}, bf16[384,512]{1,0:T(8,128)(2,1)}, u32[]{:S(2)}, u32[]{:S(2)}) collective-permute-start(bf16[384,512]{1,0:T(8,128)(2,1)} %get-tuple-element.22), channel_id=1, source_target_pairs={{0,16},{8,24},{16,0},{24,8},{1,17},{9,25},{17,1},{25,9},{2,18},{10... | collective-permute-start | bytes 1179656 | tf_op jit(solution)/shard_map/ppermute | solution.py:268
  25.2 0.0 copy-done
  25.2 0.0 copy-done.3
  25.2 7.3 %input_grad.1 = bf16[192,2048]{1,0:T(8,128)(2,1)} custom-call(s32[3]{0:T(128)S(1)} %pad_add_fusion.place, bf16[96,3584]{1,0:T(8,128)(2,1)S(1)} %copy-done.3, bf16[96,3584]{1,0:T(8,128)(2,1)S(1)} %collective-permute-done.2.rest_1_.rest_2_, bf16[2048,3584]{1,0:T(8,128)(2,1)S(1)} %copy-done), custom_call_target="tpu_custom_call" | custom-call | flops 1 | bytes 1 | tf_op jit(solution)/shard_map/input_grad/pallas_call | solution.py:31
  32.6 4.9 %all-to-all-start = ((bf16[4,48,2048]{2,1,0:T(8,128)(2,1)}), bf16[4,48,2048]{2,1,0:T(8,128)(2,1)}, u32[]{:S(2)}, u32[]{:S(2)}) async-start(bf16[4,48,2048]{2,1,0:T(8,128)(2,1)} %bitcast.3), calls=%async_computation | async-start | bytes 1572864 | tf_op jit(solution)/shard_map/all_to_all | solution.py:336
  37.4 0.0 collective-permute-start.7
  37.4 0.5 collective-permute-start.8
  38.0 9.3 %collective-permute-done.5.rest_2_ = bf16[384,512]{1,0:T(8,128)(2,1)} collective-permute-done((bf16[384,512]{1,0:T(8,128)(2,1)}, bf16[384,512]{1,0:T(8,128)(2,1)}, u32[]{:S(2)}, u32[]{:S(2)}) %collective-permute-start.5) | collective-permute-done | bytes 393248 | tf_op jit(solution)/shard_map/ppermute | solution.py:268
  47.3 0.0 collective-permute-start.6
  47.3 0.0 collective-permute-done.9.rest_6_
  47.3 0.5 collective-permute-start.10
  47.8 0.0 collective-permute-done.1
  47.8 2.1 %add_convert_fusion = bf16[96,3584]{1,0:T(8,128)(2,1)} fusion(bf16[96,3584]{1,0:T(8,128)(2,1)} %collective-permute-done.1, bf16[96,3584]{1,0:T(8,128)(2,1)S(1)} %get-tuple-element.16), kind=kLoop, calls=%fused_computation | loop fusion | flops 1376256 | bytes 2064384 | tf_op jit(solution)/shard_map/convert_element_type | solution.py:350
  49.9 0.0 collective-permute-done.6.rest_3_
  49.9 0.0 copy-done.2
  49.9 0.0 copy-start.7
  49.9 0.9 %copy-done.7 = bf16[192,512]{1,0:T(8,128)(2,1)S(1)} copy-done((bf16[192,512]{1,0:T(8,128)(2,1)S(1)}, bf16[192,512]{1,0:T(8,128)(2,1)}, u32[]{:S(2)}) %copy-start.7) | copy-done | bytes 196632
  50.9 1.8 %features.1.x_ref = bf16[512,768]{1,0:T(8,128)(2,1)S(1)} custom-call(s32[3]{0:T(128)S(1)} %pad_add_fusion.place, bf16[192,2048]{1,0:T(8,128)(2,1)S(1)} %copy-done.2, bf16[192,512]{1,0:T(8,128)(2,1)S(1)} %copy-done.7, bf16[384,512]{1,0:T(8,128)(2,1)} %collective-permute-done.5.rest_2_, bf16[384,512]{1,0:T(8,128)(2,1)S(1)} %collective-permute-done.6.rest_3_), custom_call_target="tpu_custom_call" | custom-call | flops 1 | bytes 1 | tf_op jit(solution)/shard_map/features/pallas_call | solution.py:31
  52.7 0.0 collective-permute-done.7.rest_3_
  52.7 0.0 collective-permute-done.8.rest_5_
  52.7 0.0 collective-permute-done.10.rest_7_
  52.7 0.0 copy-start.5
  52.7 1.1 %copy-done.5 = bf16[96,3584]{1,0:T(8,128)(2,1)S(1)} copy-done((bf16[96,3584]{1,0:T(8,128)(2,1)S(1)}, bf16[96,3584]{1,0:T(8,128)(2,1)}, u32[]{:S(2)}) %copy-start.5) | copy-done | bytes 688152
  53.8 20.4 %update.1 = (bf16[512,3584]{1,0:T(8,128)(2,1)}, f32[512,3584]{1,0:T(8,128)}, f32[512,3584]{1,0:T(8,128)}) custom-call(s32[3]{0:T(128)S(1)} %pad_add_fusion.place, bf16[512,768]{1,0:T(8,128)(2,1)S(1)} %features.1.x_ref, bf16[96,3584]{1,0:T(8,128)(2,1)S(1)} %copy-done.3, bf16[96,3584]{1,0:T(8,128)(2,1)S(1)} %copy-done.5, ...), custom_call_target="tpu_custom_call" | custom-call | flops 1 | bytes 1 | tf_op jit(solution)/shard_map/update/pallas_call | solution.py:226
  74.2 0.0 all-to-all-done
  74.2 2.0 %add_convert_fusion.1 = bf16[48,2048]{1,0:T(8,128)(2,1)} fusion(bf16[192,2048]{1,0:T(8,128)(2,1)} %bitcast.4), kind=kLoop, calls=%fused_computation.1 | loop fusion | flops 786432 | bytes 983040 | tf_op jit(solution)/shard_map/convert_element_type | solution.py:417
Async XLA Ops:
  0.6 18.7 %collective-permute-start.4 = (bf16[96,3584]{1,0:T(8,128)(2,1)}, bf16[96,3584]{1,0:T(8,128)(2,1)S(1)}, u32[]{:S(2)}, u32[]{:S(2)}) collective-permute-start(bf16[96,3584]{1,0:T(8,128)(2,1)} %rest_0_.5), channel_id=1, source_target_pairs={{0,16},{8,24},{16,0},{24,8},{1,17},{9,25},{17,1},{25,9},{2,18},{10... | collective-permute-start | bytes 2064392 | tf_op jit(solution)/shard_map/ppermute | solution.py:268
  3.6 15.7 %collective-permute-start = (bf16[96,3584]{1,0:T(8,128)(2,1)}, bf16[96,3584]{1,0:T(8,128)(2,1)S(1)}, u32[]{:S(2)}, u32[]{:S(2)}) collective-permute-start(bf16[96,3584]{1,0:T(8,128)(2,1)} %rest_0_.5), channel_id=1, source_target_pairs={{0,8},{8,0},{16,24},{24,16},{1,9},{9,1},{17,25},{25,17},{2,10},{10... | collective-permute-start | bytes 2064392 | tf_op jit(solution)/shard_map/ppermute | solution.py:274
  3.6 18.1 %collective-permute-start.2 = (bf16[96,3584]{1,0:T(8,128)(2,1)}, bf16[96,3584]{1,0:T(8,128)(2,1)S(1)}, u32[]{:S(2)}, u32[]{:S(2)}) collective-permute-start(bf16[96,3584]{1,0:T(8,128)(2,1)} %rest_0_.5), channel_id=1, source_target_pairs={{0,4},{4,0},{1,5},{5,1},{2,6},{6,2},{3,7},{7,3},{8,12},{12,8},{9,1... | collective-permute-start | bytes 2064392 | tf_op jit(solution)/shard_map/ppermute | solution.py:268
  5.2 1.1 %copy-start.1 = (bf16[192,2048]{1,0:T(8,128)(2,1)S(1)}, bf16[192,2048]{1,0:T(8,128)(2,1)}, u32[]{:S(2)}) copy-start(bf16[192,2048]{1,0:T(8,128)(2,1)} %rest_0_.4) | copy-start | bytes 2359300
  6.4 18.9 %copy-start = (bf16[2048,3584]{1,0:T(8,128)(2,1)S(1)}, bf16[2048,3584]{1,0:T(8,128)(2,1)}, u32[]{:S(2)}) copy-start(bf16[2048,3584]{1,0:T(8,128)(2,1)} %rest_8_.1) | copy-start | bytes 44040196
  6.4 18.9 %copy-start.3 = (bf16[96,3584]{1,0:T(8,128)(2,1)S(1)}, bf16[96,3584]{1,0:T(8,128)(2,1)}, u32[]{:S(2)}) copy-start(bf16[96,3584]{1,0:T(8,128)(2,1)} %rest_0_.5) | copy-start | bytes 2064388
  14.0 1.5 %collective-permute-start.3 = (bf16[192,512]{1,0:T(8,128)(2,1)S(1)}, bf16[192,512]{1,0:T(8,128)(2,1)S(1)}, u32[]{:S(2)}, u32[]{:S(2)}) collective-permute-start(bf16[192,512]{1,0:T(8,128)(2,1)S(1)} %get-tuple-element.19), channel_id=1, source_target_pairs={{0,8},{8,0},{16,24},{24,16},{1,9},{9,1},{17,25},{25,17},{2,10},{10... | collective-permute-start | bytes 589832 | tf_op jit(solution)/shard_map/ppermute | solution.py:274
  15.5 0.7 copy-start.6
  19.3 0.8 %copy-start.4 = (bf16[96,3584]{1,0:T(8,128)(2,1)}, bf16[96,3584]{1,0:T(8,128)(2,1)S(1)}, u32[]{:S(2)}) copy-start(bf16[96,3584]{1,0:T(8,128)(2,1)S(1)} %collective-permute-done.rest_1_) | copy-start | bytes 2064388
  21.7 25.6 %collective-permute-start.9 = (bf16[96,3584]{1,0:T(8,128)(2,1)S(1)}, bf16[96,3584]{1,0:T(8,128)(2,1)}, u32[]{:S(2)}, u32[]{:S(2)}) collective-permute-start(bf16[96,3584]{1,0:T(8,128)(2,1)S(1)} %collective-permute-done.2.rest_1_.rest_2_), channel_id=1, source_target_pairs={{0,16},{8,24},{16,0},{24,8},{1,17},{9,25},{17,1},{25,9},{2,18},{10... | collective-permute-start | bytes 2064392 | tf_op jit(solution)/shard_map/ppermute | solution.py:268
  22.0 25.8 %collective-permute-start.1 = (bf16[96,3584]{1,0:T(8,128)(2,1)}, bf16[96,3584]{1,0:T(8,128)(2,1)}, u32[]{:S(2)}, u32[]{:S(2)}) collective-permute-start(bf16[96,3584]{1,0:T(8,128)(2,1)} %get-tuple-element.18), channel_id=1, source_target_pairs={{0,4},{4,0},{1,5},{5,1},{2,6},{6,2},{3,7},{7,3},{8,12},{12,8},{9,1... | collective-permute-start | bytes 2064392 | tf_op jit(solution)/shard_map/ppermute | solution.py:268
  23.8 26.2 %copy-start.2 = (bf16[192,2048]{1,0:T(8,128)(2,1)S(1)}, bf16[192,2048]{1,0:T(8,128)(2,1)}, u32[]{:S(2)}) copy-start(bf16[192,2048]{1,0:T(8,128)(2,1)} %rest_0_.4) | copy-start | bytes 2359300
  23.8 23.5 %collective-permute-start.5 = (bf16[384,512]{1,0:T(8,128)(2,1)}, bf16[384,512]{1,0:T(8,128)(2,1)}, u32[]{:S(2)}, u32[]{:S(2)}) collective-permute-start(bf16[384,512]{1,0:T(8,128)(2,1)} %get-tuple-element.22), channel_id=1, source_target_pairs={{0,16},{8,24},{16,0},{24,8},{1,17},{9,25},{17,1},{25,9},{2,18},{10... | collective-permute-start | bytes 1179656 | tf_op jit(solution)/shard_map/ppermute | solution.py:268
  32.6 41.6 %all-to-all-start = ((bf16[4,48,2048]{2,1,0:T(8,128)(2,1)}), bf16[4,48,2048]{2,1,0:T(8,128)(2,1)}, u32[]{:S(2)}, u32[]{:S(2)}) async-start(bf16[4,48,2048]{2,1,0:T(8,128)(2,1)} %bitcast.3), calls=%async_computation | async-start | bytes 1572864 | tf_op jit(solution)/shard_map/all_to_all | solution.py:336
  37.4 15.3 %collective-permute-start.7 = (bf16[96,3584]{1,0:T(8,128)(2,1)S(1)}, bf16[96,3584]{1,0:T(8,128)(2,1)S(1)}, u32[]{:S(2)}, u32[]{:S(2)}) collective-permute-start(bf16[96,3584]{1,0:T(8,128)(2,1)S(1)} %collective-permute-done.2.rest_1_.rest_2_), channel_id=1, source_target_pairs={{0,8},{8,0},{16,24},{24,16},{1,9},{9,1},{17,25},{25,17},{2,10},{10... | collective-permute-start | bytes 2064392 | tf_op jit(solution)/shard_map/ppermute | solution.py:274
  37.4 15.3 %collective-permute-start.8 = (bf16[96,3584]{1,0:T(8,128)(2,1)S(1)}, bf16[96,3584]{1,0:T(8,128)(2,1)S(1)}, u32[]{:S(2)}, u32[]{:S(2)}) collective-permute-start(bf16[96,3584]{1,0:T(8,128)(2,1)S(1)} %collective-permute-done.4.rest_4_), channel_id=1, source_target_pairs={{0,8},{8,0},{16,24},{24,16},{1,9},{9,1},{17,25},{25,17},{2,10},{10... | collective-permute-start | bytes 2064392 | tf_op jit(solution)/shard_map/ppermute | solution.py:274
  47.3 2.6 %collective-permute-start.6 = (bf16[384,512]{1,0:T(8,128)(2,1)}, bf16[384,512]{1,0:T(8,128)(2,1)S(1)}, u32[]{:S(2)}, u32[]{:S(2)}) collective-permute-start(bf16[384,512]{1,0:T(8,128)(2,1)} %collective-permute-done.5.rest_2_), channel_id=1, source_target_pairs={{0,8},{8,0},{16,24},{24,16},{1,9},{9,1},{17,25},{25,17},{2,10},{10... | collective-permute-start | bytes 1179656 | tf_op jit(solution)/shard_map/ppermute | solution.py:274
  47.3 5.4 %collective-permute-start.10 = (bf16[96,3584]{1,0:T(8,128)(2,1)}, bf16[96,3584]{1,0:T(8,128)(2,1)S(1)}, u32[]{:S(2)}, u32[]{:S(2)}) collective-permute-start(bf16[96,3584]{1,0:T(8,128)(2,1)} %collective-permute-done.9.rest_6_), channel_id=1, source_target_pairs={{0,8},{8,0},{16,24},{24,16},{1,9},{9,1},{17,25},{25,17},{2,10},{10... | collective-permute-start | bytes 2064392 | tf_op jit(solution)/shard_map/ppermute | solution.py:274
  49.9 0.9 %copy-start.7 = (bf16[192,512]{1,0:T(8,128)(2,1)S(1)}, bf16[192,512]{1,0:T(8,128)(2,1)}, u32[]{:S(2)}) copy-start(bf16[192,512]{1,0:T(8,128)(2,1)} %copy-done.6) | copy-start | bytes 589828
  52.7 1.1 %copy-start.5 = (bf16[96,3584]{1,0:T(8,128)(2,1)S(1)}, bf16[96,3584]{1,0:T(8,128)(2,1)}, u32[]{:S(2)}) copy-start(bf16[96,3584]{1,0:T(8,128)(2,1)} %copy-done.4) | copy-start | bytes 2064388

commit v9 on v8

--- a/solution.py
+++ b/solution.py
@@ -108,7 +108,7 @@
             pltpu.VMEM((depth, width), BF16),
             pltpu.SemaphoreType.DMA((width // part,)),
         ],
-        28,
+        24,
         (place, inputs, in_hbm(weight)),
     )
 
@@ -139,7 +139,7 @@
         columns(n_row * own, block),
         struct((n_row * own, depth), BF16),
         [pltpu.VMEM((n_row * own, width), BF16)],
-        14,
+        6,
         (place, *by_row, in_vmem(weight)),
     )
 
@@ -164,8 +164,31 @@
         fixed((slice_rows, n_dp * tokens)),
         struct((slice_rows, n_dp * tokens), BF16),
         [pltpu.VMEM((n_dp * tokens, slice_rows), BF16)],
-        16,
+        6,
         (place, inputs, *held),
+    )
+
+
+def total_kernel(place, parts, out):
+    share = out.shape[0]
+    whole = parts[:share, :].astype(F32)
+    for k in range(1, parts.shape[0] // share):
+        whole = whole + parts[k * share : (k + 1) * share, :].astype(F32)
+    out[...] = whole.astype(BF16)
+
+
+def total_call(place, parts, n):
+    rows, width = parts.shape
+    return run(
+        total_kernel,
+        "total",
+        (1,),
+        [fixed((rows, width))],
+        fixed((rows // n, width)),
+        struct((rows // n, width), BF16),
+        [],
+        8,
+        (place, parts),
     )
 
 
@@ -243,9 +266,9 @@
             struct((rows, width), F32),
         ],
         input_output_aliases={6 + len(pieces) + k: k for k in range(len(made))},
-        compiler_params=pltpu.CompilerParams(vmem_limit_bytes=22 * MIB),
+        compiler_params=pltpu.CompilerParams(vmem_limit_bytes=18 * MIB),
         cost_estimate=pl.CostEstimate(flops=1, bytes_accessed=1, transcendentals=0),
-    )(place, features, *pieces, *map(in_hbm, held), *made)
+    )(place, features, *pieces, in_hbm(held[0]), *map(in_vmem, held[1:]), *made)
 
 
 def after(value, *others):
@@ -317,7 +340,7 @@
     ]
     near = [swap_cores(to_send.pop(0))] if cores == 2 else []
     first = [by_chip[c, 0] for c in range(1, chips)]
-    far = [chip_shift(c)(after(to_send[c - 1], *first)) for c in range(1, chips)]
+    far = [chip_shift(c)(to_send[c - 1]) for c in range(1, chips)]
     for s in range(1, n_row):
         by_row[s] = after(by_row[s], parts[0], *near, *first, *swapped.values())
         if cores == 2:
@@ -326,8 +349,26 @@
         for c in range(1, chips):
             swapped[c, 0] = swap_cores(by_chip[c, 0])
 
+    held, sources = list(near), [(functools.partial(dp_of, c=0, flip=0), 0)]
+    if cores == 2:
+        sources.append((functools.partial(dp_of, c=0, flip=1), 0))
+    for c in range(1, chips):
+        for f in flips:
+            piece = far[c - 1]
+            held.append(swap_cores(after(piece, *first, *by_row[1:])) if f else piece)
+            sources.append((functools.partial(dp_of, c=c, flip=f), f * tokens))
     if tiled:
-        gpart = input_grad_call(place, by_row, weight, n_row)
+        features = features_call(place, inputs, held, sources, slice_rows)
+    else:
+        mine = lax.dynamic_slice_in_dim(inputs, dp * slice_rows, slice_rows, 1)
+        features = in_order(
+            [mine] + [h[skip : skip + tokens] for h, (_, skip) in zip(held, sources[1:])],
+            [origin(dp) for origin, _ in sources],
+            tokens,
+        )
+    if tiled:
+        ready = [by_row[0]] + [after(piece, features) for piece in by_row[1:]]
+        gpart = input_grad_call(place, ready, weight, n_row)
     else:
         gathered = in_order(by_row, [lax.rem(row - s + n_row, n_row) for s in range(n_row)], own)
         gpart = lax.dot_general(
@@ -349,14 +390,6 @@
         outputs = outputs + part.astype(F32)
     outputs = outputs.astype(BF16)
 
-    held, sources = list(near), [(functools.partial(dp_of, c=0, flip=0), 0)]
-    if cores == 2:
-        sources.append((functools.partial(dp_of, c=0, flip=1), 0))
-    for c in range(1, chips):
-        for f in flips:
-            piece = far[c - 1]
-            held.append(swap_cores(piece) if f else piece)
-            sources.append((functools.partial(dp_of, c=c, flip=f), f * tokens))
     by_chip.update({(0, s): by_row[s] for s in range(n_row)})
     origins = []
     for c in range(chips):
@@ -383,19 +416,12 @@
         return pieces
 
     if tiled:
-        features = features_call(place, inputs, held, sources, slice_rows)
         held = (weight, anchor, first_moment, second_moment)
         made = []
         for k, (start, stop) in enumerate(cuts):
             made = update_call(place, features, pieces_of(k, *made[:1]), origins, start, stop, held, made)
         new_weight, new_first, new_second = made
     else:
-        mine = lax.dynamic_slice_in_dim(inputs, dp * slice_rows, slice_rows, 1)
-        features = in_order(
-            [mine] + [h[skip : skip + tokens] for h, (_, skip) in zip(held, sources[1:])],
-            [origin(dp) for origin, _ in sources],
-            tokens,
-        )
         gathered = in_order(pieces_of(0), [origin(dp, row) for origin in origins], own)
         summed = lax.dot_general(
             features, gathered, (((0,), (0,)), ((), ())), preferred_element_type=F32
@@ -412,9 +438,12 @@
         )
         new_weight = new_weight.astype(BF16)
     gparts = after(gparts, new_first)
-    input_grad = sum(
-        lax.slice_in_dim(gparts, k * share, (k + 1) * share).astype(F32) for k in range(n_col)
-    ).astype(BF16)
+    if tiled:
+        input_grad = total_call(place, gparts, n_col)
+    else:
+        input_grad = sum(
+            lax.slice_in_dim(gparts, k * share, (k + 1) * share).astype(F32) for k in range(n_col)
+        ).astype(BF16)
     return (outputs, input_grad, new_weight, new_first, new_second)
 
 

time: 76.6 us -> 76.7 us (level)
  local copies, waits for them, and re-layouts: 4.69 us -> 12.4 us
  Pallas kernels: 37.1 us -> 33.4 us
  waiting for transfers between devices: 15.3 us -> 13.4 us
  other arithmetic: 4.17 us -> 2.39 us
    unnamed x16 -> x22, local copies, waits for them, and re-layouts: 4.69 us -> 12.4 us
    ppermute x5, waiting for transfers between devices: 14 us -> 8.74 us  [along(): lax.ppermute(a, axis, [(i, (i + shift) % n) for i in range(n)])]
    pallas_call x1, Pallas kernels: 20.4 us -> 16.3 us  [update_call(): pl.pallas_call(functools.partial(update_kernel, origins, tokens_all, math...]
    ppermute x6, waiting for transfers between devices: 1.23 us -> 4.65 us  [swap_cores(): return lax.ppermute(a, 'dp', [(i, i ^ 1) for i in range(n_dp)])]
    convert_element_type x1 -> x0, other arithmetic: 2 us -> none  [per_device(): input_grad = sum((lax.slice_in_dim(gparts, k * share, (k + 1) * share).as...]
    ppermute x6, starting transfers between devices: 1.32 us -> 0.52 us  [swap_cores(): return lax.ppermute(a, 'dp', [(i, i ^ 1) for i in range(n_dp)])]
    pallas_call x3 -> x4, Pallas kernels: 16.8 us -> 17.1 us  [run(): pl.pallas_call(kernel, name=name, grid_spec=pltpu.PrefetchScalarGridSpec(...]
  transfers between devices with their start and end apart: 12 -> 12, of which waited for: 4 -> 8; matrix products, arithmetic and copies ran while one was open for 3% -> 3% of each run, Pallas kernels for 49% -> 42%
where the time goes in v9:
time: 76.7 us; the launch traced here: 76.3 us
  Pallas kernels  33.4 us (44%)
  starting transfers between devices  14 us (18%)
  waiting for transfers between devices  13.4 us (17%)
  local copies, waits for them, and re-layouts  12.4 us (16%)
  other arithmetic  2.39 us (3%)
    pallas_call x4, Pallas kernels, run(): pl.pallas_call(kernel, name=name, grid_spec=pltpu.PrefetchScalarGridSpec(...  17.1 us
    pallas_call x1, Pallas kernels, update_call(): pl.pallas_call(functools.partial(update_kernel, origins, tokens_all, math...  16.3 us
    unnamed x22, local copies, waits for them, and re-layouts  12.4 us
    ppermute x5, waiting for transfers between devices, along(): lax.ppermute(a, axis, [(i, (i + shift) % n) for i in range(n)])  8.74 us
    ppermute x5, starting transfers between devices, along(): lax.ppermute(a, axis, [(i, (i + shift) % n) for i in range(n)])  8.01 us
    all_to_all x1, starting transfers between devices, per_device(): gparts = lax.all_to_all(gpart, 'col', 0, 0, tiled=True)  5.44 us
    ppermute x6, waiting for transfers between devices, swap_cores(): return lax.ppermute(a, 'dp', [(i, i ^ 1) for i in range(n_dp)])  4.65 us
    convert_element_type x1, other arithmetic, per_device(): outputs = outputs.astype(BF16)  2.31 us
  transfers between devices with their start and end apart: 12, of which 8 were waited for; matrix products, arithmetic and copies ran while one was open for 3% of the time, Pallas kernels for 42%

profile of v9, /device:TPU:0, one launch (start us, length us, event | category | flops | bytes accessed | tf_op | source)
XLA Modules:
  0.0 76.3 jit_solution(3334637614503295260)
XLA Ops:
  0.6 3.0 %collective-permute-start.4 = (bf16[96,3584]{1,0:T(8,128)(2,1)}, bf16[96,3584]{1,0:T(8,128)(2,1)S(1)}, u32[]{:S(2)}, u32[]{:S(2)}) collective-permute-start(bf16[96,3584]{1,0:T(8,128)(2,1)} %rest_0_.5), channel_id=1, source_target_pairs={{0,16},{8,24},{16,0},{24,8},{1,17},{9,25},{17,1},{25,9},{2,18},{10... | collective-permute-start | bytes 2064392 | tf_op jit(solution)/shard_map/ppermute | solution.py:291
  3.6 0.0 collective-permute-start
  3.6 1.5 %collective-permute-start.2 = (bf16[96,3584]{1,0:T(8,128)(2,1)}, bf16[96,3584]{1,0:T(8,128)(2,1)S(1)}, u32[]{:S(2)}, u32[]{:S(2)}) collective-permute-start(bf16[96,3584]{1,0:T(8,128)(2,1)} %rest_0_.5), channel_id=1, source_target_pairs={{0,4},{4,0},{1,5},{5,1},{2,6},{6,2},{3,7},{7,3},{8,12},{12,8},{9,1... | collective-permute-start | bytes 2064392 | tf_op jit(solution)/shard_map/ppermute | solution.py:291
  5.2 0.1 pad_add_fusion.place
  5.2 0.0 copy-start.4
  5.2 1.1 %copy-done.4 = bf16[192,2048]{1,0:T(8,128)(2,1)S(1)} copy-done((bf16[192,2048]{1,0:T(8,128)(2,1)S(1)}, bf16[192,2048]{1,0:T(8,128)(2,1)}, u32[]{:S(2)}) %copy-start.4) | copy-done | bytes 786456
  6.4 0.0 copy-start
  6.4 0.0 copy-start.5
  6.4 7.6 %forward.1 = (bf16[96,3584]{1,0:T(8,128)(2,1)S(1)}, bf16[96,3584]{1,0:T(8,128)(2,1)}, bf16[192,512]{1,0:T(8,128)(2,1)S(1)}, bf16[384,512]{1,0:T(8,128)(2,1)S(1)}) custom-call(s32[3]{0:T(128)S(1)} %pad_add_fusion.place, bf16[192,2048]{1,0:T(8,128)(2,1)S(1)} %copy-done.4, bf16[2048,3584]{1,0:T(8,128)(2,1)} %rest_8_.1), custom_call_target="tpu_custom_call" | custom-call | flops 1 | bytes 1 | tf_op jit(solution)/shard_map/forward/pallas_call | solution.py:31
  14.0 0.0 copy-start.6
  14.0 0.6 collective-permute-start.5
  14.6 0.0 collective-permute-start.3
  14.6 1.4 %collective-permute-done.3.rest_1_ = bf16[192,512]{1,0:T(8,128)(2,1)S(1)} collective-permute-done((bf16[192,512]{1,0:T(8,128)(2,1)S(1)}, bf16[192,512]{1,0:T(8,128)(2,1)S(1)}, u32[]{:S(2)}, u32[]{:S(2)}) %collective-permute-start.3) | collective-permute-done | bytes 196640 | tf_op jit(solution)/shard_map/ppermute | solution.py:297
  16.0 4.1 %collective-permute-done.4.rest_4_ = bf16[96,3584]{1,0:T(8,128)(2,1)S(1)} collective-permute-done((bf16[96,3584]{1,0:T(8,128)(2,1)}, bf16[96,3584]{1,0:T(8,128)(2,1)S(1)}, u32[]{:S(2)}, u32[]{:S(2)}) %collective-permute-start.4) | collective-permute-done | bytes 688160 | tf_op jit(solution)/shard_map/ppermute | solution.py:291
  20.1 0.0 copy-start.7
  20.1 0.0 collective-permute-done.rest_1_
  20.1 0.0 copy-start.9
  20.1 0.9 %copy-done.9 = bf16[96,3584]{1,0:T(8,128)(2,1)} copy-done((bf16[96,3584]{1,0:T(8,128)(2,1)}, bf16[96,3584]{1,0:T(8,128)(2,1)S(1)}, u32[]{:S(2)}) %copy-start.9) | copy-done | bytes 688152
  21.0 0.7 collective-permute-done.2.rest_1_.rest_2_
  21.7 1.4 %collective-permute-start.9 = (bf16[96,3584]{1,0:T(8,128)(2,1)S(1)}, bf16[96,3584]{1,0:T(8,128)(2,1)}, u32[]{:S(2)}, u32[]{:S(2)}) collective-permute-start(bf16[96,3584]{1,0:T(8,128)(2,1)S(1)} %collective-permute-done.2.rest_1_.rest_2_), channel_id=1, source_target_pairs={{0,16},{8,24},{16,0},{24,8},{1,17},{9,25},{17,1},{25,9},{2,18},{10... | collective-permute-start | bytes 2064392 | tf_op jit(solution)/shard_map/ppermute | solution.py:291
  23.1 1.5 %collective-permute-start.1 = (bf16[96,3584]{1,0:T(8,128)(2,1)}, bf16[96,3584]{1,0:T(8,128)(2,1)}, u32[]{:S(2)}, u32[]{:S(2)}) collective-permute-start(bf16[96,3584]{1,0:T(8,128)(2,1)} %get-tuple-element.19), channel_id=1, source_target_pairs={{0,4},{4,0},{1,5},{5,1},{2,6},{6,2},{3,7},{7,3},{8,12},{12,8},{9,1... | collective-permute-start | bytes 2064392 | tf_op jit(solution)/shard_map/ppermute | solution.py:291
  24.6 4.0 %collective-permute-done.5.rest_2_ = bf16[384,512]{1,0:T(8,128)(2,1)S(1)} collective-permute-done((bf16[384,512]{1,0:T(8,128)(2,1)S(1)}, bf16[384,512]{1,0:T(8,128)(2,1)S(1)}, u32[]{:S(2)}, u32[]{:S(2)}) %collective-permute-start.5) | collective-permute-done | bytes 393248 | tf_op jit(solution)/shard_map/ppermute | solution.py:291
  28.5 0.0 collective-permute-start.6
  28.5 0.0 copy-done.7
  28.5 1.7 %collective-permute-done.6.rest_3_ = bf16[384,512]{1,0:T(8,128)(2,1)S(1)} collective-permute-done((bf16[384,512]{1,0:T(8,128)(2,1)S(1)}, bf16[384,512]{1,0:T(8,128)(2,1)S(1)}, u32[]{:S(2)}, u32[]{:S(2)}) %collective-permute-start.6) | collective-permute-done | bytes 393248 | tf_op jit(solution)/shard_map/ppermute | solution.py:297
  30.3 0.9 %features.1.x_ref = bf16[512,768]{1,0:T(8,128)(2,1)S(1)} custom-call(s32[3]{0:T(128)S(1)} %pad_add_fusion.place, bf16[192,2048]{1,0:T(8,128)(2,1)S(1)} %copy-done.4, bf16[192,512]{1,0:T(8,128)(2,1)S(1)} %collective-permute-done.3.rest_1_, bf16[384,512]{1,0:T(8,128)(2,1)S(1)} %collective-permute-done.5.rest_2_, ...), custom_call_target="tpu_custom_call" | custom-call | flops 1 | bytes 1 | tf_op jit(solution)/shard_map/features/pallas_call | solution.py:31
  31.1 0.0 copy-done
  31.1 0.0 copy-done.5
  31.1 7.3 %input_grad.1 = bf16[192,2048]{1,0:T(8,128)(2,1)} custom-call(s32[3]{0:T(128)S(1)} %pad_add_fusion.place, bf16[96,3584]{1,0:T(8,128)(2,1)S(1)} %copy-done.5, bf16[96,3584]{1,0:T(8,128)(2,1)S(1)} %collective-permute-done.2.rest_1_.rest_2_, bf16[2048,3584]{1,0:T(8,128)(2,1)S(1)} %copy-done), custom_call_target="tpu_custom_call" | custom-call | flops 1 | bytes 1 | tf_op jit(solution)/shard_map/input_grad/pallas_call | solution.py:31
  38.5 0.0 copy-done.6
  38.5 5.4 %all-to-all-start = ((bf16[4,48,2048]{2,1,0:T(8,128)(2,1)}), bf16[4,48,2048]{2,1,0:T(8,128)(2,1)S(1)}, u32[]{:S(2)}, u32[]{:S(2)}) async-start(bf16[4,48,2048]{2,1,0:T(8,128)(2,1)} %bitcast.3), calls=%async_computation | async-start | bytes 1572864 | tf_op jit(solution)/shard_map/all_to_all | solution.py:377
  43.9 0.0 collective-permute-start.7
  43.9 0.5 collective-permute-start.8
  44.4 0.0 collective-permute-done.9.rest_6_
  44.4 0.0 collective-permute-start.10
  44.4 0.0 collective-permute-done.1
  44.4 2.3 %add_convert_fusion = bf16[96,3584]{1,0:T(8,128)(2,1)} fusion(bf16[96,3584]{1,0:T(8,128)(2,1)} %collective-permute-done.1, bf16[96,3584]{1,0:T(8,128)(2,1)} %copy-done.6), kind=kLoop, calls=%fused_computation | loop fusion | flops 1376256 | bytes 2064384 | tf_op jit(solution)/shard_map/convert_element_type | solution.py:391
  46.7 0.3 collective-permute-done.7.rest_3_
  47.0 0.2 collective-permute-done.8.rest_5_
  47.2 1.0 %collective-permute-done.10.rest_7_ = bf16[96,3584]{1,0:T(8,128)(2,1)S(1)} collective-permute-done((bf16[96,3584]{1,0:T(8,128)(2,1)}, bf16[96,3584]{1,0:T(8,128)(2,1)S(1)}, u32[]{:S(2)}, u32[]{:S(2)}) %collective-permute-start.10) | collective-permute-done | bytes 688160 | tf_op jit(solution)/shard_map/ppermute | solution.py:297
  48.2 0.0 copy-start.1
  48.2 3.1 %copy-done.1 = f32[512,3584]{1,0:T(8,128)S(1)} copy-done((f32[512,3584]{1,0:T(8,128)S(1)}, f32[512,3584]{1,0:T(8,128)}, u32[]{:S(2)}) %copy-start.1) | copy-done | bytes 7340056
  51.3 0.0 copy-start.2
  51.3 3.1 %copy-done.2 = f32[512,3584]{1,0:T(8,128)S(1)} copy-done((f32[512,3584]{1,0:T(8,128)S(1)}, f32[512,3584]{1,0:T(8,128)}, u32[]{:S(2)}) %copy-start.2) | copy-done | bytes 7340056
  54.4 0.0 copy-start.3
  54.4 2.0 %copy-done.3 = bf16[512,3584]{1,0:T(8,128)(2,1)S(1)} copy-done((bf16[512,3584]{1,0:T(8,128)(2,1)S(1)}, bf16[512,3584]{1,0:T(8,128)(2,1)}, u32[]{:S(2)}) %copy-start.3) | copy-done | bytes 3670040
  56.4 0.0 copy-start.8
  56.4 1.1 %copy-done.8 = bf16[96,3584]{1,0:T(8,128)(2,1)S(1)} copy-done((bf16[96,3584]{1,0:T(8,128)(2,1)S(1)}, bf16[96,3584]{1,0:T(8,128)(2,1)}, u32[]{:S(2)}) %copy-start.8) | copy-done | bytes 688152
  57.5 0.0 copy-start.10
  57.5 1.1 %copy-done.10 = bf16[96,3584]{1,0:T(8,128)(2,1)S(1)} copy-done((bf16[96,3584]{1,0:T(8,128)(2,1)S(1)}, bf16[96,3584]{1,0:T(8,128)(2,1)}, u32[]{:S(2)}) %copy-start.10) | copy-done | bytes 688152
  58.6 16.3 %update.1 = (bf16[512,3584]{1,0:T(8,128)(2,1)}, f32[512,3584]{1,0:T(8,128)}, f32[512,3584]{1,0:T(8,128)}) custom-call(s32[3]{0:T(128)S(1)} %pad_add_fusion.place, bf16[512,768]{1,0:T(8,128)(2,1)S(1)} %features.1.x_ref, bf16[96,3584]{1,0:T(8,128)(2,1)S(1)} %copy-done.5, bf16[96,3584]{1,0:T(8,128)(2,1)S(1)} %copy-done.10, ...), custom_call_target="tpu_custom_call" | custom-call | flops 1 | bytes 1 | tf_op jit(solution)/shard_map/update/pallas_call | solution.py:249
  75.0 0.0 all-to-all-done
  75.0 1.3 %total.1 = bf16[48,2048]{1,0:T(8,128)(2,1)} custom-call(s32[3]{0:T(128)S(1)} %pad_add_fusion.place, bf16[192,2048]{1,0:T(8,128)(2,1)S(1)} %bitcast.5), custom_call_target="tpu_custom_call" | custom-call | flops 1 | bytes 1 | tf_op jit(solution)/shard_map/total/pallas_call | solution.py:31
Async XLA Ops:
  0.6 19.5 %collective-permute-start.4 = (bf16[96,3584]{1,0:T(8,128)(2,1)}, bf16[96,3584]{1,0:T(8,128)(2,1)S(1)}, u32[]{:S(2)}, u32[]{:S(2)}) collective-permute-start(bf16[96,3584]{1,0:T(8,128)(2,1)} %rest_0_.5), channel_id=1, source_target_pairs={{0,16},{8,24},{16,0},{24,8},{1,17},{9,25},{17,1},{25,9},{2,18},{10... | collective-permute-start | bytes 2064392 | tf_op jit(solution)/shard_map/ppermute | solution.py:291
  3.6 16.5 %collective-permute-start = (bf16[96,3584]{1,0:T(8,128)(2,1)}, bf16[96,3584]{1,0:T(8,128)(2,1)S(1)}, u32[]{:S(2)}, u32[]{:S(2)}) collective-permute-start(bf16[96,3584]{1,0:T(8,128)(2,1)} %rest_0_.5), channel_id=1, source_target_pairs={{0,8},{8,0},{16,24},{24,16},{1,9},{9,1},{17,25},{25,17},{2,10},{10... | collective-permute-start | bytes 2064392 | tf_op jit(solution)/shard_map/ppermute | solution.py:297
  3.6 18.1 %collective-permute-start.2 = (bf16[96,3584]{1,0:T(8,128)(2,1)}, bf16[96,3584]{1,0:T(8,128)(2,1)S(1)}, u32[]{:S(2)}, u32[]{:S(2)}) collective-permute-start(bf16[96,3584]{1,0:T(8,128)(2,1)} %rest_0_.5), channel_id=1, source_target_pairs={{0,4},{4,0},{1,5},{5,1},{2,6},{6,2},{3,7},{7,3},{8,12},{12,8},{9,1... | collective-permute-start | bytes 2064392 | tf_op jit(solution)/shard_map/ppermute | solution.py:291
  5.2 1.1 %copy-start.4 = (bf16[192,2048]{1,0:T(8,128)(2,1)S(1)}, bf16[192,2048]{1,0:T(8,128)(2,1)}, u32[]{:S(2)}) copy-start(bf16[192,2048]{1,0:T(8,128)(2,1)} %rest_0_.3) | copy-start | bytes 2359300
  6.4 24.8 %copy-start = (bf16[2048,3584]{1,0:T(8,128)(2,1)S(1)}, bf16[2048,3584]{1,0:T(8,128)(2,1)}, u32[]{:S(2)}) copy-start(bf16[2048,3584]{1,0:T(8,128)(2,1)} %rest_8_.1) | copy-start | bytes 44040196
  6.4 24.8 %copy-start.5 = (bf16[96,3584]{1,0:T(8,128)(2,1)S(1)}, bf16[96,3584]{1,0:T(8,128)(2,1)}, u32[]{:S(2)}) copy-start(bf16[96,3584]{1,0:T(8,128)(2,1)} %rest_0_.5) | copy-start | bytes 2064388
  14.0 24.5 %copy-start.6 = (bf16[96,3584]{1,0:T(8,128)(2,1)}, bf16[96,3584]{1,0:T(8,128)(2,1)S(1)}, u32[]{:S(2)}) copy-start(bf16[96,3584]{1,0:T(8,128)(2,1)S(1)} %get-tuple-element.17) | copy-start | bytes 2064388
  14.0 14.5 %collective-permute-start.5 = (bf16[384,512]{1,0:T(8,128)(2,1)S(1)}, bf16[384,512]{1,0:T(8,128)(2,1)S(1)}, u32[]{:S(2)}, u32[]{:S(2)}) collective-permute-start(bf16[384,512]{1,0:T(8,128)(2,1)S(1)} %get-tuple-element.22), channel_id=1, source_target_pairs={{0,16},{8,24},{16,0},{24,8},{1,17},{9,25},{17,1},{25,9},{2,18},{10... | collective-permute-start | bytes 1179656 | tf_op jit(solution)/shard_map/ppermute | solution.py:291
  14.6 1.4 %collective-permute-start.3 = (bf16[192,512]{1,0:T(8,128)(2,1)S(1)}, bf16[192,512]{1,0:T(8,128)(2,1)S(1)}, u32[]{:S(2)}, u32[]{:S(2)}) collective-permute-start(bf16[192,512]{1,0:T(8,128)(2,1)S(1)} %get-tuple-element.20), channel_id=1, source_target_pairs={{0,8},{8,0},{16,24},{24,16},{1,9},{9,1},{17,25},{25,17},{2,10},{10... | collective-permute-start | bytes 589832 | tf_op jit(solution)/shard_map/ppermute | solution.py:297
  20.1 8.4 %copy-start.7 = (bf16[96,3584]{1,0:T(8,128)(2,1)}, bf16[96,3584]{1,0:T(8,128)(2,1)S(1)}, u32[]{:S(2)}) copy-start(bf16[96,3584]{1,0:T(8,128)(2,1)S(1)} %collective-permute-done.4.rest_4_) | copy-start | bytes 2064388
  20.1 0.9 %copy-start.9 = (bf16[96,3584]{1,0:T(8,128)(2,1)}, bf16[96,3584]{1,0:T(8,128)(2,1)S(1)}, u32[]{:S(2)}) copy-start(bf16[96,3584]{1,0:T(8,128)(2,1)S(1)} %collective-permute-done.rest_1_) | copy-start | bytes 2064388
  21.7 22.7 %collective-permute-start.9 = (bf16[96,3584]{1,0:T(8,128)(2,1)S(1)}, bf16[96,3584]{1,0:T(8,128)(2,1)}, u32[]{:S(2)}, u32[]{:S(2)}) collective-permute-start(bf16[96,3584]{1,0:T(8,128)(2,1)S(1)} %collective-permute-done.2.rest_1_.rest_2_), channel_id=1, source_target_pairs={{0,16},{8,24},{16,0},{24,8},{1,17},{9,25},{17,1},{25,9},{2,18},{10... | collective-permute-start | bytes 2064392 | tf_op jit(solution)/shard_map/ppermute | solution.py:291
  23.1 21.4 %collective-permute-start.1 = (bf16[96,3584]{1,0:T(8,128)(2,1)}, bf16[96,3584]{1,0:T(8,128)(2,1)}, u32[]{:S(2)}, u32[]{:S(2)}) collective-permute-start(bf16[96,3584]{1,0:T(8,128)(2,1)} %get-tuple-element.19), channel_id=1, source_target_pairs={{0,4},{4,0},{1,5},{5,1},{2,6},{6,2},{3,7},{7,3},{8,12},{12,8},{9,1... | collective-permute-start | bytes 2064392 | tf_op jit(solution)/shard_map/ppermute | solution.py:291
  28.5 1.7 %collective-permute-start.6 = (bf16[384,512]{1,0:T(8,128)(2,1)S(1)}, bf16[384,512]{1,0:T(8,128)(2,1)S(1)}, u32[]{:S(2)}, u32[]{:S(2)}) collective-permute-start(bf16[384,512]{1,0:T(8,128)(2,1)S(1)} %collective-permute-done.5.rest_2_), channel_id=1, source_target_pairs={{0,8},{8,0},{16,24},{24,16},{1,9},{9,1},{17,25},{25,17},{2,10},{10... | collective-permute-start | bytes 1179656 | tf_op jit(solution)/shard_map/ppermute | solution.py:297
  38.5 36.5 %all-to-all-start = ((bf16[4,48,2048]{2,1,0:T(8,128)(2,1)}), bf16[4,48,2048]{2,1,0:T(8,128)(2,1)S(1)}, u32[]{:S(2)}, u32[]{:S(2)}) async-start(bf16[4,48,2048]{2,1,0:T(8,128)(2,1)} %bitcast.3), calls=%async_computation | async-start | bytes 1572864 | tf_op jit(solution)/shard_map/all_to_all | solution.py:377
  43.9 3.1 %collective-permute-start.7 = (bf16[96,3584]{1,0:T(8,128)(2,1)S(1)}, bf16[96,3584]{1,0:T(8,128)(2,1)S(1)}, u32[]{:S(2)}, u32[]{:S(2)}) collective-permute-start(bf16[96,3584]{1,0:T(8,128)(2,1)S(1)} %collective-permute-done.2.rest_1_.rest_2_), channel_id=1, source_target_pairs={{0,8},{8,0},{16,24},{24,16},{1,9},{9,1},{17,25},{25,17},{2,10},{10... | collective-permute-start | bytes 2064392 | tf_op jit(solution)/shard_map/ppermute | solution.py:297
  43.9 3.3 %collective-permute-start.8 = (bf16[96,3584]{1,0:T(8,128)(2,1)}, bf16[96,3584]{1,0:T(8,128)(2,1)S(1)}, u32[]{:S(2)}, u32[]{:S(2)}) collective-permute-start(bf16[96,3584]{1,0:T(8,128)(2,1)} %copy-done.7), channel_id=1, source_target_pairs={{0,8},{8,0},{16,24},{24,16},{1,9},{9,1},{17,25},{25,17},{2,10},{10... | collective-permute-start | bytes 2064392 | tf_op jit(solution)/shard_map/ppermute | solution.py:297
  44.4 3.8 %collective-permute-start.10 = (bf16[96,3584]{1,0:T(8,128)(2,1)}, bf16[96,3584]{1,0:T(8,128)(2,1)S(1)}, u32[]{:S(2)}, u32[]{:S(2)}) collective-permute-start(bf16[96,3584]{1,0:T(8,128)(2,1)} %collective-permute-done.9.rest_6_), channel_id=1, source_target_pairs={{0,8},{8,0},{16,24},{24,16},{1,9},{9,1},{17,25},{25,17},{2,10},{10... | collective-permute-start | bytes 2064392 | tf_op jit(solution)/shard_map/ppermute | solution.py:297
  48.2 3.1 %copy-start.1 = (f32[512,3584]{1,0:T(8,128)S(1)}, f32[512,3584]{1,0:T(8,128)}, u32[]{:S(2)}) copy-start(f32[512,3584]{1,0:T(8,128)} %rest_10_.1) | copy-start | bytes 22020100
  51.3 3.1 %copy-start.2 = (f32[512,3584]{1,0:T(8,128)S(1)}, f32[512,3584]{1,0:T(8,128)}, u32[]{:S(2)}) copy-start(f32[512,3584]{1,0:T(8,128)} %rest_11_.1) | copy-start | bytes 22020100
  54.4 2.0 %copy-start.3 = (bf16[512,3584]{1,0:T(8,128)(2,1)S(1)}, bf16[512,3584]{1,0:T(8,128)(2,1)}, u32[]{:S(2)}) copy-start(bf16[512,3584]{1,0:T(8,128)(2,1)} %rest_9_.1) | copy-start | bytes 11010052
  56.4 1.1 %copy-start.8 = (bf16[96,3584]{1,0:T(8,128)(2,1)S(1)}, bf16[96,3584]{1,0:T(8,128)(2,1)}, u32[]{:S(2)}) copy-start(bf16[96,3584]{1,0:T(8,128)(2,1)} %copy-done.7) | copy-start | bytes 2064388
  57.5 1.1 %copy-start.10 = (bf16[96,3584]{1,0:T(8,128)(2,1)S(1)}, bf16[96,3584]{1,0:T(8,128)(2,1)}, u32[]{:S(2)}) copy-start(bf16[96,3584]{1,0:T(8,128)(2,1)} %copy-done.9) | copy-start | bytes 2064388

commit v10 on v9

--- a/solution.py
+++ b/solution.py
@@ -207,68 +207,89 @@
     return current - (scale * first) * invert(spread), first, second
 
 
-def update_kernel(origins, tokens_all, chunk, place, x_ref, *rest):
+def hold_kernel(place, *refs):
+    n = (len(refs) - 1) // 2
+    sems = refs[-1]
+    copies = []
+    for k, (source, target) in enumerate(zip(refs[:n], refs[n:-1])):
+        rows = target.shape[0]
+        start = pl.multiple_of(place[0] * rows, rows) if source.shape[0] > rows else 0
+        copies.append(
+            pltpu.make_async_copy(source.at[pl.ds(start, rows), :], target, sems.at[k])
+        )
+    for copy in copies:
+        copy.start()
+    for copy in copies:
+        copy.wait()
+
+
+def hold_call(place, arrays, rows):
+    n = len(arrays)
+    return run(
+        hold_kernel,
+        "hold",
+        (1,),
+        [pl.BlockSpec(memory_space=pltpu.HBM)] * n,
+        [pl.BlockSpec(memory_space=pl.ANY)] * n,
+        [pltpu.VMEM((rows, a.shape[1]), a.dtype) for a in arrays],
+        [pltpu.SemaphoreType.DMA((n,))],
+        4,
+        (place, *map(in_hbm, arrays)),
+    )
+
+
+def update_kernel(origins, tokens_all, chunk, part, place, x_ref, *rest):
     n = len(origins)
     pieces = rest[:n]
-    w_ref, a_ref, m_ref, v_ref = rest[n : n + 4]
-    new_w, new_m, new_v, cs, acc = rest[-5:]
-    own = pieces[0].shape[0]
-    for piece, origin in zip(pieces, origins):
-        cs[pl.ds(pl.multiple_of(origin(place[0], place[1]) * own, own), own), :] = piece[...]
-    acc[...] = jnp.dot(x_ref[...], cs[...], preferred_element_type=F32)
-
-    @pl.loop(0, acc.shape[0] // chunk, unroll=4)
-    def _(i):
-        at = pl.ds(pl.multiple_of(i * chunk, chunk), chunk)
-        weight, first, second = updated(
-            acc[at, :],
-            tokens_all,
-            w_ref[at, :].astype(F32),
-            a_ref[at, :].astype(F32),
-            m_ref[at, :],
-            v_ref[at, :],
-            inverse,
-        )
-        new_w[at, :] = weight.astype(BF16)
-        new_m[at, :] = first
-        new_v[at, :] = second
-
-
-def update_call(place, features, pieces, origins, start, stop, held, made):
-    weight, anchor, first, second = held
-    rows, width = first.shape
+    w_ref, a_ref, m_ref, v_ref, new_w, new_m, new_v, cs = rest[n:]
+    own, width = pieces[0].shape
+
+    @pl.when(pl.program_id(0) == 0)
+    def _():
+        for piece, origin in zip(pieces, origins):
+            start = pl.multiple_of(origin(place[0], place[1]) * own, own)
+            cs[pl.ds(start, own), :] = piece[...]
+
+    for c in range(0, width, part):
+        across = slice(c, c + part)
+        summed = jnp.dot(x_ref[...], cs[:, across], preferred_element_type=F32)
+        for r in range(0, x_ref.shape[0], chunk):
+            at = (slice(r, r + chunk), across)
+            weight, first, second = updated(
+                summed[r : r + chunk],
+                tokens_all,
+                w_ref[at].astype(F32),
+                a_ref[at].astype(F32),
+                m_ref[at],
+                v_ref[at],
+                inverse,
+            )
+            new_w[at] = weight.astype(BF16)
+            new_m[at] = first
+            new_v[at] = second
+
+
+def update_call(place, features, pieces, origins, held):
+    rows, width = held[1].shape
     tokens_all = features.shape[1]
-    block = block_of(math.gcd(start, stop), 512)
-    own = pieces[0].shape[0]
-    base = start // block
-
-    def from_base(rows):
-        return pl.BlockSpec((rows, block), lambda j, place: (0, j + base))
-
-    tile = from_base(rows)
-    return pl.pallas_call(
-        functools.partial(update_kernel, origins, tokens_all, math.gcd(rows, 32)),
-        name="update",
-        grid_spec=pltpu.PrefetchScalarGridSpec(
-            num_scalar_prefetch=1,
-            grid=((stop - start) // block,),
-            in_specs=[fixed((rows, tokens_all))]
-            + [from_base(own) if p.shape[1] == width else columns(own, block) for p in pieces]
-            + [pl.BlockSpec((rows, block), lambda j, place: (place[0], j + base))]
-            + [tile] * 3
-            + [pl.BlockSpec(memory_space=pltpu.HBM)] * len(made),
-            out_specs=[tile] * 3,
-            scratch_shapes=[pltpu.VMEM((tokens_all, block), BF16), pltpu.VMEM((rows, block), F32)],
+    block = math.gcd(rows, 128)
+    tile = pl.BlockSpec((block, width), lambda j, place: (j, 0))
+    return run(
+        functools.partial(
+            update_kernel, origins, tokens_all, math.gcd(block, 32), block_of(width, 512)
         ),
-        out_shape=[
-            struct((rows, width), BF16),
-            struct((rows, width), F32),
-            struct((rows, width), F32),
-        ],
-        input_output_aliases={6 + len(pieces) + k: k for k in range(len(made))},
-        compiler_params=pltpu.CompilerParams(vmem_limit_bytes=18 * MIB),
-        cost_estimate=pl.CostEstimate(flops=1, bytes_accessed=1, transcendentals=0),
-    )(place, features, *pieces, in_hbm(held[0]), *map(in_vmem, held[1:]), *made)
+        "update",
+        (rows // block,),
+        [pl.BlockSpec((block, tokens_all), lambda j, place: (j, 0))]
+        + [fixed(piece.shape) for piece in pieces]
+        + [pl.BlockSpec((block, width), lambda j, place: (place[0] * (rows // block) + j, 0))]
+        + [tile] * 3,
+        [tile] * 3,
+        [struct((rows, width), BF16), struct((rows, width), F32), struct((rows, width), F32)],
+        [pltpu.VMEM((tokens_all, width), BF16)],
+        22,
+        (place, features, *pieces, *held),
+    )
 
 
 def after(value, *others):
@@ -340,7 +361,11 @@
     ]
     near = [swap_cores(to_send.pop(0))] if cores == 2 else []
     first = [by_chip[c, 0] for c in range(1, chips)]
-    far = [chip_shift(c)(to_send[c - 1]) for c in range(1, chips)]
+    kept = []
+    if tiled:
+        arrays = (after(first_moment, parts[0]), second_moment)
+        kept = hold_call(place, arrays, slice_rows)
+    far = [chip_shift(c)(after(to_send[c - 1], *kept)) for c in range(1, chips)]
     for s in range(1, n_row):
         by_row[s] = after(by_row[s], parts[0], *near, *first, *swapped.values())
         if cores == 2:
@@ -375,16 +400,9 @@
             gathered, weight, (((1,), (1,)), ((), ())), preferred_element_type=F32
         ).astype(BF16)
     gparts = lax.all_to_all(gpart, "col", 0, 0, tiled=True)
-    width = cotangent.shape[1]
-    cuts = [(0, width)]
-    relayed = [{} for _ in cuts]
-    for k, (start, stop) in enumerate(cuts):
-        for s in range(1, n_row):
-            for c in range(1, chips):
-                piece = lax.slice_in_dim(by_row[s], start, stop, axis=1)
-                if k:
-                    piece = after(piece, *sums)
-                relayed[k][c, s] = chip_shift(c)(piece)
+    for s in range(1, n_row):
+        for c in range(1, chips):
+            by_chip[c, s] = chip_shift(c)(by_row[s])
     outputs = parts[0].astype(F32)
     for part in sums:
         outputs = outputs + part.astype(F32)
@@ -401,28 +419,21 @@
 
                 origins.append(origin)
 
-    def pieces_of(k, *before):
-        pieces = []
-        for c in range(chips):
-            for s in range(n_row):
-                piece = by_chip[c, s] if (c, s) in by_chip else relayed[k][c, s]
-                pieces.append(piece)
-                if cores == 2:
-                    if (c, s) in by_chip and (c, s) not in swapped:
-                        swapped[c, s] = swap_cores(piece)
-                    pieces.append(
-                        swapped[c, s] if (c, s) in swapped else swap_cores(after(piece, *before))
-                    )
-        return pieces
-
-    if tiled:
-        held = (weight, anchor, first_moment, second_moment)
-        made = []
-        for k, (start, stop) in enumerate(cuts):
-            made = update_call(place, features, pieces_of(k, *made[:1]), origins, start, stop, held, made)
-        new_weight, new_first, new_second = made
+    pieces = []
+    for c in range(chips):
+        for s in range(n_row):
+            pieces.append(by_chip[c, s])
+            if cores == 2:
+                if (c, s) not in swapped:
+                    swapped[c, s] = swap_cores(by_chip[c, s])
+                pieces.append(swapped[c, s])
+
+    if tiled:
+        new_weight, new_first, new_second = update_call(
+            place, features, pieces, origins, (in_hbm(weight), in_hbm(anchor), *kept)
+        )
     else:
-        gathered = in_order(pieces_of(0), [origin(dp, row) for origin in origins], own)
+        gathered = in_order(pieces, [origin(dp, row) for origin in origins], own)
         summed = lax.dot_general(
             features, gathered, (((0,), (0,)), ((), ())), preferred_element_type=F32
         )

time: 76.7 us -> 79.4 us (1.035)
  Pallas kernels: 33.4 us -> 36.5 us
  local copies, waits for them, and re-layouts: 12.4 us -> 15.4 us
  waiting for transfers between devices: 13.4 us -> 11.3 us
  starting transfers between devices: 14 us -> 12.6 us
    pallas_call x4 -> x6, Pallas kernels: 17.1 us -> 36.5 us  [run(): pl.pallas_call(kernel, name=name, grid_spec=pltpu.PrefetchScalarGridSpec(...]
    pallas_call x1 -> x0, Pallas kernels: 16.3 us -> none  [update_call(): pl.pallas_call(functools.partial(update_kernel, origins, tokens_all, math...]
    unnamed x22 -> x32, local copies, waits for them, and re-layouts: 12.4 us -> 15.4 us
    ppermute x5, starting transfers between devices: 8.01 us -> 6.69 us  [along(): lax.ppermute(a, axis, [(i, (i + shift) % n) for i in range(n)])]
    ppermute x6, waiting for transfers between devices: 4.65 us -> 3.33 us  [swap_cores(): return lax.ppermute(a, 'dp', [(i, i ^ 1) for i in range(n_dp)])]
  transfers between devices with their start and end apart: 12 -> 12, of which waited for: 8 -> 5; matrix products, arithmetic and copies ran while one was open for 3% -> 3% of each run, Pallas kernels for 42% -> 45%
where the time goes in v10:
time: 79.4 us; the launch traced here: 78.9 us
  Pallas kernels  36.5 us (46%)
  local copies, waits for them, and re-layouts  15.4 us (19%)
  starting transfers between devices  12.6 us (16%)
  waiting for transfers between devices  11.3 us (14%)
  other arithmetic  2.39 us (3%)
    pallas_call x6, Pallas kernels, run(): pl.pallas_call(kernel, name=name, grid_spec=pltpu.PrefetchScalarGridSpec(...  36.5 us
    unnamed x32, local copies, waits for them, and re-layouts  15.4 us
    ppermute x5, waiting for transfers between devices, along(): lax.ppermute(a, axis, [(i, (i + shift) % n) for i in range(n)])  7.95 us
    ppermute x5, starting transfers between devices, along(): lax.ppermute(a, axis, [(i, (i + shift) % n) for i in range(n)])  6.69 us
    all_to_all x1, starting transfers between devices, per_device(): gparts = lax.all_to_all(gpart, 'col', 0, 0, tiled=True)  4.85 us
    ppermute x6, waiting for transfers between devices, swap_cores(): return lax.ppermute(a, 'dp', [(i, i ^ 1) for i in range(n_dp)])  3.33 us
    convert_element_type x1, other arithmetic, per_device(): outputs = outputs.astype(BF16)  2.31 us
  transfers between devices with their start and end apart: 12, of which 5 were waited for; matrix products, arithmetic and copies ran while one was open for 3% of the time, Pallas kernels for 45%

profile of v10, /device:TPU:0, one launch (start us, length us, event | category | flops | bytes accessed | tf_op | source)
XLA Modules:
  0.0 78.9 jit_solution(7785569478097153142)
XLA Ops:
  0.6 0.5 collective-permute-start
  1.1 2.6 %collective-permute-start.4 = (bf16[96,3584]{1,0:T(8,128)(2,1)}, bf16[96,3584]{1,0:T(8,128)(2,1)S(1)}, u32[]{:S(2)}, u32[]{:S(2)}) collective-permute-start(bf16[96,3584]{1,0:T(8,128)(2,1)} %rest_0_.5), channel_id=1, source_target_pairs={{0,16},{8,24},{16,0},{24,8},{1,17},{9,25},{17,1},{25,9},{2,18},{10... | collective-permute-start | bytes 2064392 | tf_op jit(solution)/shard_map/ppermute | solution.py:312
  3.7 1.5 %collective-permute-start.2 = (bf16[96,3584]{1,0:T(8,128)(2,1)}, bf16[96,3584]{1,0:T(8,128)(2,1)S(1)}, u32[]{:S(2)}, u32[]{:S(2)}) collective-permute-start(bf16[96,3584]{1,0:T(8,128)(2,1)} %rest_0_.5), channel_id=1, source_target_pairs={{0,4},{4,0},{1,5},{5,1},{2,6},{6,2},{3,7},{7,3},{8,12},{12,8},{9,1... | collective-permute-start | bytes 2064392 | tf_op jit(solution)/shard_map/ppermute | solution.py:312
  5.2 0.1 pad_add_fusion.place
  5.3 0.0 copy-start.4
  5.3 1.1 %copy-done.4 = bf16[192,2048]{1,0:T(8,128)(2,1)S(1)} copy-done((bf16[192,2048]{1,0:T(8,128)(2,1)S(1)}, bf16[192,2048]{1,0:T(8,128)(2,1)}, u32[]{:S(2)}) %copy-start.4) | copy-done | bytes 786456
  6.4 0.0 slice-start
  6.4 0.0 slice-start.1
  6.5 7.6 %forward.1 = (bf16[96,3584]{1,0:T(8,128)(2,1)S(1)}, bf16[96,3584]{1,0:T(8,128)(2,1)}, bf16[192,512]{1,0:T(8,128)(2,1)S(1)}, bf16[384,512]{1,0:T(8,128)(2,1)S(1)}) custom-call(s32[3]{0:T(128)S(1)} %pad_add_fusion.place, bf16[192,2048]{1,0:T(8,128)(2,1)S(1)} %copy-done.4, bf16[2048,3584]{1,0:T(8,128)(2,1)} %rest_8_.1), custom_call_target="tpu_custom_call" | custom-call | flops 1 | bytes 1 | tf_op jit(solution)/shard_map/forward/pallas_call | solution.py:31
  14.1 0.0 copy-start.7
  14.1 0.8 %copy-done.7 = bf16[96,3584]{1,0:T(8,128)(2,1)} copy-done((bf16[96,3584]{1,0:T(8,128)(2,1)}, bf16[96,3584]{1,0:T(8,128)(2,1)S(1)}, u32[]{:S(2)}) %copy-start.7) | copy-done | bytes 688152
  14.9 0.0 copy-start.5
  14.9 0.0 slice-start.2
  14.9 0.0 slice-start.3
  15.0 0.0 copy-start.6
  15.0 6.0 %hold.1 = (f32[512,3584]{1,0:T(8,128)S(1)}, f32[512,3584]{1,0:T(8,128)S(1)}) custom-call(s32[3]{0:T(128)S(1)} %pad_add_fusion.place, f32[512,3584]{1,0:T(8,128)} %refs_0_, f32[512,3584]{1,0:T(8,128)} %refs_1_.1), custom_call_target="tpu_custom_call" | custom-call | flops 1 | bytes 1 | tf_op jit(solution)/shard_map/hold/pallas_call | solution.py:31
  21.0 0.0 copy-start
  21.0 3.7 %copy-done = f32[512,3584]{1,0:T(8,128)} copy-done((f32[512,3584]{1,0:T(8,128)}, f32[512,3584]{1,0:T(8,128)S(1)}, u32[]{:S(2)}) %copy-start) | copy-done | bytes 7340056
  24.7 0.0 copy-start.2
  24.7 0.5 collective-permute-start.5
  25.2 0.0 collective-permute-start.3
  25.2 0.0 collective-permute-done.rest_1_
  25.2 0.0 copy-start.8
  25.2 1.3 %copy-done.8 = bf16[96,3584]{1,0:T(8,128)(2,1)} copy-done((bf16[96,3584]{1,0:T(8,128)(2,1)}, bf16[96,3584]{1,0:T(8,128)(2,1)S(1)}, u32[]{:S(2)}) %copy-start.8) | copy-done | bytes 688152
  26.5 0.1 collective-permute-done.3.rest_1_
  26.6 0.0 collective-permute-done.4.rest_4_
  26.6 0.0 copy-start.10
  26.6 0.0 collective-permute-done.2.rest_1_.rest_2_
  26.6 1.6 %collective-permute-start.9 = (bf16[96,3584]{1,0:T(8,128)(2,1)S(1)}, bf16[96,3584]{1,0:T(8,128)(2,1)}, u32[]{:S(2)}, u32[]{:S(2)}) collective-permute-start(bf16[96,3584]{1,0:T(8,128)(2,1)S(1)} %collective-permute-done.2.rest_1_.rest_2_), channel_id=1, source_target_pairs={{0,16},{8,24},{16,0},{24,8},{1,17},{9,25},{17,1},{25,9},{2,18},{10... | collective-permute-start | bytes 2064392 | tf_op jit(solution)/shard_map/ppermute | solution.py:312
  28.3 0.4 collective-permute-start.1
  28.7 7.9 %collective-permute-done.5.rest_2_ = bf16[384,512]{1,0:T(8,128)(2,1)S(1)} collective-permute-done((bf16[384,512]{1,0:T(8,128)(2,1)S(1)}, bf16[384,512]{1,0:T(8,128)(2,1)S(1)}, u32[]{:S(2)}, u32[]{:S(2)}) %collective-permute-start.5) | collective-permute-done | bytes 393248 | tf_op jit(solution)/shard_map/ppermute | solution.py:312
  36.7 0.0 collective-permute-start.6
  36.7 0.0 copy-done.10
  36.7 1.7 %collective-permute-done.6.rest_3_ = bf16[384,512]{1,0:T(8,128)(2,1)S(1)} collective-permute-done((bf16[384,512]{1,0:T(8,128)(2,1)S(1)}, bf16[384,512]{1,0:T(8,128)(2,1)S(1)}, u32[]{:S(2)}, u32[]{:S(2)}) %collective-permute-start.6) | collective-permute-done | bytes 393248 | tf_op jit(solution)/shard_map/ppermute | solution.py:318
  38.4 0.0 copy-done.5
  38.4 0.9 %features.1.x_ref = bf16[512,768]{1,0:T(8,128)(2,1)S(1)} custom-call(s32[3]{0:T(128)S(1)} %pad_add_fusion.place, bf16[192,2048]{1,0:T(8,128)(2,1)S(1)} %copy-done.5, bf16[192,512]{1,0:T(8,128)(2,1)S(1)} %collective-permute-done.3.rest_1_, bf16[384,512]{1,0:T(8,128)(2,1)S(1)} %collective-permute-done.5.rest_2_, ...), custom_call_target="tpu_custom_call" | custom-call | flops 1 | bytes 1 | tf_op jit(solution)/shard_map/features/pallas_call | solution.py:31
  39.2 0.0 slice-done
  39.3 0.0 slice-done.1
  39.3 0.0 slice-done.2
  39.3 0.0 slice-done.3
  39.3 0.0 copy-done.6
  39.3 7.3 %input_grad.1 = bf16[192,2048]{1,0:T(8,128)(2,1)} custom-call(s32[3]{0:T(128)S(1)} %pad_add_fusion.place, bf16[96,3584]{1,0:T(8,128)(2,1)S(1)} %copy-done.6, bf16[96,3584]{1,0:T(8,128)(2,1)S(1)} %collective-permute-done.2.rest_1_.rest_2_, bf16[2048,3584]{1,0:T(8,128)(2,1)S(1)} %bitcast.6), custom_call_target="tpu_custom_call" | custom-call | flops 1 | bytes 1 | tf_op jit(solution)/shard_map/input_grad/pallas_call | solution.py:31
  46.6 0.0 copy-done.2
  46.6 4.9 %all-to-all-start = ((bf16[4,48,2048]{2,1,0:T(8,128)(2,1)}), bf16[4,48,2048]{2,1,0:T(8,128)(2,1)S(1)}, u32[]{:S(2)}, u32[]{:S(2)}) async-start(bf16[4,48,2048]{2,1,0:T(8,128)(2,1)} %bitcast.3), calls=%async_computation | async-start | bytes 1572864 | tf_op jit(solution)/shard_map/all_to_all | solution.py:402
  51.5 0.0 collective-permute-start.7
  51.5 0.5 collective-permute-start.8
  52.0 0.0 collective-permute-done.9.rest_6_
  52.0 0.0 collective-permute-start.10
  52.0 0.0 collective-permute-done.1
  52.0 2.3 %add_convert_fusion = bf16[96,3584]{1,0:T(8,128)(2,1)} fusion(bf16[96,3584]{1,0:T(8,128)(2,1)} %collective-permute-done.1, bf16[96,3584]{1,0:T(8,128)(2,1)} %copy-done.7), kind=kLoop, calls=%fused_computation | loop fusion | flops 1376256 | bytes 2064384 | tf_op jit(solution)/shard_map/convert_element_type | solution.py:409
  54.3 0.5 collective-permute-done.8.rest_5_
  54.8 0.0 collective-permute-done.7.rest_3_
  54.8 1.0 %collective-permute-done.10.rest_7_ = bf16[96,3584]{1,0:T(8,128)(2,1)S(1)} collective-permute-done((bf16[96,3584]{1,0:T(8,128)(2,1)}, bf16[96,3584]{1,0:T(8,128)(2,1)S(1)}, u32[]{:S(2)}, u32[]{:S(2)}) %collective-permute-start.10) | collective-permute-done | bytes 688160 | tf_op jit(solution)/shard_map/ppermute | solution.py:318
  55.8 0.0 copy-start.1
  55.8 3.1 %copy-done.1 = f32[512,3584]{1,0:T(8,128)S(1)} copy-done((f32[512,3584]{1,0:T(8,128)S(1)}, f32[512,3584]{1,0:T(8,128)}, u32[]{:S(2)}) %copy-start.1) | copy-done | bytes 7340056
  58.9 0.0 copy-start.3
  58.9 3.1 %copy-done.3 = f32[512,3584]{1,0:T(8,128)S(1)} copy-done((f32[512,3584]{1,0:T(8,128)S(1)}, f32[512,3584]{1,0:T(8,128)}, u32[]{:S(2)}) %copy-start.3) | copy-done | bytes 7340056
  62.0 0.0 copy-start.9
  62.0 1.1 %copy-done.9 = bf16[96,3584]{1,0:T(8,128)(2,1)S(1)} copy-done((bf16[96,3584]{1,0:T(8,128)(2,1)S(1)}, bf16[96,3584]{1,0:T(8,128)(2,1)}, u32[]{:S(2)}) %copy-start.9) | copy-done | bytes 688152
  63.1 0.0 copy-start.11
  63.1 1.1 %copy-done.11 = bf16[96,3584]{1,0:T(8,128)(2,1)S(1)} copy-done((bf16[96,3584]{1,0:T(8,128)(2,1)S(1)}, bf16[96,3584]{1,0:T(8,128)(2,1)}, u32[]{:S(2)}) %copy-start.11) | copy-done | bytes 688152
  64.2 13.4 %update.1 = (bf16[512,3584]{1,0:T(8,128)(2,1)}, f32[512,3584]{1,0:T(8,128)}, f32[512,3584]{1,0:T(8,128)}) custom-call(s32[3]{0:T(128)S(1)} %pad_add_fusion.place, bf16[512,768]{1,0:T(8,128)(2,1)S(1)} %features.1.x_ref, bf16[96,3584]{1,0:T(8,128)(2,1)S(1)} %copy-done.6, bf16[96,3584]{1,0:T(8,128)(2,1)S(1)} %copy-done.9, ...), custom_call_target="tpu_custom_call" | custom-call | flops 1 | bytes 1 | tf_op jit(solution)/shard_map/update/pallas_call | solution.py:31
  77.5 0.0 all-to-all-done
  77.6 1.3 %total.1 = bf16[48,2048]{1,0:T(8,128)(2,1)} custom-call(s32[3]{0:T(128)S(1)} %pad_add_fusion.place, bf16[192,2048]{1,0:T(8,128)(2,1)S(1)} %bitcast.7), custom_call_target="tpu_custom_call" | custom-call | flops 1 | bytes 1 | tf_op jit(solution)/shard_map/total/pallas_call | solution.py:31
  (1 shorter events, 0.0 us)
Async XLA Ops:
  0.6 24.6 %collective-permute-start = (bf16[96,3584]{1,0:T(8,128)(2,1)}, bf16[96,3584]{1,0:T(8,128)(2,1)S(1)}, u32[]{:S(2)}, u32[]{:S(2)}) collective-permute-start(bf16[96,3584]{1,0:T(8,128)(2,1)} %rest_0_.5), channel_id=1, source_target_pairs={{0,8},{8,0},{16,24},{24,16},{1,9},{9,1},{17,25},{25,17},{2,10},{10... | collective-permute-start | bytes 2064392 | tf_op jit(solution)/shard_map/ppermute | solution.py:318
  1.1 25.5 %collective-permute-start.4 = (bf16[96,3584]{1,0:T(8,128)(2,1)}, bf16[96,3584]{1,0:T(8,128)(2,1)S(1)}, u32[]{:S(2)}, u32[]{:S(2)}) collective-permute-start(bf16[96,3584]{1,0:T(8,128)(2,1)} %rest_0_.5), channel_id=1, source_target_pairs={{0,16},{8,24},{16,0},{24,8},{1,17},{9,25},{17,1},{25,9},{2,18},{10... | collective-permute-start | bytes 2064392 | tf_op jit(solution)/shard_map/ppermute | solution.py:312
  3.7 22.9 %collective-permute-start.2 = (bf16[96,3584]{1,0:T(8,128)(2,1)}, bf16[96,3584]{1,0:T(8,128)(2,1)S(1)}, u32[]{:S(2)}, u32[]{:S(2)}) collective-permute-start(bf16[96,3584]{1,0:T(8,128)(2,1)} %rest_0_.5), channel_id=1, source_target_pairs={{0,4},{4,0},{1,5},{5,1},{2,6},{6,2},{3,7},{7,3},{8,12},{12,8},{9,1... | collective-permute-start | bytes 2064392 | tf_op jit(solution)/shard_map/ppermute | solution.py:312
  5.3 1.1 %copy-start.4 = (bf16[192,2048]{1,0:T(8,128)(2,1)S(1)}, bf16[192,2048]{1,0:T(8,128)(2,1)}, u32[]{:S(2)}) copy-start(bf16[192,2048]{1,0:T(8,128)(2,1)} %rest_0_.3) | copy-start | bytes 2359300
  6.4 32.8 %slice-start = ((s8[14680064]{0:T(1024)(128)(4,1)}), s8[4194304]{0:T(1024)(128)(4,1)S(1)}, s32[]{:S(2)}) async-start(s8[14680064]{0:T(1024)(128)(4,1)} %bitcast.5), calls=%async_computation.1 | async-start | bytes 8388608
  6.4 32.8 %slice-start.1 = ((s8[14680064]{0:T(1024)(128)(4,1)}), s8[2097152]{0:T(1024)(128)(4,1)S(1)}, s32[]{:S(2)}) async-start(s8[14680064]{0:T(1024)(128)(4,1)} %bitcast.5), calls=%async_computation.2 | async-start | bytes 4194304
  14.1 0.8 %copy-start.7 = (bf16[96,3584]{1,0:T(8,128)(2,1)}, bf16[96,3584]{1,0:T(8,128)(2,1)S(1)}, u32[]{:S(2)}) copy-start(bf16[96,3584]{1,0:T(8,128)(2,1)S(1)} %get-tuple-element.21) | copy-start | bytes 2064388
  14.9 23.4 %copy-start.5 = (bf16[192,2048]{1,0:T(8,128)(2,1)S(1)}, bf16[192,2048]{1,0:T(8,128)(2,1)}, u32[]{:S(2)}) copy-start(bf16[192,2048]{1,0:T(8,128)(2,1)} %rest_0_.3) | copy-start | bytes 2359300
  14.9 24.3 %slice-start.2 = ((s8[14680064]{0:T(1024)(128)(4,1)}), s8[4194304]{0:T(1024)(128)(4,1)S(1)}, s32[]{:S(2)}) async-start(s8[14680064]{0:T(1024)(128)(4,1)} %bitcast.5), calls=%async_computation.3 | async-start | bytes 8388608
  14.9 24.3 %slice-start.3 = ((s8[14680064]{0:T(1024)(128)(4,1)}), s8[4194304]{0:T(1024)(128)(4,1)S(1)}, s32[]{:S(2)}) async-start(s8[14680064]{0:T(1024)(128)(4,1)} %bitcast.5), calls=%async_computation.4 | async-start | bytes 8388608
  15.0 24.3 %copy-start.6 = (bf16[96,3584]{1,0:T(8,128)(2,1)S(1)}, bf16[96,3584]{1,0:T(8,128)(2,1)}, u32[]{:S(2)}) copy-start(bf16[96,3584]{1,0:T(8,128)(2,1)} %rest_0_.5) | copy-start | bytes 2064388
  21.0 3.7 %copy-start = (f32[512,3584]{1,0:T(8,128)}, f32[512,3584]{1,0:T(8,128)S(1)}, u32[]{:S(2)}) copy-start(f32[512,3584]{1,0:T(8,128)S(1)} %get-tuple-element.28.rest_10_) | copy-start | bytes 22020100
  24.7 22.0 %copy-start.2 = (f32[512,3584]{1,0:T(8,128)}, f32[512,3584]{1,0:T(8,128)S(1)}, u32[]{:S(2)}) copy-start(f32[512,3584]{1,0:T(8,128)S(1)} %get-tuple-element.29.rest_11_) | copy-start | bytes 22020100
  24.7 12.0 %collective-permute-start.5 = (bf16[384,512]{1,0:T(8,128)(2,1)S(1)}, bf16[384,512]{1,0:T(8,128)(2,1)S(1)}, u32[]{:S(2)}, u32[]{:S(2)}) collective-permute-start(bf16[384,512]{1,0:T(8,128)(2,1)S(1)} %get-tuple-element.30), channel_id=1, source_target_pairs={{0,16},{8,24},{16,0},{24,8},{1,17},{9,25},{17,1},{25,9},{2,18},{10... | collective-permute-start | bytes 1179656 | tf_op jit(solution)/shard_map/ppermute | solution.py:312
  25.2 1.4 %collective-permute-start.3 = (bf16[192,512]{1,0:T(8,128)(2,1)S(1)}, bf16[192,512]{1,0:T(8,128)(2,1)S(1)}, u32[]{:S(2)}, u32[]{:S(2)}) collective-permute-start(bf16[192,512]{1,0:T(8,128)(2,1)S(1)} %get-tuple-element.24), channel_id=1, source_target_pairs={{0,8},{8,0},{16,24},{24,16},{1,9},{9,1},{17,25},{25,17},{2,10},{10... | collective-permute-start | bytes 589832 | tf_op jit(solution)/shard_map/ppermute | solution.py:318
  25.2 1.3 %copy-start.8 = (bf16[96,3584]{1,0:T(8,128)(2,1)}, bf16[96,3584]{1,0:T(8,128)(2,1)S(1)}, u32[]{:S(2)}) copy-start(bf16[96,3584]{1,0:T(8,128)(2,1)S(1)} %collective-permute-done.rest_1_) | copy-start | bytes 2064388
  26.6 10.0 %copy-start.10 = (bf16[96,3584]{1,0:T(8,128)(2,1)}, bf16[96,3584]{1,0:T(8,128)(2,1)S(1)}, u32[]{:S(2)}) copy-start(bf16[96,3584]{1,0:T(8,128)(2,1)S(1)} %collective-permute-done.4.rest_4_) | copy-start | bytes 2064388
  26.6 25.4 %collective-permute-start.9 = (bf16[96,3584]{1,0:T(8,128)(2,1)S(1)}, bf16[96,3584]{1,0:T(8,128)(2,1)}, u32[]{:S(2)}, u32[]{:S(2)}) collective-permute-start(bf16[96,3584]{1,0:T(8,128)(2,1)S(1)} %collective-permute-done.2.rest_1_.rest_2_), channel_id=1, source_target_pairs={{0,16},{8,24},{16,0},{24,8},{1,17},{9,25},{17,1},{25,9},{2,18},{10... | collective-permute-start | bytes 2064392 | tf_op jit(solution)/shard_map/ppermute | solution.py:312
  28.3 23.7 %collective-permute-start.1 = (bf16[96,3584]{1,0:T(8,128)(2,1)}, bf16[96,3584]{1,0:T(8,128)(2,1)}, u32[]{:S(2)}, u32[]{:S(2)}) collective-permute-start(bf16[96,3584]{1,0:T(8,128)(2,1)} %get-tuple-element.23), channel_id=1, source_target_pairs={{0,4},{4,0},{1,5},{5,1},{2,6},{6,2},{3,7},{7,3},{8,12},{12,8},{9,1... | collective-permute-start | bytes 2064392 | tf_op jit(solution)/shard_map/ppermute | solution.py:312
  36.7 1.7 %collective-permute-start.6 = (bf16[384,512]{1,0:T(8,128)(2,1)S(1)}, bf16[384,512]{1,0:T(8,128)(2,1)S(1)}, u32[]{:S(2)}, u32[]{:S(2)}) collective-permute-start(bf16[384,512]{1,0:T(8,128)(2,1)S(1)} %collective-permute-done.5.rest_2_), channel_id=1, source_target_pairs={{0,8},{8,0},{16,24},{24,16},{1,9},{9,1},{17,25},{25,17},{2,10},{10... | collective-permute-start | bytes 1179656 | tf_op jit(solution)/shard_map/ppermute | solution.py:318
  46.6 30.9 %all-to-all-start = ((bf16[4,48,2048]{2,1,0:T(8,128)(2,1)}), bf16[4,48,2048]{2,1,0:T(8,128)(2,1)S(1)}, u32[]{:S(2)}, u32[]{:S(2)}) async-start(bf16[4,48,2048]{2,1,0:T(8,128)(2,1)} %bitcast.3), calls=%async_computation | async-start | bytes 1572864 | tf_op jit(solution)/shard_map/all_to_all | solution.py:402
  51.5 3.3 %collective-permute-start.7 = (bf16[96,3584]{1,0:T(8,128)(2,1)S(1)}, bf16[96,3584]{1,0:T(8,128)(2,1)S(1)}, u32[]{:S(2)}, u32[]{:S(2)}) collective-permute-start(bf16[96,3584]{1,0:T(8,128)(2,1)S(1)} %collective-permute-done.2.rest_1_.rest_2_), channel_id=1, source_target_pairs={{0,8},{8,0},{16,24},{24,16},{1,9},{9,1},{17,25},{25,17},{2,10},{10... | collective-permute-start | bytes 2064392 | tf_op jit(solution)/shard_map/ppermute | solution.py:318
  51.5 3.3 %collective-permute-start.8 = (bf16[96,3584]{1,0:T(8,128)(2,1)}, bf16[96,3584]{1,0:T(8,128)(2,1)S(1)}, u32[]{:S(2)}, u32[]{:S(2)}) collective-permute-start(bf16[96,3584]{1,0:T(8,128)(2,1)} %copy-done.10), channel_id=1, source_target_pairs={{0,8},{8,0},{16,24},{24,16},{1,9},{9,1},{17,25},{25,17},{2,10},{10... | collective-permute-start | bytes 2064392 | tf_op jit(solution)/shard_map/ppermute | solution.py:318
  52.0 3.8 %collective-permute-start.10 = (bf16[96,3584]{1,0:T(8,128)(2,1)}, bf16[96,3584]{1,0:T(8,128)(2,1)S(1)}, u32[]{:S(2)}, u32[]{:S(2)}) collective-permute-start(bf16[96,3584]{1,0:T(8,128)(2,1)} %collective-permute-done.9.rest_6_), channel_id=1, source_target_pairs={{0,8},{8,0},{16,24},{24,16},{1,9},{9,1},{17,25},{25,17},{2,10},{10... | collective-permute-start | bytes 2064392 | tf_op jit(solution)/shard_map/ppermute | solution.py:318
  55.8 3.1 %copy-start.1 = (f32[512,3584]{1,0:T(8,128)S(1)}, f32[512,3584]{1,0:T(8,128)}, u32[]{:S(2)}) copy-start(f32[512,3584]{1,0:T(8,128)} %copy-done) | copy-start | bytes 22020100
  58.9 3.1 %copy-start.3 = (f32[512,3584]{1,0:T(8,128)S(1)}, f32[512,3584]{1,0:T(8,128)}, u32[]{:S(2)}) copy-start(f32[512,3584]{1,0:T(8,128)} %copy-done.2) | copy-start | bytes 22020100
  62.0 1.1 %copy-start.9 = (bf16[96,3584]{1,0:T(8,128)(2,1)S(1)}, bf16[96,3584]{1,0:T(8,128)(2,1)}, u32[]{:S(2)}) copy-start(bf16[96,3584]{1,0:T(8,128)(2,1)} %copy-done.8) | copy-start | bytes 2064388
  63.1 1.1 %copy-start.11 = (bf16[96,3584]{1,0:T(8,128)(2,1)S(1)}, bf16[96,3584]{1,0:T(8,128)(2,1)}, u32[]{:S(2)}) copy-start(bf16[96,3584]{1,0:T(8,128)(2,1)} %copy-done.10) | copy-start | bytes 2064388

commit v11 on v10

--- a/solution.py
+++ b/solution.py
@@ -189,6 +189,28 @@
         [],
         8,
         (place, parts),
+    )
+
+
+def sum_kernel(place, *refs):
+    whole = refs[0][...].astype(F32)
+    for part in refs[1:-1]:
+        whole = whole + part[...].astype(F32)
+    refs[-1][...] = whole.astype(BF16)
+
+
+def sum_call(place, parts):
+    shape = parts[0].shape
+    return run(
+        sum_kernel,
+        "outputs",
+        (1,),
+        [fixed(shape)] * len(parts),
+        fixed(shape),
+        struct(shape, BF16),
+        [],
+        8,
+        (place, *parts),
     )
 
 
@@ -403,10 +425,10 @@
     for s in range(1, n_row):
         for c in range(1, chips):
             by_chip[c, s] = chip_shift(c)(by_row[s])
-    outputs = parts[0].astype(F32)
-    for part in sums:
-        outputs = outputs + part.astype(F32)
-    outputs = outputs.astype(BF16)
+    if tiled:
+        outputs = sum_call(place, [parts[0], *sums])
+    else:
+        outputs = sum(part.astype(F32) for part in [parts[0], *sums]).astype(BF16)
 
     by_chip.update({(0, s): by_row[s] for s in range(n_row)})
     origins = []

time: 79.4 us -> 94.6 us (1.19)
  waiting for transfers between devices: 11.3 us -> 27 us
  other arithmetic: 2.39 us -> 0.08 us
  local copies, waits for them, and re-layouts: 15.4 us -> 17.3 us
    ppermute x5, waiting for transfers between devices: 7.95 us -> 24.6 us  [along(): lax.ppermute(a, axis, [(i, (i + shift) % n) for i in range(n)])]
    convert_element_type x1 -> x0, other arithmetic: 2.31 us -> none  [per_device(): outputs = outputs.astype(BF16)]
    unnamed x32 -> x36, local copies, waits for them, and re-layouts: 15.4 us -> 17.3 us
    pallas_call x6 -> x7, Pallas kernels: 36.5 us -> 37.2 us  [run(): pl.pallas_call(kernel, name=name, grid_spec=pltpu.PrefetchScalarGridSpec(...]
  transfers between devices with their start and end apart: 12 -> 12, of which waited for: 5 -> 5; matrix products, arithmetic and copies ran while one was open for 3% -> 0% of each run, Pallas kernels for 45% -> 38%
where the time goes in v11:
time: 94.6 us; the launch traced here: 94.1 us
  Pallas kernels  37.2 us (39%)
  waiting for transfers between devices  27 us (29%)
  local copies, waits for them, and re-layouts  17.3 us (18%)
  starting transfers between devices  11.7 us (12%)
    pallas_call x7, Pallas kernels, run(): pl.pallas_call(kernel, name=name, grid_spec=pltpu.PrefetchScalarGridSpec(...  37.2 us
    ppermute x5, waiting for transfers between devices, along(): lax.ppermute(a, axis, [(i, (i + shift) % n) for i in range(n)])  24.6 us
    unnamed x36, local copies, waits for them, and re-layouts  17.3 us
    ppermute x5, starting transfers between devices, along(): lax.ppermute(a, axis, [(i, (i + shift) % n) for i in range(n)])  6.1 us
    all_to_all x1, starting transfers between devices, per_device(): gparts = lax.all_to_all(gpart, 'col', 0, 0, tiled=True)  4.87 us
    ppermute x6, waiting for transfers between devices, swap_cores(): return lax.ppermute(a, 'dp', [(i, i ^ 1) for i in range(n_dp)])  2.39 us
  transfers between devices with their start and end apart: 12, of which 5 were waited for; matrix products, arithmetic and copies ran while one was open for 0% of the time, Pallas kernels for 38%

profile of v11, /device:TPU:0, one launch (start us, length us, event | category | flops | bytes accessed | tf_op | source)
XLA Modules:
  0.0 94.1 jit_solution(9507382146440555958)
XLA Ops:
  0.6 3.0 %collective-permute-start.4 = (bf16[96,3584]{1,0:T(8,128)(2,1)}, bf16[96,3584]{1,0:T(8,128)(2,1)S(1)}, u32[]{:S(2)}, u32[]{:S(2)}) collective-permute-start(bf16[96,3584]{1,0:T(8,128)(2,1)} %rest_0_.5), channel_id=1, source_target_pairs={{0,16},{8,24},{16,0},{24,8},{1,17},{9,25},{17,1},{25,9},{2,18},{10... | collective-permute-start | bytes 2064392 | tf_op jit(solution)/shard_map/ppermute | solution.py:334
  3.6 1.5 %collective-permute-start.2 = (bf16[96,3584]{1,0:T(8,128)(2,1)}, bf16[96,3584]{1,0:T(8,128)(2,1)S(1)}, u32[]{:S(2)}, u32[]{:S(2)}) collective-permute-start(bf16[96,3584]{1,0:T(8,128)(2,1)} %rest_0_.5), channel_id=1, source_target_pairs={{0,4},{4,0},{1,5},{5,1},{2,6},{6,2},{3,7},{7,3},{8,12},{12,8},{9,1... | collective-permute-start | bytes 2064392 | tf_op jit(solution)/shard_map/ppermute | solution.py:334
  5.2 0.0 collective-permute-start
  5.2 0.1 pad_add_fusion.place
  5.2 0.0 copy-start.4
  5.2 1.1 %copy-done.4 = bf16[192,2048]{1,0:T(8,128)(2,1)S(1)} copy-done((bf16[192,2048]{1,0:T(8,128)(2,1)S(1)}, bf16[192,2048]{1,0:T(8,128)(2,1)}, u32[]{:S(2)}) %copy-start.4) | copy-done | bytes 786456
  6.4 0.0 slice-start.1
  6.4 6.8 %forward.1 = (bf16[96,3584]{1,0:T(8,128)(2,1)S(1)}, bf16[96,3584]{1,0:T(8,128)(2,1)S(1)}, bf16[192,512]{1,0:T(8,128)(2,1)S(1)}, bf16[384,512]{1,0:T(8,128)(2,1)S(1)}) custom-call(s32[3]{0:T(128)S(1)} %pad_add_fusion.place, bf16[192,2048]{1,0:T(8,128)(2,1)S(1)} %copy-done.4, bf16[2048,3584]{1,0:T(8,128)(2,1)} %rest_8_.1), custom_call_target="tpu_custom_call" | custom-call | flops 1 | bytes 1 | tf_op jit(solution)/shard_map/forward/pallas_call | solution.py:31
  13.2 0.0 copy-start.7
  13.2 0.8 copy-done.7
  14.0 0.0 copy-start.13
  14.0 0.8 copy-done.13
  14.9 0.0 copy-start.5
  14.9 0.0 slice-start.2
  14.9 0.0 slice-start.3
  14.9 0.0 copy-start.6
  14.9 6.0 %hold.1 = (f32[512,3584]{1,0:T(8,128)S(1)}, f32[512,3584]{1,0:T(8,128)S(1)}) custom-call(s32[3]{0:T(128)S(1)} %pad_add_fusion.place, f32[512,3584]{1,0:T(8,128)} %refs_0_, f32[512,3584]{1,0:T(8,128)} %refs_1_.1), custom_call_target="tpu_custom_call" | custom-call | flops 1 | bytes 1 | tf_op jit(solution)/shard_map/hold/pallas_call | solution.py:31
  20.9 0.0 copy-start
  20.9 3.7 %copy-done = f32[512,3584]{1,0:T(8,128)} copy-done((f32[512,3584]{1,0:T(8,128)}, f32[512,3584]{1,0:T(8,128)S(1)}, u32[]{:S(2)}) %copy-start) | copy-done | bytes 7340056
  24.6 0.0 copy-start.2
  24.6 0.5 collective-permute-start.5
  25.1 0.2 collective-permute-start.3
  25.4 1.2 %collective-permute-done.3.rest_1_ = bf16[192,512]{1,0:T(8,128)(2,1)S(1)} collective-permute-done((bf16[192,512]{1,0:T(8,128)(2,1)S(1)}, bf16[192,512]{1,0:T(8,128)(2,1)S(1)}, u32[]{:S(2)}, u32[]{:S(2)}) %collective-permute-start.3) | collective-permute-done | bytes 196640 | tf_op jit(solution)/shard_map/ppermute | solution.py:340
  26.6 0.0 collective-permute-done.4.rest_4_
  26.6 0.0 copy-start.9
  26.6 0.0 collective-permute-done.2.rest_1_.rest_2_
  26.6 0.0 collective-permute-done.rest_1_
  26.6 0.0 copy-start.11
  26.6 1.3 %copy-done.11 = bf16[96,3584]{1,0:T(8,128)(2,1)} copy-done((bf16[96,3584]{1,0:T(8,128)(2,1)}, bf16[96,3584]{1,0:T(8,128)(2,1)S(1)}, u32[]{:S(2)}) %copy-start.11) | copy-done | bytes 688152
  27.9 8.2 %collective-permute-done.5.rest_2_ = bf16[384,512]{1,0:T(8,128)(2,1)S(1)} collective-permute-done((bf16[384,512]{1,0:T(8,128)(2,1)S(1)}, bf16[384,512]{1,0:T(8,128)(2,1)S(1)}, u32[]{:S(2)}, u32[]{:S(2)}) %collective-permute-start.5) | collective-permute-done | bytes 393248 | tf_op jit(solution)/shard_map/ppermute | solution.py:334
  36.1 0.0 collective-permute-start.6
  36.1 0.5 collective-permute-start.9
  36.7 0.0 copy-done.9
  36.7 1.2 %collective-permute-done.6.rest_3_ = bf16[384,512]{1,0:T(8,128)(2,1)S(1)} collective-permute-done((bf16[384,512]{1,0:T(8,128)(2,1)S(1)}, bf16[384,512]{1,0:T(8,128)(2,1)S(1)}, u32[]{:S(2)}, u32[]{:S(2)}) %collective-permute-start.6) | collective-permute-done | bytes 393248 | tf_op jit(solution)/shard_map/ppermute | solution.py:340
  37.8 0.0 copy-done.5
  37.8 0.9 features.1.x_ref
  38.7 0.0 slice-done
  38.7 0.0 slice-done.1
  38.7 0.0 slice-done.2
  38.7 0.0 slice-done.3
  38.7 0.0 copy-done.6
  38.8 7.3 %input_grad.1 = bf16[192,2048]{1,0:T(8,128)(2,1)} custom-call(s32[3]{0:T(128)S(1)} %pad_add_fusion.place, bf16[96,3584]{1,0:T(8,128)(2,1)S(1)} %copy-done.6, bf16[96,3584]{1,0:T(8,128)(2,1)S(1)} %collective-permute-done.2.rest_1_.rest_2_, bf16[2048,3584]{1,0:T(8,128)(2,1)S(1)} %bitcast.6), custom_call_target="tpu_custom_call" | custom-call | flops 1 | bytes 1 | tf_op jit(solution)/shard_map/input_grad/pallas_call | solution.py:31
  46.1 0.0 copy-done.2
  46.1 4.9 %all-to-all-start = ((bf16[4,48,2048]{2,1,0:T(8,128)(2,1)}), bf16[4,48,2048]{2,1,0:T(8,128)(2,1)S(1)}, u32[]{:S(2)}, u32[]{:S(2)}) async-start(bf16[4,48,2048]{2,1,0:T(8,128)(2,1)} %bitcast.3), calls=%async_computation | async-start | bytes 1572864 | tf_op jit(solution)/shard_map/all_to_all | solution.py:424
  50.9 0.5 collective-permute-start.1
  51.4 0.0 collective-permute-start.7
  51.5 0.5 collective-permute-start.8
  52.0 2.1 %collective-permute-done.9.rest_6_ = bf16[96,3584]{1,0:T(8,128)(2,1)} collective-permute-done((bf16[96,3584]{1,0:T(8,128)(2,1)S(1)}, bf16[96,3584]{1,0:T(8,128)(2,1)}, u32[]{:S(2)}, u32[]{:S(2)}) %collective-permute-start.9) | collective-permute-done | bytes 688160 | tf_op jit(solution)/shard_map/ppermute | solution.py:334
  54.1 0.0 collective-permute-start.10
  54.1 14.3 %collective-permute-done.1.refs_1_ = bf16[96,3584]{1,0:T(8,128)(2,1)S(1)} collective-permute-done((bf16[96,3584]{1,0:T(8,128)(2,1)}, bf16[96,3584]{1,0:T(8,128)(2,1)S(1)}, u32[]{:S(2)}, u32[]{:S(2)}) %collective-permute-start.1) | collective-permute-done | bytes 688160 | tf_op jit(solution)/shard_map/ppermute | solution.py:334
  68.4 0.0 copy-start.8
  68.4 1.1 %copy-done.8 = bf16[96,3584]{1,0:T(8,128)(2,1)S(1)} copy-done((bf16[96,3584]{1,0:T(8,128)(2,1)S(1)}, bf16[96,3584]{1,0:T(8,128)(2,1)}, u32[]{:S(2)}) %copy-start.8) | copy-done | bytes 688152
  69.5 1.5 %outputs.1 = bf16[96,3584]{1,0:T(8,128)(2,1)} custom-call(s32[3]{0:T(128)S(1)} %pad_add_fusion.place, bf16[96,3584]{1,0:T(8,128)(2,1)S(1)} %copy-done.8, bf16[96,3584]{1,0:T(8,128)(2,1)S(1)} %collective-permute-done.1.refs_1_), custom_call_target="tpu_custom_call" | custom-call | flops 1 | bytes 1 | tf_op jit(solution)/shard_map/outputs/pallas_call | solution.py:31
  71.0 0.0 collective-permute-done.8.rest_5_
  71.0 0.0 collective-permute-done.7.rest_3_
  71.0 0.0 collective-permute-done.10.rest_7_
  71.0 0.0 copy-start.1
  71.0 3.1 %copy-done.1 = f32[512,3584]{1,0:T(8,128)S(1)} copy-done((f32[512,3584]{1,0:T(8,128)S(1)}, f32[512,3584]{1,0:T(8,128)}, u32[]{:S(2)}) %copy-start.1) | copy-done | bytes 7340056
  74.1 3.1 %copy-done.3 = f32[512,3584]{1,0:T(8,128)S(1)} copy-done((f32[512,3584]{1,0:T(8,128)S(1)}, f32[512,3584]{1,0:T(8,128)}, u32[]{:S(2)}) %copy-start.3) | copy-done | bytes 7340056
  77.2 1.1 %copy-done.10 = bf16[96,3584]{1,0:T(8,128)(2,1)S(1)} copy-done((bf16[96,3584]{1,0:T(8,128)(2,1)S(1)}, bf16[96,3584]{1,0:T(8,128)(2,1)}, u32[]{:S(2)}) %copy-start.10) | copy-done | bytes 688152
  78.3 1.1 %copy-done.12 = bf16[96,3584]{1,0:T(8,128)(2,1)S(1)} copy-done((bf16[96,3584]{1,0:T(8,128)(2,1)S(1)}, bf16[96,3584]{1,0:T(8,128)(2,1)}, u32[]{:S(2)}) %copy-start.12) | copy-done | bytes 688152
  79.4 13.4 %update.1 = (bf16[512,3584]{1,0:T(8,128)(2,1)}, f32[512,3584]{1,0:T(8,128)}, f32[512,3584]{1,0:T(8,128)}) custom-call(s32[3]{0:T(128)S(1)} %pad_add_fusion.place, bf16[512,768]{1,0:T(8,128)(2,1)S(1)} %features.1.x_ref, bf16[96,3584]{1,0:T(8,128)(2,1)S(1)} %copy-done.6, bf16[96,3584]{1,0:T(8,128)(2,1)S(1)} %copy-done.12, ...), custom_call_target="tpu_custom_call" | custom-call | flops 1 | bytes 1 | tf_op jit(solution)/shard_map/update/pallas_call | solution.py:31
  92.7 0.0 all-to-all-done
  92.7 1.3 %total.1 = bf16[48,2048]{1,0:T(8,128)(2,1)} custom-call(s32[3]{0:T(128)S(1)} %pad_add_fusion.place, bf16[192,2048]{1,0:T(8,128)(2,1)S(1)} %bitcast.7), custom_call_target="tpu_custom_call" | custom-call | flops 1 | bytes 1 | tf_op jit(solution)/shard_map/total/pallas_call | solution.py:31
  (5 shorter events, 0.0 us)
Async XLA Ops:
  0.6 25.9 %collective-permute-start.4 = (bf16[96,3584]{1,0:T(8,128)(2,1)}, bf16[96,3584]{1,0:T(8,128)(2,1)S(1)}, u32[]{:S(2)}, u32[]{:S(2)}) collective-permute-start(bf16[96,3584]{1,0:T(8,128)(2,1)} %rest_0_.5), channel_id=1, source_target_pairs={{0,16},{8,24},{16,0},{24,8},{1,17},{9,25},{17,1},{25,9},{2,18},{10... | collective-permute-start | bytes 2064392 | tf_op jit(solution)/shard_map/ppermute | solution.py:334
  3.6 22.9 %collective-permute-start.2 = (bf16[96,3584]{1,0:T(8,128)(2,1)}, bf16[96,3584]{1,0:T(8,128)(2,1)S(1)}, u32[]{:S(2)}, u32[]{:S(2)}) collective-permute-start(bf16[96,3584]{1,0:T(8,128)(2,1)} %rest_0_.5), channel_id=1, source_target_pairs={{0,4},{4,0},{1,5},{5,1},{2,6},{6,2},{3,7},{7,3},{8,12},{12,8},{9,1... | collective-permute-start | bytes 2064392 | tf_op jit(solution)/shard_map/ppermute | solution.py:334
  5.2 21.4 %collective-permute-start = (bf16[96,3584]{1,0:T(8,128)(2,1)}, bf16[96,3584]{1,0:T(8,128)(2,1)S(1)}, u32[]{:S(2)}, u32[]{:S(2)}) collective-permute-start(bf16[96,3584]{1,0:T(8,128)(2,1)} %rest_0_.5), channel_id=1, source_target_pairs={{0,8},{8,0},{16,24},{24,16},{1,9},{9,1},{17,25},{25,17},{2,10},{10... | collective-permute-start | bytes 2064392 | tf_op jit(solution)/shard_map/ppermute | solution.py:340
  5.2 1.1 %copy-start.4 = (bf16[192,2048]{1,0:T(8,128)(2,1)S(1)}, bf16[192,2048]{1,0:T(8,128)(2,1)}, u32[]{:S(2)}) copy-start(bf16[192,2048]{1,0:T(8,128)(2,1)} %rest_0_.3) | copy-start | bytes 2359300
  6.4 32.3 %slice-start = ((s8[14680064]{0:T(1024)(128)(4,1)}), s8[4194304]{0:T(1024)(128)(4,1)S(1)}, s32[]{:S(2)}) async-start(s8[14680064]{0:T(1024)(128)(4,1)} %bitcast.5), calls=%async_computation.1 | async-start | bytes 8388608
  6.4 32.3 %slice-start.1 = ((s8[14680064]{0:T(1024)(128)(4,1)}), s8[2097152]{0:T(1024)(128)(4,1)S(1)}, s32[]{:S(2)}) async-start(s8[14680064]{0:T(1024)(128)(4,1)} %bitcast.5), calls=%async_computation.2 | async-start | bytes 4194304
  13.2 0.8 copy-start.7
  14.0 0.8 copy-start.13
  14.9 23.0 %copy-start.5 = (bf16[192,2048]{1,0:T(8,128)(2,1)S(1)}, bf16[192,2048]{1,0:T(8,128)(2,1)}, u32[]{:S(2)}) copy-start(bf16[192,2048]{1,0:T(8,128)(2,1)} %rest_0_.3) | copy-start | bytes 2359300
  14.9 23.8 %slice-start.2 = ((s8[14680064]{0:T(1024)(128)(4,1)}), s8[4194304]{0:T(1024)(128)(4,1)S(1)}, s32[]{:S(2)}) async-start(s8[14680064]{0:T(1024)(128)(4,1)} %bitcast.5), calls=%async_computation.3 | async-start | bytes 8388608
  14.9 23.9 %slice-start.3 = ((s8[14680064]{0:T(1024)(128)(4,1)}), s8[4194304]{0:T(1024)(128)(4,1)S(1)}, s32[]{:S(2)}) async-start(s8[14680064]{0:T(1024)(128)(4,1)} %bitcast.5), calls=%async_computation.4 | async-start | bytes 8388608
  14.9 23.9 %copy-start.6 = (bf16[96,3584]{1,0:T(8,128)(2,1)S(1)}, bf16[96,3584]{1,0:T(8,128)(2,1)}, u32[]{:S(2)}) copy-start(bf16[96,3584]{1,0:T(8,128)(2,1)} %rest_0_.5) | copy-start | bytes 2064388
  20.9 3.7 %copy-start = (f32[512,3584]{1,0:T(8,128)}, f32[512,3584]{1,0:T(8,128)S(1)}, u32[]{:S(2)}) copy-start(f32[512,3584]{1,0:T(8,128)S(1)} %get-tuple-element.28.rest_10_) | copy-start | bytes 22020100
  24.6 21.5 %copy-start.2 = (f32[512,3584]{1,0:T(8,128)}, f32[512,3584]{1,0:T(8,128)S(1)}, u32[]{:S(2)}) copy-start(f32[512,3584]{1,0:T(8,128)S(1)} %get-tuple-element.29.rest_11_) | copy-start | bytes 22020100
  24.6 11.5 %collective-permute-start.5 = (bf16[384,512]{1,0:T(8,128)(2,1)S(1)}, bf16[384,512]{1,0:T(8,128)(2,1)S(1)}, u32[]{:S(2)}, u32[]{:S(2)}) collective-permute-start(bf16[384,512]{1,0:T(8,128)(2,1)S(1)} %get-tuple-element.30), channel_id=1, source_target_pairs={{0,16},{8,24},{16,0},{24,8},{1,17},{9,25},{17,1},{25,9},{2,18},{10... | collective-permute-start | bytes 1179656 | tf_op jit(solution)/shard_map/ppermute | solution.py:334
  25.1 1.4 %collective-permute-start.3 = (bf16[192,512]{1,0:T(8,128)(2,1)S(1)}, bf16[192,512]{1,0:T(8,128)(2,1)S(1)}, u32[]{:S(2)}, u32[]{:S(2)}) collective-permute-start(bf16[192,512]{1,0:T(8,128)(2,1)S(1)} %get-tuple-element.24), channel_id=1, source_target_pairs={{0,8},{8,0},{16,24},{24,16},{1,9},{9,1},{17,25},{25,17},{2,10},{10... | collective-permute-start | bytes 589832 | tf_op jit(solution)/shard_map/ppermute | solution.py:340
  26.6 10.1 %copy-start.9 = (bf16[96,3584]{1,0:T(8,128)(2,1)}, bf16[96,3584]{1,0:T(8,128)(2,1)S(1)}, u32[]{:S(2)}) copy-start(bf16[96,3584]{1,0:T(8,128)(2,1)S(1)} %collective-permute-done.4.rest_4_) | copy-start | bytes 2064388
  26.6 1.3 %copy-start.11 = (bf16[96,3584]{1,0:T(8,128)(2,1)}, bf16[96,3584]{1,0:T(8,128)(2,1)S(1)}, u32[]{:S(2)}) copy-start(bf16[96,3584]{1,0:T(8,128)(2,1)S(1)} %collective-permute-done.rest_1_) | copy-start | bytes 2064388
  36.1 1.7 %collective-permute-start.6 = (bf16[384,512]{1,0:T(8,128)(2,1)S(1)}, bf16[384,512]{1,0:T(8,128)(2,1)S(1)}, u32[]{:S(2)}, u32[]{:S(2)}) collective-permute-start(bf16[384,512]{1,0:T(8,128)(2,1)S(1)} %collective-permute-done.5.rest_2_), channel_id=1, source_target_pairs={{0,8},{8,0},{16,24},{24,16},{1,9},{9,1},{17,25},{25,17},{2,10},{10... | collective-permute-start | bytes 1179656 | tf_op jit(solution)/shard_map/ppermute | solution.py:340
  36.1 18.0 %collective-permute-start.9 = (bf16[96,3584]{1,0:T(8,128)(2,1)S(1)}, bf16[96,3584]{1,0:T(8,128)(2,1)}, u32[]{:S(2)}, u32[]{:S(2)}) collective-permute-start(bf16[96,3584]{1,0:T(8,128)(2,1)S(1)} %collective-permute-done.2.rest_1_.rest_2_), channel_id=1, source_target_pairs={{0,16},{8,24},{16,0},{24,8},{1,17},{9,25},{17,1},{25,9},{2,18},{10... | collective-permute-start | bytes 2064392 | tf_op jit(solution)/shard_map/ppermute | solution.py:334
  46.1 46.7 %all-to-all-start = ((bf16[4,48,2048]{2,1,0:T(8,128)(2,1)}), bf16[4,48,2048]{2,1,0:T(8,128)(2,1)S(1)}, u32[]{:S(2)}, u32[]{:S(2)}) async-start(bf16[4,48,2048]{2,1,0:T(8,128)(2,1)} %bitcast.3), calls=%async_computation | async-start | bytes 1572864 | tf_op jit(solution)/shard_map/all_to_all | solution.py:424
  50.9 17.4 %collective-permute-start.1 = (bf16[96,3584]{1,0:T(8,128)(2,1)}, bf16[96,3584]{1,0:T(8,128)(2,1)S(1)}, u32[]{:S(2)}, u32[]{:S(2)}) collective-permute-start(bf16[96,3584]{1,0:T(8,128)(2,1)} %copy-done.13), channel_id=1, source_target_pairs={{0,4},{4,0},{1,5},{5,1},{2,6},{6,2},{3,7},{7,3},{8,12},{12,8},{9,1... | collective-permute-start | bytes 2064392 | tf_op jit(solution)/shard_map/ppermute | solution.py:334
  51.4 19.6 %collective-permute-start.7 = (bf16[96,3584]{1,0:T(8,128)(2,1)S(1)}, bf16[96,3584]{1,0:T(8,128)(2,1)S(1)}, u32[]{:S(2)}, u32[]{:S(2)}) collective-permute-start(bf16[96,3584]{1,0:T(8,128)(2,1)S(1)} %collective-permute-done.2.rest_1_.rest_2_), channel_id=1, source_target_pairs={{0,8},{8,0},{16,24},{24,16},{1,9},{9,1},{17,25},{25,17},{2,10},{10... | collective-permute-start | bytes 2064392 | tf_op jit(solution)/shard_map/ppermute | solution.py:340
  51.5 19.5 %collective-permute-start.8 = (bf16[96,3584]{1,0:T(8,128)(2,1)}, bf16[96,3584]{1,0:T(8,128)(2,1)S(1)}, u32[]{:S(2)}, u32[]{:S(2)}) collective-permute-start(bf16[96,3584]{1,0:T(8,128)(2,1)} %copy-done.9), channel_id=1, source_target_pairs={{0,8},{8,0},{16,24},{24,16},{1,9},{9,1},{17,25},{25,17},{2,10},{10... | collective-permute-start | bytes 2064392 | tf_op jit(solution)/shard_map/ppermute | solution.py:340
  54.1 16.9 %collective-permute-start.10 = (bf16[96,3584]{1,0:T(8,128)(2,1)}, bf16[96,3584]{1,0:T(8,128)(2,1)S(1)}, u32[]{:S(2)}, u32[]{:S(2)}) collective-permute-start(bf16[96,3584]{1,0:T(8,128)(2,1)} %collective-permute-done.9.rest_6_), channel_id=1, source_target_pairs={{0,8},{8,0},{16,24},{24,16},{1,9},{9,1},{17,25},{25,17},{2,10},{10... | collective-permute-start | bytes 2064392 | tf_op jit(solution)/shard_map/ppermute | solution.py:340
  68.4 1.1 %copy-start.8 = (bf16[96,3584]{1,0:T(8,128)(2,1)S(1)}, bf16[96,3584]{1,0:T(8,128)(2,1)}, u32[]{:S(2)}) copy-start(bf16[96,3584]{1,0:T(8,128)(2,1)} %copy-done.7) | copy-start | bytes 2064388
  71.0 3.1 %copy-start.1 = (f32[512,3584]{1,0:T(8,128)S(1)}, f32[512,3584]{1,0:T(8,128)}, u32[]{:S(2)}) copy-start(f32[512,3584]{1,0:T(8,128)} %copy-done) | copy-start | bytes 22020100
  74.1 3.1 %copy-start.3 = (f32[512,3584]{1,0:T(8,128)S(1)}, f32[512,3584]{1,0:T(8,128)}, u32[]{:S(2)}) copy-start(f32[512,3584]{1,0:T(8,128)} %copy-done.2) | copy-start | bytes 22020100
  77.2 1.1 %copy-start.10 = (bf16[96,3584]{1,0:T(8,128)(2,1)S(1)}, bf16[96,3584]{1,0:T(8,128)(2,1)}, u32[]{:S(2)}) copy-start(bf16[96,3584]{1,0:T(8,128)(2,1)} %copy-done.9) | copy-start | bytes 2064388
  78.3 1.1 %copy-start.12 = (bf16[96,3584]{1,0:T(8,128)(2,1)S(1)}, bf16[96,3584]{1,0:T(8,128)(2,1)}, u32[]{:S(2)}) copy-start(bf16[96,3584]{1,0:T(8,128)(2,1)} %copy-done.11) | copy-start | bytes 2064388

commit v12 on v10

--- a/solution.py
+++ b/solution.py
@@ -207,37 +207,6 @@
     return current - (scale * first) * invert(spread), first, second
 
 
-def hold_kernel(place, *refs):
-    n = (len(refs) - 1) // 2
-    sems = refs[-1]
-    copies = []
-    for k, (source, target) in enumerate(zip(refs[:n], refs[n:-1])):
-        rows = target.shape[0]
-        start = pl.multiple_of(place[0] * rows, rows) if source.shape[0] > rows else 0
-        copies.append(
-            pltpu.make_async_copy(source.at[pl.ds(start, rows), :], target, sems.at[k])
-        )
-    for copy in copies:
-        copy.start()
-    for copy in copies:
-        copy.wait()
-
-
-def hold_call(place, arrays, rows):
-    n = len(arrays)
-    return run(
-        hold_kernel,
-        "hold",
-        (1,),
-        [pl.BlockSpec(memory_space=pltpu.HBM)] * n,
-        [pl.BlockSpec(memory_space=pl.ANY)] * n,
-        [pltpu.VMEM((rows, a.shape[1]), a.dtype) for a in arrays],
-        [pltpu.SemaphoreType.DMA((n,))],
-        4,
-        (place, *map(in_hbm, arrays)),
-    )
-
-
 def update_kernel(origins, tokens_all, chunk, part, place, x_ref, *rest):
     n = len(origins)
     pieces = rest[:n]
@@ -287,7 +256,7 @@
         [tile] * 3,
         [struct((rows, width), BF16), struct((rows, width), F32), struct((rows, width), F32)],
         [pltpu.VMEM((tokens_all, width), BF16)],
-        22,
+        38,
         (place, features, *pieces, *held),
     )
 
@@ -361,11 +330,7 @@
     ]
     near = [swap_cores(to_send.pop(0))] if cores == 2 else []
     first = [by_chip[c, 0] for c in range(1, chips)]
-    kept = []
-    if tiled:
-        arrays = (after(first_moment, parts[0]), second_moment)
-        kept = hold_call(place, arrays, slice_rows)
-    far = [chip_shift(c)(after(to_send[c - 1], *kept)) for c in range(1, chips)]
+    far = [chip_shift(c)(to_send[c - 1]) for c in range(1, chips)]
     for s in range(1, n_row):
         by_row[s] = after(by_row[s], parts[0], *near, *first, *swapped.values())
         if cores == 2:
@@ -429,8 +394,9 @@
                 pieces.append(swapped[c, s])
 
     if tiled:
+        streamed = map(in_hbm, (weight, anchor, first_moment, second_moment))
         new_weight, new_first, new_second = update_call(
-            place, features, pieces, origins, (in_hbm(weight), in_hbm(anchor), *kept)
+            place, features, pieces, origins, tuple(streamed)
         )
     else:
         gathered = in_order(pieces, [origin(dp, row) for origin in origins], own)

time: 79.4 us -> 69.4 us (0.87)
  local copies, waits for them, and re-layouts: 15.4 us -> 4.23 us
  Pallas kernels: 36.5 us -> 34.4 us
  waiting for transfers between devices: 11.3 us -> 13.4 us
  starting transfers between devices: 12.6 us -> 14 us
    unnamed x32 -> x16, local copies, waits for them, and re-layouts: 15.4 us -> 4.23 us
    pallas_call x6 -> x5, Pallas kernels: 36.5 us -> 34.4 us  [run(): pl.pallas_call(kernel, name=name, grid_spec=pltpu.PrefetchScalarGridSpec(...]
    ppermute x5, starting transfers between devices: 6.69 us -> 8.01 us  [along(): lax.ppermute(a, axis, [(i, (i + shift) % n) for i in range(n)])]
    ppermute x6, waiting for transfers between devices: 3.33 us -> 4.65 us  [swap_cores(): return lax.ppermute(a, 'dp', [(i, i ^ 1) for i in range(n_dp)])]
  transfers between devices with their start and end apart: 12 -> 12, of which waited for: 5 -> 8; matrix products, arithmetic and copies ran while one was open for 3% -> 3% of each run, Pallas kernels for 45% -> 48%
where the time goes in v12:
time: 69.4 us; the launch traced here: 69 us
  Pallas kernels  34.4 us (50%)
  starting transfers between devices  14 us (20%)
  waiting for transfers between devices  13.4 us (19%)
  local copies, waits for them, and re-layouts  4.23 us (6%)
  other arithmetic  2.39 us (3%)
  between operations  0.7 us (1%)
    pallas_call x5, Pallas kernels, run(): pl.pallas_call(kernel, name=name, grid_spec=pltpu.PrefetchScalarGridSpec(...  34.4 us
    ppermute x5, waiting for transfers between devices, along(): lax.ppermute(a, axis, [(i, (i + shift) % n) for i in range(n)])  8.74 us
    ppermute x5, starting transfers between devices, along(): lax.ppermute(a, axis, [(i, (i + shift) % n) for i in range(n)])  8.01 us
    all_to_all x1, starting transfers between devices, per_device(): gparts = lax.all_to_all(gpart, 'col', 0, 0, tiled=True)  5.44 us
    ppermute x6, waiting for transfers between devices, swap_cores(): return lax.ppermute(a, 'dp', [(i, i ^ 1) for i in range(n_dp)])  4.65 us
    unnamed x16, local copies, waits for them, and re-layouts  4.23 us
    convert_element_type x1, other arithmetic, per_device(): outputs = outputs.astype(BF16)  2.31 us
  transfers between devices with their start and end apart: 12, of which 8 were waited for; matrix products, arithmetic and copies ran while one was open for 3% of the time, Pallas kernels for 48%

profile of v12, /device:TPU:0, one launch (start us, length us, event | category | flops | bytes accessed | tf_op | source)
XLA Modules:
  0.0 69.0 jit_solution(17322141896285057093)
XLA Ops:
  0.6 3.0 %collective-permute-start.4 = (bf16[96,3584]{1,0:T(8,128)(2,1)}, bf16[96,3584]{1,0:T(8,128)(2,1)S(1)}, u32[]{:S(2)}, u32[]{:S(2)}) collective-permute-start(bf16[96,3584]{1,0:T(8,128)(2,1)} %rest_0_.5), channel_id=1, source_target_pairs={{0,16},{8,24},{16,0},{24,8},{1,17},{9,25},{17,1},{25,9},{2,18},{10... | collective-permute-start | bytes 2064392 | tf_op jit(solution)/shard_map/ppermute | solution.py:281
  3.6 0.0 collective-permute-start
  3.6 1.5 %collective-permute-start.2 = (bf16[96,3584]{1,0:T(8,128)(2,1)}, bf16[96,3584]{1,0:T(8,128)(2,1)S(1)}, u32[]{:S(2)}, u32[]{:S(2)}) collective-permute-start(bf16[96,3584]{1,0:T(8,128)(2,1)} %rest_0_.5), channel_id=1, source_target_pairs={{0,4},{4,0},{1,5},{5,1},{2,6},{6,2},{3,7},{7,3},{8,12},{12,8},{9,1... | collective-permute-start | bytes 2064392 | tf_op jit(solution)/shard_map/ppermute | solution.py:281
  5.2 0.1 pad_add_fusion.place
  5.2 0.0 copy-start.1
  5.2 1.1 %copy-done.1 = bf16[192,2048]{1,0:T(8,128)(2,1)S(1)} copy-done((bf16[192,2048]{1,0:T(8,128)(2,1)S(1)}, bf16[192,2048]{1,0:T(8,128)(2,1)}, u32[]{:S(2)}) %copy-start.1) | copy-done | bytes 786456
  6.4 0.0 copy-start
  6.4 0.0 copy-start.2
  6.4 7.6 %forward.1 = (bf16[96,3584]{1,0:T(8,128)(2,1)S(1)}, bf16[96,3584]{1,0:T(8,128)(2,1)}, bf16[192,512]{1,0:T(8,128)(2,1)S(1)}, bf16[384,512]{1,0:T(8,128)(2,1)S(1)}) custom-call(s32[3]{0:T(128)S(1)} %pad_add_fusion.place, bf16[192,2048]{1,0:T(8,128)(2,1)S(1)} %copy-done.1, bf16[2048,3584]{1,0:T(8,128)(2,1)} %rest_8_.1), custom_call_target="tpu_custom_call" | custom-call | flops 1 | bytes 1 | tf_op jit(solution)/shard_map/forward/pallas_call | solution.py:31
  14.0 0.0 copy-start.3
  14.0 0.6 collective-permute-start.5
  14.6 0.0 collective-permute-start.3
  14.6 1.4 %collective-permute-done.3.rest_1_ = bf16[192,512]{1,0:T(8,128)(2,1)S(1)} collective-permute-done((bf16[192,512]{1,0:T(8,128)(2,1)S(1)}, bf16[192,512]{1,0:T(8,128)(2,1)S(1)}, u32[]{:S(2)}, u32[]{:S(2)}) %collective-permute-start.3) | collective-permute-done | bytes 196640 | tf_op jit(solution)/shard_map/ppermute | solution.py:287
  16.0 4.1 %collective-permute-done.4.rest_4_ = bf16[96,3584]{1,0:T(8,128)(2,1)S(1)} collective-permute-done((bf16[96,3584]{1,0:T(8,128)(2,1)}, bf16[96,3584]{1,0:T(8,128)(2,1)S(1)}, u32[]{:S(2)}, u32[]{:S(2)}) %collective-permute-start.4) | collective-permute-done | bytes 688160 | tf_op jit(solution)/shard_map/ppermute | solution.py:281
  20.1 0.0 copy-start.4
  20.1 0.0 collective-permute-done.rest_1_
  20.1 0.0 copy-start.6
  20.1 0.9 %copy-done.6 = bf16[96,3584]{1,0:T(8,128)(2,1)} copy-done((bf16[96,3584]{1,0:T(8,128)(2,1)}, bf16[96,3584]{1,0:T(8,128)(2,1)S(1)}, u32[]{:S(2)}) %copy-start.6) | copy-done | bytes 688152
  21.0 0.7 %collective-permute-done.2.rest_1_.rest_2_ = bf16[96,3584]{1,0:T(8,128)(2,1)S(1)} collective-permute-done((bf16[96,3584]{1,0:T(8,128)(2,1)}, bf16[96,3584]{1,0:T(8,128)(2,1)S(1)}, u32[]{:S(2)}, u32[]{:S(2)}) %collective-permute-start.2) | collective-permute-done | bytes 688160 | tf_op jit(solution)/shard_map/ppermute | solution.py:281
  21.7 1.4 %collective-permute-start.9 = (bf16[96,3584]{1,0:T(8,128)(2,1)S(1)}, bf16[96,3584]{1,0:T(8,128)(2,1)}, u32[]{:S(2)}, u32[]{:S(2)}) collective-permute-start(bf16[96,3584]{1,0:T(8,128)(2,1)S(1)} %collective-permute-done.2.rest_1_.rest_2_), channel_id=1, source_target_pairs={{0,16},{8,24},{16,0},{24,8},{1,17},{9,25},{17,1},{25,9},{2,18},{10... | collective-permute-start | bytes 2064392 | tf_op jit(solution)/shard_map/ppermute | solution.py:281
  23.1 1.5 %collective-permute-start.1 = (bf16[96,3584]{1,0:T(8,128)(2,1)}, bf16[96,3584]{1,0:T(8,128)(2,1)}, u32[]{:S(2)}, u32[]{:S(2)}) collective-permute-start(bf16[96,3584]{1,0:T(8,128)(2,1)} %get-tuple-element.19), channel_id=1, source_target_pairs={{0,4},{4,0},{1,5},{5,1},{2,6},{6,2},{3,7},{7,3},{8,12},{12,8},{9,1... | collective-permute-start | bytes 2064392 | tf_op jit(solution)/shard_map/ppermute | solution.py:281
  24.6 4.0 %collective-permute-done.5.rest_2_ = bf16[384,512]{1,0:T(8,128)(2,1)S(1)} collective-permute-done((bf16[384,512]{1,0:T(8,128)(2,1)S(1)}, bf16[384,512]{1,0:T(8,128)(2,1)S(1)}, u32[]{:S(2)}, u32[]{:S(2)}) %collective-permute-start.5) | collective-permute-done | bytes 393248 | tf_op jit(solution)/shard_map/ppermute | solution.py:281
  28.5 0.0 collective-permute-start.6
  28.5 0.0 copy-done.4
  28.5 1.7 %collective-permute-done.6.rest_3_ = bf16[384,512]{1,0:T(8,128)(2,1)S(1)} collective-permute-done((bf16[384,512]{1,0:T(8,128)(2,1)S(1)}, bf16[384,512]{1,0:T(8,128)(2,1)S(1)}, u32[]{:S(2)}, u32[]{:S(2)}) %collective-permute-start.6) | collective-permute-done | bytes 393248 | tf_op jit(solution)/shard_map/ppermute | solution.py:287
  30.3 0.9 %features.1.x_ref = bf16[512,768]{1,0:T(8,128)(2,1)S(1)} custom-call(s32[3]{0:T(128)S(1)} %pad_add_fusion.place, bf16[192,2048]{1,0:T(8,128)(2,1)S(1)} %copy-done.1, bf16[192,512]{1,0:T(8,128)(2,1)S(1)} %collective-permute-done.3.rest_1_, bf16[384,512]{1,0:T(8,128)(2,1)S(1)} %collective-permute-done.5.rest_2_, ...), custom_call_target="tpu_custom_call" | custom-call | flops 1 | bytes 1 | tf_op jit(solution)/shard_map/features/pallas_call | solution.py:31
  31.1 0.0 copy-done
  31.1 0.0 copy-done.2
  31.1 7.3 %input_grad.1 = bf16[192,2048]{1,0:T(8,128)(2,1)} custom-call(s32[3]{0:T(128)S(1)} %pad_add_fusion.place, bf16[96,3584]{1,0:T(8,128)(2,1)S(1)} %copy-done.2, bf16[96,3584]{1,0:T(8,128)(2,1)S(1)} %collective-permute-done.2.rest_1_.rest_2_, bf16[2048,3584]{1,0:T(8,128)(2,1)S(1)} %copy-done), custom_call_target="tpu_custom_call" | custom-call | flops 1 | bytes 1 | tf_op jit(solution)/shard_map/input_grad/pallas_call | solution.py:31
  38.4 0.0 copy-done.3
  38.4 5.4 %all-to-all-start = ((bf16[4,48,2048]{2,1,0:T(8,128)(2,1)}), bf16[4,48,2048]{2,1,0:T(8,128)(2,1)S(1)}, u32[]{:S(2)}, u32[]{:S(2)}) async-start(bf16[4,48,2048]{2,1,0:T(8,128)(2,1)} %bitcast.3), calls=%async_computation | async-start | bytes 1572864 | tf_op jit(solution)/shard_map/all_to_all | solution.py:367
  43.9 0.0 collective-permute-start.7
  43.9 0.5 collective-permute-start.8
  44.4 0.0 collective-permute-done.9.rest_6_
  44.4 0.0 collective-permute-start.10
  44.4 0.0 collective-permute-done.1
  44.4 2.3 %add_convert_fusion = bf16[96,3584]{1,0:T(8,128)(2,1)} fusion(bf16[96,3584]{1,0:T(8,128)(2,1)} %collective-permute-done.1, bf16[96,3584]{1,0:T(8,128)(2,1)} %copy-done.3), kind=kLoop, calls=%fused_computation | loop fusion | flops 1376256 | bytes 2064384 | tf_op jit(solution)/shard_map/convert_element_type | solution.py:374
  46.7 0.3 collective-permute-done.7.rest_3_
  47.0 0.2 collective-permute-done.8.rest_5_
  47.2 1.0 %collective-permute-done.10.rest_7_ = bf16[96,3584]{1,0:T(8,128)(2,1)S(1)} collective-permute-done((bf16[96,3584]{1,0:T(8,128)(2,1)}, bf16[96,3584]{1,0:T(8,128)(2,1)S(1)}, u32[]{:S(2)}, u32[]{:S(2)}) %collective-permute-start.10) | collective-permute-done | bytes 688160 | tf_op jit(solution)/shard_map/ppermute | solution.py:287
  48.2 0.0 copy-start.5
  48.2 1.1 %copy-done.5 = bf16[96,3584]{1,0:T(8,128)(2,1)S(1)} copy-done((bf16[96,3584]{1,0:T(8,128)(2,1)S(1)}, bf16[96,3584]{1,0:T(8,128)(2,1)}, u32[]{:S(2)}) %copy-start.5) | copy-done | bytes 688152
  49.3 0.0 copy-start.7
  49.3 1.1 %copy-done.7 = bf16[96,3584]{1,0:T(8,128)(2,1)S(1)} copy-done((bf16[96,3584]{1,0:T(8,128)(2,1)S(1)}, bf16[96,3584]{1,0:T(8,128)(2,1)}, u32[]{:S(2)}) %copy-start.7) | copy-done | bytes 688152
  50.4 17.3 %update.1 = (bf16[512,3584]{1,0:T(8,128)(2,1)}, f32[512,3584]{1,0:T(8,128)}, f32[512,3584]{1,0:T(8,128)}) custom-call(s32[3]{0:T(128)S(1)} %pad_add_fusion.place, bf16[512,768]{1,0:T(8,128)(2,1)S(1)} %features.1.x_ref, bf16[96,3584]{1,0:T(8,128)(2,1)S(1)} %copy-done.2, bf16[96,3584]{1,0:T(8,128)(2,1)S(1)} %copy-done.7, ...), custom_call_target="tpu_custom_call" | custom-call | flops 1 | bytes 1 | tf_op jit(solution)/shard_map/update/pallas_call | solution.py:31
  67.7 0.0 all-to-all-done
  67.7 1.3 %total.1 = bf16[48,2048]{1,0:T(8,128)(2,1)} custom-call(s32[3]{0:T(128)S(1)} %pad_add_fusion.place, bf16[192,2048]{1,0:T(8,128)(2,1)S(1)} %bitcast.5), custom_call_target="tpu_custom_call" | custom-call | flops 1 | bytes 1 | tf_op jit(solution)/shard_map/total/pallas_call | solution.py:31
Async XLA Ops:
  0.6 19.5 %collective-permute-start.4 = (bf16[96,3584]{1,0:T(8,128)(2,1)}, bf16[96,3584]{1,0:T(8,128)(2,1)S(1)}, u32[]{:S(2)}, u32[]{:S(2)}) collective-permute-start(bf16[96,3584]{1,0:T(8,128)(2,1)} %rest_0_.5), channel_id=1, source_target_pairs={{0,16},{8,24},{16,0},{24,8},{1,17},{9,25},{17,1},{25,9},{2,18},{10... | collective-permute-start | bytes 2064392 | tf_op jit(solution)/shard_map/ppermute | solution.py:281
  3.6 16.5 %collective-permute-start = (bf16[96,3584]{1,0:T(8,128)(2,1)}, bf16[96,3584]{1,0:T(8,128)(2,1)S(1)}, u32[]{:S(2)}, u32[]{:S(2)}) collective-permute-start(bf16[96,3584]{1,0:T(8,128)(2,1)} %rest_0_.5), channel_id=1, source_target_pairs={{0,8},{8,0},{16,24},{24,16},{1,9},{9,1},{17,25},{25,17},{2,10},{10... | collective-permute-start | bytes 2064392 | tf_op jit(solution)/shard_map/ppermute | solution.py:287
  3.6 18.1 %collective-permute-start.2 = (bf16[96,3584]{1,0:T(8,128)(2,1)}, bf16[96,3584]{1,0:T(8,128)(2,1)S(1)}, u32[]{:S(2)}, u32[]{:S(2)}) collective-permute-start(bf16[96,3584]{1,0:T(8,128)(2,1)} %rest_0_.5), channel_id=1, source_target_pairs={{0,4},{4,0},{1,5},{5,1},{2,6},{6,2},{3,7},{7,3},{8,12},{12,8},{9,1... | collective-permute-start | bytes 2064392 | tf_op jit(solution)/shard_map/ppermute | solution.py:281
  5.2 1.1 %copy-start.1 = (bf16[192,2048]{1,0:T(8,128)(2,1)S(1)}, bf16[192,2048]{1,0:T(8,128)(2,1)}, u32[]{:S(2)}) copy-start(bf16[192,2048]{1,0:T(8,128)(2,1)} %rest_0_.3) | copy-start | bytes 2359300
  6.4 24.8 %copy-start = (bf16[2048,3584]{1,0:T(8,128)(2,1)S(1)}, bf16[2048,3584]{1,0:T(8,128)(2,1)}, u32[]{:S(2)}) copy-start(bf16[2048,3584]{1,0:T(8,128)(2,1)} %rest_8_.1) | copy-start | bytes 44040196
  6.4 24.8 %copy-start.2 = (bf16[96,3584]{1,0:T(8,128)(2,1)S(1)}, bf16[96,3584]{1,0:T(8,128)(2,1)}, u32[]{:S(2)}) copy-start(bf16[96,3584]{1,0:T(8,128)(2,1)} %rest_0_.5) | copy-start | bytes 2064388
  14.0 24.5 %copy-start.3 = (bf16[96,3584]{1,0:T(8,128)(2,1)}, bf16[96,3584]{1,0:T(8,128)(2,1)S(1)}, u32[]{:S(2)}) copy-start(bf16[96,3584]{1,0:T(8,128)(2,1)S(1)} %get-tuple-element.17) | copy-start | bytes 2064388
  14.0 14.5 %collective-permute-start.5 = (bf16[384,512]{1,0:T(8,128)(2,1)S(1)}, bf16[384,512]{1,0:T(8,128)(2,1)S(1)}, u32[]{:S(2)}, u32[]{:S(2)}) collective-permute-start(bf16[384,512]{1,0:T(8,128)(2,1)S(1)} %get-tuple-element.22), channel_id=1, source_target_pairs={{0,16},{8,24},{16,0},{24,8},{1,17},{9,25},{17,1},{25,9},{2,18},{10... | collective-permute-start | bytes 1179656 | tf_op jit(solution)/shard_map/ppermute | solution.py:281
  14.6 1.4 %collective-permute-start.3 = (bf16[192,512]{1,0:T(8,128)(2,1)S(1)}, bf16[192,512]{1,0:T(8,128)(2,1)S(1)}, u32[]{:S(2)}, u32[]{:S(2)}) collective-permute-start(bf16[192,512]{1,0:T(8,128)(2,1)S(1)} %get-tuple-element.20), channel_id=1, source_target_pairs={{0,8},{8,0},{16,24},{24,16},{1,9},{9,1},{17,25},{25,17},{2,10},{10... | collective-permute-start | bytes 589832 | tf_op jit(solution)/shard_map/ppermute | solution.py:287
  20.1 8.4 %copy-start.4 = (bf16[96,3584]{1,0:T(8,128)(2,1)}, bf16[96,3584]{1,0:T(8,128)(2,1)S(1)}, u32[]{:S(2)}) copy-start(bf16[96,3584]{1,0:T(8,128)(2,1)S(1)} %collective-permute-done.4.rest_4_) | copy-start | bytes 2064388
  20.1 0.9 %copy-start.6 = (bf16[96,3584]{1,0:T(8,128)(2,1)}, bf16[96,3584]{1,0:T(8,128)(2,1)S(1)}, u32[]{:S(2)}) copy-start(bf16[96,3584]{1,0:T(8,128)(2,1)S(1)} %collective-permute-done.rest_1_) | copy-start | bytes 2064388
  21.7 22.7 %collective-permute-start.9 = (bf16[96,3584]{1,0:T(8,128)(2,1)S(1)}, bf16[96,3584]{1,0:T(8,128)(2,1)}, u32[]{:S(2)}, u32[]{:S(2)}) collective-permute-start(bf16[96,3584]{1,0:T(8,128)(2,1)S(1)} %collective-permute-done.2.rest_1_.rest_2_), channel_id=1, source_target_pairs={{0,16},{8,24},{16,0},{24,8},{1,17},{9,25},{17,1},{25,9},{2,18},{10... | collective-permute-start | bytes 2064392 | tf_op jit(solution)/shard_map/ppermute | solution.py:281
  23.1 21.4 %collective-permute-start.1 = (bf16[96,3584]{1,0:T(8,128)(2,1)}, bf16[96,3584]{1,0:T(8,128)(2,1)}, u32[]{:S(2)}, u32[]{:S(2)}) collective-permute-start(bf16[96,3584]{1,0:T(8,128)(2,1)} %get-tuple-element.19), channel_id=1, source_target_pairs={{0,4},{4,0},{1,5},{5,1},{2,6},{6,2},{3,7},{7,3},{8,12},{12,8},{9,1... | collective-permute-start | bytes 2064392 | tf_op jit(solution)/shard_map/ppermute | solution.py:281
  28.5 1.7 %collective-permute-start.6 = (bf16[384,512]{1,0:T(8,128)(2,1)S(1)}, bf16[384,512]{1,0:T(8,128)(2,1)S(1)}, u32[]{:S(2)}, u32[]{:S(2)}) collective-permute-start(bf16[384,512]{1,0:T(8,128)(2,1)S(1)} %collective-permute-done.5.rest_2_), channel_id=1, source_target_pairs={{0,8},{8,0},{16,24},{24,16},{1,9},{9,1},{17,25},{25,17},{2,10},{10... | collective-permute-start | bytes 1179656 | tf_op jit(solution)/shard_map/ppermute | solution.py:287
  38.4 29.3 %all-to-all-start = ((bf16[4,48,2048]{2,1,0:T(8,128)(2,1)}), bf16[4,48,2048]{2,1,0:T(8,128)(2,1)S(1)}, u32[]{:S(2)}, u32[]{:S(2)}) async-start(bf16[4,48,2048]{2,1,0:T(8,128)(2,1)} %bitcast.3), calls=%async_computation | async-start | bytes 1572864 | tf_op jit(solution)/shard_map/all_to_all | solution.py:367
  43.9 3.1 %collective-permute-start.7 = (bf16[96,3584]{1,0:T(8,128)(2,1)S(1)}, bf16[96,3584]{1,0:T(8,128)(2,1)S(1)}, u32[]{:S(2)}, u32[]{:S(2)}) collective-permute-start(bf16[96,3584]{1,0:T(8,128)(2,1)S(1)} %collective-permute-done.2.rest_1_.rest_2_), channel_id=1, source_target_pairs={{0,8},{8,0},{16,24},{24,16},{1,9},{9,1},{17,25},{25,17},{2,10},{10... | collective-permute-start | bytes 2064392 | tf_op jit(solution)/shard_map/ppermute | solution.py:287
  43.9 3.3 %collective-permute-start.8 = (bf16[96,3584]{1,0:T(8,128)(2,1)}, bf16[96,3584]{1,0:T(8,128)(2,1)S(1)}, u32[]{:S(2)}, u32[]{:S(2)}) collective-permute-start(bf16[96,3584]{1,0:T(8,128)(2,1)} %copy-done.4), channel_id=1, source_target_pairs={{0,8},{8,0},{16,24},{24,16},{1,9},{9,1},{17,25},{25,17},{2,10},{10... | collective-permute-start | bytes 2064392 | tf_op jit(solution)/shard_map/ppermute | solution.py:287
  44.4 3.8 %collective-permute-start.10 = (bf16[96,3584]{1,0:T(8,128)(2,1)}, bf16[96,3584]{1,0:T(8,128)(2,1)S(1)}, u32[]{:S(2)}, u32[]{:S(2)}) collective-permute-start(bf16[96,3584]{1,0:T(8,128)(2,1)} %collective-permute-done.9.rest_6_), channel_id=1, source_target_pairs={{0,8},{8,0},{16,24},{24,16},{1,9},{9,1},{17,25},{25,17},{2,10},{10... | collective-permute-start | bytes 2064392 | tf_op jit(solution)/shard_map/ppermute | solution.py:287
  48.2 1.1 %copy-start.5 = (bf16[96,3584]{1,0:T(8,128)(2,1)S(1)}, bf16[96,3584]{1,0:T(8,128)(2,1)}, u32[]{:S(2)}) copy-start(bf16[96,3584]{1,0:T(8,128)(2,1)} %copy-done.4) | copy-start | bytes 2064388
  49.3 1.1 %copy-start.7 = (bf16[96,3584]{1,0:T(8,128)(2,1)S(1)}, bf16[96,3584]{1,0:T(8,128)(2,1)}, u32[]{:S(2)}) copy-start(bf16[96,3584]{1,0:T(8,128)(2,1)} %copy-done.6) | copy-start | bytes 2064388

commit v13 on v12

--- a/solution.py
+++ b/solution.py
@@ -169,26 +169,32 @@
     )
 
 
-def total_kernel(place, parts, out):
-    share = out.shape[0]
-    whole = parts[:share, :].astype(F32)
-    for k in range(1, parts.shape[0] // share):
-        whole = whole + parts[k * share : (k + 1) * share, :].astype(F32)
-    out[...] = whole.astype(BF16)
-
-
-def total_call(place, parts, n):
+def total(parts):
+    whole = parts[0].astype(F32)
+    for part in parts[1:]:
+        whole = whole + part.astype(F32)
+    return whole.astype(BF16)
+
+
+def totals_kernel(n, place, parts, *rest):
+    sums, (grad, out) = rest[:-2], rest[-2:]
+    share = grad.shape[0]
+    grad[...] = total([parts[k * share : (k + 1) * share, :] for k in range(n)])
+    out[...] = total([part[...] for part in sums])
+
+
+def totals_call(place, parts, sums, n):
     rows, width = parts.shape
     return run(
-        total_kernel,
-        "total",
+        functools.partial(totals_kernel, n),
+        "totals",
         (1,),
-        [fixed((rows, width))],
-        fixed((rows // n, width)),
-        struct((rows // n, width), BF16),
+        [fixed(parts.shape)] + [fixed(part.shape) for part in sums],
+        [fixed((rows // n, width)), fixed(sums[0].shape)],
+        [struct((rows // n, width), BF16), struct(sums[0].shape, BF16)],
         [],
-        8,
-        (place, parts),
+        10,
+        (place, parts, *sums),
     )
 
 
@@ -357,7 +363,7 @@
             tokens,
         )
     if tiled:
-        ready = [by_row[0]] + [after(piece, features) for piece in by_row[1:]]
+        ready = [by_row[0]] + [after(piece, *held) for piece in by_row[1:]]
         gpart = input_grad_call(place, ready, weight, n_row)
     else:
         gathered = in_order(by_row, [lax.rem(row - s + n_row, n_row) for s in range(n_row)], own)
@@ -368,11 +374,6 @@
     for s in range(1, n_row):
         for c in range(1, chips):
             by_chip[c, s] = chip_shift(c)(by_row[s])
-    outputs = parts[0].astype(F32)
-    for part in sums:
-        outputs = outputs + part.astype(F32)
-    outputs = outputs.astype(BF16)
-
     by_chip.update({(0, s): by_row[s] for s in range(n_row)})
     origins = []
     for c in range(chips):
@@ -387,11 +388,14 @@
     pieces = []
     for c in range(chips):
         for s in range(n_row):
-            pieces.append(by_chip[c, s])
+            early = c == 0 or s == 0
+            pieces.append(in_hbm(by_chip[c, s]) if tiled and early else by_chip[c, s])
             if cores == 2:
-                if (c, s) not in swapped:
-                    swapped[c, s] = swap_cores(by_chip[c, s])
-                pieces.append(swapped[c, s])
+                if (c, s) in swapped:
+                    first_swap = tiled and (c, s) == (0, 0)
+                    pieces.append(in_hbm(swapped[c, s]) if first_swap else swapped[c, s])
+                else:
+                    pieces.append(swap_cores(by_chip[c, s]))
 
     if tiled:
         streamed = map(in_hbm, (weight, anchor, first_moment, second_moment))
@@ -416,11 +420,12 @@
         new_weight = new_weight.astype(BF16)
     gparts = after(gparts, new_first)
     if tiled:
-        input_grad = total_call(place, gparts, n_col)
+        input_grad, outputs = totals_call(place, gparts, [parts[0], *sums], n_col)
     else:
-        input_grad = sum(
-            lax.slice_in_dim(gparts, k * share, (k + 1) * share).astype(F32) for k in range(n_col)
-        ).astype(BF16)
+        input_grad = total(
+            [lax.slice_in_dim(gparts, k * share, (k + 1) * share) for k in range(n_col)]
+        )
+        outputs = total([parts[0], *sums])
     return (outputs, input_grad, new_weight, new_first, new_second)
 
 

time: 69.4 us -> 71.3 us (1.027)
  waiting for transfers between devices: 13.4 us -> 17.8 us
  other arithmetic: 2.39 us -> 0.08 us
  local copies, waits for them, and re-layouts: 4.23 us -> 2.17 us
  Pallas kernels: 34.4 us -> 35.8 us
    ppermute x5, waiting for transfers between devices: 8.74 us -> 16.4 us  [along(): lax.ppermute(a, axis, [(i, (i + shift) % n) for i in range(n)])]
    ppermute x6, waiting for transfers between devices: 4.65 us -> 1.45 us  [swap_cores(): return lax.ppermute(a, 'dp', [(i, i ^ 1) for i in range(n_dp)])]
    convert_element_type x1 -> x0, other arithmetic: 2.31 us -> none  [per_device(): outputs = outputs.astype(BF16)]
    unnamed x16 -> x22, local copies, waits for them, and re-layouts: 4.23 us -> 2.17 us
    pallas_call x5, Pallas kernels: 34.4 us -> 35.8 us  [run(): pl.pallas_call(kernel, name=name, grid_spec=pltpu.PrefetchScalarGridSpec(...]
  transfers between devices with their start and end apart: 12 -> 12, of which waited for: 8 -> 5; matrix products, arithmetic and copies ran while one was open for 3% -> 0% of each run, Pallas kernels for 48% -> 47%
where the time goes in v13:
time: 71.3 us; the launch traced here: 71 us
  Pallas kernels  35.8 us (50%)
  waiting for transfers between devices  17.8 us (25%)
  starting transfers between devices  14.3 us (20%)
  local copies, waits for them, and re-layouts  2.17 us (3%)
  between operations  0.76 us (1%)
    pallas_call x5, Pallas kernels, run(): pl.pallas_call(kernel, name=name, grid_spec=pltpu.PrefetchScalarGridSpec(...  35.8 us
    ppermute x5, waiting for transfers between devices, along(): lax.ppermute(a, axis, [(i, (i + shift) % n) for i in range(n)])  16.4 us
    ppermute x5, starting transfers between devices, along(): lax.ppermute(a, axis, [(i, (i + shift) % n) for i in range(n)])  8.21 us
    all_to_all x1, starting transfers between devices, per_device(): gparts = lax.all_to_all(gpart, 'col', 0, 0, tiled=True)  5.08 us
    unnamed x22, local copies, waits for them, and re-layouts  2.17 us
    ppermute x6, waiting for transfers between devices, swap_cores(): return lax.ppermute(a, 'dp', [(i, i ^ 1) for i in range(n_dp)])  1.45 us
  transfers between devices with their start and end apart: 12, of which 5 were waited for; matrix products, arithmetic and copies ran while one was open for 0% of the time, Pallas kernels for 47%

profile of v13, /device:TPU:0, one launch (start us, length us, event | category | flops | bytes accessed | tf_op | source)
XLA Modules:
  0.0 71.0 jit_solution(2513764888119335225)
XLA Ops:
  0.6 0.5 collective-permute-start.3
  1.1 2.6 %collective-permute-start.2 = (bf16[96,3584]{1,0:T(8,128)(2,1)}, bf16[96,3584]{1,0:T(8,128)(2,1)}, u32[]{:S(2)}, u32[]{:S(2)}) collective-permute-start(bf16[96,3584]{1,0:T(8,128)(2,1)} %rest_0_.5), channel_id=1, source_target_pairs={{0,16},{8,24},{16,0},{24,8},{1,17},{9,25},{17,1},{25,9},{2,18},{10... | collective-permute-start | bytes 2064392 | tf_op jit(solution)/shard_map/ppermute | solution.py:287
  3.7 1.5 %collective-permute-start = (bf16[96,3584]{1,0:T(8,128)(2,1)}, bf16[96,3584]{1,0:T(8,128)(2,1)S(1)}, u32[]{:S(2)}, u32[]{:S(2)}) collective-permute-start(bf16[96,3584]{1,0:T(8,128)(2,1)} %rest_0_.5), channel_id=1, source_target_pairs={{0,4},{4,0},{1,5},{5,1},{2,6},{6,2},{3,7},{7,3},{8,12},{12,8},{9,1... | collective-permute-start | bytes 2064392 | tf_op jit(solution)/shard_map/ppermute | solution.py:287
  5.2 0.1 pad_add_fusion.place
  5.3 0.0 copy-start.1
  5.3 1.1 %copy-done.1 = bf16[192,2048]{1,0:T(8,128)(2,1)S(1)} copy-done((bf16[192,2048]{1,0:T(8,128)(2,1)S(1)}, bf16[192,2048]{1,0:T(8,128)(2,1)}, u32[]{:S(2)}) %copy-start.1) | copy-done | bytes 786456
  6.4 0.0 copy-start
  6.4 0.0 copy-start.3
  6.5 6.7 %forward.1 = (bf16[96,3584]{1,0:T(8,128)(2,1)S(1)}, bf16[96,3584]{1,0:T(8,128)(2,1)S(1)}, bf16[192,512]{1,0:T(8,128)(2,1)S(1)}, bf16[384,512]{1,0:T(8,128)(2,1)S(1)}) custom-call(s32[3]{0:T(128)S(1)} %pad_add_fusion.place, bf16[192,2048]{1,0:T(8,128)(2,1)S(1)} %copy-done.1, bf16[2048,3584]{1,0:T(8,128)(2,1)} %rest_8_.1), custom_call_target="tpu_custom_call" | custom-call | flops 1 | bytes 1 | tf_op jit(solution)/shard_map/forward/pallas_call | solution.py:31
  13.2 0.0 copy-start.5
  13.2 0.0 copy-start.9
  13.2 0.6 collective-permute-start.4
  13.8 0.0 collective-permute-start.1
  13.8 1.4 %collective-permute-done.1.rest_1_ = bf16[192,512]{1,0:T(8,128)(2,1)S(1)} collective-permute-done((bf16[192,512]{1,0:T(8,128)(2,1)S(1)}, bf16[192,512]{1,0:T(8,128)(2,1)S(1)}, u32[]{:S(2)}, u32[]{:S(2)}) %collective-permute-start.1) | collective-permute-done | bytes 196640 | tf_op jit(solution)/shard_map/ppermute | solution.py:293
  15.3 0.0 collective-permute-done.3.rest_1_
  15.3 0.0 copy-start.10
  15.3 5.0 %collective-permute-done.2.rest_4_ = bf16[96,3584]{1,0:T(8,128)(2,1)} collective-permute-done((bf16[96,3584]{1,0:T(8,128)(2,1)}, bf16[96,3584]{1,0:T(8,128)(2,1)}, u32[]{:S(2)}, u32[]{:S(2)}) %collective-permute-start.2) | collective-permute-done | bytes 688160 | tf_op jit(solution)/shard_map/ppermute | solution.py:287
  20.3 1.1 %collective-permute-done.rest_1_.rest_2_ = bf16[96,3584]{1,0:T(8,128)(2,1)S(1)} collective-permute-done((bf16[96,3584]{1,0:T(8,128)(2,1)}, bf16[96,3584]{1,0:T(8,128)(2,1)S(1)}, u32[]{:S(2)}, u32[]{:S(2)}) %collective-permute-start) | collective-permute-done | bytes 688160 | tf_op jit(solution)/shard_map/ppermute | solution.py:287
  21.4 0.0 copy-done.10
  21.4 0.0 copy-start.4
  21.4 0.0 copy-start.2
  21.4 6.9 %collective-permute-done.4.rest_2_ = bf16[384,512]{1,0:T(8,128)(2,1)S(1)} collective-permute-done((bf16[384,512]{1,0:T(8,128)(2,1)S(1)}, bf16[384,512]{1,0:T(8,128)(2,1)S(1)}, u32[]{:S(2)}, u32[]{:S(2)}) %collective-permute-start.4) | collective-permute-done | bytes 393248 | tf_op jit(solution)/shard_map/ppermute | solution.py:287
  28.4 0.0 collective-permute-start.5
  28.4 1.8 %collective-permute-start.8 = (bf16[96,3584]{1,0:T(8,128)(2,1)S(1)}, bf16[96,3584]{1,0:T(8,128)(2,1)}, u32[]{:S(2)}, u32[]{:S(2)}) collective-permute-start(bf16[96,3584]{1,0:T(8,128)(2,1)S(1)} %collective-permute-done.rest_1_.rest_2_), channel_id=1, source_target_pairs={{0,16},{8,24},{16,0},{24,8},{1,17},{9,25},{17,1},{25,9},{2,18},{10... | collective-permute-start | bytes 2064392 | tf_op jit(solution)/shard_map/ppermute | solution.py:287
  30.1 0.0 collective-permute-done.5.rest_3_
  30.1 0.0 copy-done
  30.1 0.0 copy-done.3
  30.2 0.0 copy-start.7
  30.2 7.3 %input_grad.1 = bf16[192,2048]{1,0:T(8,128)(2,1)} custom-call(s32[3]{0:T(128)S(1)} %pad_add_fusion.place, bf16[96,3584]{1,0:T(8,128)(2,1)S(1)} %copy-done.3, bf16[96,3584]{1,0:T(8,128)(2,1)S(1)} %collective-permute-done.rest_1_.rest_2_, bf16[2048,3584]{1,0:T(8,128)(2,1)S(1)} %copy-done), custom_call_target="tpu_custom_call" | custom-call | flops 1 | bytes 1 | tf_op jit(solution)/shard_map/input_grad/pallas_call | solution.py:31
  37.5 0.0 copy-done.5
  37.5 0.0 copy-done.9
  37.5 0.0 copy-done.7
  37.5 5.1 %all-to-all-start = ((bf16[4,48,2048]{2,1,0:T(8,128)(2,1)}), bf16[4,48,2048]{2,1,0:T(8,128)(2,1)S(1)}, u32[]{:S(2)}, u32[]{:S(2)}) async-start(bf16[4,48,2048]{2,1,0:T(8,128)(2,1)} %bitcast.3), calls=%async_computation | async-start | bytes 1572864 | tf_op jit(solution)/shard_map/all_to_all | solution.py:373
  42.6 0.0 copy-done.4
  42.6 0.0 collective-permute-start.6
  42.6 0.5 collective-permute-start.7
  43.1 3.3 %collective-permute-done.8.rest_6_ = bf16[96,3584]{1,0:T(8,128)(2,1)} collective-permute-done((bf16[96,3584]{1,0:T(8,128)(2,1)S(1)}, bf16[96,3584]{1,0:T(8,128)(2,1)}, u32[]{:S(2)}, u32[]{:S(2)}) %collective-permute-start.8) | collective-permute-done | bytes 688160 | tf_op jit(solution)/shard_map/ppermute | solution.py:287
  46.3 0.0 collective-permute-start.9
  46.4 1.8 %collective-permute-start.10 = (bf16[96,3584]{1,0:T(8,128)(2,1)}, bf16[96,3584]{1,0:T(8,128)(2,1)}, u32[]{:S(2)}, u32[]{:S(2)}) collective-permute-start(bf16[96,3584]{1,0:T(8,128)(2,1)} %copy-done.9), channel_id=1, source_target_pairs={{0,4},{4,0},{1,5},{5,1},{2,6},{6,2},{3,7},{7,3},{8,12},{12,8},{9,1... | collective-permute-start | bytes 2064392 | tf_op jit(solution)/shard_map/ppermute | solution.py:287
  48.1 0.0 copy-done.2
  48.1 0.0 copy-start.8
  48.1 1.0 %copy-done.8 = bf16[384,512]{1,0:T(8,128)(2,1)S(1)} copy-done((bf16[384,512]{1,0:T(8,128)(2,1)S(1)}, bf16[384,512]{1,0:T(8,128)(2,1)}, u32[]{:S(2)}) %copy-start.8) | copy-done | bytes 393240
  49.1 0.9 %features.1.x_ref = bf16[512,768]{1,0:T(8,128)(2,1)S(1)} custom-call(s32[3]{0:T(128)S(1)} %pad_add_fusion.place, bf16[192,2048]{1,0:T(8,128)(2,1)S(1)} %copy-done.2, bf16[192,512]{1,0:T(8,128)(2,1)S(1)} %collective-permute-done.1.rest_1_, bf16[384,512]{1,0:T(8,128)(2,1)S(1)} %collective-permute-done.4.rest_2_, bf16[384,512]{1,0:T(8,128)(2,1)S(1)} %copy-done.8), custom_call_target="tpu_custom_call" | custom-call | flops 1 | bytes 1 | tf_op jit(solution)/shard_map/features/pallas_call | solution.py:31
  50.0 0.0 copy-start.6
  50.0 0.0 collective-permute-done.7.rest_5_
  50.0 0.0 collective-permute-done.6.rest_3_
  50.0 0.0 collective-permute-done.9.rest_7_
  50.0 18.1 %update.1 = (bf16[512,3584]{1,0:T(8,128)(2,1)}, f32[512,3584]{1,0:T(8,128)}, f32[512,3584]{1,0:T(8,128)}) custom-call(s32[3]{0:T(128)S(1)} %pad_add_fusion.place, bf16[512,768]{1,0:T(8,128)(2,1)S(1)} %features.1.x_ref, bf16[96,3584]{1,0:T(8,128)(2,1)} %rest_0_.5, bf16[96,3584]{1,0:T(8,128)(2,1)} %copy-done.10, bf16[96,3584]{1,0:T(8,128)(2,1)} %copy-done.4, ...), custom_call_target="tpu_custom_call" | custom-call | flops 1 | bytes 1 | tf_op jit(solution)/shard_map/update/pallas_call | solution.py:31
  68.1 0.0 all-to-all-done
  68.1 0.0 collective-permute-done.10.rest_1_
  68.2 0.0 copy-done.6
  68.2 2.8 %totals.1 = (bf16[48,2048]{1,0:T(8,128)(2,1)}, bf16[96,3584]{1,0:T(8,128)(2,1)}) custom-call(s32[3]{0:T(128)S(1)} %pad_add_fusion.place, bf16[192,2048]{1,0:T(8,128)(2,1)S(1)} %bitcast.5, bf16[96,3584]{1,0:T(8,128)(2,1)S(1)} %copy-done.6, bf16[96,3584]{1,0:T(8,128)(2,1)} %collective-permute-done.10.rest_1_), custom_call_target="tpu_custom_call" | custom-call | flops 1 | bytes 1 | tf_op jit(solution)/shard_map/totals/pallas_call | solution.py:31
Async XLA Ops:
  0.6 14.6 %collective-permute-start.3 = (bf16[96,3584]{1,0:T(8,128)(2,1)}, bf16[96,3584]{1,0:T(8,128)(2,1)S(1)}, u32[]{:S(2)}, u32[]{:S(2)}) collective-permute-start(bf16[96,3584]{1,0:T(8,128)(2,1)} %rest_0_.5), channel_id=1, source_target_pairs={{0,8},{8,0},{16,24},{24,16},{1,9},{9,1},{17,25},{25,17},{2,10},{10... | collective-permute-start | bytes 2064392 | tf_op jit(solution)/shard_map/ppermute | solution.py:293
  1.1 19.2 %collective-permute-start.2 = (bf16[96,3584]{1,0:T(8,128)(2,1)}, bf16[96,3584]{1,0:T(8,128)(2,1)}, u32[]{:S(2)}, u32[]{:S(2)}) collective-permute-start(bf16[96,3584]{1,0:T(8,128)(2,1)} %rest_0_.5), channel_id=1, source_target_pairs={{0,16},{8,24},{16,0},{24,8},{1,17},{9,25},{17,1},{25,9},{2,18},{10... | collective-permute-start | bytes 2064392 | tf_op jit(solution)/shard_map/ppermute | solution.py:287
  3.7 17.7 %collective-permute-start = (bf16[96,3584]{1,0:T(8,128)(2,1)}, bf16[96,3584]{1,0:T(8,128)(2,1)S(1)}, u32[]{:S(2)}, u32[]{:S(2)}) collective-permute-start(bf16[96,3584]{1,0:T(8,128)(2,1)} %rest_0_.5), channel_id=1, source_target_pairs={{0,4},{4,0},{1,5},{5,1},{2,6},{6,2},{3,7},{7,3},{8,12},{12,8},{9,1... | collective-permute-start | bytes 2064392 | tf_op jit(solution)/shard_map/ppermute | solution.py:287
  5.3 1.1 %copy-start.1 = (bf16[192,2048]{1,0:T(8,128)(2,1)S(1)}, bf16[192,2048]{1,0:T(8,128)(2,1)}, u32[]{:S(2)}) copy-start(bf16[192,2048]{1,0:T(8,128)(2,1)} %rest_0_.4) | copy-start | bytes 2359300
  6.4 23.7 %copy-start = (bf16[2048,3584]{1,0:T(8,128)(2,1)S(1)}, bf16[2048,3584]{1,0:T(8,128)(2,1)}, u32[]{:S(2)}) copy-start(bf16[2048,3584]{1,0:T(8,128)(2,1)} %rest_8_.1) | copy-start | bytes 44040196
  6.4 23.7 %copy-start.3 = (bf16[96,3584]{1,0:T(8,128)(2,1)S(1)}, bf16[96,3584]{1,0:T(8,128)(2,1)}, u32[]{:S(2)}) copy-start(bf16[96,3584]{1,0:T(8,128)(2,1)} %rest_0_.5) | copy-start | bytes 2064388
  13.2 24.3 %copy-start.5 = (bf16[96,3584]{1,0:T(8,128)(2,1)}, bf16[96,3584]{1,0:T(8,128)(2,1)S(1)}, u32[]{:S(2)}) copy-start(bf16[96,3584]{1,0:T(8,128)(2,1)S(1)} %get-tuple-element.19.rest_0_) | copy-start | bytes 2064388
  13.2 24.3 %copy-start.9 = (bf16[96,3584]{1,0:T(8,128)(2,1)}, bf16[96,3584]{1,0:T(8,128)(2,1)S(1)}, u32[]{:S(2)}) copy-start(bf16[96,3584]{1,0:T(8,128)(2,1)S(1)} %get-tuple-element.28) | copy-start | bytes 2064388
  13.2 15.1 %collective-permute-start.4 = (bf16[384,512]{1,0:T(8,128)(2,1)S(1)}, bf16[384,512]{1,0:T(8,128)(2,1)S(1)}, u32[]{:S(2)}, u32[]{:S(2)}) collective-permute-start(bf16[384,512]{1,0:T(8,128)(2,1)S(1)} %get-tuple-element.22), channel_id=1, source_target_pairs={{0,16},{8,24},{16,0},{24,8},{1,17},{9,25},{17,1},{25,9},{2,18},{10... | collective-permute-start | bytes 1179656 | tf_op jit(solution)/shard_map/ppermute | solution.py:287
  13.8 1.4 %collective-permute-start.1 = (bf16[192,512]{1,0:T(8,128)(2,1)S(1)}, bf16[192,512]{1,0:T(8,128)(2,1)S(1)}, u32[]{:S(2)}, u32[]{:S(2)}) collective-permute-start(bf16[192,512]{1,0:T(8,128)(2,1)S(1)} %get-tuple-element.20), channel_id=1, source_target_pairs={{0,8},{8,0},{16,24},{24,16},{1,9},{9,1},{17,25},{25,17},{2,10},{10... | collective-permute-start | bytes 589832 | tf_op jit(solution)/shard_map/ppermute | solution.py:293
  15.3 6.2 %copy-start.10 = (bf16[96,3584]{1,0:T(8,128)(2,1)}, bf16[96,3584]{1,0:T(8,128)(2,1)S(1)}, u32[]{:S(2)}) copy-start(bf16[96,3584]{1,0:T(8,128)(2,1)S(1)} %collective-permute-done.3.rest_1_) | copy-start | bytes 2064388
  21.4 21.1 %copy-start.4 = (bf16[96,3584]{1,0:T(8,128)(2,1)}, bf16[96,3584]{1,0:T(8,128)(2,1)S(1)}, u32[]{:S(2)}) copy-start(bf16[96,3584]{1,0:T(8,128)(2,1)S(1)} %collective-permute-done.rest_1_.rest_2_) | copy-start | bytes 2064388
  21.4 26.7 %copy-start.2 = (bf16[192,2048]{1,0:T(8,128)(2,1)S(1)}, bf16[192,2048]{1,0:T(8,128)(2,1)}, u32[]{:S(2)}) copy-start(bf16[192,2048]{1,0:T(8,128)(2,1)} %rest_0_.4) | copy-start | bytes 2359300
  28.4 1.8 %collective-permute-start.5 = (bf16[384,512]{1,0:T(8,128)(2,1)S(1)}, bf16[384,512]{1,0:T(8,128)(2,1)S(1)}, u32[]{:S(2)}, u32[]{:S(2)}) collective-permute-start(bf16[384,512]{1,0:T(8,128)(2,1)S(1)} %collective-permute-done.4.rest_2_), channel_id=1, source_target_pairs={{0,8},{8,0},{16,24},{24,16},{1,9},{9,1},{17,25},{25,17},{2,10},{10... | collective-permute-start | bytes 1179656 | tf_op jit(solution)/shard_map/ppermute | solution.py:293
  28.4 18.0 %collective-permute-start.8 = (bf16[96,3584]{1,0:T(8,128)(2,1)S(1)}, bf16[96,3584]{1,0:T(8,128)(2,1)}, u32[]{:S(2)}, u32[]{:S(2)}) collective-permute-start(bf16[96,3584]{1,0:T(8,128)(2,1)S(1)} %collective-permute-done.rest_1_.rest_2_), channel_id=1, source_target_pairs={{0,16},{8,24},{16,0},{24,8},{1,17},{9,25},{17,1},{25,9},{2,18},{10... | collective-permute-start | bytes 2064392 | tf_op jit(solution)/shard_map/ppermute | solution.py:287
  30.2 7.3 %copy-start.7 = (bf16[384,512]{1,0:T(8,128)(2,1)}, bf16[384,512]{1,0:T(8,128)(2,1)S(1)}, u32[]{:S(2)}) copy-start(bf16[384,512]{1,0:T(8,128)(2,1)S(1)} %collective-permute-done.5.rest_3_) | copy-start | bytes 1179652
  37.5 30.6 %all-to-all-start = ((bf16[4,48,2048]{2,1,0:T(8,128)(2,1)}), bf16[4,48,2048]{2,1,0:T(8,128)(2,1)S(1)}, u32[]{:S(2)}, u32[]{:S(2)}) async-start(bf16[4,48,2048]{2,1,0:T(8,128)(2,1)} %bitcast.3), calls=%async_computation | async-start | bytes 1572864 | tf_op jit(solution)/shard_map/all_to_all | solution.py:373
  42.6 7.4 %collective-permute-start.6 = (bf16[96,3584]{1,0:T(8,128)(2,1)S(1)}, bf16[96,3584]{1,0:T(8,128)(2,1)S(1)}, u32[]{:S(2)}, u32[]{:S(2)}) collective-permute-start(bf16[96,3584]{1,0:T(8,128)(2,1)S(1)} %collective-permute-done.rest_1_.rest_2_), channel_id=1, source_target_pairs={{0,8},{8,0},{16,24},{24,16},{1,9},{9,1},{17,25},{25,17},{2,10},{10... | collective-permute-start | bytes 2064392 | tf_op jit(solution)/shard_map/ppermute | solution.py:293
  42.6 7.4 %collective-permute-start.7 = (bf16[96,3584]{1,0:T(8,128)(2,1)}, bf16[96,3584]{1,0:T(8,128)(2,1)S(1)}, u32[]{:S(2)}, u32[]{:S(2)}) collective-permute-start(bf16[96,3584]{1,0:T(8,128)(2,1)} %collective-permute-done.2.rest_4_), channel_id=1, source_target_pairs={{0,8},{8,0},{16,24},{24,16},{1,9},{9,1},{17,25},{25,17},{2,10},{10... | collective-permute-start | bytes 2064392 | tf_op jit(solution)/shard_map/ppermute | solution.py:293
  46.3 3.7 %collective-permute-start.9 = (bf16[96,3584]{1,0:T(8,128)(2,1)}, bf16[96,3584]{1,0:T(8,128)(2,1)S(1)}, u32[]{:S(2)}, u32[]{:S(2)}) collective-permute-start(bf16[96,3584]{1,0:T(8,128)(2,1)} %collective-permute-done.8.rest_6_), channel_id=1, source_target_pairs={{0,8},{8,0},{16,24},{24,16},{1,9},{9,1},{17,25},{25,17},{2,10},{10... | collective-permute-start | bytes 2064392 | tf_op jit(solution)/shard_map/ppermute | solution.py:293
  46.4 21.8 %collective-permute-start.10 = (bf16[96,3584]{1,0:T(8,128)(2,1)}, bf16[96,3584]{1,0:T(8,128)(2,1)}, u32[]{:S(2)}, u32[]{:S(2)}) collective-permute-start(bf16[96,3584]{1,0:T(8,128)(2,1)} %copy-done.9), channel_id=1, source_target_pairs={{0,4},{4,0},{1,5},{5,1},{2,6},{6,2},{3,7},{7,3},{8,12},{12,8},{9,1... | collective-permute-start | bytes 2064392 | tf_op jit(solution)/shard_map/ppermute | solution.py:287
  48.1 1.0 %copy-start.8 = (bf16[384,512]{1,0:T(8,128)(2,1)S(1)}, bf16[384,512]{1,0:T(8,128)(2,1)}, u32[]{:S(2)}) copy-start(bf16[384,512]{1,0:T(8,128)(2,1)} %copy-done.7) | copy-start | bytes 1179652
  50.0 18.2 %copy-start.6 = (bf16[96,3584]{1,0:T(8,128)(2,1)S(1)}, bf16[96,3584]{1,0:T(8,128)(2,1)}, u32[]{:S(2)}) copy-start(bf16[96,3584]{1,0:T(8,128)(2,1)} %copy-done.5) | copy-start | bytes 2064388

commit v14 on v13

--- a/solution.py
+++ b/solution.py
@@ -336,7 +336,7 @@
     ]
     near = [swap_cores(to_send.pop(0))] if cores == 2 else []
     first = [by_chip[c, 0] for c in range(1, chips)]
-    far = [chip_shift(c)(to_send[c - 1]) for c in range(1, chips)]
+    far = [chip_shift(c)(after(to_send[c - 1], *first)) for c in range(1, chips)]
     for s in range(1, n_row):
         by_row[s] = after(by_row[s], parts[0], *near, *first, *swapped.values())
         if cores == 2:
@@ -351,7 +351,7 @@
     for c in range(1, chips):
         for f in flips:
             piece = far[c - 1]
-            held.append(swap_cores(after(piece, *first, *by_row[1:])) if f else piece)
+            held.append(swap_cores(piece) if f else piece)
             sources.append((functools.partial(dp_of, c=c, flip=f), f * tokens))
     if tiled:
         features = features_call(place, inputs, held, sources, slice_rows)
@@ -363,8 +363,7 @@
             tokens,
         )
     if tiled:
-        ready = [by_row[0]] + [after(piece, *held) for piece in by_row[1:]]
-        gpart = input_grad_call(place, ready, weight, n_row)
+        gpart = input_grad_call(place, by_row, weight, n_row)
     else:
         gathered = in_order(by_row, [lax.rem(row - s + n_row, n_row) for s in range(n_row)], own)
         gpart = lax.dot_general(
@@ -373,7 +372,7 @@
     gparts = lax.all_to_all(gpart, "col", 0, 0, tiled=True)
     for s in range(1, n_row):
         for c in range(1, chips):
-            by_chip[c, s] = chip_shift(c)(by_row[s])
+            by_chip[c, s] = along("row", n_row, s)(by_chip[c, 0])
     by_chip.update({(0, s): by_row[s] for s in range(n_row)})
     origins = []
     for c in range(chips):

time: 71.3 us -> 68.2 us (0.957)
  waiting for transfers between devices: 17.8 us -> 15 us
  local copies, waits for them, and re-layouts: 2.17 us -> 1.31 us
    ppermute x5, waiting for transfers between devices: 16.4 us -> 13.3 us  [along(): lax.ppermute(a, axis, [(i, (i + shift) % n) for i in range(n)])]
    ppermute x5, starting transfers between devices: 8.21 us -> 9.3 us  [along(): lax.ppermute(a, axis, [(i, (i + shift) % n) for i in range(n)])]
    unnamed x22 -> x16, local copies, waits for them, and re-layouts: 2.17 us -> 1.31 us
  transfers between devices with their start and end apart: 12 -> 12, of which waited for: 5 -> 5; matrix products, arithmetic and copies ran while one was open for 0% -> 0% of each run, Pallas kernels for 47% -> 49%
where the time goes in v14:
time: 68.2 us; the launch traced here: 68 us
  Pallas kernels  35.8 us (52%)
  starting transfers between devices  15 us (22%)
  waiting for transfers between devices  15 us (22%)
  local copies, waits for them, and re-layouts  1.31 us (2%)
  between operations  0.74 us (1%)
    pallas_call x5, Pallas kernels, run(): pl.pallas_call(kernel, name=name, grid_spec=pltpu.PrefetchScalarGridSpec(...  35.8 us
    ppermute x5, waiting for transfers between devices, along(): lax.ppermute(a, axis, [(i, (i + shift) % n) for i in range(n)])  13.3 us
    ppermute x5, starting transfers between devices, along(): lax.ppermute(a, axis, [(i, (i + shift) % n) for i in range(n)])  9.3 us
    all_to_all x1, starting transfers between devices, per_device(): gparts = lax.all_to_all(gpart, 'col', 0, 0, tiled=True)  4.87 us
    ppermute x6, waiting for transfers between devices, swap_cores(): return lax.ppermute(a, 'dp', [(i, i ^ 1) for i in range(n_dp)])  1.73 us
  transfers between devices with their start and end apart: 12, of which 5 were waited for; matrix products, arithmetic and copies ran while one was open for 0% of the time, Pallas kernels for 49%

profile of v14, /device:TPU:0, one launch (start us, length us, event | category | flops | bytes accessed | tf_op | source)
XLA Modules:
  0.0 68.0 jit_solution(16154554445792498681)
XLA Ops:
  0.6 3.0 %collective-permute-start.2 = (bf16[96,3584]{1,0:T(8,128)(2,1)}, bf16[96,3584]{1,0:T(8,128)(2,1)}, u32[]{:S(2)}, u32[]{:S(2)}) collective-permute-start(bf16[96,3584]{1,0:T(8,128)(2,1)} %rest_0_.5), channel_id=1, source_target_pairs={{0,16},{8,24},{16,0},{24,8},{1,17},{9,25},{17,1},{25,9},{2,18},{10... | collective-permute-start | bytes 2064392 | tf_op jit(solution)/shard_map/ppermute | solution.py:287
  3.6 0.0 collective-permute-start.3
  3.6 1.5 %collective-permute-start = (bf16[96,3584]{1,0:T(8,128)(2,1)}, bf16[96,3584]{1,0:T(8,128)(2,1)S(1)}, u32[]{:S(2)}, u32[]{:S(2)}) collective-permute-start(bf16[96,3584]{1,0:T(8,128)(2,1)} %rest_0_.5), channel_id=1, source_target_pairs={{0,4},{4,0},{1,5},{5,1},{2,6},{6,2},{3,7},{7,3},{8,12},{12,8},{9,1... | collective-permute-start | bytes 2064392 | tf_op jit(solution)/shard_map/ppermute | solution.py:287
  5.2 0.1 pad_add_fusion.place
  5.2 0.0 copy-start.1
  5.2 1.1 %copy-done.1 = bf16[192,2048]{1,0:T(8,128)(2,1)S(1)} copy-done((bf16[192,2048]{1,0:T(8,128)(2,1)S(1)}, bf16[192,2048]{1,0:T(8,128)(2,1)}, u32[]{:S(2)}) %copy-start.1) | copy-done | bytes 786456
  6.4 0.0 copy-start
  6.4 0.0 copy-start.3
  6.4 6.7 %forward.1 = (bf16[96,3584]{1,0:T(8,128)(2,1)S(1)}, bf16[96,3584]{1,0:T(8,128)(2,1)S(1)}, bf16[192,512]{1,0:T(8,128)(2,1)S(1)}, bf16[384,512]{1,0:T(8,128)(2,1)S(1)}) custom-call(s32[3]{0:T(128)S(1)} %pad_add_fusion.place, bf16[192,2048]{1,0:T(8,128)(2,1)S(1)} %copy-done.1, bf16[2048,3584]{1,0:T(8,128)(2,1)} %rest_8_.1), custom_call_target="tpu_custom_call" | custom-call | flops 1 | bytes 1 | tf_op jit(solution)/shard_map/forward/pallas_call | solution.py:31
  13.1 0.0 copy-start.5
  13.1 0.3 collective-permute-start.1
  13.4 6.0 %collective-permute-done.2.rest_4_ = bf16[96,3584]{1,0:T(8,128)(2,1)} collective-permute-done((bf16[96,3584]{1,0:T(8,128)(2,1)}, bf16[96,3584]{1,0:T(8,128)(2,1)}, u32[]{:S(2)}, u32[]{:S(2)}) %collective-permute-start.2) | collective-permute-done | bytes 688160 | tf_op jit(solution)/shard_map/ppermute | solution.py:287
  19.4 1.8 %collective-permute-start.8 = (bf16[96,3584]{1,0:T(8,128)(2,1)}, bf16[96,3584]{1,0:T(8,128)(2,1)}, u32[]{:S(2)}, u32[]{:S(2)}) collective-permute-start(bf16[96,3584]{1,0:T(8,128)(2,1)} %collective-permute-done.2.rest_4_), channel_id=1, source_target_pairs={{0,4},{4,0},{1,5},{5,1},{2,6},{6,2},{3,7},{7,3},{8,12},{12,8},{9,1... | collective-permute-start | bytes 2064392 | tf_op jit(solution)/shard_map/ppermute | solution.py:287
  21.2 0.0 collective-permute-done.1.rest_1_
  21.2 0.0 collective-permute-done.3.rest_1_
  21.2 0.0 copy-start.7
  21.2 0.7 %collective-permute-done.rest_1_.rest_2_ = bf16[96,3584]{1,0:T(8,128)(2,1)S(1)} collective-permute-done((bf16[96,3584]{1,0:T(8,128)(2,1)}, bf16[96,3584]{1,0:T(8,128)(2,1)S(1)}, u32[]{:S(2)}, u32[]{:S(2)}) %collective-permute-start) | collective-permute-done | bytes 688160 | tf_op jit(solution)/shard_map/ppermute | solution.py:287
  21.8 0.2 copy-done.7
  22.0 0.0 copy-start.4
  22.0 0.0 copy-done
  22.0 0.0 copy-done.3
  22.0 0.0 copy-start.2
  22.0 7.3 %input_grad.1 = bf16[192,2048]{1,0:T(8,128)(2,1)} custom-call(s32[3]{0:T(128)S(1)} %pad_add_fusion.place, bf16[96,3584]{1,0:T(8,128)(2,1)S(1)} %copy-done.3, bf16[96,3584]{1,0:T(8,128)(2,1)S(1)} %collective-permute-done.rest_1_.rest_2_, bf16[2048,3584]{1,0:T(8,128)(2,1)S(1)} %copy-done), custom_call_target="tpu_custom_call" | custom-call | flops 1 | bytes 1 | tf_op jit(solution)/shard_map/input_grad/pallas_call | solution.py:31
  29.4 0.0 copy-done.5
  29.4 4.9 %all-to-all-start = ((bf16[4,48,2048]{2,1,0:T(8,128)(2,1)}), bf16[4,48,2048]{2,1,0:T(8,128)(2,1)S(1)}, u32[]{:S(2)}, u32[]{:S(2)}) async-start(bf16[4,48,2048]{2,1,0:T(8,128)(2,1)} %bitcast.3), calls=%async_computation | async-start | bytes 1572864 | tf_op jit(solution)/shard_map/all_to_all | solution.py:372
  34.2 1.5 %collective-permute-start.4 = (bf16[384,512]{1,0:T(8,128)(2,1)S(1)}, bf16[384,512]{1,0:T(8,128)(2,1)S(1)}, u32[]{:S(2)}, u32[]{:S(2)}) collective-permute-start(bf16[384,512]{1,0:T(8,128)(2,1)S(1)} %get-tuple-element.22), channel_id=1, source_target_pairs={{0,16},{8,24},{16,0},{24,8},{1,17},{9,25},{17,1},{25,9},{2,18},{10... | collective-permute-start | bytes 1179656 | tf_op jit(solution)/shard_map/ppermute | solution.py:287
  35.7 0.0 copy-done.4
  35.7 0.0 collective-permute-start.6
  35.7 0.5 collective-permute-start.7
  36.2 0.3 collective-permute-done.8.rest_6_
  36.5 0.0 collective-permute-start.9
  36.6 1.5 %collective-permute-start.10 = (bf16[96,3584]{1,0:T(8,128)(2,1)S(1)}, bf16[96,3584]{1,0:T(8,128)(2,1)}, u32[]{:S(2)}, u32[]{:S(2)}) collective-permute-start(bf16[96,3584]{1,0:T(8,128)(2,1)S(1)} %get-tuple-element.26), channel_id=1, source_target_pairs={{0,4},{4,0},{1,5},{5,1},{2,6},{6,2},{3,7},{7,3},{8,12},{12,8},{9,1... | collective-permute-start | bytes 2064392 | tf_op jit(solution)/shard_map/ppermute | solution.py:287
  38.1 6.3 %collective-permute-done.4.rest_2_ = bf16[384,512]{1,0:T(8,128)(2,1)S(1)} collective-permute-done((bf16[384,512]{1,0:T(8,128)(2,1)S(1)}, bf16[384,512]{1,0:T(8,128)(2,1)S(1)}, u32[]{:S(2)}, u32[]{:S(2)}) %collective-permute-start.4) | collective-permute-done | bytes 393248 | tf_op jit(solution)/shard_map/ppermute | solution.py:287
  44.4 0.0 collective-permute-start.5
  44.4 1.7 %collective-permute-done.5.rest_3_ = bf16[384,512]{1,0:T(8,128)(2,1)S(1)} collective-permute-done((bf16[384,512]{1,0:T(8,128)(2,1)S(1)}, bf16[384,512]{1,0:T(8,128)(2,1)S(1)}, u32[]{:S(2)}, u32[]{:S(2)}) %collective-permute-start.5) | collective-permute-done | bytes 393248 | tf_op jit(solution)/shard_map/ppermute | solution.py:293
  46.1 0.0 copy-done.2
  46.1 0.9 %features.1.x_ref = bf16[512,768]{1,0:T(8,128)(2,1)S(1)} custom-call(s32[3]{0:T(128)S(1)} %pad_add_fusion.place, bf16[192,2048]{1,0:T(8,128)(2,1)S(1)} %copy-done.2, bf16[192,512]{1,0:T(8,128)(2,1)S(1)} %collective-permute-done.1.rest_1_, bf16[384,512]{1,0:T(8,128)(2,1)S(1)} %collective-permute-done.4.rest_2_, ...), custom_call_target="tpu_custom_call" | custom-call | flops 1 | bytes 1 | tf_op jit(solution)/shard_map/features/pallas_call | solution.py:31
  47.0 0.0 copy-start.6
  47.0 0.0 collective-permute-done.6.rest_3_
  47.0 0.0 collective-permute-done.7.rest_5_
  47.0 0.0 collective-permute-done.9.rest_7_
  47.0 18.1 %update.1 = (bf16[512,3584]{1,0:T(8,128)(2,1)}, f32[512,3584]{1,0:T(8,128)}, f32[512,3584]{1,0:T(8,128)}) custom-call(s32[3]{0:T(128)S(1)} %pad_add_fusion.place, bf16[512,768]{1,0:T(8,128)(2,1)S(1)} %features.1.x_ref, bf16[96,3584]{1,0:T(8,128)(2,1)} %rest_0_.5, bf16[96,3584]{1,0:T(8,128)(2,1)} %copy-done.7, bf16[96,3584]{1,0:T(8,128)(2,1)} %copy-done.4, ...), custom_call_target="tpu_custom_call" | custom-call | flops 1 | bytes 1 | tf_op jit(solution)/shard_map/update/pallas_call | solution.py:31
  65.1 0.0 all-to-all-done
  65.2 0.0 collective-permute-done.10.rest_1_
  65.2 0.0 copy-done.6
  65.2 2.8 %totals.1 = (bf16[48,2048]{1,0:T(8,128)(2,1)}, bf16[96,3584]{1,0:T(8,128)(2,1)}) custom-call(s32[3]{0:T(128)S(1)} %pad_add_fusion.place, bf16[192,2048]{1,0:T(8,128)(2,1)S(1)} %bitcast.5, bf16[96,3584]{1,0:T(8,128)(2,1)S(1)} %copy-done.6, bf16[96,3584]{1,0:T(8,128)(2,1)} %collective-permute-done.10.rest_1_), custom_call_target="tpu_custom_call" | custom-call | flops 1 | bytes 1 | tf_op jit(solution)/shard_map/totals/pallas_call | solution.py:31
Async XLA Ops:
  0.6 18.8 %collective-permute-start.2 = (bf16[96,3584]{1,0:T(8,128)(2,1)}, bf16[96,3584]{1,0:T(8,128)(2,1)}, u32[]{:S(2)}, u32[]{:S(2)}) collective-permute-start(bf16[96,3584]{1,0:T(8,128)(2,1)} %rest_0_.5), channel_id=1, source_target_pairs={{0,16},{8,24},{16,0},{24,8},{1,17},{9,25},{17,1},{25,9},{2,18},{10... | collective-permute-start | bytes 2064392 | tf_op jit(solution)/shard_map/ppermute | solution.py:287
  3.6 17.5 %collective-permute-start.3 = (bf16[96,3584]{1,0:T(8,128)(2,1)}, bf16[96,3584]{1,0:T(8,128)(2,1)S(1)}, u32[]{:S(2)}, u32[]{:S(2)}) collective-permute-start(bf16[96,3584]{1,0:T(8,128)(2,1)} %rest_0_.5), channel_id=1, source_target_pairs={{0,8},{8,0},{16,24},{24,16},{1,9},{9,1},{17,25},{25,17},{2,10},{10... | collective-permute-start | bytes 2064392 | tf_op jit(solution)/shard_map/ppermute | solution.py:293
  3.6 18.2 %collective-permute-start = (bf16[96,3584]{1,0:T(8,128)(2,1)}, bf16[96,3584]{1,0:T(8,128)(2,1)S(1)}, u32[]{:S(2)}, u32[]{:S(2)}) collective-permute-start(bf16[96,3584]{1,0:T(8,128)(2,1)} %rest_0_.5), channel_id=1, source_target_pairs={{0,4},{4,0},{1,5},{5,1},{2,6},{6,2},{3,7},{7,3},{8,12},{12,8},{9,1... | collective-permute-start | bytes 2064392 | tf_op jit(solution)/shard_map/ppermute | solution.py:287
  5.2 1.1 %copy-start.1 = (bf16[192,2048]{1,0:T(8,128)(2,1)S(1)}, bf16[192,2048]{1,0:T(8,128)(2,1)}, u32[]{:S(2)}) copy-start(bf16[192,2048]{1,0:T(8,128)(2,1)} %rest_0_.4) | copy-start | bytes 2359300
  6.4 15.6 %copy-start = (bf16[2048,3584]{1,0:T(8,128)(2,1)S(1)}, bf16[2048,3584]{1,0:T(8,128)(2,1)}, u32[]{:S(2)}) copy-start(bf16[2048,3584]{1,0:T(8,128)(2,1)} %rest_8_.1) | copy-start | bytes 44040196
  6.4 15.6 %copy-start.3 = (bf16[96,3584]{1,0:T(8,128)(2,1)S(1)}, bf16[96,3584]{1,0:T(8,128)(2,1)}, u32[]{:S(2)}) copy-start(bf16[96,3584]{1,0:T(8,128)(2,1)} %rest_0_.5) | copy-start | bytes 2064388
  13.1 16.2 %copy-start.5 = (bf16[96,3584]{1,0:T(8,128)(2,1)}, bf16[96,3584]{1,0:T(8,128)(2,1)S(1)}, u32[]{:S(2)}) copy-start(bf16[96,3584]{1,0:T(8,128)(2,1)S(1)} %get-tuple-element.18.rest_0_) | copy-start | bytes 2064388
  13.1 8.0 %collective-permute-start.1 = (bf16[192,512]{1,0:T(8,128)(2,1)S(1)}, bf16[192,512]{1,0:T(8,128)(2,1)S(1)}, u32[]{:S(2)}, u32[]{:S(2)}) collective-permute-start(bf16[192,512]{1,0:T(8,128)(2,1)S(1)} %get-tuple-element.19), channel_id=1, source_target_pairs={{0,8},{8,0},{16,24},{24,16},{1,9},{9,1},{17,25},{25,17},{2,10},{10... | collective-permute-start | bytes 589832 | tf_op jit(solution)/shard_map/ppermute | solution.py:293
  19.4 17.2 %collective-permute-start.8 = (bf16[96,3584]{1,0:T(8,128)(2,1)}, bf16[96,3584]{1,0:T(8,128)(2,1)}, u32[]{:S(2)}, u32[]{:S(2)}) collective-permute-start(bf16[96,3584]{1,0:T(8,128)(2,1)} %collective-permute-done.2.rest_4_), channel_id=1, source_target_pairs={{0,4},{4,0},{1,5},{5,1},{2,6},{6,2},{3,7},{7,3},{8,12},{12,8},{9,1... | collective-permute-start | bytes 2064392 | tf_op jit(solution)/shard_map/ppermute | solution.py:287
  21.2 0.8 %copy-start.7 = (bf16[96,3584]{1,0:T(8,128)(2,1)}, bf16[96,3584]{1,0:T(8,128)(2,1)S(1)}, u32[]{:S(2)}) copy-start(bf16[96,3584]{1,0:T(8,128)(2,1)S(1)} %collective-permute-done.3.rest_1_) | copy-start | bytes 2064388
  22.0 13.7 %copy-start.4 = (bf16[96,3584]{1,0:T(8,128)(2,1)}, bf16[96,3584]{1,0:T(8,128)(2,1)S(1)}, u32[]{:S(2)}) copy-start(bf16[96,3584]{1,0:T(8,128)(2,1)S(1)} %collective-permute-done.rest_1_.rest_2_) | copy-start | bytes 2064388
  22.0 24.1 %copy-start.2 = (bf16[192,2048]{1,0:T(8,128)(2,1)S(1)}, bf16[192,2048]{1,0:T(8,128)(2,1)}, u32[]{:S(2)}) copy-start(bf16[192,2048]{1,0:T(8,128)(2,1)} %rest_0_.4) | copy-start | bytes 2359300
  29.4 35.8 %all-to-all-start = ((bf16[4,48,2048]{2,1,0:T(8,128)(2,1)}), bf16[4,48,2048]{2,1,0:T(8,128)(2,1)S(1)}, u32[]{:S(2)}, u32[]{:S(2)}) async-start(bf16[4,48,2048]{2,1,0:T(8,128)(2,1)} %bitcast.3), calls=%async_computation | async-start | bytes 1572864 | tf_op jit(solution)/shard_map/all_to_all | solution.py:372
  34.2 10.2 %collective-permute-start.4 = (bf16[384,512]{1,0:T(8,128)(2,1)S(1)}, bf16[384,512]{1,0:T(8,128)(2,1)S(1)}, u32[]{:S(2)}, u32[]{:S(2)}) collective-permute-start(bf16[384,512]{1,0:T(8,128)(2,1)S(1)} %get-tuple-element.22), channel_id=1, source_target_pairs={{0,16},{8,24},{16,0},{24,8},{1,17},{9,25},{17,1},{25,9},{2,18},{10... | collective-permute-start | bytes 1179656 | tf_op jit(solution)/shard_map/ppermute | solution.py:287
  35.7 11.3 %collective-permute-start.6 = (bf16[96,3584]{1,0:T(8,128)(2,1)S(1)}, bf16[96,3584]{1,0:T(8,128)(2,1)S(1)}, u32[]{:S(2)}, u32[]{:S(2)}) collective-permute-start(bf16[96,3584]{1,0:T(8,128)(2,1)S(1)} %collective-permute-done.rest_1_.rest_2_), channel_id=1, source_target_pairs={{0,8},{8,0},{16,24},{24,16},{1,9},{9,1},{17,25},{25,17},{2,10},{10... | collective-permute-start | bytes 2064392 | tf_op jit(solution)/shard_map/ppermute | solution.py:293
  35.7 11.3 %collective-permute-start.7 = (bf16[96,3584]{1,0:T(8,128)(2,1)}, bf16[96,3584]{1,0:T(8,128)(2,1)S(1)}, u32[]{:S(2)}, u32[]{:S(2)}) collective-permute-start(bf16[96,3584]{1,0:T(8,128)(2,1)} %collective-permute-done.2.rest_4_), channel_id=1, source_target_pairs={{0,8},{8,0},{16,24},{24,16},{1,9},{9,1},{17,25},{25,17},{2,10},{10... | collective-permute-start | bytes 2064392 | tf_op jit(solution)/shard_map/ppermute | solution.py:293
  36.5 10.5 %collective-permute-start.9 = (bf16[96,3584]{1,0:T(8,128)(2,1)}, bf16[96,3584]{1,0:T(8,128)(2,1)S(1)}, u32[]{:S(2)}, u32[]{:S(2)}) collective-permute-start(bf16[96,3584]{1,0:T(8,128)(2,1)} %collective-permute-done.8.rest_6_), channel_id=1, source_target_pairs={{0,8},{8,0},{16,24},{24,16},{1,9},{9,1},{17,25},{25,17},{2,10},{10... | collective-permute-start | bytes 2064392 | tf_op jit(solution)/shard_map/ppermute | solution.py:293
  36.6 28.6 %collective-permute-start.10 = (bf16[96,3584]{1,0:T(8,128)(2,1)S(1)}, bf16[96,3584]{1,0:T(8,128)(2,1)}, u32[]{:S(2)}, u32[]{:S(2)}) collective-permute-start(bf16[96,3584]{1,0:T(8,128)(2,1)S(1)} %get-tuple-element.26), channel_id=1, source_target_pairs={{0,4},{4,0},{1,5},{5,1},{2,6},{6,2},{3,7},{7,3},{8,12},{12,8},{9,1... | collective-permute-start | bytes 2064392 | tf_op jit(solution)/shard_map/ppermute | solution.py:287
  44.4 1.7 %collective-permute-start.5 = (bf16[384,512]{1,0:T(8,128)(2,1)S(1)}, bf16[384,512]{1,0:T(8,128)(2,1)S(1)}, u32[]{:S(2)}, u32[]{:S(2)}) collective-permute-start(bf16[384,512]{1,0:T(8,128)(2,1)S(1)} %collective-permute-done.4.rest_2_), channel_id=1, source_target_pairs={{0,8},{8,0},{16,24},{24,16},{1,9},{9,1},{17,25},{25,17},{2,10},{10... | collective-permute-start | bytes 1179656 | tf_op jit(solution)/shard_map/ppermute | solution.py:293
  47.0 18.2 %copy-start.6 = (bf16[96,3584]{1,0:T(8,128)(2,1)S(1)}, bf16[96,3584]{1,0:T(8,128)(2,1)}, u32[]{:S(2)}) copy-start(bf16[96,3584]{1,0:T(8,128)(2,1)} %copy-done.5) | copy-start | bytes 2064388

commit v15 on v14

--- a/solution.py
+++ b/solution.py
@@ -394,7 +394,7 @@
                     first_swap = tiled and (c, s) == (0, 0)
                     pieces.append(in_hbm(swapped[c, s]) if first_swap else swapped[c, s])
                 else:
-                    pieces.append(swap_cores(by_chip[c, s]))
+                    pieces.append(swap_cores(after(by_chip[c, s], features)))
 
     if tiled:
         streamed = map(in_hbm, (weight, anchor, first_moment, second_moment))

time: 68.2 us -> 61.6 us (0.903)
  waiting for transfers between devices: 15 us -> 9.83 us
  Pallas kernels: 35.8 us -> 34.8 us
    ppermute x5, waiting for transfers between devices: 13.3 us -> 7.86 us  [along(): lax.ppermute(a, axis, [(i, (i + shift) % n) for i in range(n)])]
    pallas_call x5, Pallas kernels: 35.8 us -> 34.8 us  [run(): pl.pallas_call(kernel, name=name, grid_spec=pltpu.PrefetchScalarGridSpec(...]
  transfers between devices with their start and end apart: 12 -> 12, of which waited for: 5 -> 4; matrix products, arithmetic and copies ran while one was open for 0% -> 0% of each run, Pallas kernels for 49% -> 54%
where the time goes in v15:
time: 61.6 us; the launch traced here: 61.4 us
  Pallas kernels  34.8 us (56%)
  starting transfers between devices  14.8 us (24%)
  waiting for transfers between devices  9.83 us (16%)
  local copies, waits for them, and re-layouts  1.17 us (2%)
  between operations  0.75 us (1%)
    pallas_call x5, Pallas kernels, run(): pl.pallas_call(kernel, name=name, grid_spec=pltpu.PrefetchScalarGridSpec(...  34.8 us
    ppermute x5, starting transfers between devices, along(): lax.ppermute(a, axis, [(i, (i + shift) % n) for i in range(n)])  9.3 us
    ppermute x5, waiting for transfers between devices, along(): lax.ppermute(a, axis, [(i, (i + shift) % n) for i in range(n)])  7.86 us
    all_to_all x1, starting transfers between devices, per_device(): gparts = lax.all_to_all(gpart, 'col', 0, 0, tiled=True)  4.88 us
    ppermute x6, waiting for transfers between devices, swap_cores(): return lax.ppermute(a, 'dp', [(i, i ^ 1) for i in range(n_dp)])  1.97 us
  transfers between devices with their start and end apart: 12, of which 4 were waited for; matrix products, arithmetic and copies ran while one was open for 0% of the time, Pallas kernels for 54%

profile of v15, /device:TPU:0, one launch (start us, length us, event | category | flops | bytes accessed | tf_op | source)
XLA Modules:
  0.0 61.4 jit_solution(13334979549098330093)
XLA Ops:
  0.6 3.0 %collective-permute-start.2 = (bf16[96,3584]{1,0:T(8,128)(2,1)}, bf16[96,3584]{1,0:T(8,128)(2,1)}, u32[]{:S(2)}, u32[]{:S(2)}) collective-permute-start(bf16[96,3584]{1,0:T(8,128)(2,1)} %rest_0_.5), channel_id=1, source_target_pairs={{0,16},{8,24},{16,0},{24,8},{1,17},{9,25},{17,1},{25,9},{2,18},{10... | collective-permute-start | bytes 2064392 | tf_op jit(solution)/shard_map/ppermute | solution.py:287
  3.6 0.0 collective-permute-start.3
  3.6 1.5 %collective-permute-start = (bf16[96,3584]{1,0:T(8,128)(2,1)}, bf16[96,3584]{1,0:T(8,128)(2,1)S(1)}, u32[]{:S(2)}, u32[]{:S(2)}) collective-permute-start(bf16[96,3584]{1,0:T(8,128)(2,1)} %rest_0_.5), channel_id=1, source_target_pairs={{0,4},{4,0},{1,5},{5,1},{2,6},{6,2},{3,7},{7,3},{8,12},{12,8},{9,1... | collective-permute-start | bytes 2064392 | tf_op jit(solution)/shard_map/ppermute | solution.py:287
  5.2 0.1 pad_add_fusion.place
  5.2 0.0 copy-start.1
  5.2 1.1 %copy-done.1 = bf16[192,2048]{1,0:T(8,128)(2,1)S(1)} copy-done((bf16[192,2048]{1,0:T(8,128)(2,1)S(1)}, bf16[192,2048]{1,0:T(8,128)(2,1)}, u32[]{:S(2)}) %copy-start.1) | copy-done | bytes 786456
  6.4 0.0 copy-start
  6.4 0.0 copy-start.3
  6.4 6.9 %forward.1 = (bf16[96,3584]{1,0:T(8,128)(2,1)S(1)}, bf16[96,3584]{1,0:T(8,128)(2,1)S(1)}, bf16[192,512]{1,0:T(8,128)(2,1)S(1)}, bf16[384,512]{1,0:T(8,128)(2,1)}) custom-call(s32[3]{0:T(128)S(1)} %pad_add_fusion.place, bf16[192,2048]{1,0:T(8,128)(2,1)S(1)} %copy-done.1, bf16[2048,3584]{1,0:T(8,128)(2,1)} %rest_8_.1), custom_call_target="tpu_custom_call" | custom-call | flops 1 | bytes 1 | tf_op jit(solution)/shard_map/forward/pallas_call | solution.py:31
  13.3 0.0 copy-start.5
  13.3 6.1 %collective-permute-done.2.rest_4_ = bf16[96,3584]{1,0:T(8,128)(2,1)} collective-permute-done((bf16[96,3584]{1,0:T(8,128)(2,1)}, bf16[96,3584]{1,0:T(8,128)(2,1)}, u32[]{:S(2)}, u32[]{:S(2)}) %collective-permute-start.2) | collective-permute-done | bytes 688160 | tf_op jit(solution)/shard_map/ppermute | solution.py:287
  19.4 1.7 %collective-permute-start.4 = (bf16[384,512]{1,0:T(8,128)(2,1)}, bf16[384,512]{1,0:T(8,128)(2,1)S(1)}, u32[]{:S(2)}, u32[]{:S(2)}) collective-permute-start(bf16[384,512]{1,0:T(8,128)(2,1)} %get-tuple-element.23), channel_id=1, source_target_pairs={{0,16},{8,24},{16,0},{24,8},{1,17},{9,25},{17,1},{25,9},{2,18},{10... | collective-permute-start | bytes 1179656 | tf_op jit(solution)/shard_map/ppermute | solution.py:287
  21.1 0.0 collective-permute-start.1
  21.1 1.5 %collective-permute-start.8 = (bf16[96,3584]{1,0:T(8,128)(2,1)}, bf16[96,3584]{1,0:T(8,128)(2,1)}, u32[]{:S(2)}, u32[]{:S(2)}) collective-permute-start(bf16[96,3584]{1,0:T(8,128)(2,1)} %collective-permute-done.2.rest_4_), channel_id=1, source_target_pairs={{0,4},{4,0},{1,5},{5,1},{2,6},{6,2},{3,7},{7,3},{8,12},{12,8},{9,1... | collective-permute-start | bytes 2064392 | tf_op jit(solution)/shard_map/ppermute | solution.py:287
  22.6 0.0 collective-permute-done.1.rest_1_
  22.7 0.0 collective-permute-done.3.rest_1_
  22.7 0.0 copy-start.7
  22.7 0.0 collective-permute-done.rest_1_.rest_2_
  22.7 0.0 copy-start.4
  22.7 0.0 copy-done
  22.7 0.0 copy-done.3
  22.7 0.0 copy-start.2
  22.7 7.3 %input_grad.1 = bf16[192,2048]{1,0:T(8,128)(2,1)} custom-call(s32[3]{0:T(128)S(1)} %pad_add_fusion.place, bf16[96,3584]{1,0:T(8,128)(2,1)S(1)} %copy-done.3, bf16[96,3584]{1,0:T(8,128)(2,1)S(1)} %collective-permute-done.rest_1_.rest_2_, bf16[2048,3584]{1,0:T(8,128)(2,1)S(1)} %copy-done), custom_call_target="tpu_custom_call" | custom-call | flops 1 | bytes 1 | tf_op jit(solution)/shard_map/input_grad/pallas_call | solution.py:31
  30.0 0.0 copy-done.5
  30.0 0.0 copy-done.7
  30.0 4.9 %all-to-all-start = ((bf16[4,48,2048]{2,1,0:T(8,128)(2,1)}), bf16[4,48,2048]{2,1,0:T(8,128)(2,1)S(1)}, u32[]{:S(2)}, u32[]{:S(2)}) async-start(bf16[4,48,2048]{2,1,0:T(8,128)(2,1)} %bitcast.3), calls=%async_computation | async-start | bytes 1572864 | tf_op jit(solution)/shard_map/all_to_all | solution.py:372
  34.9 0.0 collective-permute-done.4.rest_2_
  34.9 0.0 collective-permute-start.5
  34.9 0.0 copy-done.4
  34.9 0.5 collective-permute-start.6
  35.4 0.1 collective-permute-start.7
  35.5 1.1 %collective-permute-done.5.rest_3_ = bf16[384,512]{1,0:T(8,128)(2,1)S(1)} collective-permute-done((bf16[384,512]{1,0:T(8,128)(2,1)S(1)}, bf16[384,512]{1,0:T(8,128)(2,1)S(1)}, u32[]{:S(2)}, u32[]{:S(2)}) %collective-permute-start.5) | collective-permute-done | bytes 393248 | tf_op jit(solution)/shard_map/ppermute | solution.py:293
  36.6 0.0 copy-done.2
  36.7 0.9 %features.1.x_ref = bf16[512,768]{1,0:T(8,128)(2,1)S(1)} custom-call(s32[3]{0:T(128)S(1)} %pad_add_fusion.place, bf16[192,2048]{1,0:T(8,128)(2,1)S(1)} %copy-done.2, bf16[192,512]{1,0:T(8,128)(2,1)S(1)} %collective-permute-done.1.rest_1_, bf16[384,512]{1,0:T(8,128)(2,1)S(1)} %collective-permute-done.4.rest_2_, ...), custom_call_target="tpu_custom_call" | custom-call | flops 1 | bytes 1 | tf_op jit(solution)/shard_map/features/pallas_call | solution.py:31
  37.5 1.8 %collective-permute-done.8.rest_6_ = bf16[96,3584]{1,0:T(8,128)(2,1)} collective-permute-done((bf16[96,3584]{1,0:T(8,128)(2,1)}, bf16[96,3584]{1,0:T(8,128)(2,1)}, u32[]{:S(2)}, u32[]{:S(2)}) %collective-permute-start.8) | collective-permute-done | bytes 688160 | tf_op jit(solution)/shard_map/ppermute | solution.py:287
  39.3 0.0 collective-permute-start.9
  39.3 0.0 copy-start.6
  39.3 1.5 %collective-permute-start.10 = (bf16[96,3584]{1,0:T(8,128)(2,1)S(1)}, bf16[96,3584]{1,0:T(8,128)(2,1)S(1)}, u32[]{:S(2)}, u32[]{:S(2)}) collective-permute-start(bf16[96,3584]{1,0:T(8,128)(2,1)S(1)} %get-tuple-element.28), channel_id=1, source_target_pairs={{0,4},{4,0},{1,5},{5,1},{2,6},{6,2},{3,7},{7,3},{8,12},{12,8},{9,1... | collective-permute-start | bytes 2064392 | tf_op jit(solution)/shard_map/ppermute | solution.py:287
  40.8 0.0 collective-permute-done.6.rest_3_
  40.8 0.0 collective-permute-done.7.rest_5_
  40.8 0.8 %collective-permute-done.9.rest_7_ = bf16[96,3584]{1,0:T(8,128)(2,1)S(1)} collective-permute-done((bf16[96,3584]{1,0:T(8,128)(2,1)}, bf16[96,3584]{1,0:T(8,128)(2,1)S(1)}, u32[]{:S(2)}, u32[]{:S(2)}) %collective-permute-start.9) | collective-permute-done | bytes 688160 | tf_op jit(solution)/shard_map/ppermute | solution.py:293
  41.6 18.1 %update.1 = (bf16[512,3584]{1,0:T(8,128)(2,1)}, f32[512,3584]{1,0:T(8,128)}, f32[512,3584]{1,0:T(8,128)}) custom-call(s32[3]{0:T(128)S(1)} %pad_add_fusion.place, bf16[512,768]{1,0:T(8,128)(2,1)S(1)} %features.1.x_ref, bf16[96,3584]{1,0:T(8,128)(2,1)} %rest_0_.5, bf16[96,3584]{1,0:T(8,128)(2,1)} %copy-done.7, bf16[96,3584]{1,0:T(8,128)(2,1)} %copy-done.4, ...), custom_call_target="tpu_custom_call" | custom-call | flops 1 | bytes 1 | tf_op jit(solution)/shard_map/update/pallas_call | solution.py:31
  59.7 0.0 all-to-all-done
  59.7 0.0 collective-permute-done.10.rest_1_
  59.8 0.0 copy-done.6
  59.8 1.6 %totals.1 = (bf16[48,2048]{1,0:T(8,128)(2,1)}, bf16[96,3584]{1,0:T(8,128)(2,1)}) custom-call(s32[3]{0:T(128)S(1)} %pad_add_fusion.place, bf16[192,2048]{1,0:T(8,128)(2,1)S(1)} %bitcast.5, bf16[96,3584]{1,0:T(8,128)(2,1)S(1)} %copy-done.6, bf16[96,3584]{1,0:T(8,128)(2,1)S(1)} %collective-permute-done.10.rest_1_), custom_call_target="tpu_custom_call" | custom-call | flops 1 | bytes 1 | tf_op jit(solution)/shard_map/totals/pallas_call | solution.py:31
Async XLA Ops:
  0.6 18.8 %collective-permute-start.2 = (bf16[96,3584]{1,0:T(8,128)(2,1)}, bf16[96,3584]{1,0:T(8,128)(2,1)}, u32[]{:S(2)}, u32[]{:S(2)}) collective-permute-start(bf16[96,3584]{1,0:T(8,128)(2,1)} %rest_0_.5), channel_id=1, source_target_pairs={{0,16},{8,24},{16,0},{24,8},{1,17},{9,25},{17,1},{25,9},{2,18},{10... | collective-permute-start | bytes 2064392 | tf_op jit(solution)/shard_map/ppermute | solution.py:287
  3.6 19.0 %collective-permute-start.3 = (bf16[96,3584]{1,0:T(8,128)(2,1)}, bf16[96,3584]{1,0:T(8,128)(2,1)S(1)}, u32[]{:S(2)}, u32[]{:S(2)}) collective-permute-start(bf16[96,3584]{1,0:T(8,128)(2,1)} %rest_0_.5), channel_id=1, source_target_pairs={{0,8},{8,0},{16,24},{24,16},{1,9},{9,1},{17,25},{25,17},{2,10},{10... | collective-permute-start | bytes 2064392 | tf_op jit(solution)/shard_map/ppermute | solution.py:293
  3.6 19.0 %collective-permute-start = (bf16[96,3584]{1,0:T(8,128)(2,1)}, bf16[96,3584]{1,0:T(8,128)(2,1)S(1)}, u32[]{:S(2)}, u32[]{:S(2)}) collective-permute-start(bf16[96,3584]{1,0:T(8,128)(2,1)} %rest_0_.5), channel_id=1, source_target_pairs={{0,4},{4,0},{1,5},{5,1},{2,6},{6,2},{3,7},{7,3},{8,12},{12,8},{9,1... | collective-permute-start | bytes 2064392 | tf_op jit(solution)/shard_map/ppermute | solution.py:287
  5.2 1.1 %copy-start.1 = (bf16[192,2048]{1,0:T(8,128)(2,1)S(1)}, bf16[192,2048]{1,0:T(8,128)(2,1)}, u32[]{:S(2)}) copy-start(bf16[192,2048]{1,0:T(8,128)(2,1)} %rest_0_.4) | copy-start | bytes 2359300
  6.4 16.3 %copy-start = (bf16[2048,3584]{1,0:T(8,128)(2,1)S(1)}, bf16[2048,3584]{1,0:T(8,128)(2,1)}, u32[]{:S(2)}) copy-start(bf16[2048,3584]{1,0:T(8,128)(2,1)} %rest_8_.1) | copy-start | bytes 44040196
  6.4 16.3 %copy-start.3 = (bf16[96,3584]{1,0:T(8,128)(2,1)S(1)}, bf16[96,3584]{1,0:T(8,128)(2,1)}, u32[]{:S(2)}) copy-start(bf16[96,3584]{1,0:T(8,128)(2,1)} %rest_0_.5) | copy-start | bytes 2064388
  13.3 16.7 %copy-start.5 = (bf16[96,3584]{1,0:T(8,128)(2,1)}, bf16[96,3584]{1,0:T(8,128)(2,1)S(1)}, u32[]{:S(2)}) copy-start(bf16[96,3584]{1,0:T(8,128)(2,1)S(1)} %get-tuple-element.19.rest_0_) | copy-start | bytes 2064388
  19.4 15.5 %collective-permute-start.4 = (bf16[384,512]{1,0:T(8,128)(2,1)}, bf16[384,512]{1,0:T(8,128)(2,1)S(1)}, u32[]{:S(2)}, u32[]{:S(2)}) collective-permute-start(bf16[384,512]{1,0:T(8,128)(2,1)} %get-tuple-element.23), channel_id=1, source_target_pairs={{0,16},{8,24},{16,0},{24,8},{1,17},{9,25},{17,1},{25,9},{2,18},{10... | collective-permute-start | bytes 1179656 | tf_op jit(solution)/shard_map/ppermute | solution.py:287
  21.1 1.5 %collective-permute-start.1 = (bf16[192,512]{1,0:T(8,128)(2,1)S(1)}, bf16[192,512]{1,0:T(8,128)(2,1)S(1)}, u32[]{:S(2)}, u32[]{:S(2)}) collective-permute-start(bf16[192,512]{1,0:T(8,128)(2,1)S(1)} %get-tuple-element.20), channel_id=1, source_target_pairs={{0,8},{8,0},{16,24},{24,16},{1,9},{9,1},{17,25},{25,17},{2,10},{10... | collective-permute-start | bytes 589832 | tf_op jit(solution)/shard_map/ppermute | solution.py:293
  21.1 18.2 %collective-permute-start.8 = (bf16[96,3584]{1,0:T(8,128)(2,1)}, bf16[96,3584]{1,0:T(8,128)(2,1)}, u32[]{:S(2)}, u32[]{:S(2)}) collective-permute-start(bf16[96,3584]{1,0:T(8,128)(2,1)} %collective-permute-done.2.rest_4_), channel_id=1, source_target_pairs={{0,4},{4,0},{1,5},{5,1},{2,6},{6,2},{3,7},{7,3},{8,12},{12,8},{9,1... | collective-permute-start | bytes 2064392 | tf_op jit(solution)/shard_map/ppermute | solution.py:287
  22.7 7.4 %copy-start.7 = (bf16[96,3584]{1,0:T(8,128)(2,1)}, bf16[96,3584]{1,0:T(8,128)(2,1)S(1)}, u32[]{:S(2)}) copy-start(bf16[96,3584]{1,0:T(8,128)(2,1)S(1)} %collective-permute-done.3.rest_1_) | copy-start | bytes 2064388
  22.7 12.3 %copy-start.4 = (bf16[96,3584]{1,0:T(8,128)(2,1)}, bf16[96,3584]{1,0:T(8,128)(2,1)S(1)}, u32[]{:S(2)}) copy-start(bf16[96,3584]{1,0:T(8,128)(2,1)S(1)} %collective-permute-done.rest_1_.rest_2_) | copy-start | bytes 2064388
  22.7 14.0 %copy-start.2 = (bf16[192,2048]{1,0:T(8,128)(2,1)S(1)}, bf16[192,2048]{1,0:T(8,128)(2,1)}, u32[]{:S(2)}) copy-start(bf16[192,2048]{1,0:T(8,128)(2,1)} %rest_0_.4) | copy-start | bytes 2359300
  30.0 29.7 %all-to-all-start = ((bf16[4,48,2048]{2,1,0:T(8,128)(2,1)}), bf16[4,48,2048]{2,1,0:T(8,128)(2,1)S(1)}, u32[]{:S(2)}, u32[]{:S(2)}) async-start(bf16[4,48,2048]{2,1,0:T(8,128)(2,1)} %bitcast.3), calls=%async_computation | async-start | bytes 1572864 | tf_op jit(solution)/shard_map/all_to_all | solution.py:372
  34.9 1.7 %collective-permute-start.5 = (bf16[384,512]{1,0:T(8,128)(2,1)S(1)}, bf16[384,512]{1,0:T(8,128)(2,1)S(1)}, u32[]{:S(2)}, u32[]{:S(2)}) collective-permute-start(bf16[384,512]{1,0:T(8,128)(2,1)S(1)} %collective-permute-done.4.rest_2_), channel_id=1, source_target_pairs={{0,8},{8,0},{16,24},{24,16},{1,9},{9,1},{17,25},{25,17},{2,10},{10... | collective-permute-start | bytes 1179656 | tf_op jit(solution)/shard_map/ppermute | solution.py:293
  34.9 5.9 %collective-permute-start.6 = (bf16[96,3584]{1,0:T(8,128)(2,1)S(1)}, bf16[96,3584]{1,0:T(8,128)(2,1)S(1)}, u32[]{:S(2)}, u32[]{:S(2)}) collective-permute-start(bf16[96,3584]{1,0:T(8,128)(2,1)S(1)} %collective-permute-done.rest_1_.rest_2_), channel_id=1, source_target_pairs={{0,8},{8,0},{16,24},{24,16},{1,9},{9,1},{17,25},{25,17},{2,10},{10... | collective-permute-start | bytes 2064392 | tf_op jit(solution)/shard_map/ppermute | solution.py:293
  35.4 5.4 %collective-permute-start.7 = (bf16[96,3584]{1,0:T(8,128)(2,1)}, bf16[96,3584]{1,0:T(8,128)(2,1)S(1)}, u32[]{:S(2)}, u32[]{:S(2)}) collective-permute-start(bf16[96,3584]{1,0:T(8,128)(2,1)} %collective-permute-done.2.rest_4_), channel_id=1, source_target_pairs={{0,8},{8,0},{16,24},{24,16},{1,9},{9,1},{17,25},{25,17},{2,10},{10... | collective-permute-start | bytes 2064392 | tf_op jit(solution)/shard_map/ppermute | solution.py:293
  39.3 2.4 %collective-permute-start.9 = (bf16[96,3584]{1,0:T(8,128)(2,1)}, bf16[96,3584]{1,0:T(8,128)(2,1)S(1)}, u32[]{:S(2)}, u32[]{:S(2)}) collective-permute-start(bf16[96,3584]{1,0:T(8,128)(2,1)} %collective-permute-done.8.rest_6_), channel_id=1, source_target_pairs={{0,8},{8,0},{16,24},{24,16},{1,9},{9,1},{17,25},{25,17},{2,10},{10... | collective-permute-start | bytes 2064392 | tf_op jit(solution)/shard_map/ppermute | solution.py:293
  39.3 20.5 %copy-start.6 = (bf16[96,3584]{1,0:T(8,128)(2,1)S(1)}, bf16[96,3584]{1,0:T(8,128)(2,1)}, u32[]{:S(2)}) copy-start(bf16[96,3584]{1,0:T(8,128)(2,1)} %copy-done.5) | copy-start | bytes 2064388
  39.3 20.5 %collective-permute-start.10 = (bf16[96,3584]{1,0:T(8,128)(2,1)S(1)}, bf16[96,3584]{1,0:T(8,128)(2,1)S(1)}, u32[]{:S(2)}, u32[]{:S(2)}) collective-permute-start(bf16[96,3584]{1,0:T(8,128)(2,1)S(1)} %get-tuple-element.28), channel_id=1, source_target_pairs={{0,4},{4,0},{1,5},{5,1},{2,6},{6,2},{3,7},{7,3},{8,12},{12,8},{9,1... | collective-permute-start | bytes 2064392 | tf_op jit(solution)/shard_map/ppermute | solution.py:287

commit v16 on v15

--- a/solution.py
+++ b/solution.py
@@ -146,26 +146,33 @@
 
 def features_kernel(sources, tokens, place, *rest):
     n = len(sources)
-    pieces, out, xs = rest[:n], rest[n], rest[n + 1]
+    pieces, moment, out, held, xs, sem = rest[:n], *rest[n:]
+    copy = pltpu.make_async_copy(moment, held, sem)
+    copy.start()
     for piece, (origin, skip) in zip(pieces, sources):
         start = pl.multiple_of(origin(place[0]) * tokens, tokens)
         xs[pl.ds(start, tokens), :] = piece[skip : skip + tokens, :]
     out[...] = xs[...].T
-
-
-def features_call(place, inputs, held, sources, slice_rows):
+    copy.wait()
+
+
+def features_call(place, inputs, held, sources, slice_rows, moment):
     tokens, n_dp = inputs.shape[0], len(sources)
     return run(
         functools.partial(features_kernel, sources, tokens),
         "features",
         (1,),
         [pl.BlockSpec((tokens, slice_rows), lambda j, place: (0, place[0]))]
-        + [fixed(piece.shape) for piece in held],
-        fixed((slice_rows, n_dp * tokens)),
-        struct((slice_rows, n_dp * tokens), BF16),
-        [pltpu.VMEM((n_dp * tokens, slice_rows), BF16)],
+        + [fixed(piece.shape) for piece in held]
+        + [pl.BlockSpec(memory_space=pltpu.HBM)],
+        [fixed((slice_rows, n_dp * tokens)), pl.BlockSpec(memory_space=pl.ANY)],
+        [
+            struct((slice_rows, n_dp * tokens), BF16),
+            pltpu.VMEM(moment.shape, moment.dtype),
+        ],
+        [pltpu.VMEM((n_dp * tokens, slice_rows), BF16), pltpu.SemaphoreType.DMA],
         6,
-        (place, inputs, *held),
+        (place, inputs, *held, in_hbm(moment)),
     )
 
 
@@ -262,7 +269,7 @@
         [tile] * 3,
         [struct((rows, width), BF16), struct((rows, width), F32), struct((rows, width), F32)],
         [pltpu.VMEM((tokens_all, width), BF16)],
-        38,
+        31,
         (place, features, *pieces, *held),
     )
 
@@ -354,7 +361,9 @@
             held.append(swap_cores(piece) if f else piece)
             sources.append((functools.partial(dp_of, c=c, flip=f), f * tokens))
     if tiled:
-        features = features_call(place, inputs, held, sources, slice_rows)
+        features, first_held = features_call(
+            place, inputs, held, sources, slice_rows, first_moment
+        )
     else:
         mine = lax.dynamic_slice_in_dim(inputs, dp * slice_rows, slice_rows, 1)
         features = in_order(
@@ -397,9 +406,9 @@
                     pieces.append(swap_cores(after(by_chip[c, s], features)))
 
     if tiled:
-        streamed = map(in_hbm, (weight, anchor, first_moment, second_moment))
+        streamed = (in_hbm(weight), in_hbm(anchor), first_held, in_hbm(second_moment))
         new_weight, new_first, new_second = update_call(
-            place, features, pieces, origins, tuple(streamed)
+            place, features, pieces, origins, streamed
         )
     else:
         gathered = in_order(pieces, [origin(dp, row) for origin in origins], own)

time: 61.6 us -> 63.6 us (1.032)
  Pallas kernels: 34.8 us -> 37 us
  local copies, waits for them, and re-layouts: 1.17 us -> 2.01 us
  starting transfers between devices: 14.8 us -> 14 us
    ppermute x5, waiting for transfers between devices: 7.86 us -> 5.41 us  [along(): lax.ppermute(a, axis, [(i, (i + shift) % n) for i in range(n)])]
    ppermute x6, waiting for transfers between devices: 1.97 us -> 4.26 us  [swap_cores(): return lax.ppermute(a, 'dp', [(i, i ^ 1) for i in range(n_dp)])]
    pallas_call x5, Pallas kernels: 34.8 us -> 37 us  [run(): pl.pallas_call(kernel, name=name, grid_spec=pltpu.PrefetchScalarGridSpec(...]
    ppermute x5, starting transfers between devices: 9.3 us -> 8.3 us  [along(): lax.ppermute(a, axis, [(i, (i + shift) % n) for i in range(n)])]
    unnamed x16, local copies, waits for them, and re-layouts: 1.17 us -> 2.01 us
  transfers between devices with their start and end apart: 12 -> 12, of which waited for: 4 -> 4; matrix products, arithmetic and copies ran while one was open for 0% -> 0% of each run, Pallas kernels for 54% -> 56%
where the time goes in v16:
time: 63.6 us; the launch traced here: 63.4 us
  Pallas kernels  37 us (58%)
  starting transfers between devices  14 us (22%)
  waiting for transfers between devices  9.68 us (15%)
  local copies, waits for them, and re-layouts  2.01 us (3%)
  between operations  0.72 us (1%)
    pallas_call x5, Pallas kernels, run(): pl.pallas_call(kernel, name=name, grid_spec=pltpu.PrefetchScalarGridSpec(...  37 us
    ppermute x5, starting transfers between devices, along(): lax.ppermute(a, axis, [(i, (i + shift) % n) for i in range(n)])  8.3 us
    ppermute x5, waiting for transfers between devices, along(): lax.ppermute(a, axis, [(i, (i + shift) % n) for i in range(n)])  5.41 us
    all_to_all x1, starting transfers between devices, per_device(): gparts = lax.all_to_all(gpart, 'col', 0, 0, tiled=True)  4.87 us
    ppermute x6, waiting for transfers between devices, swap_cores(): return lax.ppermute(a, 'dp', [(i, i ^ 1) for i in range(n_dp)])  4.26 us
    unnamed x16, local copies, waits for them, and re-layouts  2.01 us
  transfers between devices with their start and end apart: 12, of which 4 were waited for; matrix products, arithmetic and copies ran while one was open for 0% of the time, Pallas kernels for 56%

profile of v16, /device:TPU:0, one launch (start us, length us, event | category | flops | bytes accessed | tf_op | source)
XLA Modules:
  0.0 63.4 jit_solution(18240492554868616819)
XLA Ops:
  0.6 3.0 %collective-permute-start.2 = (bf16[96,3584]{1,0:T(8,128)(2,1)}, bf16[96,3584]{1,0:T(8,128)(2,1)}, u32[]{:S(2)}, u32[]{:S(2)}) collective-permute-start(bf16[96,3584]{1,0:T(8,128)(2,1)} %rest_0_.5), channel_id=1, source_target_pairs={{0,16},{8,24},{16,0},{24,8},{1,17},{9,25},{17,1},{25,9},{2,18},{10... | collective-permute-start | bytes 2064392 | tf_op jit(solution)/shard_map/ppermute | solution.py:294
  3.6 0.0 collective-permute-start.3
  3.6 1.5 %collective-permute-start = (bf16[96,3584]{1,0:T(8,128)(2,1)}, bf16[96,3584]{1,0:T(8,128)(2,1)S(1)}, u32[]{:S(2)}, u32[]{:S(2)}) collective-permute-start(bf16[96,3584]{1,0:T(8,128)(2,1)} %rest_0_.5), channel_id=1, source_target_pairs={{0,4},{4,0},{1,5},{5,1},{2,6},{6,2},{3,7},{7,3},{8,12},{12,8},{9,1... | collective-permute-start | bytes 2064392 | tf_op jit(solution)/shard_map/ppermute | solution.py:294
  5.2 0.1 pad_add_fusion.place
  5.2 0.0 copy-start.1
  5.2 1.1 %copy-done.1 = bf16[192,2048]{1,0:T(8,128)(2,1)S(1)} copy-done((bf16[192,2048]{1,0:T(8,128)(2,1)S(1)}, bf16[192,2048]{1,0:T(8,128)(2,1)}, u32[]{:S(2)}) %copy-start.1) | copy-done | bytes 786456
  6.4 0.0 copy-start
  6.4 0.0 copy-start.3
  6.4 7.6 %forward.1 = (bf16[96,3584]{1,0:T(8,128)(2,1)S(1)}, bf16[96,3584]{1,0:T(8,128)(2,1)}, bf16[192,512]{1,0:T(8,128)(2,1)S(1)}, bf16[384,512]{1,0:T(8,128)(2,1)}) custom-call(s32[3]{0:T(128)S(1)} %pad_add_fusion.place, bf16[192,2048]{1,0:T(8,128)(2,1)S(1)} %copy-done.1, bf16[2048,3584]{1,0:T(8,128)(2,1)} %rest_8_.1), custom_call_target="tpu_custom_call" | custom-call | flops 1 | bytes 1 | tf_op jit(solution)/shard_map/forward/pallas_call | solution.py:31
  14.0 0.0 copy-start.5
  14.0 5.4 %collective-permute-done.2.rest_4_ = bf16[96,3584]{1,0:T(8,128)(2,1)} collective-permute-done((bf16[96,3584]{1,0:T(8,128)(2,1)}, bf16[96,3584]{1,0:T(8,128)(2,1)}, u32[]{:S(2)}, u32[]{:S(2)}) %collective-permute-start.2) | collective-permute-done | bytes 688160 | tf_op jit(solution)/shard_map/ppermute | solution.py:294
  19.4 1.7 %collective-permute-start.4 = (bf16[384,512]{1,0:T(8,128)(2,1)}, bf16[384,512]{1,0:T(8,128)(2,1)S(1)}, u32[]{:S(2)}, u32[]{:S(2)}) collective-permute-start(bf16[384,512]{1,0:T(8,128)(2,1)} %get-tuple-element.25), channel_id=1, source_target_pairs={{0,16},{8,24},{16,0},{24,8},{1,17},{9,25},{17,1},{25,9},{2,18},{10... | collective-permute-start | bytes 1179656 | tf_op jit(solution)/shard_map/ppermute | solution.py:294
  21.1 1.5 %collective-permute-start.8 = (bf16[96,3584]{1,0:T(8,128)(2,1)}, bf16[96,3584]{1,0:T(8,128)(2,1)}, u32[]{:S(2)}, u32[]{:S(2)}) collective-permute-start(bf16[96,3584]{1,0:T(8,128)(2,1)} %collective-permute-done.2.rest_4_), channel_id=1, source_target_pairs={{0,4},{4,0},{1,5},{5,1},{2,6},{6,2},{3,7},{7,3},{8,12},{12,8},{9,1... | collective-permute-start | bytes 2064392 | tf_op jit(solution)/shard_map/ppermute | solution.py:294
  22.6 0.0 collective-permute-start.1
  22.6 1.4 %collective-permute-done.1.rest_1_ = bf16[192,512]{1,0:T(8,128)(2,1)S(1)} collective-permute-done((bf16[192,512]{1,0:T(8,128)(2,1)S(1)}, bf16[192,512]{1,0:T(8,128)(2,1)S(1)}, u32[]{:S(2)}, u32[]{:S(2)}) %collective-permute-start.1) | collective-permute-done | bytes 196640 | tf_op jit(solution)/shard_map/ppermute | solution.py:300
  24.1 0.0 collective-permute-done.3.rest_1_
  24.1 0.0 copy-start.7
  24.1 0.0 collective-permute-done.rest_1_.rest_2_
  24.1 0.9 %copy-done.7 = bf16[96,3584]{1,0:T(8,128)(2,1)} copy-done((bf16[96,3584]{1,0:T(8,128)(2,1)}, bf16[96,3584]{1,0:T(8,128)(2,1)S(1)}, u32[]{:S(2)}) %copy-start.7) | copy-done | bytes 688152
  25.0 0.0 copy-start.4
  25.0 0.0 copy-done
  25.0 0.0 copy-done.3
  25.0 0.0 copy-start.2
  25.0 7.3 %input_grad.1 = bf16[192,2048]{1,0:T(8,128)(2,1)} custom-call(s32[3]{0:T(128)S(1)} %pad_add_fusion.place, bf16[96,3584]{1,0:T(8,128)(2,1)S(1)} %copy-done.3, bf16[96,3584]{1,0:T(8,128)(2,1)S(1)} %collective-permute-done.rest_1_.rest_2_, bf16[2048,3584]{1,0:T(8,128)(2,1)S(1)} %copy-done), custom_call_target="tpu_custom_call" | custom-call | flops 1 | bytes 1 | tf_op jit(solution)/shard_map/input_grad/pallas_call | solution.py:31
  32.3 0.0 copy-done.5
  32.3 4.9 %all-to-all-start = ((bf16[4,48,2048]{2,1,0:T(8,128)(2,1)}), bf16[4,48,2048]{2,1,0:T(8,128)(2,1)S(1)}, u32[]{:S(2)}, u32[]{:S(2)}) async-start(bf16[4,48,2048]{2,1,0:T(8,128)(2,1)} %bitcast.3), calls=%async_computation | async-start | bytes 1572864 | tf_op jit(solution)/shard_map/all_to_all | solution.py:381
  37.2 0.0 collective-permute-done.4.rest_2_
  37.2 0.0 collective-permute-start.5
  37.2 0.0 copy-done.4
  37.2 0.5 collective-permute-start.6
  37.7 0.1 collective-permute-start.7
  37.8 1.1 %collective-permute-done.5.rest_3_ = bf16[384,512]{1,0:T(8,128)(2,1)S(1)} collective-permute-done((bf16[384,512]{1,0:T(8,128)(2,1)S(1)}, bf16[384,512]{1,0:T(8,128)(2,1)S(1)}, u32[]{:S(2)}, u32[]{:S(2)}) %collective-permute-start.5) | collective-permute-done | bytes 393248 | tf_op jit(solution)/shard_map/ppermute | solution.py:300
  38.9 0.0 copy-done.2
  38.9 3.6 %features.1 = (bf16[512,768]{1,0:T(8,128)(2,1)S(1)}, f32[512,3584]{1,0:T(8,128)S(1)}) custom-call(s32[3]{0:T(128)S(1)} %pad_add_fusion.place, bf16[192,2048]{1,0:T(8,128)(2,1)S(1)} %copy-done.2, bf16[192,512]{1,0:T(8,128)(2,1)S(1)} %collective-permute-done.1.rest_1_, bf16[384,512]{1,0:T(8,128)(2,1)S(1)} %collective-permute-done.4.rest_2_, ...), custom_call_target="tpu_custom_call" | custom-call | flops 1 | bytes 1 | tf_op jit(solution)/shard_map/features/pallas_call | solution.py:31
  42.5 0.0 collective-permute-done.8.rest_6_
  42.6 0.2 collective-permute-start.9
  42.8 0.5 collective-permute-start.10
  43.3 0.0 collective-permute-done.6.rest_3_
  43.3 0.0 collective-permute-done.7.rest_5_
  43.3 1.7 %collective-permute-done.9.rest_7_ = bf16[96,3584]{1,0:T(8,128)(2,1)S(1)} collective-permute-done((bf16[96,3584]{1,0:T(8,128)(2,1)}, bf16[96,3584]{1,0:T(8,128)(2,1)S(1)}, u32[]{:S(2)}, u32[]{:S(2)}) %collective-permute-start.9) | collective-permute-done | bytes 688160 | tf_op jit(solution)/shard_map/ppermute | solution.py:300
  45.0 0.0 copy-start.6
  45.0 16.7 %update.1 = (bf16[512,3584]{1,0:T(8,128)(2,1)}, f32[512,3584]{1,0:T(8,128)}, f32[512,3584]{1,0:T(8,128)}) custom-call(s32[3]{0:T(128)S(1)} %pad_add_fusion.place, bf16[512,768]{1,0:T(8,128)(2,1)S(1)} %get-tuple-element.26.x_ref, bf16[96,3584]{1,0:T(8,128)(2,1)} %rest_0_.5, bf16[96,3584]{1,0:T(8,128)(2,1)} %copy-done.7, bf16[96,3584]{1,0:T(8,128)(2,1)} %copy-done.4, ...), custom_call_target="tpu_custom_call" | custom-call | flops 1 | bytes 1 | tf_op jit(solution)/shard_map/update/pallas_call | solution.py:31
  61.7 0.0 all-to-all-done
  61.7 0.0 collective-permute-done.10.rest_1_
  61.7 0.0 copy-done.6
  61.8 1.6 %totals.1 = (bf16[48,2048]{1,0:T(8,128)(2,1)}, bf16[96,3584]{1,0:T(8,128)(2,1)}) custom-call(s32[3]{0:T(128)S(1)} %pad_add_fusion.place, bf16[192,2048]{1,0:T(8,128)(2,1)S(1)} %bitcast.5, bf16[96,3584]{1,0:T(8,128)(2,1)S(1)} %copy-done.6, bf16[96,3584]{1,0:T(8,128)(2,1)S(1)} %collective-permute-done.10.rest_1_), custom_call_target="tpu_custom_call" | custom-call | flops 1 | bytes 1 | tf_op jit(solution)/shard_map/totals/pallas_call | solution.py:31
Async XLA Ops:
  0.6 18.8 %collective-permute-start.2 = (bf16[96,3584]{1,0:T(8,128)(2,1)}, bf16[96,3584]{1,0:T(8,128)(2,1)}, u32[]{:S(2)}, u32[]{:S(2)}) collective-permute-start(bf16[96,3584]{1,0:T(8,128)(2,1)} %rest_0_.5), channel_id=1, source_target_pairs={{0,16},{8,24},{16,0},{24,8},{1,17},{9,25},{17,1},{25,9},{2,18},{10... | collective-permute-start | bytes 2064392 | tf_op jit(solution)/shard_map/ppermute | solution.py:294
  3.6 20.5 %collective-permute-start.3 = (bf16[96,3584]{1,0:T(8,128)(2,1)}, bf16[96,3584]{1,0:T(8,128)(2,1)S(1)}, u32[]{:S(2)}, u32[]{:S(2)}) collective-permute-start(bf16[96,3584]{1,0:T(8,128)(2,1)} %rest_0_.5), channel_id=1, source_target_pairs={{0,8},{8,0},{16,24},{24,16},{1,9},{9,1},{17,25},{25,17},{2,10},{10... | collective-permute-start | bytes 2064392 | tf_op jit(solution)/shard_map/ppermute | solution.py:300
  3.6 20.5 %collective-permute-start = (bf16[96,3584]{1,0:T(8,128)(2,1)}, bf16[96,3584]{1,0:T(8,128)(2,1)S(1)}, u32[]{:S(2)}, u32[]{:S(2)}) collective-permute-start(bf16[96,3584]{1,0:T(8,128)(2,1)} %rest_0_.5), channel_id=1, source_target_pairs={{0,4},{4,0},{1,5},{5,1},{2,6},{6,2},{3,7},{7,3},{8,12},{12,8},{9,1... | collective-permute-start | bytes 2064392 | tf_op jit(solution)/shard_map/ppermute | solution.py:294
  5.2 1.1 %copy-start.1 = (bf16[192,2048]{1,0:T(8,128)(2,1)S(1)}, bf16[192,2048]{1,0:T(8,128)(2,1)}, u32[]{:S(2)}) copy-start(bf16[192,2048]{1,0:T(8,128)(2,1)} %rest_0_.4) | copy-start | bytes 2359300
  6.4 18.6 %copy-start = (bf16[2048,3584]{1,0:T(8,128)(2,1)S(1)}, bf16[2048,3584]{1,0:T(8,128)(2,1)}, u32[]{:S(2)}) copy-start(bf16[2048,3584]{1,0:T(8,128)(2,1)} %rest_8_.1) | copy-start | bytes 44040196
  6.4 18.6 %copy-start.3 = (bf16[96,3584]{1,0:T(8,128)(2,1)S(1)}, bf16[96,3584]{1,0:T(8,128)(2,1)}, u32[]{:S(2)}) copy-start(bf16[96,3584]{1,0:T(8,128)(2,1)} %rest_0_.5) | copy-start | bytes 2064388
  14.0 18.3 %copy-start.5 = (bf16[96,3584]{1,0:T(8,128)(2,1)}, bf16[96,3584]{1,0:T(8,128)(2,1)S(1)}, u32[]{:S(2)}) copy-start(bf16[96,3584]{1,0:T(8,128)(2,1)S(1)} %get-tuple-element.21.rest_0_) | copy-start | bytes 2064388
  19.4 17.8 %collective-permute-start.4 = (bf16[384,512]{1,0:T(8,128)(2,1)}, bf16[384,512]{1,0:T(8,128)(2,1)S(1)}, u32[]{:S(2)}, u32[]{:S(2)}) collective-permute-start(bf16[384,512]{1,0:T(8,128)(2,1)} %get-tuple-element.25), channel_id=1, source_target_pairs={{0,16},{8,24},{16,0},{24,8},{1,17},{9,25},{17,1},{25,9},{2,18},{10... | collective-permute-start | bytes 1179656 | tf_op jit(solution)/shard_map/ppermute | solution.py:294
  21.1 21.4 %collective-permute-start.8 = (bf16[96,3584]{1,0:T(8,128)(2,1)}, bf16[96,3584]{1,0:T(8,128)(2,1)}, u32[]{:S(2)}, u32[]{:S(2)}) collective-permute-start(bf16[96,3584]{1,0:T(8,128)(2,1)} %collective-permute-done.2.rest_4_), channel_id=1, source_target_pairs={{0,4},{4,0},{1,5},{5,1},{2,6},{6,2},{3,7},{7,3},{8,12},{12,8},{9,1... | collective-permute-start | bytes 2064392 | tf_op jit(solution)/shard_map/ppermute | solution.py:294
  22.6 1.4 %collective-permute-start.1 = (bf16[192,512]{1,0:T(8,128)(2,1)S(1)}, bf16[192,512]{1,0:T(8,128)(2,1)S(1)}, u32[]{:S(2)}, u32[]{:S(2)}) collective-permute-start(bf16[192,512]{1,0:T(8,128)(2,1)S(1)} %get-tuple-element.22), channel_id=1, source_target_pairs={{0,8},{8,0},{16,24},{24,16},{1,9},{9,1},{17,25},{25,17},{2,10},{10... | collective-permute-start | bytes 589832 | tf_op jit(solution)/shard_map/ppermute | solution.py:300
  24.1 0.9 %copy-start.7 = (bf16[96,3584]{1,0:T(8,128)(2,1)}, bf16[96,3584]{1,0:T(8,128)(2,1)S(1)}, u32[]{:S(2)}) copy-start(bf16[96,3584]{1,0:T(8,128)(2,1)S(1)} %collective-permute-done.3.rest_1_) | copy-start | bytes 2064388
  25.0 12.2 %copy-start.4 = (bf16[96,3584]{1,0:T(8,128)(2,1)}, bf16[96,3584]{1,0:T(8,128)(2,1)S(1)}, u32[]{:S(2)}) copy-start(bf16[96,3584]{1,0:T(8,128)(2,1)S(1)} %collective-permute-done.rest_1_.rest_2_) | copy-start | bytes 2064388
  25.0 13.9 %copy-start.2 = (bf16[192,2048]{1,0:T(8,128)(2,1)S(1)}, bf16[192,2048]{1,0:T(8,128)(2,1)}, u32[]{:S(2)}) copy-start(bf16[192,2048]{1,0:T(8,128)(2,1)} %rest_0_.4) | copy-start | bytes 2359300
  32.3 29.4 %all-to-all-start = ((bf16[4,48,2048]{2,1,0:T(8,128)(2,1)}), bf16[4,48,2048]{2,1,0:T(8,128)(2,1)S(1)}, u32[]{:S(2)}, u32[]{:S(2)}) async-start(bf16[4,48,2048]{2,1,0:T(8,128)(2,1)} %bitcast.3), calls=%async_computation | async-start | bytes 1572864 | tf_op jit(solution)/shard_map/all_to_all | solution.py:381
  37.2 1.7 %collective-permute-start.5 = (bf16[384,512]{1,0:T(8,128)(2,1)S(1)}, bf16[384,512]{1,0:T(8,128)(2,1)S(1)}, u32[]{:S(2)}, u32[]{:S(2)}) collective-permute-start(bf16[384,512]{1,0:T(8,128)(2,1)S(1)} %collective-permute-done.4.rest_2_), channel_id=1, source_target_pairs={{0,8},{8,0},{16,24},{24,16},{1,9},{9,1},{17,25},{25,17},{2,10},{10... | collective-permute-start | bytes 1179656 | tf_op jit(solution)/shard_map/ppermute | solution.py:300
  37.2 6.1 %collective-permute-start.6 = (bf16[96,3584]{1,0:T(8,128)(2,1)S(1)}, bf16[96,3584]{1,0:T(8,128)(2,1)S(1)}, u32[]{:S(2)}, u32[]{:S(2)}) collective-permute-start(bf16[96,3584]{1,0:T(8,128)(2,1)S(1)} %collective-permute-done.rest_1_.rest_2_), channel_id=1, source_target_pairs={{0,8},{8,0},{16,24},{24,16},{1,9},{9,1},{17,25},{25,17},{2,10},{10... | collective-permute-start | bytes 2064392 | tf_op jit(solution)/shard_map/ppermute | solution.py:300
  37.7 5.6 %collective-permute-start.7 = (bf16[96,3584]{1,0:T(8,128)(2,1)}, bf16[96,3584]{1,0:T(8,128)(2,1)S(1)}, u32[]{:S(2)}, u32[]{:S(2)}) collective-permute-start(bf16[96,3584]{1,0:T(8,128)(2,1)} %collective-permute-done.2.rest_4_), channel_id=1, source_target_pairs={{0,8},{8,0},{16,24},{24,16},{1,9},{9,1},{17,25},{25,17},{2,10},{10... | collective-permute-start | bytes 2064392 | tf_op jit(solution)/shard_map/ppermute | solution.py:300
  42.6 2.4 %collective-permute-start.9 = (bf16[96,3584]{1,0:T(8,128)(2,1)}, bf16[96,3584]{1,0:T(8,128)(2,1)S(1)}, u32[]{:S(2)}, u32[]{:S(2)}) collective-permute-start(bf16[96,3584]{1,0:T(8,128)(2,1)} %collective-permute-done.8.rest_6_), channel_id=1, source_target_pairs={{0,8},{8,0},{16,24},{24,16},{1,9},{9,1},{17,25},{25,17},{2,10},{10... | collective-permute-start | bytes 2064392 | tf_op jit(solution)/shard_map/ppermute | solution.py:300
  42.8 19.0 %collective-permute-start.10 = (bf16[96,3584]{1,0:T(8,128)(2,1)}, bf16[96,3584]{1,0:T(8,128)(2,1)S(1)}, u32[]{:S(2)}, u32[]{:S(2)}) collective-permute-start(bf16[96,3584]{1,0:T(8,128)(2,1)} %get-tuple-element.32), channel_id=1, source_target_pairs={{0,4},{4,0},{1,5},{5,1},{2,6},{6,2},{3,7},{7,3},{8,12},{12,8},{9,1... | collective-permute-start | bytes 2064392 | tf_op jit(solution)/shard_map/ppermute | solution.py:294
  45.0 16.8 %copy-start.6 = (bf16[96,3584]{1,0:T(8,128)(2,1)S(1)}, bf16[96,3584]{1,0:T(8,128)(2,1)}, u32[]{:S(2)}) copy-start(bf16[96,3584]{1,0:T(8,128)(2,1)} %copy-done.5) | copy-start | bytes 2064388

commit v17 on v15

--- a/solution.py
+++ b/solution.py
@@ -336,7 +336,7 @@
     ]
     near = [swap_cores(to_send.pop(0))] if cores == 2 else []
     first = [by_chip[c, 0] for c in range(1, chips)]
-    far = [chip_shift(c)(after(to_send[c - 1], *first)) for c in range(1, chips)]
+    far = [chip_shift(c)(to_send[c - 1]) for c in range(1, chips)]
     for s in range(1, n_row):
         by_row[s] = after(by_row[s], parts[0], *near, *first, *swapped.values())
         if cores == 2:

time: 61.6 us -> 59.6 us (0.968)
  waiting for transfers between devices: 9.83 us -> 8.57 us
  starting transfers between devices: 14.8 us -> 14 us
    ppermute x5, waiting for transfers between devices: 7.86 us -> 6.31 us  [along(): lax.ppermute(a, axis, [(i, (i + shift) % n) for i in range(n)])]
    ppermute x5, starting transfers between devices: 9.3 us -> 8.3 us  [along(): lax.ppermute(a, axis, [(i, (i + shift) % n) for i in range(n)])]
  transfers between devices with their start and end apart: 12 -> 12, of which waited for: 4 -> 3; matrix products, arithmetic and copies ran while one was open for 0% -> 0% of each run, Pallas kernels for 54% -> 56%
where the time goes in v17:
time: 59.6 us; the launch traced here: 59.4 us
  Pallas kernels  34.8 us (58%)
  starting transfers between devices  14 us (23%)
  waiting for transfers between devices  8.57 us (14%)
  local copies, waits for them, and re-layouts  1.17 us (2%)
  between operations  0.76 us (1%)
    pallas_call x5, Pallas kernels, run(): pl.pallas_call(kernel, name=name, grid_spec=pltpu.PrefetchScalarGridSpec(...  34.8 us
    ppermute x5, starting transfers between devices, along(): lax.ppermute(a, axis, [(i, (i + shift) % n) for i in range(n)])  8.3 us
    ppermute x5, waiting for transfers between devices, along(): lax.ppermute(a, axis, [(i, (i + shift) % n) for i in range(n)])  6.31 us
    all_to_all x1, starting transfers between devices, per_device(): gparts = lax.all_to_all(gpart, 'col', 0, 0, tiled=True)  4.87 us
    ppermute x6, waiting for transfers between devices, swap_cores(): return lax.ppermute(a, 'dp', [(i, i ^ 1) for i in range(n_dp)])  2.26 us
  transfers between devices with their start and end apart: 12, of which 3 were waited for; matrix products, arithmetic and copies ran while one was open for 0% of the time, Pallas kernels for 56%

profile of v17, /device:TPU:0, one launch (start us, length us, event | category | flops | bytes accessed | tf_op | source)
XLA Modules:
  0.0 59.4 jit_solution(13187093136461502567)
XLA Ops:
  0.6 3.0 %collective-permute-start.2 = (bf16[96,3584]{1,0:T(8,128)(2,1)}, bf16[96,3584]{1,0:T(8,128)(2,1)}, u32[]{:S(2)}, u32[]{:S(2)}) collective-permute-start(bf16[96,3584]{1,0:T(8,128)(2,1)} %rest_0_.5), channel_id=1, source_target_pairs={{0,16},{8,24},{16,0},{24,8},{1,17},{9,25},{17,1},{25,9},{2,18},{10... | collective-permute-start | bytes 2064392 | tf_op jit(solution)/shard_map/ppermute | solution.py:287
  3.6 0.0 collective-permute-start.3
  3.6 1.5 %collective-permute-start = (bf16[96,3584]{1,0:T(8,128)(2,1)}, bf16[96,3584]{1,0:T(8,128)(2,1)S(1)}, u32[]{:S(2)}, u32[]{:S(2)}) collective-permute-start(bf16[96,3584]{1,0:T(8,128)(2,1)} %rest_0_.5), channel_id=1, source_target_pairs={{0,4},{4,0},{1,5},{5,1},{2,6},{6,2},{3,7},{7,3},{8,12},{12,8},{9,1... | collective-permute-start | bytes 2064392 | tf_op jit(solution)/shard_map/ppermute | solution.py:287
  5.2 0.1 pad_add_fusion.place
  5.2 0.0 copy-start.1
  5.2 1.1 %copy-done.1 = bf16[192,2048]{1,0:T(8,128)(2,1)S(1)} copy-done((bf16[192,2048]{1,0:T(8,128)(2,1)S(1)}, bf16[192,2048]{1,0:T(8,128)(2,1)}, u32[]{:S(2)}) %copy-start.1) | copy-done | bytes 786456
  6.4 0.0 copy-start
  6.4 0.0 copy-start.3
  6.4 6.9 %forward.1 = (bf16[96,3584]{1,0:T(8,128)(2,1)S(1)}, bf16[96,3584]{1,0:T(8,128)(2,1)S(1)}, bf16[192,512]{1,0:T(8,128)(2,1)S(1)}, bf16[384,512]{1,0:T(8,128)(2,1)}) custom-call(s32[3]{0:T(128)S(1)} %pad_add_fusion.place, bf16[192,2048]{1,0:T(8,128)(2,1)S(1)} %copy-done.1, bf16[2048,3584]{1,0:T(8,128)(2,1)} %rest_8_.1), custom_call_target="tpu_custom_call" | custom-call | flops 1 | bytes 1 | tf_op jit(solution)/shard_map/forward/pallas_call | solution.py:31
  13.3 0.0 copy-start.5
  13.3 0.6 %collective-permute-start.4 = (bf16[384,512]{1,0:T(8,128)(2,1)}, bf16[384,512]{1,0:T(8,128)(2,1)S(1)}, u32[]{:S(2)}, u32[]{:S(2)}) collective-permute-start(bf16[384,512]{1,0:T(8,128)(2,1)} %get-tuple-element.21), channel_id=1, source_target_pairs={{0,16},{8,24},{16,0},{24,8},{1,17},{9,25},{17,1},{25,9},{2,18},{10... | collective-permute-start | bytes 1179656 | tf_op jit(solution)/shard_map/ppermute | solution.py:287
  13.9 0.0 collective-permute-start.1
  13.9 6.3 %collective-permute-done.2.rest_4_ = bf16[96,3584]{1,0:T(8,128)(2,1)} collective-permute-done((bf16[96,3584]{1,0:T(8,128)(2,1)}, bf16[96,3584]{1,0:T(8,128)(2,1)}, u32[]{:S(2)}, u32[]{:S(2)}) %collective-permute-start.2) | collective-permute-done | bytes 688160 | tf_op jit(solution)/shard_map/ppermute | solution.py:287
  20.2 2.1 %collective-permute-start.8 = (bf16[96,3584]{1,0:T(8,128)(2,1)}, bf16[96,3584]{1,0:T(8,128)(2,1)}, u32[]{:S(2)}, u32[]{:S(2)}) collective-permute-start(bf16[96,3584]{1,0:T(8,128)(2,1)} %collective-permute-done.2.rest_4_), channel_id=1, source_target_pairs={{0,4},{4,0},{1,5},{5,1},{2,6},{6,2},{3,7},{7,3},{8,12},{12,8},{9,1... | collective-permute-start | bytes 2064392 | tf_op jit(solution)/shard_map/ppermute | solution.py:287
  22.3 0.0 collective-permute-done.1.rest_1_
  22.3 0.0 collective-permute-done.3.rest_1_
  22.3 0.0 copy-start.7
  22.3 0.0 collective-permute-done.rest_1_.rest_2_
  22.3 0.0 copy-start.4
  22.3 0.0 copy-done
  22.3 0.0 copy-done.3
  22.4 0.0 copy-start.2
  22.4 7.3 %input_grad.1 = bf16[192,2048]{1,0:T(8,128)(2,1)} custom-call(s32[3]{0:T(128)S(1)} %pad_add_fusion.place, bf16[96,3584]{1,0:T(8,128)(2,1)S(1)} %copy-done.3, bf16[96,3584]{1,0:T(8,128)(2,1)S(1)} %collective-permute-done.rest_1_.rest_2_, bf16[2048,3584]{1,0:T(8,128)(2,1)S(1)} %copy-done), custom_call_target="tpu_custom_call" | custom-call | flops 1 | bytes 1 | tf_op jit(solution)/shard_map/input_grad/pallas_call | solution.py:31
  29.7 0.0 copy-done.5
  29.7 0.0 copy-done.7
  29.7 4.9 %all-to-all-start = ((bf16[4,48,2048]{2,1,0:T(8,128)(2,1)}), bf16[4,48,2048]{2,1,0:T(8,128)(2,1)S(1)}, u32[]{:S(2)}, u32[]{:S(2)}) async-start(bf16[4,48,2048]{2,1,0:T(8,128)(2,1)} %bitcast.3), calls=%async_computation | async-start | bytes 1572864 | tf_op jit(solution)/shard_map/all_to_all | solution.py:372
  34.6 0.0 collective-permute-done.4.rest_2_
  34.6 0.0 collective-permute-start.5
  34.6 0.0 copy-done.4
  34.6 0.5 collective-permute-start.6
  35.1 0.1 collective-permute-start.7
  35.2 1.1 %collective-permute-done.5.rest_3_ = bf16[384,512]{1,0:T(8,128)(2,1)S(1)} collective-permute-done((bf16[384,512]{1,0:T(8,128)(2,1)S(1)}, bf16[384,512]{1,0:T(8,128)(2,1)S(1)}, u32[]{:S(2)}, u32[]{:S(2)}) %collective-permute-start.5) | collective-permute-done | bytes 393248 | tf_op jit(solution)/shard_map/ppermute | solution.py:293
  36.3 0.0 copy-done.2
  36.3 0.9 %features.1.x_ref = bf16[512,768]{1,0:T(8,128)(2,1)S(1)} custom-call(s32[3]{0:T(128)S(1)} %pad_add_fusion.place, bf16[192,2048]{1,0:T(8,128)(2,1)S(1)} %copy-done.2, bf16[192,512]{1,0:T(8,128)(2,1)S(1)} %collective-permute-done.1.rest_1_, bf16[384,512]{1,0:T(8,128)(2,1)S(1)} %collective-permute-done.4.rest_2_, ...), custom_call_target="tpu_custom_call" | custom-call | flops 1 | bytes 1 | tf_op jit(solution)/shard_map/features/pallas_call | solution.py:31
  37.2 0.0 collective-permute-done.8.rest_6_
  37.2 0.2 collective-permute-start.9
  37.4 0.0 copy-start.6
  37.4 1.1 %collective-permute-start.10 = (bf16[96,3584]{1,0:T(8,128)(2,1)S(1)}, bf16[96,3584]{1,0:T(8,128)(2,1)S(1)}, u32[]{:S(2)}, u32[]{:S(2)}) collective-permute-start(bf16[96,3584]{1,0:T(8,128)(2,1)S(1)} %get-tuple-element.26), channel_id=1, source_target_pairs={{0,4},{4,0},{1,5},{5,1},{2,6},{6,2},{3,7},{7,3},{8,12},{12,8},{9,1... | collective-permute-start | bytes 2064392 | tf_op jit(solution)/shard_map/ppermute | solution.py:287
  38.5 0.0 collective-permute-done.6.rest_3_
  38.5 0.0 collective-permute-done.7.rest_5_
  38.5 1.1 %collective-permute-done.9.rest_7_ = bf16[96,3584]{1,0:T(8,128)(2,1)S(1)} collective-permute-done((bf16[96,3584]{1,0:T(8,128)(2,1)}, bf16[96,3584]{1,0:T(8,128)(2,1)S(1)}, u32[]{:S(2)}, u32[]{:S(2)}) %collective-permute-start.9) | collective-permute-done | bytes 688160 | tf_op jit(solution)/shard_map/ppermute | solution.py:293
  39.6 18.1 %update.1 = (bf16[512,3584]{1,0:T(8,128)(2,1)}, f32[512,3584]{1,0:T(8,128)}, f32[512,3584]{1,0:T(8,128)}) custom-call(s32[3]{0:T(128)S(1)} %pad_add_fusion.place, bf16[512,768]{1,0:T(8,128)(2,1)S(1)} %features.1.x_ref, bf16[96,3584]{1,0:T(8,128)(2,1)} %rest_0_.5, bf16[96,3584]{1,0:T(8,128)(2,1)} %copy-done.7, bf16[96,3584]{1,0:T(8,128)(2,1)} %copy-done.4, ...), custom_call_target="tpu_custom_call" | custom-call | flops 1 | bytes 1 | tf_op jit(solution)/shard_map/update/pallas_call | solution.py:31
  57.7 0.0 all-to-all-done
  57.7 0.0 collective-permute-done.10.rest_1_
  57.7 0.0 copy-done.6
  57.7 1.6 %totals.1 = (bf16[48,2048]{1,0:T(8,128)(2,1)}, bf16[96,3584]{1,0:T(8,128)(2,1)}) custom-call(s32[3]{0:T(128)S(1)} %pad_add_fusion.place, bf16[192,2048]{1,0:T(8,128)(2,1)S(1)} %bitcast.5, bf16[96,3584]{1,0:T(8,128)(2,1)S(1)} %copy-done.6, bf16[96,3584]{1,0:T(8,128)(2,1)S(1)} %collective-permute-done.10.rest_1_), custom_call_target="tpu_custom_call" | custom-call | flops 1 | bytes 1 | tf_op jit(solution)/shard_map/totals/pallas_call | solution.py:31
Async XLA Ops:
  0.6 19.6 %collective-permute-start.2 = (bf16[96,3584]{1,0:T(8,128)(2,1)}, bf16[96,3584]{1,0:T(8,128)(2,1)}, u32[]{:S(2)}, u32[]{:S(2)}) collective-permute-start(bf16[96,3584]{1,0:T(8,128)(2,1)} %rest_0_.5), channel_id=1, source_target_pairs={{0,16},{8,24},{16,0},{24,8},{1,17},{9,25},{17,1},{25,9},{2,18},{10... | collective-permute-start | bytes 2064392 | tf_op jit(solution)/shard_map/ppermute | solution.py:287
  3.6 18.7 %collective-permute-start.3 = (bf16[96,3584]{1,0:T(8,128)(2,1)}, bf16[96,3584]{1,0:T(8,128)(2,1)S(1)}, u32[]{:S(2)}, u32[]{:S(2)}) collective-permute-start(bf16[96,3584]{1,0:T(8,128)(2,1)} %rest_0_.5), channel_id=1, source_target_pairs={{0,8},{8,0},{16,24},{24,16},{1,9},{9,1},{17,25},{25,17},{2,10},{10... | collective-permute-start | bytes 2064392 | tf_op jit(solution)/shard_map/ppermute | solution.py:293
  3.6 18.7 %collective-permute-start = (bf16[96,3584]{1,0:T(8,128)(2,1)}, bf16[96,3584]{1,0:T(8,128)(2,1)S(1)}, u32[]{:S(2)}, u32[]{:S(2)}) collective-permute-start(bf16[96,3584]{1,0:T(8,128)(2,1)} %rest_0_.5), channel_id=1, source_target_pairs={{0,4},{4,0},{1,5},{5,1},{2,6},{6,2},{3,7},{7,3},{8,12},{12,8},{9,1... | collective-permute-start | bytes 2064392 | tf_op jit(solution)/shard_map/ppermute | solution.py:287
  5.2 1.1 %copy-start.1 = (bf16[192,2048]{1,0:T(8,128)(2,1)S(1)}, bf16[192,2048]{1,0:T(8,128)(2,1)}, u32[]{:S(2)}) copy-start(bf16[192,2048]{1,0:T(8,128)(2,1)} %rest_0_.4) | copy-start | bytes 2359300
  6.4 16.0 %copy-start = (bf16[2048,3584]{1,0:T(8,128)(2,1)S(1)}, bf16[2048,3584]{1,0:T(8,128)(2,1)}, u32[]{:S(2)}) copy-start(bf16[2048,3584]{1,0:T(8,128)(2,1)} %rest_8_.1) | copy-start | bytes 44040196
  6.4 16.0 %copy-start.3 = (bf16[96,3584]{1,0:T(8,128)(2,1)S(1)}, bf16[96,3584]{1,0:T(8,128)(2,1)}, u32[]{:S(2)}) copy-start(bf16[96,3584]{1,0:T(8,128)(2,1)} %rest_0_.5) | copy-start | bytes 2064388
  13.3 16.4 %copy-start.5 = (bf16[96,3584]{1,0:T(8,128)(2,1)}, bf16[96,3584]{1,0:T(8,128)(2,1)S(1)}, u32[]{:S(2)}) copy-start(bf16[96,3584]{1,0:T(8,128)(2,1)S(1)} %get-tuple-element.18.rest_0_) | copy-start | bytes 2064388
  13.3 21.3 %collective-permute-start.4 = (bf16[384,512]{1,0:T(8,128)(2,1)}, bf16[384,512]{1,0:T(8,128)(2,1)S(1)}, u32[]{:S(2)}, u32[]{:S(2)}) collective-permute-start(bf16[384,512]{1,0:T(8,128)(2,1)} %get-tuple-element.21), channel_id=1, source_target_pairs={{0,16},{8,24},{16,0},{24,8},{1,17},{9,25},{17,1},{25,9},{2,18},{10... | collective-permute-start | bytes 1179656 | tf_op jit(solution)/shard_map/ppermute | solution.py:287
  13.9 8.4 %collective-permute-start.1 = (bf16[192,512]{1,0:T(8,128)(2,1)S(1)}, bf16[192,512]{1,0:T(8,128)(2,1)S(1)}, u32[]{:S(2)}, u32[]{:S(2)}) collective-permute-start(bf16[192,512]{1,0:T(8,128)(2,1)S(1)} %get-tuple-element.19), channel_id=1, source_target_pairs={{0,8},{8,0},{16,24},{24,16},{1,9},{9,1},{17,25},{25,17},{2,10},{10... | collective-permute-start | bytes 589832 | tf_op jit(solution)/shard_map/ppermute | solution.py:293
  20.2 17.0 %collective-permute-start.8 = (bf16[96,3584]{1,0:T(8,128)(2,1)}, bf16[96,3584]{1,0:T(8,128)(2,1)}, u32[]{:S(2)}, u32[]{:S(2)}) collective-permute-start(bf16[96,3584]{1,0:T(8,128)(2,1)} %collective-permute-done.2.rest_4_), channel_id=1, source_target_pairs={{0,4},{4,0},{1,5},{5,1},{2,6},{6,2},{3,7},{7,3},{8,12},{12,8},{9,1... | collective-permute-start | bytes 2064392 | tf_op jit(solution)/shard_map/ppermute | solution.py:287
  22.3 7.4 %copy-start.7 = (bf16[96,3584]{1,0:T(8,128)(2,1)}, bf16[96,3584]{1,0:T(8,128)(2,1)S(1)}, u32[]{:S(2)}) copy-start(bf16[96,3584]{1,0:T(8,128)(2,1)S(1)} %collective-permute-done.3.rest_1_) | copy-start | bytes 2064388
  22.3 12.3 %copy-start.4 = (bf16[96,3584]{1,0:T(8,128)(2,1)}, bf16[96,3584]{1,0:T(8,128)(2,1)S(1)}, u32[]{:S(2)}) copy-start(bf16[96,3584]{1,0:T(8,128)(2,1)S(1)} %collective-permute-done.rest_1_.rest_2_) | copy-start | bytes 2064388
  22.4 14.0 %copy-start.2 = (bf16[192,2048]{1,0:T(8,128)(2,1)S(1)}, bf16[192,2048]{1,0:T(8,128)(2,1)}, u32[]{:S(2)}) copy-start(bf16[192,2048]{1,0:T(8,128)(2,1)} %rest_0_.4) | copy-start | bytes 2359300
  29.7 28.0 %all-to-all-start = ((bf16[4,48,2048]{2,1,0:T(8,128)(2,1)}), bf16[4,48,2048]{2,1,0:T(8,128)(2,1)S(1)}, u32[]{:S(2)}, u32[]{:S(2)}) async-start(bf16[4,48,2048]{2,1,0:T(8,128)(2,1)} %bitcast.3), calls=%async_computation | async-start | bytes 1572864 | tf_op jit(solution)/shard_map/all_to_all | solution.py:372
  34.6 1.7 %collective-permute-start.5 = (bf16[384,512]{1,0:T(8,128)(2,1)S(1)}, bf16[384,512]{1,0:T(8,128)(2,1)S(1)}, u32[]{:S(2)}, u32[]{:S(2)}) collective-permute-start(bf16[384,512]{1,0:T(8,128)(2,1)S(1)} %collective-permute-done.4.rest_2_), channel_id=1, source_target_pairs={{0,8},{8,0},{16,24},{24,16},{1,9},{9,1},{17,25},{25,17},{2,10},{10... | collective-permute-start | bytes 1179656 | tf_op jit(solution)/shard_map/ppermute | solution.py:293
  34.6 3.9 %collective-permute-start.6 = (bf16[96,3584]{1,0:T(8,128)(2,1)S(1)}, bf16[96,3584]{1,0:T(8,128)(2,1)S(1)}, u32[]{:S(2)}, u32[]{:S(2)}) collective-permute-start(bf16[96,3584]{1,0:T(8,128)(2,1)S(1)} %collective-permute-done.rest_1_.rest_2_), channel_id=1, source_target_pairs={{0,8},{8,0},{16,24},{24,16},{1,9},{9,1},{17,25},{25,17},{2,10},{10... | collective-permute-start | bytes 2064392 | tf_op jit(solution)/shard_map/ppermute | solution.py:293
  35.1 3.4 %collective-permute-start.7 = (bf16[96,3584]{1,0:T(8,128)(2,1)}, bf16[96,3584]{1,0:T(8,128)(2,1)S(1)}, u32[]{:S(2)}, u32[]{:S(2)}) collective-permute-start(bf16[96,3584]{1,0:T(8,128)(2,1)} %collective-permute-done.2.rest_4_), channel_id=1, source_target_pairs={{0,8},{8,0},{16,24},{24,16},{1,9},{9,1},{17,25},{25,17},{2,10},{10... | collective-permute-start | bytes 2064392 | tf_op jit(solution)/shard_map/ppermute | solution.py:293
  37.2 2.4 %collective-permute-start.9 = (bf16[96,3584]{1,0:T(8,128)(2,1)}, bf16[96,3584]{1,0:T(8,128)(2,1)S(1)}, u32[]{:S(2)}, u32[]{:S(2)}) collective-permute-start(bf16[96,3584]{1,0:T(8,128)(2,1)} %collective-permute-done.8.rest_6_), channel_id=1, source_target_pairs={{0,8},{8,0},{16,24},{24,16},{1,9},{9,1},{17,25},{25,17},{2,10},{10... | collective-permute-start | bytes 2064392 | tf_op jit(solution)/shard_map/ppermute | solution.py:293
  37.4 20.3 %copy-start.6 = (bf16[96,3584]{1,0:T(8,128)(2,1)S(1)}, bf16[96,3584]{1,0:T(8,128)(2,1)}, u32[]{:S(2)}) copy-start(bf16[96,3584]{1,0:T(8,128)(2,1)} %copy-done.5) | copy-start | bytes 2064388
  37.4 20.3 %collective-permute-start.10 = (bf16[96,3584]{1,0:T(8,128)(2,1)S(1)}, bf16[96,3584]{1,0:T(8,128)(2,1)S(1)}, u32[]{:S(2)}, u32[]{:S(2)}) collective-permute-start(bf16[96,3584]{1,0:T(8,128)(2,1)S(1)} %get-tuple-element.26), channel_id=1, source_target_pairs={{0,4},{4,0},{1,5},{5,1},{2,6},{6,2},{3,7},{7,3},{8,12},{12,8},{9,1... | collective-permute-start | bytes 2064392 | tf_op jit(solution)/shard_map/ppermute | solution.py:287
